TPU v7x, 32 devices: a whole 2x2x4 slice. The times are simulated.
32 devices in a mesh: grp: 2 (over y), sp: 4 (over x, core), ch: 4 (over z).
Axes of the slice: x: 2, y: 2, z: 4, core: 2. Of those that a mesh axis runs over, the one named last changes fastest.
Arguments:
- features: bfloat16 [256, 8, 640], P('ch', ('grp', 'sp')), parts along dimension 1, may hold values from -6 to 6
- weights: bfloat16 [27, 256, 256], P(None, 'ch'), may hold values from -0.109375 to 0.109375
- cotangent: bfloat16 [256, 8, 640], P('ch', ('grp', 'sp')), parts along dimension 1, may hold values from -6 to 6
Outputs:
- output: float32 [256, 8, 640], P('ch', ('grp', 'sp')), parts along dimension 1
- input_grad: float32 [256, 8, 640], P('ch', ('grp', 'sp')), parts along dimension 1
- weight_grad: float32 [54, 256, 256], P('grp', 'ch', 'sp'), parts along dimension 0
There are 2 independent parts, one for each index of `grp`. A program takes and returns all parts, laid end to end along the dimension named above; an argument that names none is the same for every part. Nothing has to cross between parts.
All inputs are finite; a program needn't handle non-finite values.
Results may differ from a plain program's by a relative error of at most 0.0003.
Values may be sent and summed in bfloat16 or wider, within the bound.
No kernel may reach another device: no remote copies, remote signals or barrier semaphores. Data moves between devices by JAX's collectives and lax.ppermute only.
A program may use at most 64 MiB of HBM per device.

v0:
```python
import math

import jax
import jax.numpy as jnp
from jax import lax
from jax.sharding import PartitionSpec as P

NX = 64
NY = 10


def extended(array, sides, width):
    for axis, dim in sides:
        count, length = (lax.axis_size(axis), array.shape[dim])
        up = [(i, (i + 1) % count) for i in range(count - 1)]
        down = [(j, i) for i, j in up]
        last = lax.slice_in_dim(array, length - width, length, axis=dim)
        leading = lax.slice_in_dim(array, 0, width, axis=dim)
        before = lax.ppermute(last, axis, up)
        after = lax.ppermute(leading, axis, down)
        array = jnp.concatenate([before, array, after], axis=dim)
    return array


def pad_plane(block, rows, cols):
    count = block.shape[0]
    depth_all = block.shape[1]
    shaped = block.reshape(count, depth_all, rows, cols)
    return jnp.pad(shaped, ((0, 0), (0, 0), (1, 1), (1, 1)))


def moved_block(padded, dz, dy, dx, depth, rows, cols):
    count = padded.shape[0]
    part = padded[:, 1 + dz : 1 + dz + depth, 1 + dy : 1 + dy + rows, 1 + dx : 1 + dx + cols]
    return part.reshape(count, depth * rows * cols)


def offsets_of(tap):
    return (tap // 9 - 1, tap // 3 % 3 - 1, tap % 3 - 1)


def per_device(features, weights, cotangent):
    blocks, depth, plane = features.shape
    rows = NY
    cols = NX
    cells = depth * plane
    flat_grad = cotangent.reshape(blocks, cells)
    zfeat = extended(features, (("sp", 1),), 1)
    start_total = jnp.zeros((blocks, cells), jnp.float32)
    total = start_total
    padded = pad_plane(lax.all_gather(zfeat, "ch", axis=0, tiled=True), rows, cols)
    grads = []
    for fold_tap in range(27):
        fold_dz, fold_dy, fold_dx = offsets_of(fold_tap)
        moved = moved_block(padded, fold_dz, fold_dy, fold_dx, depth, rows, cols)
        total = total + jnp.dot(weights[fold_tap], moved, preferred_element_type=jnp.float32)
        grads.append(
            lax.dot_general(
                flat_grad, moved, (((1,), (1,)), ((), ())), preferred_element_type=jnp.float32
            )
        )
    filt = jnp.stack(grads)
    total, filt = (total, filt)
    output = total.reshape(blocks, depth, plane)
    zgrad = extended(cotangent, (("sp", 1),), 1)
    everyone = lax.all_gather(zgrad, "ch", axis=0, tiled=True)
    mine = lax.all_to_all(weights, "ch", split_axis=2, concat_axis=1, tiled=True)
    padded_all = pad_plane(everyone, rows, cols)
    acc = jnp.zeros((blocks, cells), jnp.float32)
    for tap in range(27):
        dz, dy, dx = offsets_of(tap)
        opposite = moved_block(padded_all, -dz, -dy, -dx, depth, rows, cols)
        acc = acc + lax.dot_general(
            mine[tap], opposite, (((0,), (0,)), ((), ())), preferred_element_type=jnp.float32
        )
    back = acc.reshape(blocks, depth, plane)
    factor = 1.0 / math.sqrt(lax.axis_size("sp") * depth * plane)
    weight_grad = lax.psum_scatter(filt * factor, "sp", scatter_dimension=2, tiled=True)
    return (output, back, weight_grad)


def solution(mesh):
    return jax.shard_map(
        per_device,
        mesh=mesh,
        in_specs=(P("ch", ("grp", "sp"), None), P(None, "ch", None), P("ch", ("grp", "sp"), None)),
        out_specs=(
            P("ch", ("grp", "sp"), None),
            P("ch", ("grp", "sp"), None),
            P("grp", "ch", "sp"),
        ),
        check_vma=False,
    )
```

profile of v0, /device:TPU:0, one launch (start us, length us, event | category | flops | bytes accessed | tf_op | source)
XLA Modules:
  0.0 187.0 jit_solution(1002184061052205875)
XLA Ops:
  7.2 2.4 %collective-permute-start = (bf16[64,1,640]{2,0,1:T(8,128)(2,1)}, bf16[64,1,640]{2,0,1:T(8,128)(2,1)S(1)}, u32[]{:S(2)}, u32[]{:S(2)}) collective-permute-start(bf16[64,1,640]{2,0,1:T(8,128)(2,1)} %param.3), channel_id=1, source_target_pairs={{0,4},{4,8},{8,12},{1,5},{5,9},{9,13},{2,6},{6,10},{10,14},{3,7},{... | collective-permute-start | bytes 245768 | tf_op jit(solution)/shard_map/ppermute | solution.py:19
  9.5 1.3 collective-permute-start.1
  10.8 1.3 collective-permute-start.3
  12.1 5.8 %collective-permute-start.2 = (bf16[64,1,640]{2,0,1:T(8,128)(2,1)}, bf16[64,1,640]{2,0,1:T(8,128)(2,1)S(1)}, u32[]{:S(2)}, u32[]{:S(2)}) collective-permute-start(bf16[64,1,640]{2,0,1:T(8,128)(2,1)} %param.5), channel_id=1, source_target_pairs={{0,4},{4,8},{8,12},{1,5},{5,9},{9,13},{2,6},{6,10},{10,14},{3,7},{... | collective-permute-start | bytes 245768 | tf_op jit(solution)/shard_map/ppermute | solution.py:19
  17.9 3.9 %copy.19 = bf16[27,64,256]{1,0,2:T(8,128)(2,1)S(1)} copy(bf16[27,64,256]{2,1,0:T(8,128)(2,1)} %param.4) | data formatting | bytes 1769472 | tf_op args[1]
  21.8 2.4 %reshape.298 = bf16[4,2,55296]{2,1,0:T(2,128)(2,1)} reshape(bf16[256,27,64]{2,1,0:T(8,128)(2,1)S(1)} %bitcast.622) | data formatting | bytes 1769472
  24.2 4.9 %all-to-all-start = ((bf16[4,2,55296]{2,1,0:T(2,128)(2,1)}), bf16[4,2,55296]{2,1,0:T(2,128)(2,1)}, u32[]{:S(2)}, u32[]{:S(2)}) async-start(bf16[4,2,55296]{2,1,0:T(2,128)(2,1)} %reshape.298), calls=%async_computation | async-start | bytes 1769472 | tf_op jit(solution)/shard_map/all_to_all | solution.py:67
  29.2 39.0 %all_gather.6 = bf16[256,3,640]{2,0,1:T(8,128)(2,1)S(1)} all-gather(bf16[64,3,640]{2,0,1:T(8,128)(2,1)S(1)} %pad_maximum_fusion), channel_id=1, replica_groups=mesh['grp'=2,'sp'=4,'ch'=4] {'ch'}, dimensions={0}, use_global_device_ids=true | all-gather | bytes 1228800 | tf_op jit(solution)/shard_map/all_gather | solution.py:51
  68.8 1.5 fusion.136
  70.4 3.1 %pad_slice_fusion.32 = (bf16[256,1,10,64]{0,3,2,1:T(8,128)(2,1)}, bf16[256,1,10,64]{0,3,2,1:T(8,128)(2,1)}, bf16[256,1,10,64]{0,3,2,1:T(8,128)(2,1)}, bf16[256,1...) fusion(bf16[256,3,10,64]{0,3,2,1:T(8,128)(2,1)S(1)} %bitcast.620), kind=kLoop, calls=%fused_computation.33 | loop fusion | bytes 7208960 | tf_op jit(solution)/shard_map/slice | solution.py:34
  73.8 0.8 fusion.50
  74.6 20.8 %all_gather.7 = bf16[256,3,640]{2,0,1:T(8,128)(2,1)S(1)} all-gather(bf16[64,3,640]{2,0,1:T(8,128)(2,1)S(1)} %pad_maximum_fusion.1), channel_id=1, replica_groups=mesh['grp'=2,'sp'=4,'ch'=4] {'ch'}, dimensions={0}, use_global_device_ids=true | all-gather | bytes 1228800 | tf_op jit(solution)/shard_map/all_gather | solution.py:66
  96.1 1.3 convolution_bitcast_fusion.13
  97.4 1.3 convolution_bitcast_fusion.12
  98.6 1.2 convolution_bitcast_fusion.11
  100.3 0.8 fusion.49
  101.6 0.8 fusion.48
  102.4 0.8 fusion.47
  103.7 0.8 fusion.46
  104.5 0.8 fusion.45
  105.8 0.8 fusion.44
  106.6 0.8 fusion.43
  107.9 0.8 fusion.42
  108.7 0.8 fusion.41
  110.0 0.8 fusion.40
  110.8 0.8 fusion.39
  112.1 0.8 fusion.38
  112.9 0.8 fusion.37
  114.2 0.8 fusion.36
  115.0 0.8 fusion.35
  116.2 0.8 fusion.34
  117.3 0.8 fusion.33
  118.1 0.8 fusion.32
  119.1 0.8 fusion.31
  120.2 0.8 fusion.30
  121.2 0.8 fusion.29
  122.0 0.8 fusion.28
  122.8 0.8 fusion.27
  123.6 0.8 fusion.26
  124.7 0.8 copy.21
  126.5 4.5 %copy.23 = f32[27,64,256]{1,0,2:T(8,128)} copy(f32[27,64,256]{2,1,0:T(8,128)S(1)} %broadcast_multiply_fusion) | data formatting | bytes 3538944
  131.0 4.7 %reshape.296 = f32[256,1728]{1,0:T(8,128)} reshape(f32[256,27,64]{2,1,0:T(8,128)} %bitcast.616) | data formatting | bytes 3538944
  135.7 2.9 %pad_slice_fusion.8 = (bf16[256,1,10,64]{0,3,2,1:T(8,128)(2,1)}, bf16[256,1,10,64]{0,3,2,1:T(8,128)(2,1)}, bf16[256,1,10,64]{0,3,2,1:T(8,128)(2,1)}, bf16[256,1,...) fusion(bf16[256,3,10,64]{0,3,2,1:T(8,128)(2,1)S(1)} %bitcast.617), kind=kLoop, calls=%fused_computation.9 | loop fusion | bytes 7208960 | tf_op jit(solution)/shard_map/slice | solution.py:34
  138.6 1.6 fusion.135
  140.2 3.6 %reshape.299 = bf16[256,27,64]{2,1,0:T(8,128)(2,1)S(1)} reshape(bf16[4,2,55296]{2,1,0:T(2,128)(2,1)} %all-to-all-done) | data formatting | bytes 1769472
  143.8 1.4 copy.26
  145.2 0.8 fusion.134
  147.4 0.7 squeeze.196
  148.1 1.6 squeeze.195
  151.8 0.7 squeeze.191
  153.3 0.7 squeeze.189
  154.0 0.7 squeeze.215
  154.7 0.7 squeeze.214
  156.2 0.7 squeeze.212
  156.9 0.7 squeeze.211
  161.9 0.7 squeeze.203
  162.6 0.7 squeeze.202
  166.2 0.7 squeeze.197
  166.9 1.2 convolution_bitcast_fusion.3
  168.2 1.0 convolution_bitcast_fusion.2
  169.2 1.0 convolution_bitcast_fusion.1
  176.4 0.8 copy.22
  177.2 1.4 reshape.297
  178.7 1.5 copy.24
  (230 shorter events, 25.8 us)
Async XLA Ops:
  7.2 21.9 %collective-permute-start = (bf16[64,1,640]{2,0,1:T(8,128)(2,1)}, bf16[64,1,640]{2,0,1:T(8,128)(2,1)S(1)}, u32[]{:S(2)}, u32[]{:S(2)}) collective-permute-start(bf16[64,1,640]{2,0,1:T(8,128)(2,1)} %param.3), channel_id=1, source_target_pairs={{0,4},{4,8},{8,12},{1,5},{5,9},{9,13},{2,6},{6,10},{10,14},{3,7},{... | collective-permute-start | bytes 245768 | tf_op jit(solution)/shard_map/ppermute | solution.py:19
  9.5 19.6 %collective-permute-start.1 = (bf16[64,1,640]{2,0,1:T(8,128)(2,1)}, bf16[64,1,640]{2,0,1:T(8,128)(2,1)S(1)}, u32[]{:S(2)}, u32[]{:S(2)}) collective-permute-start(bf16[64,1,640]{2,0,1:T(8,128)(2,1)} %param.3), channel_id=1, source_target_pairs={{4,0},{8,4},{12,8},{5,1},{9,5},{13,9},{6,2},{10,6},{14,10},{7,3},{... | collective-permute-start | bytes 245768 | tf_op jit(solution)/shard_map/ppermute | solution.py:20
  10.8 63.7 %collective-permute-start.3 = (bf16[64,1,640]{2,0,1:T(8,128)(2,1)}, bf16[64,1,640]{2,0,1:T(8,128)(2,1)S(1)}, u32[]{:S(2)}, u32[]{:S(2)}) collective-permute-start(bf16[64,1,640]{2,0,1:T(8,128)(2,1)} %param.5), channel_id=1, source_target_pairs={{4,0},{8,4},{12,8},{5,1},{9,5},{13,9},{6,2},{10,6},{14,10},{7,3},{... | collective-permute-start | bytes 245768 | tf_op jit(solution)/shard_map/ppermute | solution.py:20
  12.1 62.4 %collective-permute-start.2 = (bf16[64,1,640]{2,0,1:T(8,128)(2,1)}, bf16[64,1,640]{2,0,1:T(8,128)(2,1)S(1)}, u32[]{:S(2)}, u32[]{:S(2)}) collective-permute-start(bf16[64,1,640]{2,0,1:T(8,128)(2,1)} %param.5), channel_id=1, source_target_pairs={{0,4},{4,8},{8,12},{1,5},{5,9},{9,13},{2,6},{6,10},{10,14},{3,7},{... | collective-permute-start | bytes 245768 | tf_op jit(solution)/shard_map/ppermute | solution.py:19
  21.8 7.3 %copy-start.74 = (bf16[64,1,640]{2,0,1:T(8,128)(2,1)S(1)}, bf16[64,1,640]{2,0,1:T(8,128)(2,1)}, u32[]{:S(2)}) copy-start(bf16[64,1,640]{2,0,1:T(8,128)(2,1)} %param.3) | copy-start | bytes 245764
  24.2 116.0 %all-to-all-start = ((bf16[4,2,55296]{2,1,0:T(2,128)(2,1)}), bf16[4,2,55296]{2,1,0:T(2,128)(2,1)}, u32[]{:S(2)}, u32[]{:S(2)}) async-start(bf16[4,2,55296]{2,1,0:T(2,128)(2,1)} %reshape.298), calls=%async_computation | async-start | bytes 1769472 | tf_op jit(solution)/shard_map/all_to_all | solution.py:67
  29.1 148.1 %reduce-scatter.4.cloned.1.call-start = ((), (), s32[]{:S(2)}) async-start(), calls=%async_computation.2 | async-start | bytes 2293760
  70.4 3.1 %copy-start.1 = (bf16[27,64,256]{2,1,0:T(8,128)(2,1)S(1)}, bf16[27,64,256]{2,1,0:T(8,128)(2,1)}, u32[]{:S(2)}) copy-start(bf16[27,64,256]{2,1,0:T(8,128)(2,1)} %param.4) | copy-start | bytes 2654212
  70.4 3.4 %copy-start = (bf16[64,1,640]{2,0,1:T(8,128)(2,1)S(1)}, bf16[64,1,640]{2,0,1:T(8,128)(2,1)}, u32[]{:S(2)}) copy-start(bf16[64,1,640]{2,0,1:T(8,128)(2,1)} %param.5) | copy-start | bytes 245764
  96.1 3.8 %copy-start.22 = (bf16[256,1,10,64]{0,3,2,1:T(8,128)(2,1)S(1)}, bf16[256,1,10,64]{0,3,2,1:T(8,128)(2,1)}, u32[]{:S(2)}) copy-start(bf16[256,1,10,64]{0,3,2,1:T(8,128)(2,1)} %get-tuple-element.89) | copy-start | bytes 983044
  96.1 4.0 %copy-start.26 = (bf16[256,1,10,64]{0,3,2,1:T(8,128)(2,1)S(1)}, bf16[256,1,10,64]{0,3,2,1:T(8,128)(2,1)}, u32[]{:S(2)}) copy-start(bf16[256,1,10,64]{0,3,2,1:T(8,128)(2,1)} %get-tuple-element.90) | copy-start | bytes 983044
  96.1 4.2 %copy-start.14 = (bf16[256,1,10,64]{0,3,2,1:T(8,128)(2,1)S(1)}, bf16[256,1,10,64]{0,3,2,1:T(8,128)(2,1)}, u32[]{:S(2)}) copy-start(bf16[256,1,10,64]{0,3,2,1:T(8,128)(2,1)} %get-tuple-element.67) | copy-start | bytes 983044
  97.4 4.0 %copy-start.13 = (bf16[256,1,10,64]{0,3,2,1:T(8,128)(2,1)S(1)}, bf16[256,1,10,64]{0,3,2,1:T(8,128)(2,1)}, u32[]{:S(2)}) copy-start(bf16[256,1,10,64]{0,3,2,1:T(8,128)(2,1)} %get-tuple-element.68) | copy-start | bytes 983044
  99.8 2.6 %copy-start.12 = (bf16[256,1,10,64]{0,3,2,1:T(8,128)(2,1)S(1)}, bf16[256,1,10,64]{0,3,2,1:T(8,128)(2,1)}, u32[]{:S(2)}) copy-start(bf16[256,1,10,64]{0,3,2,1:T(8,128)(2,1)} %get-tuple-element.69) | copy-start | bytes 983044
  100.3 3.1 %copy-start.21 = (bf16[256,1,10,64]{0,3,2,1:T(8,128)(2,1)S(1)}, bf16[256,1,10,64]{0,3,2,1:T(8,128)(2,1)}, u32[]{:S(2)}) copy-start(bf16[256,1,10,64]{0,3,2,1:T(8,128)(2,1)} %get-tuple-element.91) | copy-start | bytes 983044
  101.4 3.1 %copy-start.11 = (bf16[256,1,10,64]{0,3,2,1:T(8,128)(2,1)S(1)}, bf16[256,1,10,64]{0,3,2,1:T(8,128)(2,1)}, u32[]{:S(2)}) copy-start(bf16[256,1,10,64]{0,3,2,1:T(8,128)(2,1)} %get-tuple-element.70) | copy-start | bytes 983044
  102.4 3.1 %copy-start.10 = (bf16[256,1,10,64]{0,3,2,1:T(8,128)(2,1)S(1)}, bf16[256,1,10,64]{0,3,2,1:T(8,128)(2,1)}, u32[]{:S(2)}) copy-start(bf16[256,1,10,64]{0,3,2,1:T(8,128)(2,1)} %get-tuple-element.71) | copy-start | bytes 983044
  103.5 3.1 %copy-start.9 = (bf16[256,1,10,64]{0,3,2,1:T(8,128)(2,1)S(1)}, bf16[256,1,10,64]{0,3,2,1:T(8,128)(2,1)}, u32[]{:S(2)}) copy-start(bf16[256,1,10,64]{0,3,2,1:T(8,128)(2,1)} %get-tuple-element.72) | copy-start | bytes 983044
  104.5 3.1 %copy-start.8 = (bf16[256,1,10,64]{0,3,2,1:T(8,128)(2,1)S(1)}, bf16[256,1,10,64]{0,3,2,1:T(8,128)(2,1)}, u32[]{:S(2)}) copy-start(bf16[256,1,10,64]{0,3,2,1:T(8,128)(2,1)} %get-tuple-element.73) | copy-start | bytes 983044
  105.6 3.2 %copy-start.7 = (bf16[256,1,10,64]{0,3,2,1:T(8,128)(2,1)S(1)}, bf16[256,1,10,64]{0,3,2,1:T(8,128)(2,1)}, u32[]{:S(2)}) copy-start(bf16[256,1,10,64]{0,3,2,1:T(8,128)(2,1)} %get-tuple-element.74) | copy-start | bytes 983044
  106.6 3.1 %copy-start.6 = (bf16[256,1,10,64]{0,3,2,1:T(8,128)(2,1)S(1)}, bf16[256,1,10,64]{0,3,2,1:T(8,128)(2,1)}, u32[]{:S(2)}) copy-start(bf16[256,1,10,64]{0,3,2,1:T(8,128)(2,1)} %get-tuple-element.75) | copy-start | bytes 983044
  107.6 3.1 %copy-start.5 = (bf16[256,1,10,64]{0,3,2,1:T(8,128)(2,1)S(1)}, bf16[256,1,10,64]{0,3,2,1:T(8,128)(2,1)}, u32[]{:S(2)}) copy-start(bf16[256,1,10,64]{0,3,2,1:T(8,128)(2,1)} %get-tuple-element.76) | copy-start | bytes 983044
  108.7 3.1 %copy-start.4 = (bf16[256,1,10,64]{0,3,2,1:T(8,128)(2,1)S(1)}, bf16[256,1,10,64]{0,3,2,1:T(8,128)(2,1)}, u32[]{:S(2)}) copy-start(bf16[256,1,10,64]{0,3,2,1:T(8,128)(2,1)} %get-tuple-element.77) | copy-start | bytes 983044
  109.7 3.1 %copy-start.20 = (bf16[256,1,10,64]{0,3,2,1:T(8,128)(2,1)S(1)}, bf16[256,1,10,64]{0,3,2,1:T(8,128)(2,1)}, u32[]{:S(2)}) copy-start(bf16[256,1,10,64]{0,3,2,1:T(8,128)(2,1)} %get-tuple-element.85) | copy-start | bytes 983044
  110.8 3.1 %copy-start.3 = (bf16[256,1,10,64]{0,3,2,1:T(8,128)(2,1)S(1)}, bf16[256,1,10,64]{0,3,2,1:T(8,128)(2,1)}, u32[]{:S(2)}) copy-start(bf16[256,1,10,64]{0,3,2,1:T(8,128)(2,1)} %get-tuple-element.78) | copy-start | bytes 983044
  111.8 3.1 %copy-start.2 = (bf16[256,1,10,64]{0,3,2,1:T(8,128)(2,1)S(1)}, bf16[256,1,10,64]{0,3,2,1:T(8,128)(2,1)}, u32[]{:S(2)}) copy-start(bf16[256,1,10,64]{0,3,2,1:T(8,128)(2,1)} %get-tuple-element.79) | copy-start | bytes 983044
  113.9 3.1 %copy-start.18 = (bf16[256,1,10,64]{0,3,2,1:T(8,128)(2,1)S(1)}, bf16[256,1,10,64]{0,3,2,1:T(8,128)(2,1)}, u32[]{:S(2)}) copy-start(bf16[256,1,10,64]{0,3,2,1:T(8,128)(2,1)} %get-tuple-element.81) | copy-start | bytes 983044
  114.2 3.1 %copy-start.19 = (bf16[256,1,10,64]{0,3,2,1:T(8,128)(2,1)S(1)}, bf16[256,1,10,64]{0,3,2,1:T(8,128)(2,1)}, u32[]{:S(2)}) copy-start(bf16[256,1,10,64]{0,3,2,1:T(8,128)(2,1)} %get-tuple-element.66) | copy-start | bytes 983044
  115.8 3.1 %copy-start.17 = (bf16[256,1,10,64]{0,3,2,1:T(8,128)(2,1)S(1)}, bf16[256,1,10,64]{0,3,2,1:T(8,128)(2,1)}, u32[]{:S(2)}) copy-start(bf16[256,1,10,64]{0,3,2,1:T(8,128)(2,1)} %get-tuple-element.82) | copy-start | bytes 983044
  116.0 3.9 %copy-start.16 = (bf16[256,1,10,64]{0,3,2,1:T(8,128)(2,1)S(1)}, bf16[256,1,10,64]{0,3,2,1:T(8,128)(2,1)}, u32[]{:S(2)}) copy-start(bf16[256,1,10,64]{0,3,2,1:T(8,128)(2,1)} %get-tuple-element.83) | copy-start | bytes 983044
  117.0 3.9 %copy-start.15 = (bf16[256,1,10,64]{0,3,2,1:T(8,128)(2,1)S(1)}, bf16[256,1,10,64]{0,3,2,1:T(8,128)(2,1)}, u32[]{:S(2)}) copy-start(bf16[256,1,10,64]{0,3,2,1:T(8,128)(2,1)} %get-tuple-element.84) | copy-start | bytes 983044
  118.9 3.9 %copy-start.25 = (bf16[256,1,10,64]{0,3,2,1:T(8,128)(2,1)S(1)}, bf16[256,1,10,64]{0,3,2,1:T(8,128)(2,1)}, u32[]{:S(2)}) copy-start(bf16[256,1,10,64]{0,3,2,1:T(8,128)(2,1)} %get-tuple-element.86) | copy-start | bytes 983044
  119.1 4.5 %copy-start.24 = (bf16[256,1,10,64]{0,3,2,1:T(8,128)(2,1)S(1)}, bf16[256,1,10,64]{0,3,2,1:T(8,128)(2,1)}, u32[]{:S(2)}) copy-start(bf16[256,1,10,64]{0,3,2,1:T(8,128)(2,1)} %get-tuple-element.87) | copy-start | bytes 983044
  122.8 2.7 %copy-start.23 = (bf16[256,1,10,64]{0,3,2,1:T(8,128)(2,1)S(1)}, bf16[256,1,10,64]{0,3,2,1:T(8,128)(2,1)}, u32[]{:S(2)}) copy-start(bf16[256,1,10,64]{0,3,2,1:T(8,128)(2,1)} %get-tuple-element.88) | copy-start | bytes 983044
  124.4 1.5 copy-start.27
  146.6 21.5 %copy-start.49 = (bf16[256,1,10,64]{0,3,2,1:T(8,128)(2,1)S(1)}, bf16[256,1,10,64]{0,3,2,1:T(8,128)(2,1)}, u32[]{:S(2)}) copy-start(bf16[256,1,10,64]{0,3,2,1:T(8,128)(2,1)} %get-tuple-element.60) | copy-start | bytes 983044
  148.1 21.1 %copy-start.48 = (bf16[256,1,10,64]{0,3,2,1:T(8,128)(2,1)S(1)}, bf16[256,1,10,64]{0,3,2,1:T(8,128)(2,1)}, u32[]{:S(2)}) copy-start(bf16[256,1,10,64]{0,3,2,1:T(8,128)(2,1)} %get-tuple-element.61) | copy-start | bytes 983044
  153.3 17.0 %copy-start.47 = (bf16[256,1,10,64]{0,3,2,1:T(8,128)(2,1)S(1)}, bf16[256,1,10,64]{0,3,2,1:T(8,128)(2,1)}, u32[]{:S(2)}) copy-start(bf16[256,1,10,64]{0,3,2,1:T(8,128)(2,1)} %get-tuple-element.62) | copy-start | bytes 983044
  156.9 13.6 %copy-start.46 = (bf16[256,1,10,64]{0,3,2,1:T(8,128)(2,1)S(1)}, bf16[256,1,10,64]{0,3,2,1:T(8,128)(2,1)}, u32[]{:S(2)}) copy-start(bf16[256,1,10,64]{0,3,2,1:T(8,128)(2,1)} %get-tuple-element.63) | copy-start | bytes 983044
  160.5 10.3 %copy-start.45 = (bf16[256,1,10,64]{0,3,2,1:T(8,128)(2,1)S(1)}, bf16[256,1,10,64]{0,3,2,1:T(8,128)(2,1)}, u32[]{:S(2)}) copy-start(bf16[256,1,10,64]{0,3,2,1:T(8,128)(2,1)} %get-tuple-element.65) | copy-start | bytes 983044
  164.0 7.0 %copy-start.41 = (bf16[256,1,10,64]{0,3,2,1:T(8,128)(2,1)S(1)}, bf16[256,1,10,64]{0,3,2,1:T(8,128)(2,1)}, u32[]{:S(2)}) copy-start(bf16[256,1,10,64]{0,3,2,1:T(8,128)(2,1)} %get-tuple-element.54) | copy-start | bytes 983044
  164.7 5.5 %copy-start.54 = (bf16[256,64]{0,1:T(8,128)(2,1)S(1)}, bf16[256,64]{0,1:T(8,128)(2,1)}, u32[]{:S(2)}) copy-start(bf16[256,64]{0,1:T(8,128)(2,1)} %squeeze.215) | copy-start | bytes 98308
  164.7 6.0 %copy-start.52 = (bf16[256,64]{0,1:T(8,128)(2,1)S(1)}, bf16[256,64]{0,1:T(8,128)(2,1)}, u32[]{:S(2)}) copy-start(bf16[256,64]{0,1:T(8,128)(2,1)} %squeeze.189) | copy-start | bytes 98308
  166.2 4.3 %copy-start.56 = (bf16[256,64]{0,1:T(8,128)(2,1)S(1)}, bf16[256,64]{0,1:T(8,128)(2,1)}, u32[]{:S(2)}) copy-start(bf16[256,64]{0,1:T(8,128)(2,1)} %squeeze.211) | copy-start | bytes 98308
  166.2 4.8 %copy-start.57 = (bf16[256,64]{0,1:T(8,128)(2,1)S(1)}, bf16[256,64]{0,1:T(8,128)(2,1)}, u32[]{:S(2)}) copy-start(bf16[256,64]{0,1:T(8,128)(2,1)} %squeeze.207) | copy-start | bytes 98308
  166.9 4.4 %copy-start.40 = (bf16[256,1,10,64]{0,3,2,1:T(8,128)(2,1)S(1)}, bf16[256,1,10,64]{0,3,2,1:T(8,128)(2,1)}, u32[]{:S(2)}) copy-start(bf16[256,1,10,64]{0,3,2,1:T(8,128)(2,1)} %get-tuple-element.55) | copy-start | bytes 983044
  166.9 4.4 %copy-start.55 = (bf16[256,64]{0,1:T(8,128)(2,1)S(1)}, bf16[256,64]{0,1:T(8,128)(2,1)}, u32[]{:S(2)}) copy-start(bf16[256,64]{0,1:T(8,128)(2,1)} %squeeze.208) | copy-start | bytes 98308
  168.1 3.4 %copy-start.39 = (bf16[256,1,10,64]{0,3,2,1:T(8,128)(2,1)S(1)}, bf16[256,1,10,64]{0,3,2,1:T(8,128)(2,1)}, u32[]{:S(2)}) copy-start(bf16[256,1,10,64]{0,3,2,1:T(8,128)(2,1)} %get-tuple-element.56) | copy-start | bytes 983044
  168.2 3.4 %copy-start.53 = (bf16[256,64]{0,1:T(8,128)(2,1)S(1)}, bf16[256,64]{0,1:T(8,128)(2,1)}, u32[]{:S(2)}) copy-start(bf16[256,64]{0,1:T(8,128)(2,1)} %squeeze.209) | copy-start | bytes 98308
  169.2 2.6 %copy-start.37 = (bf16[256,1,10,64]{0,3,2,1:T(8,128)(2,1)S(1)}, bf16[256,1,10,64]{0,3,2,1:T(8,128)(2,1)}, u32[]{:S(2)}) copy-start(bf16[256,1,10,64]{0,3,2,1:T(8,128)(2,1)} %get-tuple-element.40) | copy-start | bytes 983044
  169.2 2.6 %copy-start.71 = (bf16[256,64]{0,1:T(8,128)(2,1)S(1)}, bf16[256,64]{0,1:T(8,128)(2,1)}, u32[]{:S(2)}) copy-start(bf16[256,64]{0,1:T(8,128)(2,1)} %squeeze.190) | copy-start | bytes 98308
  170.5 1.5 copy-start.36
  170.5 1.5 copy-start.69
  170.8 1.6 copy-start.35
  170.8 1.6 copy-start.67
  171.0 1.5 copy-start.38
  171.0 1.5 copy-start.51
  171.3 1.5 copy-start.44
  171.3 1.5 copy-start.65
  171.8 1.3 copy-start.34
  171.8 1.3 copy-start.63
  172.0 1.3 copy-start.33
  172.0 1.3 copy-start.61
  172.8 1.3 copy-start.72
  (17 other events, 21.8 us)
Sparse Core Ops, SparseCore 0:
  135.8 28.9 reduce-scatter.3
where the time goes:
time: 188 us; the launch traced here: 187 us
  blocking collectives  59.8 us (32%)
  local copies, waits for them, and re-layouts  57.9 us (31%)
  matrix products  38.6 us (21%)
  starting transfers between devices  15.6 us (8%)
  between operations  14.8 us (8%)
    all_gather x1, blocking collectives, per_device(): lax.all_gather(zfeat, 'ch', axis=0, tiled=True)  39 us
    unnamed x159, local copies, waits for them, and re-layouts  24.3 us
    all_gather x1, blocking collectives, per_device(): everyone = lax.all_gather(zgrad, 'ch', axis=0, tiled=True)  20.8 us
    dot_general x27, matrix products, per_device(): lax.dot_general(flat_grad, moved, (((1,), (1,)), ((), ())), preferred_ele...  20.5 us
    squeeze x27, local copies, waits for them, and re-layouts, per_device(): mine[tap]  20.2 us
    dot_general x27, matrix products, per_device(): jnp.dot(weights[fold_tap], moved, preferred_element_type=jnp.float32)  9.24 us
    slice x4, local copies, waits for them, and re-layouts, moved_block(): padded[:, 1 + dz:1 + dz + depth, 1 + dy:1 + dy + rows, 1 + dx:1 + dx + cols]  9.18 us
    dot_general x27, matrix products, per_device(): lax.dot_general(mine[tap], opposite, (((0,), (0,)), ((), ())), preferred_...  8.82 us
  transfers between devices with their start and end apart: 6, of which 0 were waited for; matrix products, arithmetic and copies ran while one was open for 50% of the time, Pallas kernels for 0%

commit v1 on v0

v1 whole, which is shorter than its diff:
```python
import functools
import math

import jax
import jax.numpy as jnp
from jax import lax
from jax.experimental import pallas as pl
from jax.experimental.pallas import tpu as pltpu
from jax.sharding import PartitionSpec as P

NX = 64
NY = 10
CELLS = NX * NY
F32 = jnp.float32
BF16 = jnp.bfloat16
VMEM_BYTES = 48 * 1024 * 1024


def cell_mask(rows, dy, dx):
    q = lax.broadcasted_iota(jnp.int32, (rows, CELLS), 1)
    x = q % NX + dx
    y = q // NX + dy
    return (x >= 0) & (x < NX) & (y >= 0) & (y < NY)


def shifted(value, dy, dx):
    if dy == 0 and dx == 0:
        return value
    moved = pltpu.roll(value, (-(dy * NX + dx)) % CELLS, 1)
    return jnp.where(cell_mask(value.shape[0], dy, dx), moved, 0.0)


def input_grad_kernel(nz, pos_ref, cot_all_ref, w_ref, part_ref, cols_ref):
    blocks = cot_all_ref.shape[1]
    s = pos_ref[0]
    for dz in (-1, 0, 1):
        source = s - dz
        inside = (source >= 0) & (source < nz)
        plane = cot_all_ref[jnp.clip(source, 0, nz - 1)].astype(F32)
        plane = jnp.where(inside, plane, 0.0)
        for dy in (-1, 0, 1):
            for dx in (-1, 0, 1):
                tap = 9 * (dz + 1) + 3 * (dy + 1) + dx + 1
                cols_ref[tap * blocks : (tap + 1) * blocks, :] = shifted(plane, -dy, -dx).astype(BF16)
    part_ref[...] = lax.dot_general(
        w_ref[...], cols_ref[...], (((0,), (0,)), ((), ())), preferred_element_type=F32
    )


def output_kernel(nz, scale, fm_ref, f0_ref, fp_ref, w_ref, cot_all_ref, fblk_ref, out_ref, wg_ref):
    blocks = cot_all_ref.shape[1]
    cols = fblk_ref.shape[1]
    taps = 9 * blocks
    acc = None
    for dz, ref in ((-1, fm_ref), (0, f0_ref), (1, fp_ref)):
        term = jnp.dot(
            w_ref[(dz + 1) * taps : (dz + 2) * taps, :], ref[...], preferred_element_type=F32
        )
        acc = term if acc is None else acc + term
    total = None
    for dx in (-1, 0, 1):
        for dy in (-1, 0, 1):
            at = (3 * (dy + 1) + dx + 1) * blocks
            term = shifted(acc[at : at + blocks], dy, dx)
            total = term if total is None else total + term
    out_ref[:, 0, :] = total

    cots = []
    feats = []
    for z in range(nz):
        plane = cot_all_ref[z].astype(F32)
        cots.append([shifted(plane, -dy, 0).astype(BF16) for dy in (-1, 0, 1)])
        field = fblk_ref[z].astype(F32)
        feats.append(jnp.concatenate([shifted(field, 0, dx).astype(BF16) for dx in (-1, 0, 1)], 0))
    for dz in (-1, 0, 1):
        sums = None
        for z in range(nz):
            if 0 <= z - dz < nz:
                term = lax.dot_general(
                    jnp.concatenate(cots[z - dz], 0),
                    feats[z],
                    (((1,), (1,)), ((), ())),
                    preferred_element_type=F32,
                )
                sums = term if sums is None else sums + term
        if sums is None:
            sums = jnp.zeros((3 * blocks, 3 * cols), F32)
        sums = sums * scale
        for dy in range(3):
            for dx in range(3):
                tap = 9 * (dz + 1) + 3 * dy + dx
                wg_ref[tap] = sums[dy * blocks : (dy + 1) * blocks, dx * cols : (dx + 1) * cols]


def per_device(features, weights, cotangent):
    blocks, depth, plane = features.shape
    channels = weights.shape[2]
    nz = lax.axis_size("sp")
    cols = channels // nz
    w2 = weights.reshape(27 * blocks, channels)
    feat = features.reshape(blocks, plane)
    cot = cotangent.reshape(blocks, plane)

    cot_all = lax.all_gather(cot, "sp", axis=0)
    f_all = lax.all_gather(feat, "ch", axis=0, tiled=True)
    pos = lax.axis_index("sp").astype(jnp.int32).reshape(1)

    vmem = pl.BlockSpec(memory_space=pltpu.VMEM)
    smem = pl.BlockSpec(memory_space=pltpu.SMEM)
    params = pltpu.CompilerParams(vmem_limit_bytes=VMEM_BYTES)
    part = pl.pallas_call(
        functools.partial(input_grad_kernel, nz),
        out_shape=jax.ShapeDtypeStruct((channels, plane), F32),
        in_specs=[smem, vmem, vmem],
        out_specs=vmem,
        scratch_shapes=[pltpu.VMEM((27 * blocks, plane), BF16)],
        compiler_params=params,
        cost_estimate=pl.CostEstimate(
            flops=2 * 27 * blocks * channels * plane, bytes_accessed=2000000, transcendentals=0
        ),
        name="input_grad",
    )(pos, cot_all, w2)
    back = lax.psum_scatter(part, "ch", scatter_dimension=0, tiled=True)

    up = [(i, i + 1) for i in range(nz - 1)]
    down = [(i + 1, i) for i in range(nz - 1)]
    before = lax.ppermute(f_all, "sp", up)
    after = lax.ppermute(f_all, "sp", down)
    fblk = lax.all_to_all(f_all.reshape(nz, cols, plane), "sp", 0, 0)

    scale = 1.0 / math.sqrt(nz * depth * plane)
    output, weight_grad = pl.pallas_call(
        functools.partial(output_kernel, nz, scale),
        out_shape=(
            jax.ShapeDtypeStruct((blocks, 1, plane), F32),
            jax.ShapeDtypeStruct((27, blocks, cols), F32),
        ),
        in_specs=[vmem] * 6,
        out_specs=(vmem, vmem),
        compiler_params=params,
        cost_estimate=pl.CostEstimate(
            flops=4 * 27 * blocks * channels * plane, bytes_accessed=4000000, transcendentals=0
        ),
        name="output_and_weight_grad",
    )(before, f_all, after, w2, cot_all, fblk)
    return (output, back.reshape(blocks, depth, plane), weight_grad)


def solution(mesh):
    return jax.shard_map(
        per_device,
        mesh=mesh,
        in_specs=(P("ch", ("grp", "sp"), None), P(None, "ch", None), P("ch", ("grp", "sp"), None)),
        out_specs=(
            P("ch", ("grp", "sp"), None),
            P("ch", ("grp", "sp"), None),
            P("grp", "ch", "sp"),
        ),
        check_vma=False,
    )
```

time: 188 us -> 62.5 us (0.33)
  local copies, waits for them, and re-layouts: 57.9 us -> 2.92 us
  matrix products: 38.6 us -> 0 us
  blocking collectives: 59.8 us -> 37.9 us
  starting transfers between devices: 15.6 us -> 2.63 us
  Pallas kernels: 0 us -> 4.74 us
    dot_general x81 -> x0, matrix products: 38.6 us -> none  [the longest x27 20.5 us: per_device(): lax.dot_general(flat_grad, moved, (((1,), (1,)), ((), ())), preferred_ele...]
    all_gather x2, blocking collectives: 59.8 us -> 24.9 us  [the longest x1 17.2 us: per_device(): f_all = lax.all_gather(feat, 'ch', axis=0, tiled=True)]
    unnamed x159 -> x7, local copies, waits for them, and re-layouts: 24.3 us -> 2.92 us
    squeeze x27 -> x0, local copies, waits for them, and re-layouts: 20.2 us -> none  [per_device(): mine[tap]]
    all_to_all x0 -> x1, blocking collectives: none -> 12.9 us  [per_device(): fblk = lax.all_to_all(f_all.reshape(nz, cols, plane), 'sp', 0, 0)]
    slice x6 -> x0, local copies, waits for them, and re-layouts: 10.6 us -> none  [the longest x4 9.18 us: moved_block(): padded[:, 1 + dz:1 + dz + depth, 1 + dy:1 + dy + rows, 1 + dx:1 + dx + cols]]
    ppermute x4 -> x2, starting transfers between devices: 10.7 us -> 2.59 us  [the longest x1 1.3 us: per_device(): before = lax.ppermute(f_all, 'sp', up)]
    all_to_all x1 -> x0, starting transfers between devices: 4.87 us -> none  [per_device(): lax.all_to_all(weights, 'ch', split_axis=2, concat_axis=1, tiled=True)]
  transfers between devices with their start and end apart: 6 -> 3, of which waited for: 0 -> 0; matrix products, arithmetic and copies ran while one was open for 50% -> 0% of each run, Pallas kernels for 0% -> 4%
where the time goes in v1:
time: 62.5 us; the launch traced here: 62.2 us
  blocking collectives  37.9 us (61%)
  between operations  14.1 us (23%)
  Pallas kernels  4.74 us (8%)
  local copies, waits for them, and re-layouts  2.92 us (5%)
  starting transfers between devices  2.63 us (4%)
    all_gather x1, blocking collectives, per_device(): f_all = lax.all_gather(feat, 'ch', axis=0, tiled=True)  17.2 us
    all_to_all x1, blocking collectives, per_device(): fblk = lax.all_to_all(f_all.reshape(nz, cols, plane), 'sp', 0, 0)  12.9 us
    all_gather x1, blocking collectives, per_device(): cot_all = lax.all_gather(cot, 'sp', axis=0)  7.76 us
    unnamed x7, local copies, waits for them, and re-layouts  2.92 us
    pallas_call x1, Pallas kernels, per_device(): pl.pallas_call(functools.partial(output_kernel, nz, scale), out_shape=(ja...  2.7 us
    pallas_call x1, Pallas kernels, per_device(): pl.pallas_call(functools.partial(input_grad_kernel, nz), out_shape=jax.Sh...  2.04 us
    ppermute x1, starting transfers between devices, per_device(): before = lax.ppermute(f_all, 'sp', up)  1.3 us
    ppermute x1, starting transfers between devices, per_device(): after = lax.ppermute(f_all, 'sp', down)  1.29 us
  transfers between devices with their start and end apart: 3, of which 0 were waited for; matrix products, arithmetic and copies ran while one was open for 0% of the time, Pallas kernels for 4%

profile of v1, /device:TPU:0, one launch (start us, length us, event | category | flops | bytes accessed | tf_op | source)
XLA Modules:
  0.0 62.2 jit_solution(12493629703046916892)
XLA Ops:
  7.2 0.0 reduce-scatter.2.cloned.1.call-start
  7.2 7.8 %all-gather.1 = bf16[256,1,640]{2,0,1:T(8,128)(2,1)S(1)} all-gather(bf16[64,1,640]{2,0,1:T(8,128)(2,1)} %param.5), channel_id=3, replica_groups=mesh['grp'=2,'sp'=4,'ch'=4] {'sp'}, dimensions={0}, use_global_device_ids=true | all-gather | bytes 409600 | tf_op jit(solution)/shard_map/all_gather | solution.py:104
  15.0 0.0 copy-start
  15.0 1.2 %copy-done = bf16[27,64,256]{2,1,0:T(8,128)(2,1)S(1)} copy-done((bf16[27,64,256]{2,1,0:T(8,128)(2,1)S(1)}, bf16[27,64,256]{2,1,0:T(8,128)(2,1)}, u32[]{:S(2)}) %copy-start) | copy-done | bytes 884760
  16.1 0.0 copy-start.2
  16.1 2.0 %input_grad.1 = f32[256,640]{1,0:T(8,128)} custom-call(s32[1]{0:T(128)} %bitcast.4.pos_ref, bf16[4,64,640]{2,1,0:T(8,128)(2,1)S(1)} %bitcast.10, bf16[1728,256]{1,0:T(8,128)(2,1)S(1)} %bitcast.12), custom_call_target="tpu_custom_call" | custom-call | flops 566231040 | bytes 2000000 | tf_op jit(solution)/shard_map/input_grad/pallas_call | solution.py:111
  18.2 0.0 copy-start.1
  18.2 0.0 reduce-scatter.2.cloned.1.call-update
  18.2 0.0 copy-done.2
  18.2 17.2 %all-gather = bf16[256,1,640]{2,0,1:T(8,128)(2,1)S(1)} all-gather(bf16[64,1,640]{2,0,1:T(8,128)(2,1)S(1)} %copy-done.2), channel_id=2, replica_groups=mesh['grp'=2,'sp'=4,'ch'=4] {'ch'}, dimensions={0}, use_global_device_ids=true | all-gather | bytes 409600 | tf_op jit(solution)/shard_map/all_gather | solution.py:105
  35.4 1.3 %collective-permute-start = (bf16[256,640]{1,0:T(8,128)(2,1)S(1)}, bf16[256,640]{1,0:T(8,128)(2,1)S(1)}, u32[]{:S(2)}, u32[]{:S(2)}) collective-permute-start(bf16[256,640]{1,0:T(8,128)(2,1)S(1)} %bitcast.6), channel_id=1, source_target_pairs={{0,4},{4,8},{8,12},{1,5},{5,9},{9,13},{2,6},{6,10},{10,14},{3,7},{... | collective-permute-start | bytes 983048 | tf_op jit(solution)/shard_map/ppermute | solution.py:127
  36.7 1.3 %collective-permute-start.1 = (bf16[256,640]{1,0:T(8,128)(2,1)S(1)}, bf16[256,640]{1,0:T(8,128)(2,1)S(1)}, u32[]{:S(2)}, u32[]{:S(2)}) collective-permute-start(bf16[256,640]{1,0:T(8,128)(2,1)S(1)} %bitcast.7), channel_id=1, source_target_pairs={{4,0},{8,4},{12,8},{5,1},{9,5},{13,9},{6,2},{10,6},{14,10},{7,3},{... | collective-permute-start | bytes 983048 | tf_op jit(solution)/shard_map/ppermute | solution.py:128
  38.0 12.9 %all_to_all.5.fblk_ref = bf16[4,64,640]{2,1,0:T(8,128)(2,1)S(1)} all-to-all(bf16[4,64,640]{2,1,0:T(8,128)(2,1)S(1)} %bitcast.8), channel_id=1, replica_groups=mesh['grp'=2,'sp'=4,'ch'=4] {'sp'}, dimensions={0} | all-to-all | bytes 655360 | tf_op jit(solution)/shard_map/all_to_all | solution.py:129
  50.9 0.0 collective-permute-done.fm_ref
  50.9 0.0 collective-permute-done.1.fp_ref
  50.9 0.0 copy-done.1
  51.0 2.7 %output_and_weight_grad.1 = (f32[64,1,640]{2,1,0:T(1,128)}, f32[27,64,64]{2,1,0:T(8,128)}) custom-call(bf16[256,640]{1,0:T(8,128)(2,1)S(1)} %collective-permute-done.fm_ref, bf16[256,640]{1,0:T(8,128)(2,1)S(1)} %bitcast.9, bf16[256,640]{1,0:T(8,128)(2,1)S(1)} %collective-permute-done.1.fp_ref, bf16[1728,256]{1,0:T(8,128)(2,1)S(1)} %bitcast.13, ...), custom_call_target="tpu_custom_call" | custom-call | flops 1132462080 | bytes 4000000 | tf_op jit(solution)/shard_map/output_and_weight_grad/pallas_call | solution.py:132
  53.6 0.0 reduce-scatter.2.cloned.1.call-done
  53.7 1.8 %copy.6 = f32[64,1,640]{2,1,0:T(1,128)} copy(f32[64,1,640]{2,0,1:T(8,128)} %bitcast.14) | data formatting | bytes 327680
Async XLA Ops:
  7.2 46.5 %reduce-scatter.2.cloned.1.call-start = ((), (), s32[]{:S(2)}) async-start(), calls=%async_computation.2 | async-start | bytes 819200 | tf_op jit(solution)/shard_map/reduce_scatter | solution.py:123
  15.0 1.2 %copy-start = (bf16[27,64,256]{2,1,0:T(8,128)(2,1)S(1)}, bf16[27,64,256]{2,1,0:T(8,128)(2,1)}, u32[]{:S(2)}) copy-start(bf16[27,64,256]{2,1,0:T(8,128)(2,1)} %param.4) | copy-start | bytes 2654212
  16.1 2.1 %copy-start.2 = (bf16[64,1,640]{2,0,1:T(8,128)(2,1)S(1)}, bf16[64,1,640]{2,0,1:T(8,128)(2,1)}, u32[]{:S(2)}) copy-start(bf16[64,1,640]{2,0,1:T(8,128)(2,1)} %param.3) | copy-start | bytes 245764
  18.2 32.8 %copy-start.1 = (bf16[27,64,256]{2,1,0:T(8,128)(2,1)S(1)}, bf16[27,64,256]{2,1,0:T(8,128)(2,1)}, u32[]{:S(2)}) copy-start(bf16[27,64,256]{2,1,0:T(8,128)(2,1)} %param.4) | copy-start | bytes 2654212
  35.4 15.6 %collective-permute-start = (bf16[256,640]{1,0:T(8,128)(2,1)S(1)}, bf16[256,640]{1,0:T(8,128)(2,1)S(1)}, u32[]{:S(2)}, u32[]{:S(2)}) collective-permute-start(bf16[256,640]{1,0:T(8,128)(2,1)S(1)} %bitcast.6), channel_id=1, source_target_pairs={{0,4},{4,8},{8,12},{1,5},{5,9},{9,13},{2,6},{6,10},{10,14},{3,7},{... | collective-permute-start | bytes 983048 | tf_op jit(solution)/shard_map/ppermute | solution.py:127
  36.7 14.3 %collective-permute-start.1 = (bf16[256,640]{1,0:T(8,128)(2,1)S(1)}, bf16[256,640]{1,0:T(8,128)(2,1)S(1)}, u32[]{:S(2)}, u32[]{:S(2)}) collective-permute-start(bf16[256,640]{1,0:T(8,128)(2,1)S(1)} %bitcast.7), channel_id=1, source_target_pairs={{4,0},{8,4},{12,8},{5,1},{9,5},{13,9},{6,2},{10,6},{14,10},{7,3},{... | collective-permute-start | bytes 983048 | tf_op jit(solution)/shard_map/ppermute | solution.py:128
Sparse Core Ops, SparseCore 0:
  18.3 25.6 reduce-scatter.1

commit v2 on v1

v2 whole, which is shorter than its diff:
```python
import functools
import math

import jax
import jax.numpy as jnp
from jax import lax
from jax.experimental import pallas as pl
from jax.experimental.pallas import tpu as pltpu
from jax.sharding import PartitionSpec as P

NX = 64
NY = 10
CELLS = NX * NY
F32 = jnp.float32
BF16 = jnp.bfloat16
VMEM_BYTES = 48 * 1024 * 1024


def cell_mask(rows, dy, dx):
    q = lax.broadcasted_iota(jnp.int32, (rows, CELLS), 1)
    x = q % NX + dx
    y = q // NX + dy
    return (x >= 0) & (x < NX) & (y >= 0) & (y < NY)


def shifted(value, dy, dx):
    if dy == 0 and dx == 0:
        return value
    moved = pltpu.roll(value, (-(dy * NX + dx)) % CELLS, 1)
    return jnp.where(cell_mask(value.shape[0], dy, dx), moved, 0.0)


def gather_kernel(nz, nc, pos_ref, cot_ref, *refs):
    pieces = refs[:nc]
    f_ref = refs[nc]
    packs = refs[nc + 1 :]
    blocks = cot_ref.shape[0]
    cols = f_ref.shape[0] // nz
    s, c = pos_ref[0], pos_ref[1]
    for k in range(nc):
        owner = lax.rem(c + nc - k, nc)
        f_ref[pl.ds(pl.multiple_of(owner * blocks, blocks), blocks), :] = pieces[k][...]
    for k, pack in zip(range(2, nz), packs):
        goal = lax.rem(s + k, nz) if k < nz - 1 else nz - 1 - s
        goal = jnp.clip(goal, 0, nz - 1)
        pack[:cols, :] = f_ref[pl.ds(pl.multiple_of(goal * cols, cols), cols), :]
        pack[cols:, :] = cot_ref[...]


def input_grad_kernel(nc, pos_ref, before_ref, cot_ref, after_ref, w_ref, *refs):
    parts = refs[:nc]
    cols_ref, sum_ref = refs[nc:]
    blocks = cot_ref.shape[0]
    c = pos_ref[1]
    for dz, ref in ((-1, after_ref), (0, cot_ref), (1, before_ref)):
        plane = ref[...].astype(F32)
        for dy in (-1, 0, 1):
            for dx in (-1, 0, 1):
                tap = 9 * (dz + 1) + 3 * (dy + 1) + dx + 1
                cols_ref[tap * blocks : (tap + 1) * blocks, :] = shifted(plane, -dy, -dx).astype(BF16)
    sum_ref[...] = lax.dot_general(
        w_ref[...], cols_ref[...], (((0,), (0,)), ((), ())), preferred_element_type=F32
    )
    for k in range(nc):
        goal = lax.rem(c + k, nc)
        parts[k][...] = sum_ref[pl.ds(pl.multiple_of(goal * blocks, blocks), blocks), :]


def output_kernel(nz, scale, pos_ref, w_ref, cot_ref, cm_ref, cp_ref, f0_ref, fm_ref, fp_ref, *refs):
    packs = refs[: nz - 2]
    out_ref, wg_ref, c_ref, g_ref = refs[nz - 2 :]
    blocks = cot_ref.shape[0]
    cols = g_ref.shape[1]
    taps = 9 * blocks
    s = pos_ref[0]
    acc = None
    for dz, ref in ((-1, fm_ref), (0, f0_ref), (1, fp_ref)):
        term = jnp.dot(
            w_ref[(dz + 1) * taps : (dz + 2) * taps, :], ref[...], preferred_element_type=F32
        )
        acc = term if acc is None else acc + term
    total = None
    for dx in (-1, 0, 1):
        for dy in (-1, 0, 1):
            at = (3 * (dy + 1) + dx + 1) * blocks
            term = shifted(acc[at : at + blocks], dy, dx)
            total = term if total is None else total + term
    out_ref[:, 0, :] = total

    mine = pl.ds(pl.multiple_of(s * cols, cols), cols)
    c_ref[s] = cot_ref[...]
    g_ref[s] = f0_ref[mine, :]

    @pl.when(s > 0)
    def _():
        c_ref[s - 1] = cm_ref[...]
        g_ref[s - 1] = fm_ref[mine, :]

    @pl.when(s < nz - 1)
    def _():
        c_ref[s + 1] = cp_ref[...]
        g_ref[s + 1] = fp_ref[mine, :]

    for k, pack in zip(range(2, nz - 1), packs):
        source = lax.rem(s + nz - k, nz)
        c_ref[source] = pack[cols:, :]
        g_ref[source] = pack[:cols, :]

    @pl.when((s == 0) | (s == nz - 1))
    def _():
        source = nz - 1 - s
        c_ref[source] = packs[-1][cols:, :]
        g_ref[source] = packs[-1][:cols, :]

    cots = []
    feats = []
    for z in range(nz):
        plane = c_ref[z].astype(F32)
        cots.append([shifted(plane, -dy, 0).astype(BF16) for dy in (-1, 0, 1)])
        field = g_ref[z].astype(F32)
        feats.append(jnp.concatenate([shifted(field, 0, dx).astype(BF16) for dx in (-1, 0, 1)], 0))
    for dz in (-1, 0, 1):
        sums = None
        for z in range(nz):
            if 0 <= z - dz < nz:
                term = lax.dot_general(
                    jnp.concatenate(cots[z - dz], 0),
                    feats[z],
                    (((1,), (1,)), ((), ())),
                    preferred_element_type=F32,
                )
                sums = term if sums is None else sums + term
        sums = sums * scale
        for dy in range(3):
            for dx in range(3):
                tap = 9 * (dz + 1) + 3 * dy + dx
                wg_ref[tap] = sums[dy * blocks : (dy + 1) * blocks, dx * cols : (dx + 1) * cols]


def total_kernel(*refs):
    total = refs[0][...]
    for ref in refs[1:-1]:
        total = total + ref[...]
    refs[-1][:, 0, :] = total


VMEM = pl.BlockSpec(memory_space=pltpu.VMEM)
SMEM = pl.BlockSpec(memory_space=pltpu.SMEM)


def kernel_call(body, name, outs, args, scratch=(), flops=0):
    moved = sum(math.prod(a.shape) * a.dtype.itemsize for a in args + outs)
    return pl.pallas_call(
        body,
        out_shape=outs,
        in_specs=[SMEM if a.dtype == jnp.int32 else VMEM for a in args],
        out_specs=tuple(VMEM for _ in outs),
        scratch_shapes=list(scratch),
        compiler_params=pltpu.CompilerParams(vmem_limit_bytes=VMEM_BYTES),
        cost_estimate=pl.CostEstimate(flops=flops, bytes_accessed=moved, transcendentals=0),
        name=name,
    )(*args)


def per_device(features, weights, cotangent):
    blocks, depth, plane = features.shape
    channels = weights.shape[2]
    nz = lax.axis_size("sp")
    nc = lax.axis_size("ch")
    cols = channels // nz
    w2 = weights.reshape(27 * blocks, channels)
    feat = features.reshape(blocks, plane)
    cot = cotangent.reshape(blocks, plane)
    pos = jnp.stack([lax.axis_index("sp"), lax.axis_index("ch")]).astype(jnp.int32)

    def turn(count, k):
        return [(i, (i + k) % count) for i in range(count)]

    up = [(i, i + 1) for i in range(nz - 1)]
    down = [(i + 1, i) for i in range(nz - 1)]
    field = jax.ShapeDtypeStruct((blocks, plane), BF16)
    wide = jax.ShapeDtypeStruct((blocks, plane), F32)

    cot_before = lax.ppermute(cot, "sp", up)
    cot_after = lax.ppermute(cot, "sp", down)
    pieces = [feat] + [lax.ppermute(feat, "ch", turn(nc, k)) for k in range(1, nc)]

    parts = kernel_call(
        functools.partial(input_grad_kernel, nc),
        "input_grad",
        [wide] * nc,
        [pos, cot_before, cot, cot_after, w2],
        [pltpu.VMEM((27 * blocks, plane), BF16), pltpu.VMEM((channels, plane), F32)],
        2 * 27 * blocks * channels * plane,
    )
    terms = [parts[0]] + [lax.ppermute(parts[k], "ch", turn(nc, k)) for k in range(1, nc)]

    packed = jax.ShapeDtypeStruct((cols + blocks, plane), BF16)
    f_all, *packs = kernel_call(
        functools.partial(gather_kernel, nz, nc),
        "gather",
        [jax.ShapeDtypeStruct((channels, plane), BF16)] + [packed] * (nz - 2),
        [pos, cot] + pieces,
    )
    f_before = lax.ppermute(f_all, "sp", up)
    f_after = lax.ppermute(f_all, "sp", down)
    far = [lax.ppermute(packs[k - 2], "sp", turn(nz, k)) for k in range(2, nz - 1)]
    far.append(lax.ppermute(packs[-1], "sp", [(0, nz - 1), (nz - 1, 0)]))

    output, weight_grad = kernel_call(
        functools.partial(output_kernel, nz, 1.0 / math.sqrt(nz * depth * plane)),
        "output_and_weight_grad",
        [
            jax.ShapeDtypeStruct((blocks, 1, plane), F32),
            jax.ShapeDtypeStruct((27, blocks, cols), F32),
        ],
        [pos, w2, cot, cot_before, cot_after, f_all, f_before, f_after] + far,
        [pltpu.VMEM((nz, blocks, plane), BF16), pltpu.VMEM((nz, cols, plane), BF16)],
        4 * 27 * blocks * channels * plane,
    )
    (back,) = kernel_call(
        total_kernel, "total", [jax.ShapeDtypeStruct((blocks, 1, plane), F32)], terms
    )
    return (output, back, weight_grad)


def solution(mesh):
    return jax.shard_map(
        per_device,
        mesh=mesh,
        in_specs=(P("ch", ("grp", "sp"), None), P(None, "ch", None), P("ch", ("grp", "sp"), None)),
        out_specs=(
            P("ch", ("grp", "sp"), None),
            P("ch", ("grp", "sp"), None),
            P("grp", "ch", "sp"),
        ),
        check_vma=False,
    )
```

time: 62.5 us -> 43 us (0.69)
  blocking collectives: 37.9 us -> 0 us
  starting transfers between devices: 2.63 us -> 26.1 us
  between operations: 14.1 us -> 0.72 us
  waiting for transfers between devices: 0.02 us -> 6.58 us
  Pallas kernels: 4.74 us -> 7.08 us
  local copies, waits for them, and re-layouts: 2.92 us -> 2.06 us
    all_gather x2 -> x0, blocking collectives: 24.9 us -> none  [the longest x1 17.2 us: per_device(): f_all = lax.all_gather(feat, 'ch', axis=0, tiled=True)]
    ppermute x2 -> x12, starting transfers between devices: 2.59 us -> 26.1 us  [the longest x3 6.11 us: per_device(): lax.ppermute(feat, 'ch', turn(nc, k))]
    all_to_all x1 -> x0, blocking collectives: 12.9 us -> none  [per_device(): fblk = lax.all_to_all(f_all.reshape(nz, cols, plane), 'sp', 0, 0)]
    ppermute x2 -> x12, waiting for transfers between devices: 0.01 us -> 6.58 us  [the longest x3 3.01 us: per_device(): lax.ppermute(parts[k], 'ch', turn(nc, k))]
    pallas_call x2 -> x4, Pallas kernels: 4.74 us -> 7.08 us  [kernel_call(): pl.pallas_call(body, out_shape=outs, in_specs=[SMEM if a.dtype == jnp.int...]
    unnamed x7 -> x8, local copies, waits for them, and re-layouts: 2.92 us -> 2.06 us
  transfers between devices with their start and end apart: 3 -> 12, of which waited for: 0 -> 4; matrix products, arithmetic and copies ran while one was open for 0% -> 0% of each run, Pallas kernels for 4% -> 7%
where the time goes in v2:
time: 43 us; the launch traced here: 42.7 us
  starting transfers between devices  26.1 us (61%)
  Pallas kernels  7.08 us (16%)
  waiting for transfers between devices  6.58 us (15%)
  local copies, waits for them, and re-layouts  2.06 us (5%)
  between operations  0.72 us (2%)
    pallas_call x4, Pallas kernels, kernel_call(): pl.pallas_call(body, out_shape=outs, in_specs=[SMEM if a.dtype == jnp.int...  7.08 us
    ppermute x3, starting transfers between devices, per_device(): lax.ppermute(feat, 'ch', turn(nc, k))  6.11 us
    ppermute x3, starting transfers between devices, per_device(): lax.ppermute(parts[k], 'ch', turn(nc, k))  5.3 us
    ppermute x1, starting transfers between devices, per_device(): f_before = lax.ppermute(f_all, 'sp', up)  3.77 us
    ppermute x1, starting transfers between devices, per_device(): cot_before = lax.ppermute(cot, 'sp', up)  3.04 us
    ppermute x3, waiting for transfers between devices, per_device(): lax.ppermute(parts[k], 'ch', turn(nc, k))  3.01 us
    ppermute x1, starting transfers between devices, per_device(): lax.ppermute(packs[k - 2], 'sp', turn(nz, k))  2.93 us
    ppermute x1, waiting for transfers between devices, per_device(): far.append(lax.ppermute(packs[-1], 'sp', [(0, nz - 1), (nz - 1, 0)]))  2.53 us
  transfers between devices with their start and end apart: 12, of which 4 were waited for; matrix products, arithmetic and copies ran while one was open for 0% of the time, Pallas kernels for 7%

profile of v2, /device:TPU:0, one launch (start us, length us, event | category | flops | bytes accessed | tf_op | source)
XLA Modules:
  0.0 42.7 jit_solution(16591991441507542388)
XLA Ops:
  0.6 5.1 %collective-permute-start.4 = (bf16[64,640]{1,0:T(8,128)(2,1)}, bf16[64,640]{1,0:T(8,128)(2,1)S(1)}, u32[]{:S(2)}, u32[]{:S(2)}) collective-permute-start(bf16[64,640]{1,0:T(8,128)(2,1)} %bitcast.5), channel_id=1, source_target_pairs={{0,3},{1,0},{2,1},{3,2},{4,7},{5,4},{6,5},{7,6},{8,11},{9,8},{10,9... | collective-permute-start | bytes 245768 | tf_op jit(solution)/shard_map/ppermute | solution.py:186
  5.7 0.0 collective-permute-start.3
  5.7 1.0 %collective-permute-start.2 = (bf16[64,640]{1,0:T(8,128)(2,1)}, bf16[64,640]{1,0:T(8,128)(2,1)S(1)}, u32[]{:S(2)}, u32[]{:S(2)}) collective-permute-start(bf16[64,640]{1,0:T(8,128)(2,1)} %bitcast.7), channel_id=1, source_target_pairs={{0,1},{1,2},{2,3},{3,0},{4,5},{5,6},{6,7},{7,4},{8,9},{9,10},{10,1... | collective-permute-start | bytes 245768 | tf_op jit(solution)/shard_map/ppermute | solution.py:186
  6.7 1.3 %collective-permute-start.1 = (bf16[64,640]{1,0:T(8,128)(2,1)}, bf16[64,640]{1,0:T(8,128)(2,1)S(1)}, u32[]{:S(2)}, u32[]{:S(2)}) collective-permute-start(bf16[64,640]{1,0:T(8,128)(2,1)} %bitcast.9), channel_id=1, source_target_pairs={{4,0},{8,4},{12,8},{5,1},{9,5},{13,9},{6,2},{10,6},{14,10},{7,3},{... | collective-permute-start | bytes 245768 | tf_op jit(solution)/shard_map/ppermute | solution.py:185
  8.0 3.0 %collective-permute-start = (bf16[64,640]{1,0:T(8,128)(2,1)}, bf16[64,640]{1,0:T(8,128)(2,1)S(1)}, u32[]{:S(2)}, u32[]{:S(2)}) collective-permute-start(bf16[64,640]{1,0:T(8,128)(2,1)} %bitcast.10), channel_id=1, source_target_pairs={{0,4},{4,8},{8,12},{1,5},{5,9},{9,13},{2,6},{6,10},{10,14},{3,7},{... | collective-permute-start | bytes 245768 | tf_op jit(solution)/shard_map/ppermute | solution.py:184
  11.1 0.1 pad_add_fusion.pos_ref
  11.2 0.0 collective-permute-done.1.cp_ref.after_ref
  11.2 1.0 %collective-permute-done.cm_ref.before_ref = bf16[64,640]{1,0:T(8,128)(2,1)S(1)} collective-permute-done((bf16[64,640]{1,0:T(8,128)(2,1)}, bf16[64,640]{1,0:T(8,128)(2,1)S(1)}, u32[]{:S(2)}, u32[]{:S(2)}) %collective-permute-start) | collective-permute-done | bytes 81952 | tf_op jit(solution)/shard_map/ppermute | solution.py:184
  12.2 0.0 copy-start.1
  12.2 0.9 %copy-done.1 = bf16[64,1,640]{2,0,1:T(8,128)(2,1)S(1)} copy-done((bf16[64,1,640]{2,0,1:T(8,128)(2,1)S(1)}, bf16[64,1,640]{2,0,1:T(8,128)(2,1)}, u32[]{:S(2)}) %copy-start.1) | copy-done | bytes 81944
  13.1 0.0 copy-start.2
  13.1 1.2 %copy-done.2 = bf16[27,64,256]{2,1,0:T(8,128)(2,1)S(1)} copy-done((bf16[27,64,256]{2,1,0:T(8,128)(2,1)S(1)}, bf16[27,64,256]{2,1,0:T(8,128)(2,1)}, u32[]{:S(2)}) %copy-start.2) | copy-done | bytes 884760
  14.2 0.0 copy-start
  14.2 1.9 %input_grad.1 = (f32[64,640]{1,0:T(8,128)S(1)}, f32[64,640]{1,0:T(8,128)S(1)}, f32[64,640]{1,0:T(8,128)S(1)}, f32[64,640]{1,0:T(8,128)S(1)}) custom-call(s32[2]{0:T(128)S(1)} %pad_add_fusion.pos_ref, bf16[64,640]{1,0:T(8,128)(2,1)S(1)} %collective-permute-done.cm_ref.before_ref, bf16[64,640]{1,0:T(8,128)(2,1)S(1)} %bitcast.11, ...), custom_call_target="tpu_custom_call" | custom-call | flops 566231040 | bytes 1785864 | tf_op jit(solution)/shard_map/input_grad/pallas_call | solution.py:153
  16.1 0.0 copy-start.3
  16.1 2.5 %collective-permute-start.9 = (f32[64,640]{1,0:T(8,128)S(1)}, f32[64,640]{1,0:T(8,128)S(1)}, u32[]{:S(2)}, u32[]{:S(2)}) collective-permute-start(f32[64,640]{1,0:T(8,128)S(1)} %get-tuple-element.17), channel_id=1, source_target_pairs={{0,1},{1,2},{2,3},{3,0},{4,5},{5,6},{6,7},{7,4},{8,9},{9,10},{10,1... | collective-permute-start | bytes 491528 | tf_op jit(solution)/shard_map/ppermute | solution.py:196
  18.7 0.9 %collective-permute-start.10 = (f32[64,640]{1,0:T(8,128)S(1)}, f32[64,640]{1,0:T(8,128)S(1)}, u32[]{:S(2)}, u32[]{:S(2)}) collective-permute-start(f32[64,640]{1,0:T(8,128)S(1)} %get-tuple-element.18), channel_id=1, source_target_pairs={{0,2},{1,3},{2,0},{3,1},{4,6},{5,7},{6,4},{7,5},{8,10},{9,11},{10,... | collective-permute-start | bytes 491528 | tf_op jit(solution)/shard_map/ppermute | solution.py:196
  19.6 0.0 collective-permute-done.4.refs_3_
  19.6 0.0 collective-permute-done.3.refs_2_
  19.6 0.0 collective-permute-done.2.refs_1_
  19.6 0.0 copy-done
  19.6 0.6 %gather.1 = (bf16[256,640]{1,0:T(8,128)(2,1)S(1)}, bf16[128,640]{1,0:T(8,128)(2,1)S(1)}, bf16[128,640]{1,0:T(8,128)(2,1)S(1)}) custom-call(s32[2]{0:T(128)S(1)} %pad_add_fusion.pos_ref, bf16[64,640]{1,0:T(8,128)(2,1)S(1)} %bitcast.12, bf16[64,640]{1,0:T(8,128)(2,1)S(1)} %bitcast.8, bf16[64,640]{1,0:T(8,128)(2,1)S(1)} %collective-permute-done.2.refs_1_, ...), custom_call_target="tpu_custom_call" | custom-call | bytes 1064968 | tf_op jit(solution)/shard_map/gather/pallas_call | solution.py:153
  20.2 1.3 %collective-permute-start.6 = (bf16[256,640]{1,0:T(8,128)(2,1)S(1)}, bf16[256,640]{1,0:T(8,128)(2,1)S(1)}, u32[]{:S(2)}, u32[]{:S(2)}) collective-permute-start(bf16[256,640]{1,0:T(8,128)(2,1)S(1)} %get-tuple-element.12.f0_ref), channel_id=1, source_target_pairs={{4,0},{8,4},{12,8},{5,1},{9,5},{13,9},{6,2},{10,6},{14,10},{7,3},{... | collective-permute-start | bytes 983048 | tf_op jit(solution)/shard_map/ppermute | solution.py:206
  21.5 3.8 %collective-permute-start.5 = (bf16[256,640]{1,0:T(8,128)(2,1)S(1)}, bf16[256,640]{1,0:T(8,128)(2,1)S(1)}, u32[]{:S(2)}, u32[]{:S(2)}) collective-permute-start(bf16[256,640]{1,0:T(8,128)(2,1)S(1)} %get-tuple-element.12.f0_ref), channel_id=1, source_target_pairs={{0,4},{4,8},{8,12},{1,5},{5,9},{9,13},{2,6},{6,10},{10,14},{3,7},{... | collective-permute-start | bytes 983048 | tf_op jit(solution)/shard_map/ppermute | solution.py:205
  25.3 1.9 %collective-permute-start.11 = (f32[64,640]{1,0:T(8,128)S(1)}, f32[64,640]{1,0:T(8,128)S(1)}, u32[]{:S(2)}, u32[]{:S(2)}) collective-permute-start(f32[64,640]{1,0:T(8,128)S(1)} %get-tuple-element.19), channel_id=1, source_target_pairs={{0,3},{1,0},{2,1},{3,2},{4,7},{5,4},{6,5},{7,6},{8,11},{9,8},{10,9... | collective-permute-start | bytes 491528 | tf_op jit(solution)/shard_map/ppermute | solution.py:196
  27.1 0.0 collective-permute-done.9.refs_1_
  27.1 2.9 %collective-permute-start.7 = (bf16[128,640]{1,0:T(8,128)(2,1)S(1)}, bf16[128,640]{1,0:T(8,128)(2,1)S(1)}, u32[]{:S(2)}, u32[]{:S(2)}) collective-permute-start(bf16[128,640]{1,0:T(8,128)(2,1)S(1)} %get-tuple-element.13), channel_id=1, source_target_pairs={{0,8},{4,12},{8,0},{12,4},{1,9},{5,13},{9,1},{13,5},{2,10},{6,14},... | collective-permute-start | bytes 491528 | tf_op jit(solution)/shard_map/ppermute | solution.py:207
  30.1 2.0 %collective-permute-done.10.refs_2_ = f32[64,640]{1,0:T(8,128)S(1)} collective-permute-done((f32[64,640]{1,0:T(8,128)S(1)}, f32[64,640]{1,0:T(8,128)S(1)}, u32[]{:S(2)}, u32[]{:S(2)}) %collective-permute-start.10) | collective-permute-done | bytes 163872 | tf_op jit(solution)/shard_map/ppermute | solution.py:196
  32.1 2.4 %collective-permute-start.8 = (bf16[128,640]{1,0:T(8,128)(2,1)S(1)}, bf16[128,640]{1,0:T(8,128)(2,1)S(1)}, u32[]{:S(2)}, u32[]{:S(2)}) collective-permute-start(bf16[128,640]{1,0:T(8,128)(2,1)S(1)} %get-tuple-element.14), channel_id=1, source_target_pairs={{0,12},{12,0},{1,13},{13,1},{2,14},{14,2},{3,15},{15,3},{16,28},{2... | collective-permute-start | bytes 491528 | tf_op jit(solution)/shard_map/ppermute | solution.py:208
  34.5 1.0 %collective-permute-done.11.refs_3_ = f32[64,640]{1,0:T(8,128)S(1)} collective-permute-done((f32[64,640]{1,0:T(8,128)S(1)}, f32[64,640]{1,0:T(8,128)S(1)}, u32[]{:S(2)}, u32[]{:S(2)}) %collective-permute-start.11) | collective-permute-done | bytes 163872 | tf_op jit(solution)/shard_map/ppermute | solution.py:196
  35.5 0.7 %total.1 = f32[64,1,640]{2,1,0:T(1,128)} custom-call(f32[64,640]{1,0:T(8,128)S(1)} %get-tuple-element.16.refs_0_, f32[64,640]{1,0:T(8,128)S(1)} %collective-permute-done.9.refs_1_, f32[64,640]{1,0:T(8,128)S(1)} %collective-permute-done.10.refs_2_, f32[64,640]{1,0:T(8,128)S(1)} %collective-permute-done.11.refs_3_), custom_call_target="tpu_custom_call" | custom-call | bytes 819200 | tf_op jit(solution)/shard_map/total/pallas_call | solution.py:153
  36.2 0.0 collective-permute-done.7.refs_0_
  36.2 2.5 %collective-permute-done.8.refs_1_ = bf16[128,640]{1,0:T(8,128)(2,1)S(1)} collective-permute-done((bf16[128,640]{1,0:T(8,128)(2,1)S(1)}, bf16[128,640]{1,0:T(8,128)(2,1)S(1)}, u32[]{:S(2)}, u32[]{:S(2)}) %collective-permute-start.8) | collective-permute-done | bytes 163872 | tf_op jit(solution)/shard_map/ppermute | solution.py:208
  38.7 0.0 collective-permute-done.6.fp_ref
  38.8 0.0 collective-permute-done.5.fm_ref
  38.8 0.0 copy-done.3
  38.8 3.9 %output_and_weight_grad.1 = (f32[64,1,640]{2,1,0:T(1,128)}, f32[27,64,64]{2,1,0:T(8,128)}) custom-call(s32[2]{0:T(128)S(1)} %pad_add_fusion.pos_ref, bf16[1728,256]{1,0:T(8,128)(2,1)S(1)} %bitcast.15, bf16[64,640]{1,0:T(8,128)(2,1)S(1)} %bitcast.13, bf16[64,640]{1,0:T(8,128)(2,1)S(1)} %collective-permute-done.cm_ref.before_ref, ...), custom_call_target="tpu_custom_call" | custom-call | flops 1132462080 | bytes 3047432 | tf_op jit(solution)/shard_map/output_and_weight_grad/pallas_call | solution.py:153
Async XLA Ops:
  0.6 18.9 %collective-permute-start.4 = (bf16[64,640]{1,0:T(8,128)(2,1)}, bf16[64,640]{1,0:T(8,128)(2,1)S(1)}, u32[]{:S(2)}, u32[]{:S(2)}) collective-permute-start(bf16[64,640]{1,0:T(8,128)(2,1)} %bitcast.5), channel_id=1, source_target_pairs={{0,3},{1,0},{2,1},{3,2},{4,7},{5,4},{6,5},{7,6},{8,11},{9,8},{10,9... | collective-permute-start | bytes 245768 | tf_op jit(solution)/shard_map/ppermute | solution.py:186
  5.7 13.8 %collective-permute-start.3 = (bf16[64,640]{1,0:T(8,128)(2,1)}, bf16[64,640]{1,0:T(8,128)(2,1)S(1)}, u32[]{:S(2)}, u32[]{:S(2)}) collective-permute-start(bf16[64,640]{1,0:T(8,128)(2,1)} %bitcast.6), channel_id=1, source_target_pairs={{0,2},{1,3},{2,0},{3,1},{4,6},{5,7},{6,4},{7,5},{8,10},{9,11},{10,... | collective-permute-start | bytes 245768 | tf_op jit(solution)/shard_map/ppermute | solution.py:186
  5.7 13.8 %collective-permute-start.2 = (bf16[64,640]{1,0:T(8,128)(2,1)}, bf16[64,640]{1,0:T(8,128)(2,1)S(1)}, u32[]{:S(2)}, u32[]{:S(2)}) collective-permute-start(bf16[64,640]{1,0:T(8,128)(2,1)} %bitcast.7), channel_id=1, source_target_pairs={{0,1},{1,2},{2,3},{3,0},{4,5},{5,6},{6,7},{7,4},{8,9},{9,10},{10,1... | collective-permute-start | bytes 245768 | tf_op jit(solution)/shard_map/ppermute | solution.py:186
  6.7 4.4 %collective-permute-start.1 = (bf16[64,640]{1,0:T(8,128)(2,1)}, bf16[64,640]{1,0:T(8,128)(2,1)S(1)}, u32[]{:S(2)}, u32[]{:S(2)}) collective-permute-start(bf16[64,640]{1,0:T(8,128)(2,1)} %bitcast.9), channel_id=1, source_target_pairs={{4,0},{8,4},{12,8},{5,1},{9,5},{13,9},{6,2},{10,6},{14,10},{7,3},{... | collective-permute-start | bytes 245768 | tf_op jit(solution)/shard_map/ppermute | solution.py:185
  8.0 4.2 %collective-permute-start = (bf16[64,640]{1,0:T(8,128)(2,1)}, bf16[64,640]{1,0:T(8,128)(2,1)S(1)}, u32[]{:S(2)}, u32[]{:S(2)}) collective-permute-start(bf16[64,640]{1,0:T(8,128)(2,1)} %bitcast.10), channel_id=1, source_target_pairs={{0,4},{4,8},{8,12},{1,5},{5,9},{9,13},{2,6},{6,10},{10,14},{3,7},{... | collective-permute-start | bytes 245768 | tf_op jit(solution)/shard_map/ppermute | solution.py:184
  12.2 0.9 %copy-start.1 = (bf16[64,1,640]{2,0,1:T(8,128)(2,1)S(1)}, bf16[64,1,640]{2,0,1:T(8,128)(2,1)}, u32[]{:S(2)}) copy-start(bf16[64,1,640]{2,0,1:T(8,128)(2,1)} %param.5) | copy-start | bytes 245764
  13.1 1.2 %copy-start.2 = (bf16[27,64,256]{2,1,0:T(8,128)(2,1)S(1)}, bf16[27,64,256]{2,1,0:T(8,128)(2,1)}, u32[]{:S(2)}) copy-start(bf16[27,64,256]{2,1,0:T(8,128)(2,1)} %param.4) | copy-start | bytes 2654212
  14.2 5.3 %copy-start = (bf16[64,1,640]{2,0,1:T(8,128)(2,1)S(1)}, bf16[64,1,640]{2,0,1:T(8,128)(2,1)}, u32[]{:S(2)}) copy-start(bf16[64,1,640]{2,0,1:T(8,128)(2,1)} %param.3) | copy-start | bytes 245764
  16.1 22.6 %copy-start.3 = (bf16[27,64,256]{2,1,0:T(8,128)(2,1)S(1)}, bf16[27,64,256]{2,1,0:T(8,128)(2,1)}, u32[]{:S(2)}) copy-start(bf16[27,64,256]{2,1,0:T(8,128)(2,1)} %param.4) | copy-start | bytes 2654212
  16.1 11.0 %collective-permute-start.9 = (f32[64,640]{1,0:T(8,128)S(1)}, f32[64,640]{1,0:T(8,128)S(1)}, u32[]{:S(2)}, u32[]{:S(2)}) collective-permute-start(f32[64,640]{1,0:T(8,128)S(1)} %get-tuple-element.17), channel_id=1, source_target_pairs={{0,1},{1,2},{2,3},{3,0},{4,5},{5,6},{6,7},{7,4},{8,9},{9,10},{10,1... | collective-permute-start | bytes 491528 | tf_op jit(solution)/shard_map/ppermute | solution.py:196
  18.7 13.5 %collective-permute-start.10 = (f32[64,640]{1,0:T(8,128)S(1)}, f32[64,640]{1,0:T(8,128)S(1)}, u32[]{:S(2)}, u32[]{:S(2)}) collective-permute-start(f32[64,640]{1,0:T(8,128)S(1)} %get-tuple-element.18), channel_id=1, source_target_pairs={{0,2},{1,3},{2,0},{3,1},{4,6},{5,7},{6,4},{7,5},{8,10},{9,11},{10,... | collective-permute-start | bytes 491528 | tf_op jit(solution)/shard_map/ppermute | solution.py:196
  20.2 18.6 %collective-permute-start.6 = (bf16[256,640]{1,0:T(8,128)(2,1)S(1)}, bf16[256,640]{1,0:T(8,128)(2,1)S(1)}, u32[]{:S(2)}, u32[]{:S(2)}) collective-permute-start(bf16[256,640]{1,0:T(8,128)(2,1)S(1)} %get-tuple-element.12.f0_ref), channel_id=1, source_target_pairs={{4,0},{8,4},{12,8},{5,1},{9,5},{13,9},{6,2},{10,6},{14,10},{7,3},{... | collective-permute-start | bytes 983048 | tf_op jit(solution)/shard_map/ppermute | solution.py:206
  21.5 17.3 %collective-permute-start.5 = (bf16[256,640]{1,0:T(8,128)(2,1)S(1)}, bf16[256,640]{1,0:T(8,128)(2,1)S(1)}, u32[]{:S(2)}, u32[]{:S(2)}) collective-permute-start(bf16[256,640]{1,0:T(8,128)(2,1)S(1)} %get-tuple-element.12.f0_ref), channel_id=1, source_target_pairs={{0,4},{4,8},{8,12},{1,5},{5,9},{9,13},{2,6},{6,10},{10,14},{3,7},{... | collective-permute-start | bytes 983048 | tf_op jit(solution)/shard_map/ppermute | solution.py:205
  25.3 10.2 %collective-permute-start.11 = (f32[64,640]{1,0:T(8,128)S(1)}, f32[64,640]{1,0:T(8,128)S(1)}, u32[]{:S(2)}, u32[]{:S(2)}) collective-permute-start(f32[64,640]{1,0:T(8,128)S(1)} %get-tuple-element.19), channel_id=1, source_target_pairs={{0,3},{1,0},{2,1},{3,2},{4,7},{5,4},{6,5},{7,6},{8,11},{9,8},{10,9... | collective-permute-start | bytes 491528 | tf_op jit(solution)/shard_map/ppermute | solution.py:196
  27.1 9.1 %collective-permute-start.7 = (bf16[128,640]{1,0:T(8,128)(2,1)S(1)}, bf16[128,640]{1,0:T(8,128)(2,1)S(1)}, u32[]{:S(2)}, u32[]{:S(2)}) collective-permute-start(bf16[128,640]{1,0:T(8,128)(2,1)S(1)} %get-tuple-element.13), channel_id=1, source_target_pairs={{0,8},{4,12},{8,0},{12,4},{1,9},{5,13},{9,1},{13,5},{2,10},{6,14},... | collective-permute-start | bytes 491528 | tf_op jit(solution)/shard_map/ppermute | solution.py:207
  32.1 6.6 %collective-permute-start.8 = (bf16[128,640]{1,0:T(8,128)(2,1)S(1)}, bf16[128,640]{1,0:T(8,128)(2,1)S(1)}, u32[]{:S(2)}, u32[]{:S(2)}) collective-permute-start(bf16[128,640]{1,0:T(8,128)(2,1)S(1)} %get-tuple-element.14), channel_id=1, source_target_pairs={{0,12},{12,0},{1,13},{13,1},{2,14},{14,2},{3,15},{15,3},{16,28},{2... | collective-permute-start | bytes 491528 | tf_op jit(solution)/shard_map/ppermute | solution.py:208

commit v3 on v2

--- a/solution.py
+++ b/solution.py
@@ -40,20 +40,22 @@
     for k in range(nc):
         owner = lax.rem(c + nc - k, nc)
         f_ref[pl.ds(pl.multiple_of(owner * blocks, blocks), blocks), :] = pieces[k][...]
-    for k, pack in zip(range(2, nz), packs):
-        goal = lax.rem(s + k, nz) if k < nz - 1 else nz - 1 - s
-        goal = jnp.clip(goal, 0, nz - 1)
+    for k, pack in zip(range(2, nz - 1), packs):
+        goal = lax.rem(s + k, nz)
         pack[:cols, :] = f_ref[pl.ds(pl.multiple_of(goal * cols, cols), cols), :]
         pack[cols:, :] = cot_ref[...]
 
 
-def input_grad_kernel(nc, pos_ref, before_ref, cot_ref, after_ref, w_ref, *refs):
+def input_grad_kernel(nz, nc, pos_ref, before_ref, cot_ref, after_ref, w_ref, *refs):
     parts = refs[:nc]
     cols_ref, sum_ref = refs[nc:]
     blocks = cot_ref.shape[0]
-    c = pos_ref[1]
+    s, c = pos_ref[0], pos_ref[1]
+    inside = {-1: s < nz - 1, 1: s > 0}
     for dz, ref in ((-1, after_ref), (0, cot_ref), (1, before_ref)):
         plane = ref[...].astype(F32)
+        if dz:
+            plane = jnp.where(inside[dz], plane, 0.0)
         for dy in (-1, 0, 1):
             for dx in (-1, 0, 1):
                 tap = 9 * (dz + 1) + 3 * (dy + 1) + dx + 1
@@ -67,18 +69,19 @@
 
 
 def output_kernel(nz, scale, pos_ref, w_ref, cot_ref, cm_ref, cp_ref, f0_ref, fm_ref, fp_ref, *refs):
-    packs = refs[: nz - 2]
-    out_ref, wg_ref, c_ref, g_ref = refs[nz - 2 :]
+    packs = refs[: nz - 3]
+    out_ref, wg_ref, c_ref, g_ref = refs[nz - 3 :]
     blocks = cot_ref.shape[0]
     cols = g_ref.shape[1]
     taps = 9 * blocks
     s = pos_ref[0]
     acc = None
-    for dz, ref in ((-1, fm_ref), (0, f0_ref), (1, fp_ref)):
+    inside = {-1: s > 0, 1: s < nz - 1}
+    for dz, ref in ((0, f0_ref), (-1, fm_ref), (1, fp_ref)):
         term = jnp.dot(
             w_ref[(dz + 1) * taps : (dz + 2) * taps, :], ref[...], preferred_element_type=F32
         )
-        acc = term if acc is None else acc + term
+        acc = term if acc is None else acc + jnp.where(inside[dz], term, 0.0)
     total = None
     for dx in (-1, 0, 1):
         for dy in (-1, 0, 1):
@@ -91,26 +94,16 @@
     c_ref[s] = cot_ref[...]
     g_ref[s] = f0_ref[mine, :]
 
-    @pl.when(s > 0)
-    def _():
-        c_ref[s - 1] = cm_ref[...]
-        g_ref[s - 1] = fm_ref[mine, :]
-
-    @pl.when(s < nz - 1)
-    def _():
-        c_ref[s + 1] = cp_ref[...]
-        g_ref[s + 1] = fp_ref[mine, :]
-
+    for source, cot_near, f_near in (
+        (lax.rem(s + nz - 1, nz), cm_ref, fm_ref),
+        (lax.rem(s + 1, nz), cp_ref, fp_ref),
+    ):
+        c_ref[source] = cot_near[...]
+        g_ref[source] = f_near[mine, :]
     for k, pack in zip(range(2, nz - 1), packs):
         source = lax.rem(s + nz - k, nz)
         c_ref[source] = pack[cols:, :]
         g_ref[source] = pack[:cols, :]
-
-    @pl.when((s == 0) | (s == nz - 1))
-    def _():
-        source = nz - 1 - s
-        c_ref[source] = packs[-1][cols:, :]
-        g_ref[source] = packs[-1][:cols, :]
 
     cots = []
     feats = []
@@ -176,8 +169,7 @@
     def turn(count, k):
         return [(i, (i + k) % count) for i in range(count)]
 
-    up = [(i, i + 1) for i in range(nz - 1)]
-    down = [(i + 1, i) for i in range(nz - 1)]
+    up, down = turn(nz, 1), turn(nz, nz - 1)
     field = jax.ShapeDtypeStruct((blocks, plane), BF16)
     wide = jax.ShapeDtypeStruct((blocks, plane), F32)
 
@@ -186,7 +178,7 @@
     pieces = [feat] + [lax.ppermute(feat, "ch", turn(nc, k)) for k in range(1, nc)]
 
     parts = kernel_call(
-        functools.partial(input_grad_kernel, nc),
+        functools.partial(input_grad_kernel, nz, nc),
         "input_grad",
         [wide] * nc,
         [pos, cot_before, cot, cot_after, w2],
@@ -199,13 +191,12 @@
     f_all, *packs = kernel_call(
         functools.partial(gather_kernel, nz, nc),
         "gather",
-        [jax.ShapeDtypeStruct((channels, plane), BF16)] + [packed] * (nz - 2),
+        [jax.ShapeDtypeStruct((channels, plane), BF16)] + [packed] * (nz - 3),
         [pos, cot] + pieces,
     )
     f_before = lax.ppermute(f_all, "sp", up)
     f_after = lax.ppermute(f_all, "sp", down)
     far = [lax.ppermute(packs[k - 2], "sp", turn(nz, k)) for k in range(2, nz - 1)]
-    far.append(lax.ppermute(packs[-1], "sp", [(0, nz - 1), (nz - 1, 0)]))
 
     output, weight_grad = kernel_call(
         functools.partial(output_kernel, nz, 1.0 / math.sqrt(nz * depth * plane)),

time: 43 us -> 36.6 us (0.85)
  the two profiles are of different devices: /device:TPU:0 before, /device:TPU:13 now
where the time goes in v3:
time: 36.6 us; the launch traced here: 36.4 us
  waiting for transfers between devices  15.8 us (43%)
  starting transfers between devices  11 us (30%)
  Pallas kernels  6.61 us (18%)
  local copies, waits for them, and re-layouts  2.2 us (6%)
  between operations  0.71 us (2%)
    ppermute x3, waiting for transfers between devices, per_device(): lax.ppermute(parts[k], 'ch', turn(nc, k))  12.4 us
    pallas_call x4, Pallas kernels, kernel_call(): pl.pallas_call(body, out_shape=outs, in_specs=[SMEM if a.dtype == jnp.int...  6.61 us
    ppermute x3, starting transfers between devices, per_device(): lax.ppermute(feat, 'ch', turn(nc, k))  4.73 us
    ppermute x1, waiting for transfers between devices, per_device(): cot_after = lax.ppermute(cot, 'sp', down)  3.38 us
    unnamed x10, local copies, waits for them, and re-layouts  2.2 us
    ppermute x3, starting transfers between devices, per_device(): lax.ppermute(parts[k], 'ch', turn(nc, k))  1.83 us
    ppermute x1, starting transfers between devices, per_device(): cot_after = lax.ppermute(cot, 'sp', down)  1.52 us
    ppermute x1, starting transfers between devices, per_device(): f_before = lax.ppermute(f_all, 'sp', up)  1.31 us
  transfers between devices with their start and end apart: 11, of which 4 were waited for; matrix products, arithmetic and copies ran while one was open for 0% of the time, Pallas kernels for 9%

profile of v3, /device:TPU:13, one launch (start us, length us, event | category | flops | bytes accessed | tf_op | source)
XLA Modules:
  0.0 36.4 jit_solution(1272189970740805938)
XLA Ops:
  0.6 0.2 collective-permute-start.4
  0.9 2.3 %collective-permute-start.3 = (bf16[64,640]{1,0:T(8,128)(2,1)}, bf16[64,640]{1,0:T(8,128)(2,1)S(1)}, u32[]{:S(2)}, u32[]{:S(2)}) collective-permute-start(bf16[64,640]{1,0:T(8,128)(2,1)} %bitcast.6), channel_id=1, source_target_pairs={{0,2},{1,3},{2,0},{3,1},{4,6},{5,7},{6,4},{7,5},{8,10},{9,11},{10,... | collective-permute-start | bytes 245768 | tf_op jit(solution)/shard_map/ppermute | solution.py:178
  3.2 2.2 %collective-permute-start.2 = (bf16[64,640]{1,0:T(8,128)(2,1)}, bf16[64,640]{1,0:T(8,128)(2,1)S(1)}, u32[]{:S(2)}, u32[]{:S(2)}) collective-permute-start(bf16[64,640]{1,0:T(8,128)(2,1)} %bitcast.7), channel_id=1, source_target_pairs={{0,1},{1,2},{2,3},{3,0},{4,5},{5,6},{6,7},{7,4},{8,9},{9,10},{10,1... | collective-permute-start | bytes 245768 | tf_op jit(solution)/shard_map/ppermute | solution.py:178
  5.4 1.5 %collective-permute-start.1 = (bf16[64,640]{1,0:T(8,128)(2,1)}, bf16[64,640]{1,0:T(8,128)(2,1)S(1)}, u32[]{:S(2)}, u32[]{:S(2)}) collective-permute-start(bf16[64,640]{1,0:T(8,128)(2,1)} %bitcast.9), channel_id=1, source_target_pairs={{0,12},{4,0},{8,4},{12,8},{1,13},{5,1},{9,5},{13,9},{2,14},{6,2},{... | collective-permute-start | bytes 245768 | tf_op jit(solution)/shard_map/ppermute | solution.py:177
  6.9 1.1 %collective-permute-start = (bf16[64,640]{1,0:T(8,128)(2,1)}, bf16[64,640]{1,0:T(8,128)(2,1)S(1)}, u32[]{:S(2)}, u32[]{:S(2)}) collective-permute-start(bf16[64,640]{1,0:T(8,128)(2,1)} %bitcast.10), channel_id=1, source_target_pairs={{0,4},{4,8},{8,12},{12,0},{1,5},{5,9},{9,13},{13,1},{2,6},{6,10},{... | collective-permute-start | bytes 245768 | tf_op jit(solution)/shard_map/ppermute | solution.py:176
  8.0 0.1 pad_add_fusion.pos_ref
  8.0 3.4 %collective-permute-done.1.cp_ref.after_ref = bf16[64,640]{1,0:T(8,128)(2,1)S(1)} collective-permute-done((bf16[64,640]{1,0:T(8,128)(2,1)}, bf16[64,640]{1,0:T(8,128)(2,1)S(1)}, u32[]{:S(2)}, u32[]{:S(2)}) %collective-permute-start.1) | collective-permute-done | bytes 81952 | tf_op jit(solution)/shard_map/ppermute | solution.py:177
  11.4 0.0 collective-permute-done.cm_ref.before_ref
  11.4 0.0 copy-start.1
  11.4 0.9 %copy-done.1 = bf16[64,1,640]{2,0,1:T(8,128)(2,1)S(1)} copy-done((bf16[64,1,640]{2,0,1:T(8,128)(2,1)S(1)}, bf16[64,1,640]{2,0,1:T(8,128)(2,1)}, u32[]{:S(2)}) %copy-start.1) | copy-done | bytes 81944
  12.3 0.0 copy-start.3
  12.3 1.2 %copy-done.3 = bf16[27,64,256]{2,1,0:T(8,128)(2,1)S(1)} copy-done((bf16[27,64,256]{2,1,0:T(8,128)(2,1)S(1)}, bf16[27,64,256]{2,1,0:T(8,128)(2,1)}, u32[]{:S(2)}) %copy-start.3) | copy-done | bytes 884760
  13.5 0.0 copy-start
  13.5 1.9 %input_grad.1 = (f32[64,640]{1,0:T(8,128)S(1)}, f32[64,640]{1,0:T(8,128)S(1)}, f32[64,640]{1,0:T(8,128)S(1)}, f32[64,640]{1,0:T(8,128)S(1)}) custom-call(s32[2]{0:T(128)S(1)} %pad_add_fusion.pos_ref, bf16[64,640]{1,0:T(8,128)(2,1)S(1)} %collective-permute-done.cm_ref.before_ref, bf16[64,640]{1,0:T(8,128)(2,1)S(1)} %bitcast.11, ...), custom_call_target="tpu_custom_call" | custom-call | flops 566231040 | bytes 1785864 | tf_op jit(solution)/shard_map/input_grad/pallas_call | solution.py:146
  15.3 0.0 copy-start.4
  15.4 0.1 collective-permute-start.8
  15.4 0.0 collective-permute-done.4.refs_3_
  15.4 0.0 collective-permute-done.3.refs_2_
  15.4 0.0 collective-permute-done.2.refs_1_
  15.5 0.0 copy-done
  15.5 0.6 %gather.1 = (bf16[256,640]{1,0:T(8,128)(2,1)S(1)}, bf16[128,640]{1,0:T(8,128)(2,1)S(1)}) custom-call(s32[2]{0:T(128)S(1)} %pad_add_fusion.pos_ref, bf16[64,640]{1,0:T(8,128)(2,1)S(1)} %bitcast.12, bf16[64,640]{1,0:T(8,128)(2,1)S(1)} %bitcast.8, bf16[64,640]{1,0:T(8,128)(2,1)S(1)} %collective-permute-done.2.refs_1_, ...), custom_call_target="tpu_custom_call" | custom-call | bytes 901128 | tf_op jit(solution)/shard_map/gather/pallas_call | solution.py:146
  16.1 0.5 %collective-permute-start.6 = (bf16[256,640]{1,0:T(8,128)(2,1)S(1)}, bf16[256,640]{1,0:T(8,128)(2,1)S(1)}, u32[]{:S(2)}, u32[]{:S(2)}) collective-permute-start(bf16[256,640]{1,0:T(8,128)(2,1)S(1)} %get-tuple-element.11.f0_ref), channel_id=1, source_target_pairs={{0,12},{4,0},{8,4},{12,8},{1,13},{5,1},{9,5},{13,9},{2,14},{6,2},{... | collective-permute-start | bytes 983048 | tf_op jit(solution)/shard_map/ppermute | solution.py:198
  16.6 1.3 %collective-permute-start.5 = (bf16[256,640]{1,0:T(8,128)(2,1)S(1)}, bf16[256,640]{1,0:T(8,128)(2,1)S(1)}, u32[]{:S(2)}, u32[]{:S(2)}) collective-permute-start(bf16[256,640]{1,0:T(8,128)(2,1)S(1)} %get-tuple-element.11.f0_ref), channel_id=1, source_target_pairs={{0,4},{4,8},{8,12},{12,0},{1,5},{5,9},{9,13},{13,1},{2,6},{6,10},{... | collective-permute-start | bytes 983048 | tf_op jit(solution)/shard_map/ppermute | solution.py:197
  17.9 1.3 %collective-permute-start.9 = (f32[64,640]{1,0:T(8,128)S(1)}, f32[64,640]{1,0:T(8,128)S(1)}, u32[]{:S(2)}, u32[]{:S(2)}) collective-permute-start(f32[64,640]{1,0:T(8,128)S(1)} %get-tuple-element.16), channel_id=1, source_target_pairs={{0,2},{1,3},{2,0},{3,1},{4,6},{5,7},{6,4},{7,5},{8,10},{9,11},{10,... | collective-permute-start | bytes 491528 | tf_op jit(solution)/shard_map/ppermute | solution.py:188
  19.2 0.5 %collective-permute-start.10 = (f32[64,640]{1,0:T(8,128)S(1)}, f32[64,640]{1,0:T(8,128)S(1)}, u32[]{:S(2)}, u32[]{:S(2)}) collective-permute-start(f32[64,640]{1,0:T(8,128)S(1)} %get-tuple-element.17), channel_id=1, source_target_pairs={{0,3},{1,0},{2,1},{3,2},{4,7},{5,4},{6,5},{7,6},{8,11},{9,8},{10,9... | collective-permute-start | bytes 491528 | tf_op jit(solution)/shard_map/ppermute | solution.py:188
  19.6 1.1 %collective-permute-done.8.refs_1_ = f32[64,640]{1,0:T(8,128)S(1)} collective-permute-done((f32[64,640]{1,0:T(8,128)S(1)}, f32[64,640]{1,0:T(8,128)S(1)}, u32[]{:S(2)}, u32[]{:S(2)}) %collective-permute-start.8) | collective-permute-done | bytes 163872 | tf_op jit(solution)/shard_map/ppermute | solution.py:188
  20.8 0.0 collective-permute-start.7
  20.8 9.5 %collective-permute-done.9.refs_2_ = f32[64,640]{1,0:T(8,128)S(1)} collective-permute-done((f32[64,640]{1,0:T(8,128)S(1)}, f32[64,640]{1,0:T(8,128)S(1)}, u32[]{:S(2)}, u32[]{:S(2)}) %collective-permute-start.9) | collective-permute-done | bytes 163872 | tf_op jit(solution)/shard_map/ppermute | solution.py:188
  30.2 1.8 %collective-permute-done.10.refs_3_ = f32[64,640]{1,0:T(8,128)S(1)} collective-permute-done((f32[64,640]{1,0:T(8,128)S(1)}, f32[64,640]{1,0:T(8,128)S(1)}, u32[]{:S(2)}, u32[]{:S(2)}) %collective-permute-start.10) | collective-permute-done | bytes 163872 | tf_op jit(solution)/shard_map/ppermute | solution.py:188
  32.1 0.0 copy-start.2
  32.1 0.7 %total.1 = f32[64,1,640]{2,1,0:T(1,128)} custom-call(f32[64,640]{1,0:T(8,128)S(1)} %get-tuple-element.14.refs_0_, f32[64,640]{1,0:T(8,128)S(1)} %collective-permute-done.8.refs_1_, f32[64,640]{1,0:T(8,128)S(1)} %collective-permute-done.9.refs_2_, f32[64,640]{1,0:T(8,128)S(1)} %collective-permute-done.10.refs_3_), custom_call_target="tpu_custom_call" | custom-call | bytes 819200 | tf_op jit(solution)/shard_map/total/pallas_call | solution.py:146
  32.8 0.0 collective-permute-done.7.refs_0_
  32.8 0.0 collective-permute-done.6.fp_ref
  32.8 0.0 collective-permute-done.5.fm_ref
  32.8 0.0 copy-done.4
  32.8 0.1 copy-done.2
  32.9 3.4 %output_and_weight_grad.1 = (f32[64,1,640]{2,1,0:T(1,128)}, f32[27,64,64]{2,1,0:T(8,128)}) custom-call(s32[2]{0:T(128)S(1)} %pad_add_fusion.pos_ref, bf16[1728,256]{1,0:T(8,128)(2,1)S(1)} %bitcast.15, bf16[64,640]{1,0:T(8,128)(2,1)S(1)} %bitcast.13, bf16[64,640]{1,0:T(8,128)(2,1)S(1)} %collective-permute-done.cm_ref.before_ref, ...), custom_call_target="tpu_custom_call" | custom-call | flops 1132462080 | bytes 2883592 | tf_op jit(solution)/shard_map/output_and_weight_grad/pallas_call | solution.py:146
Async XLA Ops:
  0.6 14.8 %collective-permute-start.4 = (bf16[64,640]{1,0:T(8,128)(2,1)}, bf16[64,640]{1,0:T(8,128)(2,1)S(1)}, u32[]{:S(2)}, u32[]{:S(2)}) collective-permute-start(bf16[64,640]{1,0:T(8,128)(2,1)} %bitcast.5), channel_id=1, source_target_pairs={{0,3},{1,0},{2,1},{3,2},{4,7},{5,4},{6,5},{7,6},{8,11},{9,8},{10,9... | collective-permute-start | bytes 245768 | tf_op jit(solution)/shard_map/ppermute | solution.py:178
  0.9 14.6 %collective-permute-start.3 = (bf16[64,640]{1,0:T(8,128)(2,1)}, bf16[64,640]{1,0:T(8,128)(2,1)S(1)}, u32[]{:S(2)}, u32[]{:S(2)}) collective-permute-start(bf16[64,640]{1,0:T(8,128)(2,1)} %bitcast.6), channel_id=1, source_target_pairs={{0,2},{1,3},{2,0},{3,1},{4,6},{5,7},{6,4},{7,5},{8,10},{9,11},{10,... | collective-permute-start | bytes 245768 | tf_op jit(solution)/shard_map/ppermute | solution.py:178
  3.2 12.3 %collective-permute-start.2 = (bf16[64,640]{1,0:T(8,128)(2,1)}, bf16[64,640]{1,0:T(8,128)(2,1)S(1)}, u32[]{:S(2)}, u32[]{:S(2)}) collective-permute-start(bf16[64,640]{1,0:T(8,128)(2,1)} %bitcast.7), channel_id=1, source_target_pairs={{0,1},{1,2},{2,3},{3,0},{4,5},{5,6},{6,7},{7,4},{8,9},{9,10},{10,1... | collective-permute-start | bytes 245768 | tf_op jit(solution)/shard_map/ppermute | solution.py:178
  5.4 6.1 %collective-permute-start.1 = (bf16[64,640]{1,0:T(8,128)(2,1)}, bf16[64,640]{1,0:T(8,128)(2,1)S(1)}, u32[]{:S(2)}, u32[]{:S(2)}) collective-permute-start(bf16[64,640]{1,0:T(8,128)(2,1)} %bitcast.9), channel_id=1, source_target_pairs={{0,12},{4,0},{8,4},{12,8},{1,13},{5,1},{9,5},{13,9},{2,14},{6,2},{... | collective-permute-start | bytes 245768 | tf_op jit(solution)/shard_map/ppermute | solution.py:177
  6.9 4.6 %collective-permute-start = (bf16[64,640]{1,0:T(8,128)(2,1)}, bf16[64,640]{1,0:T(8,128)(2,1)S(1)}, u32[]{:S(2)}, u32[]{:S(2)}) collective-permute-start(bf16[64,640]{1,0:T(8,128)(2,1)} %bitcast.10), channel_id=1, source_target_pairs={{0,4},{4,8},{8,12},{12,0},{1,5},{5,9},{9,13},{13,1},{2,6},{6,10},{... | collective-permute-start | bytes 245768 | tf_op jit(solution)/shard_map/ppermute | solution.py:176
  11.4 0.9 %copy-start.1 = (bf16[64,1,640]{2,0,1:T(8,128)(2,1)S(1)}, bf16[64,1,640]{2,0,1:T(8,128)(2,1)}, u32[]{:S(2)}) copy-start(bf16[64,1,640]{2,0,1:T(8,128)(2,1)} %param.5) | copy-start | bytes 245764
  12.3 1.2 %copy-start.3 = (bf16[27,64,256]{2,1,0:T(8,128)(2,1)S(1)}, bf16[27,64,256]{2,1,0:T(8,128)(2,1)}, u32[]{:S(2)}) copy-start(bf16[27,64,256]{2,1,0:T(8,128)(2,1)} %param.4) | copy-start | bytes 2654212
  13.5 2.0 %copy-start = (bf16[64,1,640]{2,0,1:T(8,128)(2,1)S(1)}, bf16[64,1,640]{2,0,1:T(8,128)(2,1)}, u32[]{:S(2)}) copy-start(bf16[64,1,640]{2,0,1:T(8,128)(2,1)} %param.3) | copy-start | bytes 245764
  15.3 17.5 %copy-start.4 = (bf16[27,64,256]{2,1,0:T(8,128)(2,1)S(1)}, bf16[27,64,256]{2,1,0:T(8,128)(2,1)}, u32[]{:S(2)}) copy-start(bf16[27,64,256]{2,1,0:T(8,128)(2,1)} %param.4) | copy-start | bytes 2654212
  15.4 5.4 %collective-permute-start.8 = (f32[64,640]{1,0:T(8,128)S(1)}, f32[64,640]{1,0:T(8,128)S(1)}, u32[]{:S(2)}, u32[]{:S(2)}) collective-permute-start(f32[64,640]{1,0:T(8,128)S(1)} %get-tuple-element.15), channel_id=1, source_target_pairs={{0,1},{1,2},{2,3},{3,0},{4,5},{5,6},{6,7},{7,4},{8,9},{9,10},{10,1... | collective-permute-start | bytes 491528 | tf_op jit(solution)/shard_map/ppermute | solution.py:188
  16.1 16.7 %collective-permute-start.6 = (bf16[256,640]{1,0:T(8,128)(2,1)S(1)}, bf16[256,640]{1,0:T(8,128)(2,1)S(1)}, u32[]{:S(2)}, u32[]{:S(2)}) collective-permute-start(bf16[256,640]{1,0:T(8,128)(2,1)S(1)} %get-tuple-element.11.f0_ref), channel_id=1, source_target_pairs={{0,12},{4,0},{8,4},{12,8},{1,13},{5,1},{9,5},{13,9},{2,14},{6,2},{... | collective-permute-start | bytes 983048 | tf_op jit(solution)/shard_map/ppermute | solution.py:198
  16.6 16.2 %collective-permute-start.5 = (bf16[256,640]{1,0:T(8,128)(2,1)S(1)}, bf16[256,640]{1,0:T(8,128)(2,1)S(1)}, u32[]{:S(2)}, u32[]{:S(2)}) collective-permute-start(bf16[256,640]{1,0:T(8,128)(2,1)S(1)} %get-tuple-element.11.f0_ref), channel_id=1, source_target_pairs={{0,4},{4,8},{8,12},{12,0},{1,5},{5,9},{9,13},{13,1},{2,6},{6,10},{... | collective-permute-start | bytes 983048 | tf_op jit(solution)/shard_map/ppermute | solution.py:197
  17.9 12.4 %collective-permute-start.9 = (f32[64,640]{1,0:T(8,128)S(1)}, f32[64,640]{1,0:T(8,128)S(1)}, u32[]{:S(2)}, u32[]{:S(2)}) collective-permute-start(f32[64,640]{1,0:T(8,128)S(1)} %get-tuple-element.16), channel_id=1, source_target_pairs={{0,2},{1,3},{2,0},{3,1},{4,6},{5,7},{6,4},{7,5},{8,10},{9,11},{10,... | collective-permute-start | bytes 491528 | tf_op jit(solution)/shard_map/ppermute | solution.py:188
  19.2 12.9 %collective-permute-start.10 = (f32[64,640]{1,0:T(8,128)S(1)}, f32[64,640]{1,0:T(8,128)S(1)}, u32[]{:S(2)}, u32[]{:S(2)}) collective-permute-start(f32[64,640]{1,0:T(8,128)S(1)} %get-tuple-element.17), channel_id=1, source_target_pairs={{0,3},{1,0},{2,1},{3,2},{4,7},{5,4},{6,5},{7,6},{8,11},{9,8},{10,9... | collective-permute-start | bytes 491528 | tf_op jit(solution)/shard_map/ppermute | solution.py:188
  20.8 12.0 %collective-permute-start.7 = (bf16[128,640]{1,0:T(8,128)(2,1)S(1)}, bf16[128,640]{1,0:T(8,128)(2,1)S(1)}, u32[]{:S(2)}, u32[]{:S(2)}) collective-permute-start(bf16[128,640]{1,0:T(8,128)(2,1)S(1)} %get-tuple-element.12), channel_id=1, source_target_pairs={{0,8},{4,12},{8,0},{12,4},{1,9},{5,13},{9,1},{13,5},{2,10},{6,14},... | collective-permute-start | bytes 491528 | tf_op jit(solution)/shard_map/ppermute | solution.py:199
  32.1 0.9 %copy-start.2 = (bf16[64,1,640]{2,0,1:T(8,128)(2,1)S(1)}, bf16[64,1,640]{2,0,1:T(8,128)(2,1)}, u32[]{:S(2)}) copy-start(bf16[64,1,640]{2,0,1:T(8,128)(2,1)} %param.5) | copy-start | bytes 245764

commit v4 on v2

v4 whole, which is shorter than its diff:
```python
import functools
import math

import jax
import jax.numpy as jnp
from jax import lax
from jax.experimental import pallas as pl
from jax.experimental.pallas import tpu as pltpu
from jax.sharding import PartitionSpec as P

NX = 64
NY = 10
CELLS = NX * NY
F32 = jnp.float32
BF16 = jnp.bfloat16
VMEM_BYTES = 32 * 1024 * 1024


def cell_mask(rows, dy, dx):
    q = lax.broadcasted_iota(jnp.int32, (rows, CELLS), 1)
    x = q % NX + dx
    y = q // NX + dy
    return (x >= 0) & (x < NX) & (y >= 0) & (y < NY)


def shifted(value, dy, dx):
    if dy == 0 and dx == 0:
        return value
    moved = pltpu.roll(value, (-(dy * NX + dx)) % CELLS, 1)
    return jnp.where(cell_mask(value.shape[0], dy, dx), moved, 0.0)


def gather_kernel(nz, nc, pos_ref, token_ref, cot_ref, *refs):
    pieces = refs[:nc]
    f_ref = refs[nc]
    packs = refs[nc + 1 :]
    blocks = cot_ref.shape[0]
    cols = f_ref.shape[0] // nz
    s, c = pos_ref[0], pos_ref[1]
    for k in range(nc):
        f_ref[pl.ds(pl.multiple_of((c ^ k) * blocks, blocks), blocks), :] = pieces[k][...]
    for k, pack in zip(range(2, nz), packs):
        goal = lax.rem(s + k, nz) if k < nz - 1 else nz - 1 - s
        pack[:cols, :] = f_ref[pl.ds(pl.multiple_of(goal * cols, cols), cols), :]
        pack[cols:, :] = cot_ref[...]


def columns(cols_ref, first, plane):
    blocks = plane.shape[0]
    for dy in (-1, 0, 1):
        for dx in (-1, 0, 1):
            tap = first + 3 * (dy + 1) + dx + 1
            cols_ref[tap * blocks : (tap + 1) * blocks, :] = shifted(plane, -dy, -dx).astype(BF16)


def own_plane_kernel(cot_ref, cols_ref):
    columns(cols_ref, 0, cot_ref[...].astype(F32))


def input_grad_kernel(nz, nc, pos_ref, own_ref, even_ref, odd_ref, w_ref, *refs):
    send_ref, keep_ref, token_ref, cols_ref, sum_ref = refs
    blocks = even_ref.shape[0]
    s, c = pos_ref[0], pos_ref[1]
    token_ref[...] = jnp.zeros(token_ref.shape, F32)
    even, odd = even_ref[...].astype(F32), odd_ref[...].astype(F32)
    first = s % 2 == 0
    columns(cols_ref, 0, jnp.where(s < nz - 1, jnp.where(first, even, odd), 0.0))
    columns(cols_ref, 9, jnp.where(s > 0, jnp.where(first, odd, even), 0.0))
    taps = 9 * blocks
    over_rows = (((0,), (0,)), ((), ()))
    near = lax.dot_general(
        w_ref[taps : 2 * taps, :], own_ref[...], over_rows, preferred_element_type=F32
    )
    low = lax.dot_general(
        w_ref[:taps, :], cols_ref[:taps, :], over_rows, preferred_element_type=F32
    )
    high = lax.dot_general(
        w_ref[2 * taps :, :], cols_ref[taps:, :], over_rows, preferred_element_type=F32
    )
    sum_ref[...] = near + low + high
    for k in range(nc):
        goal = c ^ k
        block = sum_ref[pl.ds(pl.multiple_of(goal * blocks, blocks), blocks), :]
        ref = send_ref if k % 2 else keep_ref
        ref[k // 2 * blocks : (k // 2 + 1) * blocks, :] = block


def fold_kernel(blocks, keep_ref, got_ref, send_ref, left_ref):
    for k in range(keep_ref.shape[0] // blocks):
        at = slice(k * blocks, (k + 1) * blocks)
        to = slice(k // 2 * blocks, (k // 2 + 1) * blocks)
        (send_ref if k % 2 else left_ref)[to, :] = keep_ref[at, :] + got_ref[at, :]


def output_kernel(nz, scale, pos_ref, w_ref, cot_ref, ce_ref, co_ref, f0_ref, fe_ref, fo_ref, *refs):
    packs = refs[: nz - 2]
    out_ref, wg_ref, token_ref, c_ref, g_ref = refs[nz - 2 :]
    blocks = cot_ref.shape[0]
    cols = g_ref.shape[1]
    taps = 9 * blocks
    s = pos_ref[0]
    first = s % 2 == 0
    even, odd = fe_ref[...].astype(F32), fo_ref[...].astype(F32)
    fields = {
        -1: jnp.where(s > 0, jnp.where(first, odd, even), 0.0).astype(BF16),
        0: f0_ref[...],
        1: jnp.where(s < nz - 1, jnp.where(first, even, odd), 0.0).astype(BF16),
    }
    acc = None
    for dz in (-1, 0, 1):
        term = jnp.dot(
            w_ref[(dz + 1) * taps : (dz + 2) * taps, :], fields[dz], preferred_element_type=F32
        )
        acc = term if acc is None else acc + term
    total = None
    for dx in (-1, 0, 1):
        for dy in (-1, 0, 1):
            at = (3 * (dy + 1) + dx + 1) * blocks
            term = shifted(acc[at : at + blocks], dy, dx)
            total = term if total is None else total + term
    out_ref[:, 0, :] = total
    token_ref[...] = jnp.zeros(token_ref.shape, F32)

    mine = pl.ds(pl.multiple_of(s * cols, cols), cols)
    odd_source = jnp.clip(jnp.where(first, s - 1, s + 1), 0, nz - 1)
    c_ref[odd_source] = co_ref[...]
    g_ref[odd_source] = fo_ref[mine, :]
    even_source = s ^ 1
    c_ref[even_source] = ce_ref[...]
    g_ref[even_source] = fe_ref[mine, :]
    c_ref[s] = cot_ref[...]
    g_ref[s] = f0_ref[mine, :]
    for k, pack in zip(range(2, nz - 1), packs):
        source = lax.rem(s + nz - k, nz)
        c_ref[source] = pack[cols:, :]
        g_ref[source] = pack[:cols, :]

    @pl.when((s == 0) | (s == nz - 1))
    def _():
        source = nz - 1 - s
        c_ref[source] = packs[-1][cols:, :]
        g_ref[source] = packs[-1][:cols, :]

    cots = []
    feats = []
    for z in range(nz):
        plane = c_ref[z].astype(F32)
        cots.append([shifted(plane, -dy, 0).astype(BF16) for dy in (-1, 0, 1)])
        field = g_ref[z].astype(F32)
        feats.append(jnp.concatenate([shifted(field, 0, dx).astype(BF16) for dx in (-1, 0, 1)], 0))
    for dz in (-1, 0, 1):
        sums = None
        for z in range(nz):
            if 0 <= z - dz < nz:
                term = lax.dot_general(
                    jnp.concatenate(cots[z - dz], 0),
                    feats[z],
                    (((1,), (1,)), ((), ())),
                    preferred_element_type=F32,
                )
                sums = term if sums is None else sums + term
        sums = sums * scale
        for dy in range(3):
            for dx in range(3):
                tap = 9 * (dz + 1) + 3 * dy + dx
                wg_ref[tap] = sums[dy * blocks : (dy + 1) * blocks, dx * cols : (dx + 1) * cols]


def total_kernel(token_ref, keep_ref, got_ref, out_ref):
    out_ref[:, 0, :] = keep_ref[...] + got_ref[...]


VMEM = pl.BlockSpec(memory_space=pltpu.VMEM)
SMEM = pl.BlockSpec(memory_space=pltpu.SMEM)


def kernel_call(body, name, outs, args, scratch=(), flops=0):
    moved = sum(math.prod(a.shape) * a.dtype.itemsize for a in args + outs)
    return pl.pallas_call(
        body,
        out_shape=outs,
        in_specs=[SMEM if a.dtype == jnp.int32 else VMEM for a in args],
        out_specs=tuple(VMEM for _ in outs),
        scratch_shapes=list(scratch),
        compiler_params=pltpu.CompilerParams(vmem_limit_bytes=VMEM_BYTES),
        cost_estimate=pl.CostEstimate(flops=flops, bytes_accessed=moved, transcendentals=0),
        name=name,
    )(*args)


def per_device(features, weights, cotangent):
    blocks, depth, plane = features.shape
    channels = weights.shape[2]
    nz = lax.axis_size("sp")
    nc = lax.axis_size("ch")
    cols = channels // nz
    w2 = weights.reshape(27 * blocks, channels)
    feat = features.reshape(blocks, plane)
    cot = cotangent.reshape(blocks, plane)
    pos = jnp.stack([lax.axis_index("sp"), lax.axis_index("ch")]).astype(jnp.int32)

    even_pairs = [(i, i ^ 1) for i in range(nz)]
    odd_pairs = [(i, min(max(((i + 1) ^ 1) - 1, 0), nz - 1)) for i in range(nz)]
    ends = [(i, nz - 1 - i if i in (0, nz - 1) else i) for i in range(nz)]

    def mixed(k):
        return [(i, i ^ k) for i in range(nc)]

    def of(rows, dtype):
        return jax.ShapeDtypeStruct((rows, plane), dtype)

    small = jax.ShapeDtypeStruct((8, 128), F32)
    work = 2 * 27 * blocks * channels * plane

    cot_even = lax.ppermute(cot, "sp", even_pairs)
    cot_odd = lax.ppermute(cot, "sp", odd_pairs)
    (own,) = kernel_call(own_plane_kernel, "own_plane", [of(9 * blocks, BF16)], [cot], flops=work)
    feat, cot_even = lax.optimization_barrier((feat, cot_even))
    pieces = [feat] + [lax.ppermute(feat, "ch", mixed(k)) for k in range(1, nc)]

    send, keep, token = kernel_call(
        functools.partial(input_grad_kernel, nz, nc),
        "input_grad",
        [of(channels // 2, F32), of(channels // 2, F32), small],
        [pos, own, cot_even, cot_odd, w2],
        [pltpu.VMEM((18 * blocks, plane), BF16), pltpu.VMEM((channels, plane), F32)],
        work,
    )
    step = 1
    got = lax.ppermute(send, "ch", mixed(step))
    while 2 * step < nc:
        step *= 2
        rows = channels // (2 * step)
        send, keep = kernel_call(
            functools.partial(fold_kernel, blocks), "fold", [of(rows, F32)] * 2, [keep, got]
        )
        got = lax.ppermute(send, "ch", mixed(step))

    f_all, *packs = kernel_call(
        functools.partial(gather_kernel, nz, nc),
        "gather",
        [of(channels, BF16)] + [of(cols + blocks, BF16)] * (nz - 2),
        [pos, token, cot] + pieces,
    )
    f_even = lax.ppermute(f_all, "sp", even_pairs)
    f_odd = lax.ppermute(f_all, "sp", odd_pairs)
    far = [
        lax.ppermute(packs[k - 2], "sp", [(i, (i + k) % nz) for i in range(nz)])
        for k in range(2, nz - 1)
    ]
    far.append(lax.ppermute(packs[-1], "sp", ends))

    output, weight_grad, last = kernel_call(
        functools.partial(output_kernel, nz, 1.0 / math.sqrt(nz * depth * plane)),
        "output_and_weight_grad",
        [
            jax.ShapeDtypeStruct((blocks, 1, plane), F32),
            jax.ShapeDtypeStruct((27, blocks, cols), F32),
            small,
        ],
        [pos, w2, cot, cot_even, cot_odd, f_all, f_even, f_odd] + far,
        [pltpu.VMEM((nz, blocks, plane), BF16), pltpu.VMEM((nz, cols, plane), BF16)],
        4 * work,
    )
    (back,) = kernel_call(
        total_kernel, "total", [jax.ShapeDtypeStruct((blocks, 1, plane), F32)], [last, keep, got]
    )
    return (output, back, weight_grad)


def solution(mesh):
    return jax.shard_map(
        per_device,
        mesh=mesh,
        in_specs=(P("ch", ("grp", "sp"), None), P(None, "ch", None), P("ch", ("grp", "sp"), None)),
        out_specs=(
            P("ch", ("grp", "sp"), None),
            P("ch", ("grp", "sp"), None),
            P("grp", "ch", "sp"),
        ),
        check_vma=False,
    )
```

time: 43 us -> 36.9 us (0.86)
  starting transfers between devices: 26.1 us -> 17.9 us
  waiting for transfers between devices: 6.58 us -> 8.81 us
    ppermute x12 -> x11, starting transfers between devices: 26.1 us -> 17.9 us  [the longest x3 4.39 us: per_device(): pieces = [feat] + [lax.ppermute(feat, 'ch', mixed(k)) for k in range(1, nc)]]
    ppermute x12 -> x11, waiting for transfers between devices: 6.58 us -> 8.81 us  [the longest x1 5.2 us: per_device(): lax.ppermute(packs[k - 2], 'sp', [(i, (i + k) % nz) for i in range(nz)])]
    pallas_call x4 -> x6, Pallas kernels: 7.08 us -> 7.27 us  [kernel_call(): pl.pallas_call(body, out_shape=outs, in_specs=[SMEM if a.dtype == jnp.int...]
  transfers between devices with their start and end apart: 12 -> 11, of which waited for: 4 -> 4; matrix products, arithmetic and copies ran while one was open for 0% -> 0% of each run, Pallas kernels for 7% -> 18%
where the time goes in v4:
time: 36.9 us; the launch traced here: 36.6 us
  starting transfers between devices  17.9 us (49%)
  waiting for transfers between devices  8.81 us (24%)
  Pallas kernels  7.27 us (20%)
  local copies, waits for them, and re-layouts  1.84 us (5%)
  between operations  0.7 us (2%)
    pallas_call x6, Pallas kernels, kernel_call(): pl.pallas_call(body, out_shape=outs, in_specs=[SMEM if a.dtype == jnp.int...  7.27 us
    ppermute x1, waiting for transfers between devices, per_device(): lax.ppermute(packs[k - 2], 'sp', [(i, (i + k) % nz) for i in range(nz)])  5.2 us
    ppermute x3, starting transfers between devices, per_device(): pieces = [feat] + [lax.ppermute(feat, 'ch', mixed(k)) for k in range(1, nc)]  4.39 us
    ppermute x1, starting transfers between devices, per_device(): cot_even = lax.ppermute(cot, 'sp', even_pairs)  3.49 us
    ppermute x2, starting transfers between devices, per_device(): got = lax.ppermute(send, 'ch', mixed(step))  3.04 us
    ppermute x1, starting transfers between devices, per_device(): far.append(lax.ppermute(packs[-1], 'sp', ends))  2.31 us
    unnamed x8, local copies, waits for them, and re-layouts  1.84 us
    ppermute x3, waiting for transfers between devices, per_device(): pieces = [feat] + [lax.ppermute(feat, 'ch', mixed(k)) for k in range(1, nc)]  1.69 us
  transfers between devices with their start and end apart: 11, of which 4 were waited for; matrix products, arithmetic and copies ran while one was open for 0% of the time, Pallas kernels for 18%

profile of v4, /device:TPU:0, one launch (start us, length us, event | category | flops | bytes accessed | tf_op | source)
XLA Modules:
  0.0 36.6 jit_solution(3753291295544248001)
XLA Ops:
  0.6 1.5 %collective-permute-start.1 = (bf16[64,640]{1,0:T(8,128)(2,1)}, bf16[64,640]{1,0:T(8,128)(2,1)S(1)}, u32[]{:S(2)}, u32[]{:S(2)}) collective-permute-start(bf16[64,640]{1,0:T(8,128)(2,1)} %bitcast.9), channel_id=1, source_target_pairs={{0,0},{4,8},{8,4},{12,12},{1,1},{5,9},{9,5},{13,13},{2,2},{6,10},{... | collective-permute-start | bytes 245768 | tf_op jit(solution)/shard_map/ppermute | solution.py:216
  2.2 3.5 %collective-permute-start = (bf16[64,640]{1,0:T(8,128)(2,1)}, bf16[64,640]{1,0:T(8,128)(2,1)S(1)}, u32[]{:S(2)}, u32[]{:S(2)}) collective-permute-start(bf16[64,640]{1,0:T(8,128)(2,1)} %bitcast.10), channel_id=1, source_target_pairs={{0,4},{4,0},{8,12},{12,8},{1,5},{5,1},{9,13},{13,9},{2,6},{6,2},{1... | collective-permute-start | bytes 245768 | tf_op jit(solution)/shard_map/ppermute | solution.py:215
  5.7 0.1 pad_add_fusion.pos_ref
  5.7 1.1 %collective-permute-done.even_ref.ce_ref = bf16[64,640]{1,0:T(8,128)(2,1)S(1)} collective-permute-done((bf16[64,640]{1,0:T(8,128)(2,1)}, bf16[64,640]{1,0:T(8,128)(2,1)S(1)}, u32[]{:S(2)}, u32[]{:S(2)}) %collective-permute-start) | collective-permute-done | bytes 81952 | tf_op jit(solution)/shard_map/ppermute | solution.py:215
  6.8 3.6 %collective-permute-start.4 = (bf16[64,640]{1,0:T(8,128)(2,1)}, bf16[64,640]{1,0:T(8,128)(2,1)S(1)}, u32[]{:S(2)}, u32[]{:S(2)}) collective-permute-start(bf16[64,640]{1,0:T(8,128)(2,1)} %bitcast.5), channel_id=1, source_target_pairs={{0,3},{1,2},{2,1},{3,0},{4,7},{5,6},{6,5},{7,4},{8,11},{9,10},{10,... | collective-permute-start | bytes 245768 | tf_op jit(solution)/shard_map/ppermute | solution.py:219
  10.4 0.0 collective-permute-start.3
  10.4 0.8 %collective-permute-start.2 = (bf16[64,640]{1,0:T(8,128)(2,1)}, bf16[64,640]{1,0:T(8,128)(2,1)S(1)}, u32[]{:S(2)}, u32[]{:S(2)}) collective-permute-start(bf16[64,640]{1,0:T(8,128)(2,1)} %bitcast.7), channel_id=1, source_target_pairs={{0,1},{1,0},{2,3},{3,2},{4,5},{5,4},{6,7},{7,6},{8,9},{9,8},{10,11... | collective-permute-start | bytes 245768 | tf_op jit(solution)/shard_map/ppermute | solution.py:219
  11.2 0.0 copy-start.1
  11.2 0.9 %copy-done.1 = bf16[64,1,640]{2,0,1:T(8,128)(2,1)S(1)} copy-done((bf16[64,1,640]{2,0,1:T(8,128)(2,1)S(1)}, bf16[64,1,640]{2,0,1:T(8,128)(2,1)}, u32[]{:S(2)}) %copy-start.1) | copy-done | bytes 81944
  12.1 0.0 copy-start.3
  12.1 0.2 own_plane.1.own_ref
  12.3 0.0 collective-permute-done.1.odd_ref.co_ref
  12.3 0.9 %copy-done.3 = bf16[27,64,256]{2,1,0:T(8,128)(2,1)S(1)} copy-done((bf16[27,64,256]{2,1,0:T(8,128)(2,1)S(1)}, bf16[27,64,256]{2,1,0:T(8,128)(2,1)}, u32[]{:S(2)}) %copy-start.3) | copy-done | bytes 884760
  13.2 0.0 copy-start
  13.2 0.0 copy-start.2
  13.2 1.8 %input_grad.1 = (f32[128,640]{1,0:T(8,128)S(1)}, f32[128,640]{1,0:T(8,128)S(1)}, f32[8,128]{1,0:T(8,128)S(1)}) custom-call(s32[2]{0:T(128)S(1)} %pad_add_fusion.pos_ref, bf16[576,640]{1,0:T(8,128)(2,1)S(1)} %own_plane.1.own_ref, bf16[64,640]{1,0:T(8,128)(2,1)S(1)} %collective-permute-done.even_ref.ce_ref, ...), custom_call_target="tpu_custom_call" | custom-call | flops 566231040 | bytes 2445320 | tf_op jit(solution)/shard_map/input_grad/pallas_call | solution.py:179
  15.1 1.3 %collective-permute-start.9 = (f32[128,640]{1,0:T(8,128)S(1)}, f32[128,640]{1,0:T(8,128)S(1)}, u32[]{:S(2)}, u32[]{:S(2)}) collective-permute-start(f32[128,640]{1,0:T(8,128)S(1)} %get-tuple-element.25), channel_id=1, source_target_pairs={{0,1},{1,0},{2,3},{3,2},{4,5},{5,4},{6,7},{7,6},{8,9},{9,8},{10,11... | collective-permute-start | bytes 983048 | tf_op jit(solution)/shard_map/ppermute | solution.py:230
  16.4 0.0 collective-permute-done.4.refs_3_
  16.4 1.7 %collective-permute-done.3.refs_2_ = bf16[64,640]{1,0:T(8,128)(2,1)S(1)} collective-permute-done((bf16[64,640]{1,0:T(8,128)(2,1)}, bf16[64,640]{1,0:T(8,128)(2,1)S(1)}, u32[]{:S(2)}, u32[]{:S(2)}) %collective-permute-start.3) | collective-permute-done | bytes 81952 | tf_op jit(solution)/shard_map/ppermute | solution.py:219
  18.1 0.0 collective-permute-done.2.refs_1_
  18.1 0.0 copy-done
  18.1 0.0 copy-done.2
  18.1 0.6 %gather.1 = (bf16[256,640]{1,0:T(8,128)(2,1)S(1)}, bf16[128,640]{1,0:T(8,128)(2,1)S(1)}, bf16[128,640]{1,0:T(8,128)(2,1)S(1)}) custom-call(s32[2]{0:T(128)S(1)} %pad_add_fusion.pos_ref, f32[8,128]{1,0:T(8,128)S(1)} %get-tuple-element.17.token_ref, bf16[64,640]{1,0:T(8,128)(2,1)S(1)} %bitcast.12, bf16[64,640]{1,0:T(8,128)(2,1)S(1)} %bitcast.8, ...), custom_call_target="tpu_custom_call" | custom-call | bytes 1069064 | tf_op jit(solution)/shard_map/gather/pallas_call | solution.py:179
  18.7 0.7 %collective-permute-start.6 = (bf16[256,640]{1,0:T(8,128)(2,1)S(1)}, bf16[256,640]{1,0:T(8,128)(2,1)S(1)}, u32[]{:S(2)}, u32[]{:S(2)}) collective-permute-start(bf16[256,640]{1,0:T(8,128)(2,1)S(1)} %get-tuple-element.19.f0_ref), channel_id=1, source_target_pairs={{0,0},{4,8},{8,4},{12,12},{1,1},{5,9},{9,5},{13,13},{2,2},{6,10},{... | collective-permute-start | bytes 983048 | tf_op jit(solution)/shard_map/ppermute | solution.py:246
  19.4 1.5 %collective-permute-start.5 = (bf16[256,640]{1,0:T(8,128)(2,1)S(1)}, bf16[256,640]{1,0:T(8,128)(2,1)S(1)}, u32[]{:S(2)}, u32[]{:S(2)}) collective-permute-start(bf16[256,640]{1,0:T(8,128)(2,1)S(1)} %get-tuple-element.19.f0_ref), channel_id=1, source_target_pairs={{0,4},{4,0},{8,12},{12,8},{1,5},{5,1},{9,13},{13,9},{2,6},{6,2},{1... | collective-permute-start | bytes 983048 | tf_op jit(solution)/shard_map/ppermute | solution.py:245
  20.8 1.0 %collective-permute-start.7 = (bf16[128,640]{1,0:T(8,128)(2,1)S(1)}, bf16[128,640]{1,0:T(8,128)(2,1)S(1)}, u32[]{:S(2)}, u32[]{:S(2)}) collective-permute-start(bf16[128,640]{1,0:T(8,128)(2,1)S(1)} %get-tuple-element.20), channel_id=1, source_target_pairs={{0,8},{4,12},{8,0},{12,4},{1,9},{5,13},{9,1},{13,5},{2,10},{6,14},... | collective-permute-start | bytes 491528 | tf_op jit(solution)/shard_map/ppermute | solution.py:248
  21.9 2.3 %collective-permute-start.8 = (bf16[128,640]{1,0:T(8,128)(2,1)S(1)}, bf16[128,640]{1,0:T(8,128)(2,1)S(1)}, u32[]{:S(2)}, u32[]{:S(2)}) collective-permute-start(bf16[128,640]{1,0:T(8,128)(2,1)S(1)} %get-tuple-element.21), channel_id=1, source_target_pairs={{0,12},{4,4},{8,8},{12,0},{1,13},{5,5},{9,9},{13,1},{2,14},{6,6},{... | collective-permute-start | bytes 491528 | tf_op jit(solution)/shard_map/ppermute | solution.py:251
  24.2 0.8 %collective-permute-done.9.got_ref = f32[128,640]{1,0:T(8,128)S(1)} collective-permute-done((f32[128,640]{1,0:T(8,128)S(1)}, f32[128,640]{1,0:T(8,128)S(1)}, u32[]{:S(2)}, u32[]{:S(2)}) %collective-permute-start.9) | collective-permute-done | bytes 327712 | tf_op jit(solution)/shard_map/ppermute | solution.py:230
  25.1 1.7 %collective-permute-start.10 = (f32[64,640]{1,0:T(8,128)S(1)}, f32[64,640]{1,0:T(8,128)S(1)}, u32[]{:S(2)}, u32[]{:S(2)}) collective-permute-start(f32[64,640]{1,0:T(8,128)S(1)} %get-tuple-element.27), channel_id=1, source_target_pairs={{0,2},{1,3},{2,0},{3,1},{4,6},{5,7},{6,4},{7,5},{8,10},{9,11},{10,... | collective-permute-start | bytes 491528 | tf_op jit(solution)/shard_map/ppermute | solution.py:237
  26.8 5.2 %collective-permute-done.7.refs_0_ = bf16[128,640]{1,0:T(8,128)(2,1)S(1)} collective-permute-done((bf16[128,640]{1,0:T(8,128)(2,1)S(1)}, bf16[128,640]{1,0:T(8,128)(2,1)S(1)}, u32[]{:S(2)}, u32[]{:S(2)}) %collective-permute-start.7) | collective-permute-done | bytes 163872 | tf_op jit(solution)/shard_map/ppermute | solution.py:248
  32.0 0.0 collective-permute-done.8.refs_1_
  32.0 0.0 collective-permute-done.6.fo_ref
  32.0 0.0 collective-permute-done.5.fe_ref
  32.0 3.9 %output_and_weight_grad.1 = (f32[64,1,640]{2,1,0:T(1,128)}, f32[27,64,64]{2,1,0:T(8,128)}, f32[8,128]{1,0:T(8,128)S(1)}) custom-call(s32[2]{0:T(128)S(1)} %pad_add_fusion.pos_ref, bf16[1728,256]{1,0:T(8,128)(2,1)S(1)} %bitcast.15, bf16[64,640]{1,0:T(8,128)(2,1)S(1)} %bitcast.13, bf16[64,640]{1,0:T(8,128)(2,1)S(1)} %collective-permute-done.even_ref.ce_ref, ...), custom_call_target="tpu_custom_call" | custom-call | flops 2264924160 | bytes 3051528 | tf_op jit(solution)/shard_map/output_and_weight_grad/pallas_call | solution.py:179
  35.9 0.0 collective-permute-done.10.got_ref
  35.9 0.7 %total.1 = f32[64,1,640]{2,1,0:T(1,128)} custom-call(f32[8,128]{1,0:T(8,128)S(1)} %get-tuple-element.23.token_ref, f32[64,640]{1,0:T(8,128)S(1)} %get-tuple-element.26.keep_ref, f32[64,640]{1,0:T(8,128)S(1)} %collective-permute-done.10.got_ref), custom_call_target="tpu_custom_call" | custom-call | bytes 495616 | tf_op jit(solution)/shard_map/total/pallas_call | solution.py:179
  (1 shorter events, 0.0 us)
Async XLA Ops:
  0.6 11.7 %collective-permute-start.1 = (bf16[64,640]{1,0:T(8,128)(2,1)}, bf16[64,640]{1,0:T(8,128)(2,1)S(1)}, u32[]{:S(2)}, u32[]{:S(2)}) collective-permute-start(bf16[64,640]{1,0:T(8,128)(2,1)} %bitcast.9), channel_id=1, source_target_pairs={{0,0},{4,8},{8,4},{12,12},{1,1},{5,9},{9,5},{13,13},{2,2},{6,10},{... | collective-permute-start | bytes 245768 | tf_op jit(solution)/shard_map/ppermute | solution.py:216
  2.2 4.6 %collective-permute-start = (bf16[64,640]{1,0:T(8,128)(2,1)}, bf16[64,640]{1,0:T(8,128)(2,1)S(1)}, u32[]{:S(2)}, u32[]{:S(2)}) collective-permute-start(bf16[64,640]{1,0:T(8,128)(2,1)} %bitcast.10), channel_id=1, source_target_pairs={{0,4},{4,0},{8,12},{12,8},{1,5},{5,1},{9,13},{13,9},{2,6},{6,2},{1... | collective-permute-start | bytes 245768 | tf_op jit(solution)/shard_map/ppermute | solution.py:215
  6.8 9.6 %collective-permute-start.4 = (bf16[64,640]{1,0:T(8,128)(2,1)}, bf16[64,640]{1,0:T(8,128)(2,1)S(1)}, u32[]{:S(2)}, u32[]{:S(2)}) collective-permute-start(bf16[64,640]{1,0:T(8,128)(2,1)} %bitcast.5), channel_id=1, source_target_pairs={{0,3},{1,2},{2,1},{3,0},{4,7},{5,6},{6,5},{7,4},{8,11},{9,10},{10,... | collective-permute-start | bytes 245768 | tf_op jit(solution)/shard_map/ppermute | solution.py:219
  10.4 7.7 %collective-permute-start.3 = (bf16[64,640]{1,0:T(8,128)(2,1)}, bf16[64,640]{1,0:T(8,128)(2,1)S(1)}, u32[]{:S(2)}, u32[]{:S(2)}) collective-permute-start(bf16[64,640]{1,0:T(8,128)(2,1)} %bitcast.6), channel_id=1, source_target_pairs={{0,2},{1,3},{2,0},{3,1},{4,6},{5,7},{6,4},{7,5},{8,10},{9,11},{10,... | collective-permute-start | bytes 245768 | tf_op jit(solution)/shard_map/ppermute | solution.py:219
  10.4 7.7 %collective-permute-start.2 = (bf16[64,640]{1,0:T(8,128)(2,1)}, bf16[64,640]{1,0:T(8,128)(2,1)S(1)}, u32[]{:S(2)}, u32[]{:S(2)}) collective-permute-start(bf16[64,640]{1,0:T(8,128)(2,1)} %bitcast.7), channel_id=1, source_target_pairs={{0,1},{1,0},{2,3},{3,2},{4,5},{5,4},{6,7},{7,6},{8,9},{9,8},{10,11... | collective-permute-start | bytes 245768 | tf_op jit(solution)/shard_map/ppermute | solution.py:219
  11.2 0.9 %copy-start.1 = (bf16[64,1,640]{2,0,1:T(8,128)(2,1)S(1)}, bf16[64,1,640]{2,0,1:T(8,128)(2,1)}, u32[]{:S(2)}) copy-start(bf16[64,1,640]{2,0,1:T(8,128)(2,1)} %param.5) | copy-start | bytes 245764
  12.1 1.2 %copy-start.3 = (bf16[27,64,256]{2,1,0:T(8,128)(2,1)S(1)}, bf16[27,64,256]{2,1,0:T(8,128)(2,1)}, u32[]{:S(2)}) copy-start(bf16[27,64,256]{2,1,0:T(8,128)(2,1)} %param.4) | copy-start | bytes 2654212
  13.2 4.8 %copy-start = (bf16[64,1,640]{2,0,1:T(8,128)(2,1)S(1)}, bf16[64,1,640]{2,0,1:T(8,128)(2,1)}, u32[]{:S(2)}) copy-start(bf16[64,1,640]{2,0,1:T(8,128)(2,1)} %param.3) | copy-start | bytes 245764
  13.2 4.8 %copy-start.2 = (bf16[64,1,640]{2,0,1:T(8,128)(2,1)S(1)}, bf16[64,1,640]{2,0,1:T(8,128)(2,1)}, u32[]{:S(2)}) copy-start(bf16[64,1,640]{2,0,1:T(8,128)(2,1)} %param.5) | copy-start | bytes 245764
  15.1 9.9 %collective-permute-start.9 = (f32[128,640]{1,0:T(8,128)S(1)}, f32[128,640]{1,0:T(8,128)S(1)}, u32[]{:S(2)}, u32[]{:S(2)}) collective-permute-start(f32[128,640]{1,0:T(8,128)S(1)} %get-tuple-element.25), channel_id=1, source_target_pairs={{0,1},{1,0},{2,3},{3,2},{4,5},{5,4},{6,7},{7,6},{8,9},{9,8},{10,11... | collective-permute-start | bytes 983048 | tf_op jit(solution)/shard_map/ppermute | solution.py:230
  18.7 13.3 %collective-permute-start.6 = (bf16[256,640]{1,0:T(8,128)(2,1)S(1)}, bf16[256,640]{1,0:T(8,128)(2,1)S(1)}, u32[]{:S(2)}, u32[]{:S(2)}) collective-permute-start(bf16[256,640]{1,0:T(8,128)(2,1)S(1)} %get-tuple-element.19.f0_ref), channel_id=1, source_target_pairs={{0,0},{4,8},{8,4},{12,12},{1,1},{5,9},{9,5},{13,13},{2,2},{6,10},{... | collective-permute-start | bytes 983048 | tf_op jit(solution)/shard_map/ppermute | solution.py:246
  19.4 12.6 %collective-permute-start.5 = (bf16[256,640]{1,0:T(8,128)(2,1)S(1)}, bf16[256,640]{1,0:T(8,128)(2,1)S(1)}, u32[]{:S(2)}, u32[]{:S(2)}) collective-permute-start(bf16[256,640]{1,0:T(8,128)(2,1)S(1)} %get-tuple-element.19.f0_ref), channel_id=1, source_target_pairs={{0,4},{4,0},{8,12},{12,8},{1,5},{5,1},{9,13},{13,9},{2,6},{6,2},{1... | collective-permute-start | bytes 983048 | tf_op jit(solution)/shard_map/ppermute | solution.py:245
  20.8 11.2 %collective-permute-start.7 = (bf16[128,640]{1,0:T(8,128)(2,1)S(1)}, bf16[128,640]{1,0:T(8,128)(2,1)S(1)}, u32[]{:S(2)}, u32[]{:S(2)}) collective-permute-start(bf16[128,640]{1,0:T(8,128)(2,1)S(1)} %get-tuple-element.20), channel_id=1, source_target_pairs={{0,8},{4,12},{8,0},{12,4},{1,9},{5,13},{9,1},{13,5},{2,10},{6,14},... | collective-permute-start | bytes 491528 | tf_op jit(solution)/shard_map/ppermute | solution.py:248
  21.9 10.2 %collective-permute-start.8 = (bf16[128,640]{1,0:T(8,128)(2,1)S(1)}, bf16[128,640]{1,0:T(8,128)(2,1)S(1)}, u32[]{:S(2)}, u32[]{:S(2)}) collective-permute-start(bf16[128,640]{1,0:T(8,128)(2,1)S(1)} %get-tuple-element.21), channel_id=1, source_target_pairs={{0,12},{4,4},{8,8},{12,0},{1,13},{5,5},{9,9},{13,1},{2,14},{6,6},{... | collective-permute-start | bytes 491528 | tf_op jit(solution)/shard_map/ppermute | solution.py:251
  25.1 10.9 %collective-permute-start.10 = (f32[64,640]{1,0:T(8,128)S(1)}, f32[64,640]{1,0:T(8,128)S(1)}, u32[]{:S(2)}, u32[]{:S(2)}) collective-permute-start(f32[64,640]{1,0:T(8,128)S(1)} %get-tuple-element.27), channel_id=1, source_target_pairs={{0,2},{1,3},{2,0},{3,1},{4,6},{5,7},{6,4},{7,5},{8,10},{9,11},{10,... | collective-permute-start | bytes 491528 | tf_op jit(solution)/shard_map/ppermute | solution.py:237

commit v5 on v3

v5 whole, which is shorter than its diff:
```python
import functools
import math

import jax
import jax.numpy as jnp
from jax import lax
from jax.experimental import pallas as pl
from jax.experimental.pallas import tpu as pltpu
from jax.sharding import PartitionSpec as P

NX = 64
NY = 10
CELLS = NX * NY
F32 = jnp.float32
BF16 = jnp.bfloat16
W_BEGIN, W_GRAD, W_TOTAL, W_OUT = 8, 1, 4, 0
PARTS = 1
VMEM_BYTES = 32 * 1024 * 1024


def cell_mask(rows, dy, dx):
    q = lax.broadcasted_iota(jnp.int32, (rows, CELLS), 1)
    x = q % NX + dx
    y = q // NX + dy
    return (x >= 0) & (x < NX) & (y >= 0) & (y < NY)


def shifted(value, dy, dx):
    if dy == 0 and dx == 0:
        return value
    moved = pltpu.roll(value, (-(dy * NX + dx)) % CELLS, 1)
    return jnp.where(cell_mask(value.shape[0], dy, dx), moved, 0.0)


def gather_kernel(nz, nc, pos_ref, token_ref, cot_ref, *refs):
    pieces = refs[:nc]
    parts = refs[nc : nc + PARTS]
    packs = refs[nc + PARTS : -1]
    f_ref = refs[-1]
    blocks = cot_ref.shape[0]
    cols = f_ref.shape[0] // nz
    some = f_ref.shape[0] // PARTS
    s, c = pos_ref[0], pos_ref[1]
    for k in range(nc):
        f_ref[pl.ds(pl.multiple_of((c ^ k) * blocks, blocks), blocks), :] = pieces[k][...]
    for i, part in enumerate(parts):
        part[...] = f_ref[i * some : (i + 1) * some, :]
    for k, pack in zip(range(2, nz - 1), packs):
        goal = lax.rem(s + k, nz)
        pack[:cols, :] = f_ref[pl.ds(pl.multiple_of(goal * cols, cols), cols), :]
        pack[cols:, :] = cot_ref[...]


def columns(cols_ref, first, plane):
    blocks = plane.shape[0]
    for dy in (-1, 0, 1):
        for dx in (-1, 0, 1):
            tap = first + 3 * (dy + 1) + dx + 1
            cols_ref[tap * blocks : (tap + 1) * blocks, :] = shifted(plane, -dy, -dx).astype(BF16)


def token_kernel(token_ref):
    token_ref[...] = jnp.zeros(token_ref.shape, F32)


def input_grad_kernel(nz, nc, pos_ref, begin_ref, cot_ref, even_ref, odd_ref, w_ref, *refs):
    parts = refs[:nc]
    token_ref, cols_ref, sum_ref = refs[nc:]
    blocks = even_ref.shape[0]
    s, c = pos_ref[0], pos_ref[1]
    token_ref[...] = jnp.zeros(token_ref.shape, F32)
    even, odd = even_ref[...].astype(F32), odd_ref[...].astype(F32)
    first = s % 2 == 0
    columns(cols_ref, 0, jnp.where(s < nz - 1, jnp.where(first, even, odd), 0.0))
    columns(cols_ref, 9, cot_ref[...].astype(F32))
    columns(cols_ref, 18, jnp.where(s > 0, jnp.where(first, odd, even), 0.0))
    sum_ref[...] = lax.dot_general(
        w_ref[...], cols_ref[...], (((0,), (0,)), ((), ())), preferred_element_type=F32
    )
    for k in range(nc):
        parts[k][...] = sum_ref[pl.ds(pl.multiple_of((c ^ k) * blocks, blocks), blocks), :]


def output_kernel(nz, scale, pos_ref, last_ref, w_ref, cot_ref, ce_ref, co_ref, *refs):
    f_parts = [refs[i * PARTS : (i + 1) * PARTS] for i in range(3)]
    packs = refs[3 * PARTS : 3 * PARTS + nz - 3]
    out_ref, wg_ref, c_ref, g_ref, f_ref = refs[3 * PARTS + nz - 3 :]
    blocks = cot_ref.shape[0]
    cols = g_ref.shape[1]
    some = f_ref.shape[1] // PARTS
    taps = 9 * blocks
    s = pos_ref[0]
    even_at = 1 + s % 2
    for i in range(PARTS):
        rows = slice(i * some, (i + 1) * some)
        f_ref[0, rows, :] = f_parts[0][i][...]
        f_ref[even_at, rows, :] = f_parts[1][i][...]
        f_ref[3 - even_at, rows, :] = f_parts[2][i][...]
    inside = {-1: s > 0, 1: s < nz - 1}
    acc = None
    for dz in (0, 1, -1):
        term = jnp.dot(
            w_ref[(dz + 1) * taps : (dz + 2) * taps, :], f_ref[dz % 3], preferred_element_type=F32
        )
        acc = term if acc is None else acc + jnp.where(inside[dz], term, 0.0)
    total = None
    for dx in (-1, 0, 1):
        for dy in (-1, 0, 1):
            at = (3 * (dy + 1) + dx + 1) * blocks
            term = shifted(acc[at : at + blocks], dy, dx)
            total = term if total is None else total + term
    out_ref[:, 0, :] = total

    mine = pl.ds(pl.multiple_of(s * cols, cols), cols)
    odd_source = lax.rem(((s + 1) ^ 1) + nz - 1, nz)
    c_ref[odd_source] = co_ref[...]
    g_ref[odd_source] = f_ref[3 - even_at, mine, :]
    even_source = s ^ 1
    c_ref[even_source] = ce_ref[...]
    g_ref[even_source] = f_ref[even_at, mine, :]
    c_ref[s] = cot_ref[...]
    g_ref[s] = f_ref[0, mine, :]
    for k, pack in zip(range(2, nz - 1), packs):
        source = lax.rem(s + nz - k, nz)
        c_ref[source] = pack[cols:, :]
        g_ref[source] = pack[:cols, :]

    cots = []
    feats = []
    for z in range(nz):
        plane = c_ref[z].astype(F32)
        cots.append([shifted(plane, -dy, 0).astype(BF16) for dy in (-1, 0, 1)])
        field = g_ref[z].astype(F32)
        feats.append(jnp.concatenate([shifted(field, 0, dx).astype(BF16) for dx in (-1, 0, 1)], 0))
    for dz in (-1, 0, 1):
        sums = None
        for z in range(nz):
            if 0 <= z - dz < nz:
                term = lax.dot_general(
                    jnp.concatenate(cots[z - dz], 0),
                    feats[z],
                    (((1,), (1,)), ((), ())),
                    preferred_element_type=F32,
                )
                sums = term if sums is None else sums + term
        sums = sums * scale
        for dy in range(3):
            for dx in range(3):
                tap = 9 * (dz + 1) + 3 * dy + dx
                wg_ref[tap] = sums[dy * blocks : (dy + 1) * blocks, dx * cols : (dx + 1) * cols]


def total_kernel(*refs):
    total = refs[0][...]
    for ref in refs[1:-2]:
        total = total + ref[...]
    refs[-2][:, 0, :] = total
    refs[-1][...] = jnp.zeros(refs[-1].shape, F32)


VMEM = pl.BlockSpec(memory_space=pltpu.VMEM)
SMEM = pl.BlockSpec(memory_space=pltpu.SMEM)


def kernel_call(body, name, outs, args, scratch=(), weight=0):
    return pl.pallas_call(
        body,
        out_shape=outs,
        in_specs=[SMEM if a.dtype == jnp.int32 else VMEM for a in args],
        out_specs=tuple(VMEM for _ in outs),
        scratch_shapes=list(scratch),
        compiler_params=pltpu.CompilerParams(vmem_limit_bytes=VMEM_BYTES),
        cost_estimate=pl.CostEstimate(flops=weight, bytes_accessed=0, transcendentals=0),
        name=name,
    )(*args)


def per_device(features, weights, cotangent):
    blocks, depth, plane = features.shape
    channels = weights.shape[2]
    nz = lax.axis_size("sp")
    nc = lax.axis_size("ch")
    cols = channels // nz
    w2 = weights.reshape(27 * blocks, channels)
    feat = features.reshape(blocks, plane)
    cot = cotangent.reshape(blocks, plane)
    pos = jnp.stack([lax.axis_index("sp"), lax.axis_index("ch")]).astype(jnp.int32)

    even_pairs = [(i, i ^ 1) for i in range(nz)]
    odd_pairs = [(i, (((i + 1) ^ 1) - 1) % nz) for i in range(nz)]

    def mixed(k):
        return [(i, i ^ k) for i in range(nc)]

    def of(rows, dtype):
        return jax.ShapeDtypeStruct((rows, plane), dtype)

    small = jax.ShapeDtypeStruct((8, 128), F32)
    work = 2 * 27 * blocks * channels * plane

    (begin,) = kernel_call(token_kernel, "begin", [small], [], weight=W_BEGIN * work)
    cot_sent, begin = lax.optimization_barrier((cot, begin))
    cot_even = lax.ppermute(cot_sent, "sp", even_pairs)
    cot_odd = lax.ppermute(cot_sent, "sp", odd_pairs)
    feat, cot_even = lax.optimization_barrier((feat, cot_even))
    pieces = [feat] + [lax.ppermute(feat, "ch", mixed(k)) for k in range(1, nc)]

    *parts, token = kernel_call(
        functools.partial(input_grad_kernel, nz, nc),
        "input_grad",
        [of(blocks, F32)] * nc + [small],
        [pos, begin, cot, cot_even, cot_odd, w2],
        [pltpu.VMEM((27 * blocks, plane), BF16), pltpu.VMEM((channels, plane), F32)],
        W_GRAD * work,
    )
    terms = [parts[0]] + [lax.ppermute(parts[k], "ch", mixed(k)) for k in range(1, nc)]

    f_parts = kernel_call(
        functools.partial(gather_kernel, nz, nc),
        "gather",
        [of(channels // PARTS, BF16)] * PARTS + [of(cols + blocks, BF16)] * (nz - 3),
        [pos, token, cot] + pieces,
        [pltpu.VMEM((channels, plane), BF16)],
    )
    f_parts, packs = f_parts[:PARTS], f_parts[PARTS:]
    f_even = [lax.ppermute(part, "sp", even_pairs) for part in f_parts]
    f_odd = [lax.ppermute(part, "sp", odd_pairs) for part in f_parts]
    far = [
        lax.ppermute(packs[k - 2], "sp", [(i, (i + k) % nz) for i in range(nz)])
        for k in range(2, nz - 1)
    ]

    back, last = kernel_call(
        total_kernel,
        "total",
        [jax.ShapeDtypeStruct((blocks, 1, plane), F32), small],
        terms,
        weight=W_TOTAL * work,
    )
    output, weight_grad = kernel_call(
        functools.partial(output_kernel, nz, 1.0 / math.sqrt(nz * depth * plane)),
        "output_and_weight_grad",
        [
            jax.ShapeDtypeStruct((blocks, 1, plane), F32),
            jax.ShapeDtypeStruct((27, blocks, cols), F32),
        ],
        [pos, last, w2, cot, cot_even, cot_odd, *f_parts, *f_even, *f_odd, *far],
        [
            pltpu.VMEM((nz, blocks, plane), BF16),
            pltpu.VMEM((nz, cols, plane), BF16),
            pltpu.VMEM((3, channels, plane), BF16),
        ],
        W_OUT * work,
    )
    return (output, back, weight_grad)


def solution(mesh):
    return jax.shard_map(
        per_device,
        mesh=mesh,
        in_specs=(P("ch", ("grp", "sp"), None), P(None, "ch", None), P("ch", ("grp", "sp"), None)),
        out_specs=(
            P("ch", ("grp", "sp"), None),
            P("ch", ("grp", "sp"), None),
            P("grp", "ch", "sp"),
        ),
        check_vma=False,
    )
```

time: 36.6 us -> 33 us (0.902)
  the two profiles are of different devices: /device:TPU:13 before, /device:TPU:0 now
where the time goes in v5:
time: 33 us; the launch traced here: 32.9 us
  starting transfers between devices  14.7 us (45%)
  waiting for transfers between devices  10 us (30%)
  Pallas kernels  6.56 us (20%)
  local copies, waits for them, and re-layouts  0.86 us (3%)
  between operations  0.7 us (2%)
    ppermute x3, waiting for transfers between devices, per_device(): lax.ppermute(parts[k], 'ch', mixed(k))  8.36 us
    pallas_call x5, Pallas kernels, kernel_call(): pl.pallas_call(body, out_shape=outs, in_specs=[SMEM if a.dtype == jnp.int...  6.56 us
    ppermute x3, starting transfers between devices, per_device(): lax.ppermute(parts[k], 'ch', mixed(k))  4.46 us
    ppermute x3, starting transfers between devices, per_device(): pieces = [feat] + [lax.ppermute(feat, 'ch', mixed(k)) for k in range(1, nc)]  4.38 us
    ppermute x1, starting transfers between devices, per_device(): cot_odd = lax.ppermute(cot_sent, 'sp', odd_pairs)  2.6 us
    ppermute x1, waiting for transfers between devices, per_device(): lax.ppermute(packs[k - 2], 'sp', [(i, (i + k) % nz) for i in range(nz)])  1.44 us
    ppermute x1, starting transfers between devices, per_device(): f_even = [lax.ppermute(part, 'sp', even_pairs) for part in f_parts]  1.4 us
    ppermute x1, starting transfers between devices, per_device(): lax.ppermute(packs[k - 2], 'sp', [(i, (i + k) % nz) for i in range(nz)])  1.28 us
  transfers between devices with their start and end apart: 11, of which 4 were waited for; matrix products, arithmetic and copies ran while one was open for 0% of the time, Pallas kernels for 10%

profile of v5, /device:TPU:0, one launch (start us, length us, event | category | flops | bytes accessed | tf_op | source)
XLA Modules:
  0.0 32.9 jit_solution(2731848571771941621)
XLA Ops:
  0.6 0.0 copy-start.1
  0.6 0.0 copy-start.2
  0.7 0.0 copy-start
  0.7 0.8 %copy-done.1 = bf16[64,1,640]{2,0,1:T(8,128)(2,1)S(1)} copy-done((bf16[64,1,640]{2,0,1:T(8,128)(2,1)S(1)}, bf16[64,1,640]{2,0,1:T(8,128)(2,1)}, u32[]{:S(2)}) %copy-start.1) | copy-done | bytes 81944
  1.5 0.5 %collective-permute-start = (bf16[64,640]{1,0:T(8,128)(2,1)S(1)}, bf16[64,640]{1,0:T(8,128)(2,1)S(1)}, u32[]{:S(2)}, u32[]{:S(2)}) collective-permute-start(bf16[64,640]{1,0:T(8,128)(2,1)S(1)} %bitcast.7), channel_id=1, source_target_pairs={{0,4},{4,0},{8,12},{12,8},{1,5},{5,1},{9,13},{13,9},{2,6},{6,2},{1... | collective-permute-start | bytes 245768 | tf_op jit(solution)/shard_map/ppermute | solution.py:203
  2.0 2.6 %collective-permute-start.1 = (bf16[64,640]{1,0:T(8,128)(2,1)S(1)}, bf16[64,640]{1,0:T(8,128)(2,1)S(1)}, u32[]{:S(2)}, u32[]{:S(2)}) collective-permute-start(bf16[64,640]{1,0:T(8,128)(2,1)S(1)} %bitcast.8), channel_id=1, source_target_pairs={{0,12},{4,8},{8,4},{12,0},{1,13},{5,9},{9,5},{13,1},{2,14},{6,10},... | collective-permute-start | bytes 245768 | tf_op jit(solution)/shard_map/ppermute | solution.py:204
  4.6 0.0 collective-permute-done.even_ref.ce_ref
  4.6 0.0 copy-done.2
  4.6 3.6 %collective-permute-start.7 = (bf16[64,640]{1,0:T(8,128)(2,1)S(1)}, bf16[64,640]{1,0:T(8,128)(2,1)S(1)}, u32[]{:S(2)}, u32[]{:S(2)}) collective-permute-start(bf16[64,640]{1,0:T(8,128)(2,1)S(1)} %bitcast.12), channel_id=1, source_target_pairs={{0,3},{1,2},{2,1},{3,0},{4,7},{5,6},{6,5},{7,4},{8,11},{9,10},{10,... | collective-permute-start | bytes 245768 | tf_op jit(solution)/shard_map/ppermute | solution.py:206
  8.2 0.1 pad_add_fusion.pos_ref
  8.3 0.0 collective-permute-start.6
  8.3 0.8 %collective-permute-start.5 = (bf16[64,640]{1,0:T(8,128)(2,1)S(1)}, bf16[64,640]{1,0:T(8,128)(2,1)S(1)}, u32[]{:S(2)}, u32[]{:S(2)}) collective-permute-start(bf16[64,640]{1,0:T(8,128)(2,1)S(1)} %bitcast.14), channel_id=1, source_target_pairs={{0,1},{1,0},{2,3},{3,2},{4,5},{5,4},{6,7},{7,6},{8,9},{9,8},{10,11... | collective-permute-start | bytes 245768 | tf_op jit(solution)/shard_map/ppermute | solution.py:206
  9.0 0.0 collective-permute-done.1.odd_ref.co_ref
  9.0 0.0 copy-done
  9.0 1.8 %input_grad.1 = (f32[64,640]{1,0:T(8,128)S(1)}, f32[64,640]{1,0:T(8,128)S(1)}, f32[64,640]{1,0:T(8,128)S(1)}, f32[64,640]{1,0:T(8,128)S(1)}, f32[8,128]{1,0:T(8,128)S(1)}) custom-call(s32[2]{0:T(128)S(1)} %pad_add_fusion.pos_ref, f32[8,128]{1,0:T(8,128)S(1)} %begin.1.begin_ref, bf16[64,640]{1,0:T(8,128)(2,1)S(1)} %bitcast.9, ...), custom_call_target="tpu_custom_call" | custom-call | flops 566231040 | tf_op jit(solution)/shard_map/input_grad/pallas_call | solution.py:166
  10.9 1.4 %collective-permute-start.2 = (f32[64,640]{1,0:T(8,128)S(1)}, f32[64,640]{1,0:T(8,128)S(1)}, u32[]{:S(2)}, u32[]{:S(2)}) collective-permute-start(f32[64,640]{1,0:T(8,128)S(1)} %get-tuple-element.22), channel_id=1, source_target_pairs={{0,1},{1,0},{2,3},{3,2},{4,5},{5,4},{6,7},{7,6},{8,9},{9,8},{10,11... | collective-permute-start | bytes 491528 | tf_op jit(solution)/shard_map/ppermute | solution.py:216
  12.2 2.9 %collective-permute-start.3 = (f32[64,640]{1,0:T(8,128)S(1)}, f32[64,640]{1,0:T(8,128)S(1)}, u32[]{:S(2)}, u32[]{:S(2)}) collective-permute-start(f32[64,640]{1,0:T(8,128)S(1)} %get-tuple-element.23), channel_id=1, source_target_pairs={{0,2},{1,3},{2,0},{3,1},{4,6},{5,7},{6,4},{7,5},{8,10},{9,11},{10,... | collective-permute-start | bytes 491528 | tf_op jit(solution)/shard_map/ppermute | solution.py:216
  15.1 0.0 collective-permute-done.7.refs_3_
  15.1 0.2 collective-permute-start.4
  15.3 0.2 collective-permute-done.6.refs_2_
  15.6 0.0 collective-permute-done.5.refs_1_
  15.6 0.6 %gather.1 = (bf16[256,640]{1,0:T(8,128)(2,1)S(1)}, bf16[128,640]{1,0:T(8,128)(2,1)S(1)}) custom-call(s32[2]{0:T(128)S(1)} %pad_add_fusion.pos_ref, f32[8,128]{1,0:T(8,128)S(1)} %get-tuple-element.26.token_ref, bf16[64,640]{1,0:T(8,128)(2,1)S(1)} %bitcast.10, bf16[64,640]{1,0:T(8,128)(2,1)S(1)} %bitcast.15, ...), custom_call_target="tpu_custom_call" | custom-call | tf_op jit(solution)/shard_map/gather/pallas_call | solution.py:166
  16.2 0.1 collective-permute-start.9
  16.3 1.4 %collective-permute-start.8 = (bf16[256,640]{1,0:T(8,128)(2,1)S(1)}, bf16[256,640]{1,0:T(8,128)(2,1)S(1)}, u32[]{:S(2)}, u32[]{:S(2)}) collective-permute-start(bf16[256,640]{1,0:T(8,128)(2,1)S(1)} %get-tuple-element.28.refs_0_), channel_id=1, source_target_pairs={{0,4},{4,0},{8,12},{12,8},{1,5},{5,1},{9,13},{13,9},{2,6},{6,2},{1... | collective-permute-start | bytes 983048 | tf_op jit(solution)/shard_map/ppermute | solution.py:226
  17.7 3.1 %collective-permute-done.2.refs_1_ = f32[64,640]{1,0:T(8,128)S(1)} collective-permute-done((f32[64,640]{1,0:T(8,128)S(1)}, f32[64,640]{1,0:T(8,128)S(1)}, u32[]{:S(2)}, u32[]{:S(2)}) %collective-permute-start.2) | collective-permute-done | bytes 163872 | tf_op jit(solution)/shard_map/ppermute | solution.py:216
  20.7 1.3 %collective-permute-start.10 = (bf16[128,640]{1,0:T(8,128)(2,1)S(1)}, bf16[128,640]{1,0:T(8,128)(2,1)S(1)}, u32[]{:S(2)}, u32[]{:S(2)}) collective-permute-start(bf16[128,640]{1,0:T(8,128)(2,1)S(1)} %get-tuple-element.29), channel_id=1, source_target_pairs={{0,8},{4,12},{8,0},{12,4},{1,9},{5,13},{9,1},{13,5},{2,10},{6,14},... | collective-permute-start | bytes 491528 | tf_op jit(solution)/shard_map/ppermute | solution.py:229
  22.0 5.3 %collective-permute-done.3.refs_2_ = f32[64,640]{1,0:T(8,128)S(1)} collective-permute-done((f32[64,640]{1,0:T(8,128)S(1)}, f32[64,640]{1,0:T(8,128)S(1)}, u32[]{:S(2)}, u32[]{:S(2)}) %collective-permute-start.3) | collective-permute-done | bytes 163872 | tf_op jit(solution)/shard_map/ppermute | solution.py:216
  27.3 0.0 collective-permute-done.4.refs_3_
  27.3 0.7 %total.1 = (f32[64,1,640]{2,1,0:T(1,128)}, f32[8,128]{1,0:T(8,128)S(1)}) custom-call(f32[64,640]{1,0:T(8,128)S(1)} %get-tuple-element.21.refs_0_, f32[64,640]{1,0:T(8,128)S(1)} %collective-permute-done.2.refs_1_, f32[64,640]{1,0:T(8,128)S(1)} %collective-permute-done.3.refs_2_, f32[64,640]{1,0:T(8,128)S(1)} %collective-permute-done.4.refs_3_), custom_call_target="tpu_custom_call" | custom-call | flops 2264924160 | tf_op jit(solution)/shard_map/total/pallas_call | solution.py:166
  28.0 1.4 %collective-permute-done.10.refs_3_ = bf16[128,640]{1,0:T(8,128)(2,1)S(1)} collective-permute-done((bf16[128,640]{1,0:T(8,128)(2,1)S(1)}, bf16[128,640]{1,0:T(8,128)(2,1)S(1)}, u32[]{:S(2)}, u32[]{:S(2)}) %collective-permute-start.10) | collective-permute-done | bytes 163872 | tf_op jit(solution)/shard_map/ppermute | solution.py:229
  29.5 0.0 collective-permute-done.9.refs_2_
  29.5 0.0 collective-permute-done.8.refs_1_
  29.5 3.4 %output_and_weight_grad.1 = (f32[64,1,640]{2,1,0:T(1,128)}, f32[27,64,64]{2,1,0:T(8,128)}) custom-call(s32[2]{0:T(128)S(1)} %pad_add_fusion.pos_ref, f32[8,128]{1,0:T(8,128)S(1)} %get-tuple-element.25.last_ref, bf16[1728,256]{1,0:T(8,128)(2,1)S(1)} %bitcast.6, bf16[64,640]{1,0:T(8,128)(2,1)S(1)} %bitcast.11, ...), custom_call_target="tpu_custom_call" | custom-call | tf_op jit(solution)/shard_map/output_and_weight_grad/pallas_call | solution.py:166
  (1 shorter events, 0.0 us)
Async XLA Ops:
  0.6 0.9 %copy-start.1 = (bf16[64,1,640]{2,0,1:T(8,128)(2,1)S(1)}, bf16[64,1,640]{2,0,1:T(8,128)(2,1)}, u32[]{:S(2)}) copy-start(bf16[64,1,640]{2,0,1:T(8,128)(2,1)} %param.5) | copy-start | bytes 245764
  0.6 3.9 %copy-start.2 = (bf16[64,1,640]{2,0,1:T(8,128)(2,1)S(1)}, bf16[64,1,640]{2,0,1:T(8,128)(2,1)}, u32[]{:S(2)}) copy-start(bf16[64,1,640]{2,0,1:T(8,128)(2,1)} %param.3) | copy-start | bytes 245764
  0.7 8.4 %copy-start = (bf16[27,64,256]{2,1,0:T(8,128)(2,1)S(1)}, bf16[27,64,256]{2,1,0:T(8,128)(2,1)}, u32[]{:S(2)}) copy-start(bf16[27,64,256]{2,1,0:T(8,128)(2,1)} %param.4) | copy-start | bytes 2654212
  1.5 3.1 %collective-permute-start = (bf16[64,640]{1,0:T(8,128)(2,1)S(1)}, bf16[64,640]{1,0:T(8,128)(2,1)S(1)}, u32[]{:S(2)}, u32[]{:S(2)}) collective-permute-start(bf16[64,640]{1,0:T(8,128)(2,1)S(1)} %bitcast.7), channel_id=1, source_target_pairs={{0,4},{4,0},{8,12},{12,8},{1,5},{5,1},{9,13},{13,9},{2,6},{6,2},{1... | collective-permute-start | bytes 245768 | tf_op jit(solution)/shard_map/ppermute | solution.py:203
  2.0 7.1 %collective-permute-start.1 = (bf16[64,640]{1,0:T(8,128)(2,1)S(1)}, bf16[64,640]{1,0:T(8,128)(2,1)S(1)}, u32[]{:S(2)}, u32[]{:S(2)}) collective-permute-start(bf16[64,640]{1,0:T(8,128)(2,1)S(1)} %bitcast.8), channel_id=1, source_target_pairs={{0,12},{4,8},{8,4},{12,0},{1,13},{5,9},{9,5},{13,1},{2,14},{6,10},... | collective-permute-start | bytes 245768 | tf_op jit(solution)/shard_map/ppermute | solution.py:204
  4.6 10.5 %collective-permute-start.7 = (bf16[64,640]{1,0:T(8,128)(2,1)S(1)}, bf16[64,640]{1,0:T(8,128)(2,1)S(1)}, u32[]{:S(2)}, u32[]{:S(2)}) collective-permute-start(bf16[64,640]{1,0:T(8,128)(2,1)S(1)} %bitcast.12), channel_id=1, source_target_pairs={{0,3},{1,2},{2,1},{3,0},{4,7},{5,6},{6,5},{7,4},{8,11},{9,10},{10,... | collective-permute-start | bytes 245768 | tf_op jit(solution)/shard_map/ppermute | solution.py:206
  8.3 7.3 %collective-permute-start.6 = (bf16[64,640]{1,0:T(8,128)(2,1)S(1)}, bf16[64,640]{1,0:T(8,128)(2,1)S(1)}, u32[]{:S(2)}, u32[]{:S(2)}) collective-permute-start(bf16[64,640]{1,0:T(8,128)(2,1)S(1)} %bitcast.13), channel_id=1, source_target_pairs={{0,2},{1,3},{2,0},{3,1},{4,6},{5,7},{6,4},{7,5},{8,10},{9,11},{10,... | collective-permute-start | bytes 245768 | tf_op jit(solution)/shard_map/ppermute | solution.py:206
  8.3 7.3 %collective-permute-start.5 = (bf16[64,640]{1,0:T(8,128)(2,1)S(1)}, bf16[64,640]{1,0:T(8,128)(2,1)S(1)}, u32[]{:S(2)}, u32[]{:S(2)}) collective-permute-start(bf16[64,640]{1,0:T(8,128)(2,1)S(1)} %bitcast.14), channel_id=1, source_target_pairs={{0,1},{1,0},{2,3},{3,2},{4,5},{5,4},{6,7},{7,6},{8,9},{9,8},{10,11... | collective-permute-start | bytes 245768 | tf_op jit(solution)/shard_map/ppermute | solution.py:206
  10.9 9.9 %collective-permute-start.2 = (f32[64,640]{1,0:T(8,128)S(1)}, f32[64,640]{1,0:T(8,128)S(1)}, u32[]{:S(2)}, u32[]{:S(2)}) collective-permute-start(f32[64,640]{1,0:T(8,128)S(1)} %get-tuple-element.22), channel_id=1, source_target_pairs={{0,1},{1,0},{2,3},{3,2},{4,5},{5,4},{6,7},{7,6},{8,9},{9,8},{10,11... | collective-permute-start | bytes 491528 | tf_op jit(solution)/shard_map/ppermute | solution.py:216
  12.2 15.1 %collective-permute-start.3 = (f32[64,640]{1,0:T(8,128)S(1)}, f32[64,640]{1,0:T(8,128)S(1)}, u32[]{:S(2)}, u32[]{:S(2)}) collective-permute-start(f32[64,640]{1,0:T(8,128)S(1)} %get-tuple-element.23), channel_id=1, source_target_pairs={{0,2},{1,3},{2,0},{3,1},{4,6},{5,7},{6,4},{7,5},{8,10},{9,11},{10,... | collective-permute-start | bytes 491528 | tf_op jit(solution)/shard_map/ppermute | solution.py:216
  15.1 12.2 %collective-permute-start.4 = (f32[64,640]{1,0:T(8,128)S(1)}, f32[64,640]{1,0:T(8,128)S(1)}, u32[]{:S(2)}, u32[]{:S(2)}) collective-permute-start(f32[64,640]{1,0:T(8,128)S(1)} %get-tuple-element.24), channel_id=1, source_target_pairs={{0,3},{1,2},{2,1},{3,0},{4,7},{5,6},{6,5},{7,4},{8,11},{9,10},{10,... | collective-permute-start | bytes 491528 | tf_op jit(solution)/shard_map/ppermute | solution.py:216
  16.2 13.3 %collective-permute-start.9 = (bf16[256,640]{1,0:T(8,128)(2,1)S(1)}, bf16[256,640]{1,0:T(8,128)(2,1)S(1)}, u32[]{:S(2)}, u32[]{:S(2)}) collective-permute-start(bf16[256,640]{1,0:T(8,128)(2,1)S(1)} %get-tuple-element.28.refs_0_), channel_id=1, source_target_pairs={{0,12},{4,8},{8,4},{12,0},{1,13},{5,9},{9,5},{13,1},{2,14},{6,10},... | collective-permute-start | bytes 983048 | tf_op jit(solution)/shard_map/ppermute | solution.py:227
  16.3 13.2 %collective-permute-start.8 = (bf16[256,640]{1,0:T(8,128)(2,1)S(1)}, bf16[256,640]{1,0:T(8,128)(2,1)S(1)}, u32[]{:S(2)}, u32[]{:S(2)}) collective-permute-start(bf16[256,640]{1,0:T(8,128)(2,1)S(1)} %get-tuple-element.28.refs_0_), channel_id=1, source_target_pairs={{0,4},{4,0},{8,12},{12,8},{1,5},{5,1},{9,13},{13,9},{2,6},{6,2},{1... | collective-permute-start | bytes 983048 | tf_op jit(solution)/shard_map/ppermute | solution.py:226
  20.7 8.7 %collective-permute-start.10 = (bf16[128,640]{1,0:T(8,128)(2,1)S(1)}, bf16[128,640]{1,0:T(8,128)(2,1)S(1)}, u32[]{:S(2)}, u32[]{:S(2)}) collective-permute-start(bf16[128,640]{1,0:T(8,128)(2,1)S(1)} %get-tuple-element.29), channel_id=1, source_target_pairs={{0,8},{4,12},{8,0},{12,4},{1,9},{5,13},{9,1},{13,5},{2,10},{6,14},... | collective-permute-start | bytes 491528 | tf_op jit(solution)/shard_map/ppermute | solution.py:229

commit v6 on v5

--- a/solution.py
+++ b/solution.py
@@ -14,7 +14,6 @@
 F32 = jnp.float32
 BF16 = jnp.bfloat16
 W_BEGIN, W_GRAD, W_TOTAL, W_OUT = 8, 1, 4, 0
-PARTS = 1
 VMEM_BYTES = 32 * 1024 * 1024
 
 
@@ -32,19 +31,17 @@
     return jnp.where(cell_mask(value.shape[0], dy, dx), moved, 0.0)
 
 
+def odd_partner(s, nz):
+    return lax.rem(((s + 1) ^ 1) + nz - 1, nz)
+
+
 def gather_kernel(nz, nc, pos_ref, token_ref, cot_ref, *refs):
-    pieces = refs[:nc]
-    parts = refs[nc : nc + PARTS]
-    packs = refs[nc + PARTS : -1]
-    f_ref = refs[-1]
+    pieces, f_ref, packs = refs[:nc], refs[nc], refs[nc + 1 :]
     blocks = cot_ref.shape[0]
     cols = f_ref.shape[0] // nz
-    some = f_ref.shape[0] // PARTS
     s, c = pos_ref[0], pos_ref[1]
     for k in range(nc):
         f_ref[pl.ds(pl.multiple_of((c ^ k) * blocks, blocks), blocks), :] = pieces[k][...]
-    for i, part in enumerate(parts):
-        part[...] = f_ref[i * some : (i + 1) * some, :]
     for k, pack in zip(range(2, nz - 1), packs):
         goal = lax.rem(s + k, nz)
         pack[:cols, :] = f_ref[pl.ds(pl.multiple_of(goal * cols, cols), cols), :]
@@ -57,6 +54,10 @@
         for dx in (-1, 0, 1):
             tap = first + 3 * (dy + 1) + dx + 1
             cols_ref[tap * blocks : (tap + 1) * blocks, :] = shifted(plane, -dy, -dx).astype(BF16)
+
+
+def hold_kernel(*refs):
+    refs[-1][...] = jnp.zeros(refs[-1].shape, F32)
 
 
 def token_kernel(token_ref):
@@ -81,28 +82,31 @@
         parts[k][...] = sum_ref[pl.ds(pl.multiple_of((c ^ k) * blocks, blocks), blocks), :]
 
 
-def output_kernel(nz, scale, pos_ref, last_ref, w_ref, cot_ref, ce_ref, co_ref, *refs):
-    f_parts = [refs[i * PARTS : (i + 1) * PARTS] for i in range(3)]
-    packs = refs[3 * PARTS : 3 * PARTS + nz - 3]
-    out_ref, wg_ref, c_ref, g_ref, f_ref = refs[3 * PARTS + nz - 3 :]
+def conv_part(w_ref, field, dz):
+    taps = w_ref.shape[0] // 3
+    return jnp.dot(
+        w_ref[(dz + 1) * taps : (dz + 2) * taps, :], field, preferred_element_type=F32
+    )
+
+
+def output_kernel(nz, nc, scale, pos_ref, last_ref, w_ref, *refs):
+    terms = refs[:nc]
+    cot_ref, ce_ref, co_ref, f_ref, fe_ref, fo_ref = refs[nc : nc + 6]
+    packs = refs[nc + 6 : -5]
+    out_ref, back_ref, wg_ref, c_ref, g_ref = refs[-5:]
+    total = terms[0][...]
+    for term in terms[1:]:
+        total = total + term[...]
+    back_ref[:, 0, :] = total
+
     blocks = cot_ref.shape[0]
     cols = g_ref.shape[1]
-    some = f_ref.shape[1] // PARTS
-    taps = 9 * blocks
     s = pos_ref[0]
-    even_at = 1 + s % 2
-    for i in range(PARTS):
-        rows = slice(i * some, (i + 1) * some)
-        f_ref[0, rows, :] = f_parts[0][i][...]
-        f_ref[even_at, rows, :] = f_parts[1][i][...]
-        f_ref[3 - even_at, rows, :] = f_parts[2][i][...]
-    inside = {-1: s > 0, 1: s < nz - 1}
-    acc = None
-    for dz in (0, 1, -1):
-        term = jnp.dot(
-            w_ref[(dz + 1) * taps : (dz + 2) * taps, :], f_ref[dz % 3], preferred_element_type=F32
-        )
-        acc = term if acc is None else acc + jnp.where(inside[dz], term, 0.0)
+    first = s % 2 == 0
+    even, odd = fe_ref[...], fo_ref[...]
+    acc = conv_part(w_ref, f_ref[...], 0)
+    acc = acc + jnp.where(s < nz - 1, conv_part(w_ref, jnp.where(first, even, odd), 1), 0.0)
+    acc = acc + jnp.where(s > 0, conv_part(w_ref, jnp.where(first, odd, even), -1), 0.0)
     total = None
     for dx in (-1, 0, 1):
         for dy in (-1, 0, 1):
@@ -112,14 +116,13 @@
     out_ref[:, 0, :] = total
 
     mine = pl.ds(pl.multiple_of(s * cols, cols), cols)
-    odd_source = lax.rem(((s + 1) ^ 1) + nz - 1, nz)
-    c_ref[odd_source] = co_ref[...]
-    g_ref[odd_source] = f_ref[3 - even_at, mine, :]
-    even_source = s ^ 1
-    c_ref[even_source] = ce_ref[...]
-    g_ref[even_source] = f_ref[even_at, mine, :]
-    c_ref[s] = cot_ref[...]
-    g_ref[s] = f_ref[0, mine, :]
+    for source, cot, field in (
+        (s, cot_ref, f_ref),
+        (s ^ 1, ce_ref, fe_ref),
+        (odd_partner(s, nz), co_ref, fo_ref),
+    ):
+        c_ref[source] = cot[...]
+        g_ref[source] = field[mine, :]
     for k, pack in zip(range(2, nz - 1), packs):
         source = lax.rem(s + nz - k, nz)
         c_ref[source] = pack[cols:, :]
@@ -150,14 +153,6 @@
                 wg_ref[tap] = sums[dy * blocks : (dy + 1) * blocks, dx * cols : (dx + 1) * cols]
 
 
-def total_kernel(*refs):
-    total = refs[0][...]
-    for ref in refs[1:-2]:
-        total = total + ref[...]
-    refs[-2][:, 0, :] = total
-    refs[-1][...] = jnp.zeros(refs[-1].shape, F32)
-
-
 VMEM = pl.BlockSpec(memory_space=pltpu.VMEM)
 SMEM = pl.BlockSpec(memory_space=pltpu.SMEM)
 
@@ -170,7 +165,7 @@
         out_specs=tuple(VMEM for _ in outs),
         scratch_shapes=list(scratch),
         compiler_params=pltpu.CompilerParams(vmem_limit_bytes=VMEM_BYTES),
-        cost_estimate=pl.CostEstimate(flops=weight, bytes_accessed=0, transcendentals=0),
+        cost_estimate=pl.CostEstimate(flops=int(weight), bytes_accessed=0, transcendentals=0),
         name=name,
     )(*args)
 
@@ -198,11 +193,9 @@
     small = jax.ShapeDtypeStruct((8, 128), F32)
     work = 2 * 27 * blocks * channels * plane
 
+    cot_even = lax.ppermute(cot, "sp", even_pairs)
+    cot_odd = lax.ppermute(cot, "sp", odd_pairs)
     (begin,) = kernel_call(token_kernel, "begin", [small], [], weight=W_BEGIN * work)
-    cot_sent, begin = lax.optimization_barrier((cot, begin))
-    cot_even = lax.ppermute(cot_sent, "sp", even_pairs)
-    cot_odd = lax.ppermute(cot_sent, "sp", odd_pairs)
-    feat, cot_even = lax.optimization_barrier((feat, cot_even))
     pieces = [feat] + [lax.ppermute(feat, "ch", mixed(k)) for k in range(1, nc)]
 
     *parts, token = kernel_call(
@@ -215,41 +208,27 @@
     )
     terms = [parts[0]] + [lax.ppermute(parts[k], "ch", mixed(k)) for k in range(1, nc)]
 
-    f_parts = kernel_call(
+    f_all, *packs = kernel_call(
         functools.partial(gather_kernel, nz, nc),
         "gather",
-        [of(channels // PARTS, BF16)] * PARTS + [of(cols + blocks, BF16)] * (nz - 3),
+        [of(channels, BF16)] + [of(cols + blocks, BF16)] * (nz - 3),
         [pos, token, cot] + pieces,
-        [pltpu.VMEM((channels, plane), BF16)],
-    )
-    f_parts, packs = f_parts[:PARTS], f_parts[PARTS:]
-    f_even = [lax.ppermute(part, "sp", even_pairs) for part in f_parts]
-    f_odd = [lax.ppermute(part, "sp", odd_pairs) for part in f_parts]
+    )
+    f_odd = lax.ppermute(f_all, "sp", odd_pairs)
     far = [
         lax.ppermute(packs[k - 2], "sp", [(i, (i + k) % nz) for i in range(nz)])
         for k in range(2, nz - 1)
     ]
-
-    back, last = kernel_call(
-        total_kernel,
-        "total",
-        [jax.ShapeDtypeStruct((blocks, 1, plane), F32), small],
-        terms,
-        weight=W_TOTAL * work,
-    )
-    output, weight_grad = kernel_call(
-        functools.partial(output_kernel, nz, 1.0 / math.sqrt(nz * depth * plane)),
-        "output_and_weight_grad",
-        [
-            jax.ShapeDtypeStruct((blocks, 1, plane), F32),
-            jax.ShapeDtypeStruct((27, blocks, cols), F32),
-        ],
-        [pos, last, w2, cot, cot_even, cot_odd, *f_parts, *f_even, *f_odd, *far],
-        [
-            pltpu.VMEM((nz, blocks, plane), BF16),
-            pltpu.VMEM((nz, cols, plane), BF16),
-            pltpu.VMEM((3, channels, plane), BF16),
-        ],
+    f_even = lax.ppermute(f_all, "sp", even_pairs)
+
+    block = jax.ShapeDtypeStruct((blocks, 1, plane), F32)
+    (last,) = kernel_call(hold_kernel, "hold", [small], terms, weight=W_TOTAL * work)
+    output, back, weight_grad = kernel_call(
+        functools.partial(output_kernel, nz, nc, 1.0 / math.sqrt(nz * depth * plane)),
+        "outputs",
+        [block, block, jax.ShapeDtypeStruct((27, blocks, cols), F32)],
+        [pos, last, w2, *terms, cot, cot_even, cot_odd, f_all, f_even, f_odd, *far],
+        [pltpu.VMEM((nz, blocks, plane), BF16), pltpu.VMEM((nz, cols, plane), BF16)],
         W_OUT * work,
     )
     return (output, back, weight_grad)

time: 33 us -> 34.9 us (1.058)
  waiting for transfers between devices: 10 us -> 14.8 us
  starting transfers between devices: 14.7 us -> 13.2 us
  local copies, waits for them, and re-layouts: 0.86 us -> 0.01 us
  Pallas kernels: 6.56 us -> 5.88 us
    ppermute x4, waiting for transfers between devices: 0.01 us -> 2.95 us  [the longest x1 2.94 us: per_device(): cot_odd = lax.ppermute(cot, 'sp', odd_pairs)]
    ppermute x3, waiting for transfers between devices: 8.36 us -> 10.2 us  [per_device(): lax.ppermute(parts[k], 'ch', mixed(k))]
    ppermute x4, starting transfers between devices: 4.53 us -> 2.97 us  [the longest x1 1.38 us: per_device(): cot_even = lax.ppermute(cot, 'sp', even_pairs)]
    ppermute x3, starting transfers between devices: 4.38 us -> 5.76 us  [per_device(): pieces = [feat] + [lax.ppermute(feat, 'ch', mixed(k)) for k in range(1, nc)]]
    ppermute x1, starting transfers between devices: 1.28 us -> 0.01 us  [per_device(): lax.ppermute(packs[k - 2], 'sp', [(i, (i + k) % nz) for i in range(nz)])]
    unnamed x6, local copies, waits for them, and re-layouts: 0.86 us -> 0.01 us
    pallas_call x5, Pallas kernels: 6.56 us -> 5.88 us  [kernel_call(): pl.pallas_call(body, out_shape=outs, in_specs=[SMEM if a.dtype == jnp.int...]
  transfers between devices with their start and end apart: 11 -> 11, of which waited for: 4 -> 4; matrix products, arithmetic and copies ran while one was open for 0% -> 0% of each run, Pallas kernels for 10% -> 7%
where the time goes in v6:
time: 34.9 us; the launch traced here: 34.7 us
  waiting for transfers between devices  14.8 us (42%)
  starting transfers between devices  13.2 us (38%)
  Pallas kernels  5.88 us (17%)
  between operations  0.7 us (2%)
    ppermute x3, waiting for transfers between devices, per_device(): lax.ppermute(parts[k], 'ch', mixed(k))  10.2 us
    pallas_call x5, Pallas kernels, kernel_call(): pl.pallas_call(body, out_shape=outs, in_specs=[SMEM if a.dtype == jnp.int...  5.88 us
    ppermute x3, starting transfers between devices, per_device(): pieces = [feat] + [lax.ppermute(feat, 'ch', mixed(k)) for k in range(1, nc)]  5.76 us
    ppermute x3, starting transfers between devices, per_device(): lax.ppermute(parts[k], 'ch', mixed(k))  4.51 us
    ppermute x1, waiting for transfers between devices, per_device(): cot_odd = lax.ppermute(cot, 'sp', odd_pairs)  2.94 us
    ppermute x1, waiting for transfers between devices, per_device(): lax.ppermute(packs[k - 2], 'sp', [(i, (i + k) % nz) for i in range(nz)])  1.65 us
    ppermute x1, starting transfers between devices, per_device(): cot_even = lax.ppermute(cot, 'sp', even_pairs)  1.38 us
    ppermute x1, starting transfers between devices, per_device(): f_even = lax.ppermute(f_all, 'sp', even_pairs)  1.15 us
  transfers between devices with their start and end apart: 11, of which 4 were waited for; matrix products, arithmetic and copies ran while one was open for 0% of the time, Pallas kernels for 7%

profile of v6, /device:TPU:0, one launch (start us, length us, event | category | flops | bytes accessed | tf_op | source)
XLA Modules:
  0.0 34.7 jit_solution(15309837130386124381)
XLA Ops:
  0.6 5.1 %collective-permute-start.7 = (bf16[64,640]{1,0:T(8,128)(2,1)}, bf16[64,640]{1,0:T(8,128)(2,1)S(1)}, u32[]{:S(2)}, u32[]{:S(2)}) collective-permute-start(bf16[64,640]{1,0:T(8,128)(2,1)} %bitcast.12), channel_id=1, source_target_pairs={{0,3},{1,2},{2,1},{3,0},{4,7},{5,6},{6,5},{7,4},{8,11},{9,10},{10,... | collective-permute-start | bytes 245768 | tf_op jit(solution)/shard_map/ppermute | solution.py:199
  5.7 0.0 collective-permute-start.6
  5.7 0.6 %collective-permute-start.5 = (bf16[64,640]{1,0:T(8,128)(2,1)}, bf16[64,640]{1,0:T(8,128)(2,1)S(1)}, u32[]{:S(2)}, u32[]{:S(2)}) collective-permute-start(bf16[64,640]{1,0:T(8,128)(2,1)} %bitcast.14), channel_id=1, source_target_pairs={{0,1},{1,0},{2,3},{3,2},{4,5},{5,4},{6,7},{7,6},{8,9},{9,8},{10,11... | collective-permute-start | bytes 245768 | tf_op jit(solution)/shard_map/ppermute | solution.py:199
  6.4 0.4 %collective-permute-start.1 = (bf16[64,640]{1,0:T(8,128)(2,1)}, bf16[64,640]{1,0:T(8,128)(2,1)S(1)}, u32[]{:S(2)}, u32[]{:S(2)}) collective-permute-start(bf16[64,640]{1,0:T(8,128)(2,1)} %bitcast.7), channel_id=1, source_target_pairs={{0,12},{4,8},{8,4},{12,0},{1,13},{5,9},{9,5},{13,1},{2,14},{6,10},... | collective-permute-start | bytes 245768 | tf_op jit(solution)/shard_map/ppermute | solution.py:197
  6.8 1.4 %collective-permute-start = (bf16[64,640]{1,0:T(8,128)(2,1)}, bf16[64,640]{1,0:T(8,128)(2,1)S(1)}, u32[]{:S(2)}, u32[]{:S(2)}) collective-permute-start(bf16[64,640]{1,0:T(8,128)(2,1)} %bitcast.8), channel_id=1, source_target_pairs={{0,4},{4,0},{8,12},{12,8},{1,5},{5,1},{9,13},{13,9},{2,6},{6,2},{1... | collective-permute-start | bytes 245768 | tf_op jit(solution)/shard_map/ppermute | solution.py:196
  8.1 0.0 copy-start
  8.1 0.0 copy-start.1
  8.1 0.1 pad_add_fusion.pos_ref
  8.2 2.9 %collective-permute-done.1.odd_ref.refs_6_ = bf16[64,640]{1,0:T(8,128)(2,1)S(1)} collective-permute-done((bf16[64,640]{1,0:T(8,128)(2,1)}, bf16[64,640]{1,0:T(8,128)(2,1)S(1)}, u32[]{:S(2)}, u32[]{:S(2)}) %collective-permute-start.1) | collective-permute-done | bytes 81952 | tf_op jit(solution)/shard_map/ppermute | solution.py:197
  11.2 0.0 collective-permute-done.even_ref.refs_5_
  11.2 0.0 copy-done
  11.2 0.0 copy-done.1
  11.2 0.0 copy-start.2
  11.2 1.8 %input_grad.1 = (f32[64,640]{1,0:T(8,128)S(1)}, f32[64,640]{1,0:T(8,128)S(1)}, f32[64,640]{1,0:T(8,128)S(1)}, f32[64,640]{1,0:T(8,128)S(1)}, f32[8,128]{1,0:T(8,128)S(1)}) custom-call(s32[2]{0:T(128)S(1)} %pad_add_fusion.pos_ref, f32[8,128]{1,0:T(8,128)S(1)} %begin.1.begin_ref, bf16[64,640]{1,0:T(8,128)(2,1)S(1)} %bitcast.9, ...), custom_call_target="tpu_custom_call" | custom-call | flops 566231040 | tf_op jit(solution)/shard_map/input_grad/pallas_call | solution.py:161
  13.0 1.6 %collective-permute-start.2 = (f32[64,640]{1,0:T(8,128)S(1)}, f32[64,640]{1,0:T(8,128)S(1)}, u32[]{:S(2)}, u32[]{:S(2)}) collective-permute-start(f32[64,640]{1,0:T(8,128)S(1)} %get-tuple-element.11), channel_id=1, source_target_pairs={{0,1},{1,0},{2,3},{3,2},{4,5},{5,4},{6,7},{7,6},{8,9},{9,8},{10,11... | collective-permute-start | bytes 491528 | tf_op jit(solution)/shard_map/ppermute | solution.py:209
  14.6 2.9 %collective-permute-start.3 = (f32[64,640]{1,0:T(8,128)S(1)}, f32[64,640]{1,0:T(8,128)S(1)}, u32[]{:S(2)}, u32[]{:S(2)}) collective-permute-start(f32[64,640]{1,0:T(8,128)S(1)} %get-tuple-element.12), channel_id=1, source_target_pairs={{0,2},{1,3},{2,0},{3,1},{4,6},{5,7},{6,4},{7,5},{8,10},{9,11},{10,... | collective-permute-start | bytes 491528 | tf_op jit(solution)/shard_map/ppermute | solution.py:209
  17.5 0.0 collective-permute-done.7.refs_3_
  17.5 0.0 collective-permute-start.4
  17.5 0.0 collective-permute-done.6.refs_2_
  17.5 0.0 collective-permute-done.5.refs_1_
  17.5 0.0 copy-done.2
  17.6 0.6 %gather.1 = (bf16[256,640]{1,0:T(8,128)(2,1)S(1)}, bf16[128,640]{1,0:T(8,128)(2,1)S(1)}) custom-call(s32[2]{0:T(128)S(1)} %pad_add_fusion.pos_ref, f32[8,128]{1,0:T(8,128)S(1)} %get-tuple-element.14.token_ref, bf16[64,640]{1,0:T(8,128)(2,1)S(1)} %bitcast.10, bf16[64,640]{1,0:T(8,128)(2,1)S(1)} %bitcast.15, ...), custom_call_target="tpu_custom_call" | custom-call | tf_op jit(solution)/shard_map/gather/pallas_call | solution.py:161
  18.1 0.1 collective-permute-start.9
  18.2 1.2 %collective-permute-start.8 = (bf16[256,640]{1,0:T(8,128)(2,1)S(1)}, bf16[256,640]{1,0:T(8,128)(2,1)S(1)}, u32[]{:S(2)}, u32[]{:S(2)}) collective-permute-start(bf16[256,640]{1,0:T(8,128)(2,1)S(1)} %get-tuple-element.15.refs_7_), channel_id=1, source_target_pairs={{0,4},{4,0},{8,12},{12,8},{1,5},{5,1},{9,13},{13,9},{2,6},{6,2},{1... | collective-permute-start | bytes 983048 | tf_op jit(solution)/shard_map/ppermute | solution.py:222
  19.4 2.9 %collective-permute-done.2.refs_1_ = f32[64,640]{1,0:T(8,128)S(1)} collective-permute-done((f32[64,640]{1,0:T(8,128)S(1)}, f32[64,640]{1,0:T(8,128)S(1)}, u32[]{:S(2)}, u32[]{:S(2)}) %collective-permute-start.2) | collective-permute-done | bytes 163872 | tf_op jit(solution)/shard_map/ppermute | solution.py:209
  22.3 0.0 collective-permute-start.10
  22.3 7.3 %collective-permute-done.3.refs_2_ = f32[64,640]{1,0:T(8,128)S(1)} collective-permute-done((f32[64,640]{1,0:T(8,128)S(1)}, f32[64,640]{1,0:T(8,128)S(1)}, u32[]{:S(2)}, u32[]{:S(2)}) %collective-permute-start.3) | collective-permute-done | bytes 163872 | tf_op jit(solution)/shard_map/ppermute | solution.py:209
  29.6 0.0 collective-permute-done.4.refs_3_
  29.6 1.7 %collective-permute-done.10.refs_10_ = bf16[128,640]{1,0:T(8,128)(2,1)S(1)} collective-permute-done((bf16[128,640]{1,0:T(8,128)(2,1)S(1)}, bf16[128,640]{1,0:T(8,128)(2,1)S(1)}, u32[]{:S(2)}, u32[]{:S(2)}) %collective-permute-start.10) | collective-permute-done | bytes 163872 | tf_op jit(solution)/shard_map/ppermute | solution.py:219
  31.3 0.0 collective-permute-done.9.refs_9_
  31.3 0.0 collective-permute-done.8.refs_8_
  31.3 3.5 %outputs.1 = (f32[64,1,640]{2,1,0:T(1,128)}, f32[64,1,640]{2,1,0:T(1,128)}, f32[27,64,64]{2,1,0:T(8,128)}) custom-call(s32[2]{0:T(128)S(1)} %pad_add_fusion.pos_ref, f32[8,128]{1,0:T(8,128)S(1)} %hold.1.last_ref, bf16[1728,256]{1,0:T(8,128)(2,1)S(1)} %bitcast.6, f32[64,640]{1,0:T(8,128)S(1)} %get-tuple-element.10.refs_0_, ...), custom_call_target="tpu_custom_call" | custom-call | tf_op jit(solution)/shard_map/outputs/pallas_call | solution.py:161
  (2 shorter events, 0.0 us)
Async XLA Ops:
  0.6 16.9 %collective-permute-start.7 = (bf16[64,640]{1,0:T(8,128)(2,1)}, bf16[64,640]{1,0:T(8,128)(2,1)S(1)}, u32[]{:S(2)}, u32[]{:S(2)}) collective-permute-start(bf16[64,640]{1,0:T(8,128)(2,1)} %bitcast.12), channel_id=1, source_target_pairs={{0,3},{1,2},{2,1},{3,0},{4,7},{5,6},{6,5},{7,4},{8,11},{9,10},{10,... | collective-permute-start | bytes 245768 | tf_op jit(solution)/shard_map/ppermute | solution.py:199
  5.7 11.8 %collective-permute-start.6 = (bf16[64,640]{1,0:T(8,128)(2,1)}, bf16[64,640]{1,0:T(8,128)(2,1)S(1)}, u32[]{:S(2)}, u32[]{:S(2)}) collective-permute-start(bf16[64,640]{1,0:T(8,128)(2,1)} %bitcast.13), channel_id=1, source_target_pairs={{0,2},{1,3},{2,0},{3,1},{4,6},{5,7},{6,4},{7,5},{8,10},{9,11},{10,... | collective-permute-start | bytes 245768 | tf_op jit(solution)/shard_map/ppermute | solution.py:199
  5.7 11.8 %collective-permute-start.5 = (bf16[64,640]{1,0:T(8,128)(2,1)}, bf16[64,640]{1,0:T(8,128)(2,1)S(1)}, u32[]{:S(2)}, u32[]{:S(2)}) collective-permute-start(bf16[64,640]{1,0:T(8,128)(2,1)} %bitcast.14), channel_id=1, source_target_pairs={{0,1},{1,0},{2,3},{3,2},{4,5},{5,4},{6,7},{7,6},{8,9},{9,8},{10,11... | collective-permute-start | bytes 245768 | tf_op jit(solution)/shard_map/ppermute | solution.py:199
  6.4 4.8 %collective-permute-start.1 = (bf16[64,640]{1,0:T(8,128)(2,1)}, bf16[64,640]{1,0:T(8,128)(2,1)S(1)}, u32[]{:S(2)}, u32[]{:S(2)}) collective-permute-start(bf16[64,640]{1,0:T(8,128)(2,1)} %bitcast.7), channel_id=1, source_target_pairs={{0,12},{4,8},{8,4},{12,0},{1,13},{5,9},{9,5},{13,1},{2,14},{6,10},... | collective-permute-start | bytes 245768 | tf_op jit(solution)/shard_map/ppermute | solution.py:197
  6.8 4.4 %collective-permute-start = (bf16[64,640]{1,0:T(8,128)(2,1)}, bf16[64,640]{1,0:T(8,128)(2,1)S(1)}, u32[]{:S(2)}, u32[]{:S(2)}) collective-permute-start(bf16[64,640]{1,0:T(8,128)(2,1)} %bitcast.8), channel_id=1, source_target_pairs={{0,4},{4,0},{8,12},{12,8},{1,5},{5,1},{9,13},{13,9},{2,6},{6,2},{1... | collective-permute-start | bytes 245768 | tf_op jit(solution)/shard_map/ppermute | solution.py:196
  8.1 3.0 %copy-start = (bf16[27,64,256]{2,1,0:T(8,128)(2,1)S(1)}, bf16[27,64,256]{2,1,0:T(8,128)(2,1)}, u32[]{:S(2)}) copy-start(bf16[27,64,256]{2,1,0:T(8,128)(2,1)} %param.4) | copy-start | bytes 2654212
  8.1 3.0 %copy-start.1 = (bf16[64,1,640]{2,0,1:T(8,128)(2,1)S(1)}, bf16[64,1,640]{2,0,1:T(8,128)(2,1)}, u32[]{:S(2)}) copy-start(bf16[64,1,640]{2,0,1:T(8,128)(2,1)} %param.5) | copy-start | bytes 245764
  11.2 6.4 %copy-start.2 = (bf16[64,1,640]{2,0,1:T(8,128)(2,1)S(1)}, bf16[64,1,640]{2,0,1:T(8,128)(2,1)}, u32[]{:S(2)}) copy-start(bf16[64,1,640]{2,0,1:T(8,128)(2,1)} %param.3) | copy-start | bytes 245764
  13.0 9.3 %collective-permute-start.2 = (f32[64,640]{1,0:T(8,128)S(1)}, f32[64,640]{1,0:T(8,128)S(1)}, u32[]{:S(2)}, u32[]{:S(2)}) collective-permute-start(f32[64,640]{1,0:T(8,128)S(1)} %get-tuple-element.11), channel_id=1, source_target_pairs={{0,1},{1,0},{2,3},{3,2},{4,5},{5,4},{6,7},{7,6},{8,9},{9,8},{10,11... | collective-permute-start | bytes 491528 | tf_op jit(solution)/shard_map/ppermute | solution.py:209
  14.6 15.0 %collective-permute-start.3 = (f32[64,640]{1,0:T(8,128)S(1)}, f32[64,640]{1,0:T(8,128)S(1)}, u32[]{:S(2)}, u32[]{:S(2)}) collective-permute-start(f32[64,640]{1,0:T(8,128)S(1)} %get-tuple-element.12), channel_id=1, source_target_pairs={{0,2},{1,3},{2,0},{3,1},{4,6},{5,7},{6,4},{7,5},{8,10},{9,11},{10,... | collective-permute-start | bytes 491528 | tf_op jit(solution)/shard_map/ppermute | solution.py:209
  17.5 12.1 %collective-permute-start.4 = (f32[64,640]{1,0:T(8,128)S(1)}, f32[64,640]{1,0:T(8,128)S(1)}, u32[]{:S(2)}, u32[]{:S(2)}) collective-permute-start(f32[64,640]{1,0:T(8,128)S(1)} %get-tuple-element.13), channel_id=1, source_target_pairs={{0,3},{1,2},{2,1},{3,0},{4,7},{5,6},{6,5},{7,4},{8,11},{9,10},{10,... | collective-permute-start | bytes 491528 | tf_op jit(solution)/shard_map/ppermute | solution.py:209
  18.1 13.1 %collective-permute-start.9 = (bf16[256,640]{1,0:T(8,128)(2,1)S(1)}, bf16[256,640]{1,0:T(8,128)(2,1)S(1)}, u32[]{:S(2)}, u32[]{:S(2)}) collective-permute-start(bf16[256,640]{1,0:T(8,128)(2,1)S(1)} %get-tuple-element.15.refs_7_), channel_id=1, source_target_pairs={{0,12},{4,8},{8,4},{12,0},{1,13},{5,9},{9,5},{13,1},{2,14},{6,10},... | collective-permute-start | bytes 983048 | tf_op jit(solution)/shard_map/ppermute | solution.py:217
  18.2 13.0 %collective-permute-start.8 = (bf16[256,640]{1,0:T(8,128)(2,1)S(1)}, bf16[256,640]{1,0:T(8,128)(2,1)S(1)}, u32[]{:S(2)}, u32[]{:S(2)}) collective-permute-start(bf16[256,640]{1,0:T(8,128)(2,1)S(1)} %get-tuple-element.15.refs_7_), channel_id=1, source_target_pairs={{0,4},{4,0},{8,12},{12,8},{1,5},{5,1},{9,13},{13,9},{2,6},{6,2},{1... | collective-permute-start | bytes 983048 | tf_op jit(solution)/shard_map/ppermute | solution.py:222
  22.3 9.0 %collective-permute-start.10 = (bf16[128,640]{1,0:T(8,128)(2,1)S(1)}, bf16[128,640]{1,0:T(8,128)(2,1)S(1)}, u32[]{:S(2)}, u32[]{:S(2)}) collective-permute-start(bf16[128,640]{1,0:T(8,128)(2,1)S(1)} %get-tuple-element.16), channel_id=1, source_target_pairs={{0,8},{4,12},{8,0},{12,4},{1,9},{5,13},{9,1},{13,5},{2,10},{6,14},... | collective-permute-start | bytes 491528 | tf_op jit(solution)/shard_map/ppermute | solution.py:219

commit v7 on v6

--- a/solution.py
+++ b/solution.py
@@ -13,7 +13,7 @@
 CELLS = NX * NY
 F32 = jnp.float32
 BF16 = jnp.bfloat16
-W_BEGIN, W_GRAD, W_TOTAL, W_OUT = 8, 1, 4, 0
+W_BEGIN, W_GRAD, W_TOTAL, W_OUT = 8, 1, 5, 0
 VMEM_BYTES = 32 * 1024 * 1024
 
 
@@ -35,17 +35,20 @@
     return lax.rem(((s + 1) ^ 1) + nz - 1, nz)
 
 
-def gather_kernel(nz, nc, pos_ref, token_ref, cot_ref, *refs):
+def gather_kernel(nz, nc, pos_ref, token_ref, cot_ref, near_ref, *refs):
     pieces, f_ref, packs = refs[:nc], refs[nc], refs[nc + 1 :]
     blocks = cot_ref.shape[0]
-    cols = f_ref.shape[0] // nz
+    channels = nc * blocks
+    cols = channels // nz
     s, c = pos_ref[0], pos_ref[1]
     for k in range(nc):
         f_ref[pl.ds(pl.multiple_of((c ^ k) * blocks, blocks), blocks), :] = pieces[k][...]
+    f_ref[channels:, :] = near_ref[...]
     for k, pack in zip(range(2, nz - 1), packs):
         goal = lax.rem(s + k, nz)
         pack[:cols, :] = f_ref[pl.ds(pl.multiple_of(goal * cols, cols), cols), :]
-        pack[cols:, :] = cot_ref[...]
+        if nz > 4:
+            pack[cols:, :] = cot_ref[...]
 
 
 def columns(cols_ref, first, plane):
@@ -89,50 +92,70 @@
     )
 
 
-def output_kernel(nz, nc, scale, pos_ref, last_ref, w_ref, *refs):
-    terms = refs[:nc]
-    cot_ref, ce_ref, co_ref, f_ref, fe_ref, fo_ref = refs[nc : nc + 6]
-    packs = refs[nc + 6 : -5]
-    out_ref, back_ref, wg_ref, c_ref, g_ref = refs[-5:]
-    total = terms[0][...]
-    for term in terms[1:]:
-        total = total + term[...]
-    back_ref[:, 0, :] = total
-
-    blocks = cot_ref.shape[0]
-    cols = g_ref.shape[1]
-    s = pos_ref[0]
-    first = s % 2 == 0
-    even, odd = fe_ref[...], fo_ref[...]
-    acc = conv_part(w_ref, f_ref[...], 0)
-    acc = acc + jnp.where(s < nz - 1, conv_part(w_ref, jnp.where(first, even, odd), 1), 0.0)
-    acc = acc + jnp.where(s > 0, conv_part(w_ref, jnp.where(first, odd, even), -1), 0.0)
+def conv_part(w_ref, field, dz):
+    taps = w_ref.shape[0] // 3
+    return jnp.dot(
+        w_ref[(dz + 1) * taps : (dz + 2) * taps, :], field, preferred_element_type=F32
+    )
+
+
+def moved_sum(acc):
+    blocks = acc.shape[0] // 9
     total = None
     for dx in (-1, 0, 1):
         for dy in (-1, 0, 1):
             at = (3 * (dy + 1) + dx + 1) * blocks
             term = shifted(acc[at : at + blocks], dy, dx)
             total = term if total is None else total + term
-    out_ref[:, 0, :] = total
+    return total
+
+
+def moved_rows(plane):
+    plane = plane.astype(F32)
+    return jnp.concatenate([shifted(plane, -dy, 0).astype(BF16) for dy in (-1, 0, 1)], 0)
+
+
+def early_kernel(pos_ref, w_ref, f_ref, cot_ref, ce_ref, co_ref, out_ref, moved_ref, token_ref):
+    channels = w_ref.shape[1]
+    token_ref[...] = jnp.zeros(token_ref.shape, F32)
+    out_ref[...] = moved_sum(conv_part(w_ref, f_ref[:channels, :], 0))
+    for i, ref in enumerate((cot_ref, ce_ref, co_ref)):
+        moved_ref[i] = moved_rows(ref[...])
+
+
+def output_kernel(nz, nc, scale, pos_ref, last_ref, w_ref, *refs):
+    terms = refs[:nc]
+    own_ref, moved_ref, f_ref, fe_ref, fo_ref = refs[nc : nc + 5]
+    packs = refs[nc + 5 : -5]
+    out_ref, back_ref, wg_ref, c_ref, g_ref = refs[-5:]
+    total = terms[0][...]
+    for term in terms[1:]:
+        total = total + term[...]
+    back_ref[:, 0, :] = total
+
+    channels = w_ref.shape[1]
+    blocks = own_ref.shape[0]
+    cols = g_ref.shape[1]
+    s = pos_ref[0]
+    first = s % 2 == 0
+    even, odd = fe_ref[:channels, :], fo_ref[...]
+    after = conv_part(w_ref, jnp.where(first, even, odd), 1)
+    before = conv_part(w_ref, jnp.where(first, odd, even), -1)
+    acc = jnp.where(s < nz - 1, after, 0.0) + jnp.where(s > 0, before, 0.0)
+    out_ref[:, 0, :] = own_ref[...] + moved_sum(acc)
 
     mine = pl.ds(pl.multiple_of(s * cols, cols), cols)
-    for source, cot, field in (
-        (s, cot_ref, f_ref),
-        (s ^ 1, ce_ref, fe_ref),
-        (odd_partner(s, nz), co_ref, fo_ref),
-    ):
-        c_ref[source] = cot[...]
+    sources = (s, s ^ 1, odd_partner(s, nz))
+    for i, (source, field) in enumerate(zip(sources, (f_ref, fe_ref, fo_ref))):
+        c_ref[source] = moved_ref[i]
         g_ref[source] = field[mine, :]
     for k, pack in zip(range(2, nz - 1), packs):
         source = lax.rem(s + nz - k, nz)
-        c_ref[source] = pack[cols:, :]
         g_ref[source] = pack[:cols, :]
-
-    cots = []
+        c_ref[source] = moved_rows(pack[cols:, :] if nz > 4 else fe_ref[channels:, :])
+
     feats = []
     for z in range(nz):
-        plane = c_ref[z].astype(F32)
-        cots.append([shifted(plane, -dy, 0).astype(BF16) for dy in (-1, 0, 1)])
         field = g_ref[z].astype(F32)
         feats.append(jnp.concatenate([shifted(field, 0, dx).astype(BF16) for dx in (-1, 0, 1)], 0))
     for dz in (-1, 0, 1):
@@ -140,10 +163,7 @@
         for z in range(nz):
             if 0 <= z - dz < nz:
                 term = lax.dot_general(
-                    jnp.concatenate(cots[z - dz], 0),
-                    feats[z],
-                    (((1,), (1,)), ((), ())),
-                    preferred_element_type=F32,
+                    c_ref[z - dz], feats[z], (((1,), (1,)), ((), ())), preferred_element_type=F32
                 )
                 sums = term if sums is None else sums + term
         sums = sums * scale
@@ -196,6 +216,7 @@
     cot_even = lax.ppermute(cot, "sp", even_pairs)
     cot_odd = lax.ppermute(cot, "sp", odd_pairs)
     (begin,) = kernel_call(token_kernel, "begin", [small], [], weight=W_BEGIN * work)
+    feat, cot_even = lax.optimization_barrier((feat, cot_even))
     pieces = [feat] + [lax.ppermute(feat, "ch", mixed(k)) for k in range(1, nc)]
 
     *parts, token = kernel_call(
@@ -208,27 +229,34 @@
     )
     terms = [parts[0]] + [lax.ppermute(parts[k], "ch", mixed(k)) for k in range(1, nc)]
 
+    far_rows = cols if nz == 4 else cols + blocks
     f_all, *packs = kernel_call(
         functools.partial(gather_kernel, nz, nc),
         "gather",
-        [of(channels, BF16)] + [of(cols + blocks, BF16)] * (nz - 3),
-        [pos, token, cot] + pieces,
-    )
-    f_odd = lax.ppermute(f_all, "sp", odd_pairs)
+        [of(channels + blocks, BF16)] + [of(far_rows, BF16)] * (nz - 3),
+        [pos, token, cot, cot_odd] + pieces,
+    )
+    f_odd = lax.ppermute(f_all[:channels], "sp", odd_pairs)
+    f_even = lax.ppermute(f_all, "sp", even_pairs)
     far = [
         lax.ppermute(packs[k - 2], "sp", [(i, (i + k) % nz) for i in range(nz)])
         for k in range(2, nz - 1)
     ]
-    f_even = lax.ppermute(f_all, "sp", even_pairs)
+    out_own, moved, done = kernel_call(
+        early_kernel,
+        "early",
+        [of(blocks, F32), jax.ShapeDtypeStruct((3, 3 * blocks, plane), BF16), small],
+        [pos, w2, f_all, cot, cot_even, cot_odd],
+    )
 
     block = jax.ShapeDtypeStruct((blocks, 1, plane), F32)
-    (last,) = kernel_call(hold_kernel, "hold", [small], terms, weight=W_TOTAL * work)
+    (last,) = kernel_call(hold_kernel, "hold", [small], [done] + terms, weight=W_TOTAL * work)
     output, back, weight_grad = kernel_call(
         functools.partial(output_kernel, nz, nc, 1.0 / math.sqrt(nz * depth * plane)),
         "outputs",
         [block, block, jax.ShapeDtypeStruct((27, blocks, cols), F32)],
-        [pos, last, w2, *terms, cot, cot_even, cot_odd, f_all, f_even, f_odd, *far],
-        [pltpu.VMEM((nz, blocks, plane), BF16), pltpu.VMEM((nz, cols, plane), BF16)],
+        [pos, last, w2, *terms, out_own, moved, f_all, f_even, f_odd, *far],
+        [pltpu.VMEM((nz, 3 * blocks, plane), BF16), pltpu.VMEM((nz, cols, plane), BF16)],
         W_OUT * work,
     )
     return (output, back, weight_grad)

time: 34.9 us -> 32.2 us (0.923)
  waiting for transfers between devices: 14.8 us -> 11.2 us
  Pallas kernels: 5.88 us -> 6.83 us
    ppermute x1, waiting for transfers between devices: 2.94 us -> 0.01 us  [per_device(): cot_odd = lax.ppermute(cot, 'sp', odd_pairs)]
    ppermute x3, waiting for transfers between devices: 10.2 us -> 8.14 us  [per_device(): lax.ppermute(parts[k], 'ch', mixed(k))]
    ppermute x1, starting transfers between devices: 0.37 us -> 2.44 us  [per_device(): cot_odd = lax.ppermute(cot, 'sp', odd_pairs)]
    ppermute x3, starting transfers between devices: 5.76 us -> 4.39 us  [per_device(): pieces = [feat] + [lax.ppermute(feat, 'ch', mixed(k)) for k in range(1, nc)]]
    ppermute x1, waiting for transfers between devices: 0.01 us -> 1.13 us  [per_device(): cot_even = lax.ppermute(cot, 'sp', even_pairs)]
    ppermute x1, starting transfers between devices: 1.15 us -> 0.07 us  [per_device(): f_even = lax.ppermute(f_all, 'sp', even_pairs)]
    pallas_call x5 -> x6, Pallas kernels: 5.88 us -> 6.83 us  [kernel_call(): pl.pallas_call(body, out_shape=outs, in_specs=[SMEM if a.dtype == jnp.int...]
    ppermute x1, starting transfers between devices: 1.38 us -> 0.68 us  [per_device(): cot_even = lax.ppermute(cot, 'sp', even_pairs)]
  transfers between devices with their start and end apart: 11 -> 11, of which waited for: 4 -> 5; matrix products, arithmetic and copies ran while one was open for 0% -> 0% of each run, Pallas kernels for 7% -> 11%
where the time goes in v7:
time: 32.2 us; the launch traced here: 32.1 us
  starting transfers between devices  13.3 us (41%)
  waiting for transfers between devices  11.2 us (35%)
  Pallas kernels  6.83 us (21%)
  between operations  0.71 us (2%)
    ppermute x3, waiting for transfers between devices, per_device(): lax.ppermute(parts[k], 'ch', mixed(k))  8.14 us
    pallas_call x6, Pallas kernels, kernel_call(): pl.pallas_call(body, out_shape=outs, in_specs=[SMEM if a.dtype == jnp.int...  6.83 us
    ppermute x3, starting transfers between devices, per_device(): lax.ppermute(parts[k], 'ch', mixed(k))  4.47 us
    ppermute x3, starting transfers between devices, per_device(): pieces = [feat] + [lax.ppermute(feat, 'ch', mixed(k)) for k in range(1, nc)]  4.39 us
    ppermute x1, starting transfers between devices, per_device(): cot_odd = lax.ppermute(cot, 'sp', odd_pairs)  2.44 us
    ppermute x1, waiting for transfers between devices, per_device(): lax.ppermute(packs[k - 2], 'sp', [(i, (i + k) % nz) for i in range(nz)])  1.27 us
    ppermute x1, waiting for transfers between devices, per_device(): cot_even = lax.ppermute(cot, 'sp', even_pairs)  1.13 us
    ppermute x1, starting transfers between devices, per_device(): f_odd = lax.ppermute(f_all[:channels], 'sp', odd_pairs)  0.69 us
  transfers between devices with their start and end apart: 11, of which 5 were waited for; matrix products, arithmetic and copies ran while one was open for 0% of the time, Pallas kernels for 11%

profile of v7, /device:TPU:0, one launch (start us, length us, event | category | flops | bytes accessed | tf_op | source)
XLA Modules:
  0.0 32.1 jit_solution(17385961600518021016)
XLA Ops:
  0.6 0.0 copy-start.2
  0.6 0.0 copy-start
  0.7 0.0 copy-start.1
  0.7 2.4 %collective-permute-start.1 = (bf16[64,640]{1,0:T(8,128)(2,1)}, bf16[64,640]{1,0:T(8,128)(2,1)S(1)}, u32[]{:S(2)}, u32[]{:S(2)}) collective-permute-start(bf16[64,640]{1,0:T(8,128)(2,1)} %bitcast.8), channel_id=1, source_target_pairs={{0,12},{4,8},{8,4},{12,0},{1,13},{5,9},{9,5},{13,1},{2,14},{6,10},... | collective-permute-start | bytes 245768 | tf_op jit(solution)/shard_map/ppermute | solution.py:217
  3.1 0.7 %collective-permute-start = (bf16[64,640]{1,0:T(8,128)(2,1)}, bf16[64,640]{1,0:T(8,128)(2,1)S(1)}, u32[]{:S(2)}, u32[]{:S(2)}) collective-permute-start(bf16[64,640]{1,0:T(8,128)(2,1)} %bitcast.9), channel_id=1, source_target_pairs={{0,4},{4,0},{8,12},{12,8},{1,5},{5,1},{9,13},{13,9},{2,6},{6,2},{1... | collective-permute-start | bytes 245768 | tf_op jit(solution)/shard_map/ppermute | solution.py:216
  3.8 1.1 %collective-permute-done.even_ref.ce_ref = bf16[64,640]{1,0:T(8,128)(2,1)S(1)} collective-permute-done((bf16[64,640]{1,0:T(8,128)(2,1)}, bf16[64,640]{1,0:T(8,128)(2,1)S(1)}, u32[]{:S(2)}, u32[]{:S(2)}) %collective-permute-start) | collective-permute-done | bytes 81952 | tf_op jit(solution)/shard_map/ppermute | solution.py:216
  4.9 0.0 copy-done.2
  4.9 3.6 %collective-permute-start.4 = (bf16[64,640]{1,0:T(8,128)(2,1)S(1)}, bf16[64,640]{1,0:T(8,128)(2,1)S(1)}, u32[]{:S(2)}, u32[]{:S(2)}) collective-permute-start(bf16[64,640]{1,0:T(8,128)(2,1)S(1)} %bitcast.13), channel_id=1, source_target_pairs={{0,3},{1,2},{2,1},{3,0},{4,7},{5,6},{6,5},{7,4},{8,11},{9,10},{10,... | collective-permute-start | bytes 245768 | tf_op jit(solution)/shard_map/ppermute | solution.py:220
  8.5 0.0 collective-permute-start.3
  8.5 0.8 %collective-permute-start.2 = (bf16[64,640]{1,0:T(8,128)(2,1)S(1)}, bf16[64,640]{1,0:T(8,128)(2,1)S(1)}, u32[]{:S(2)}, u32[]{:S(2)}) collective-permute-start(bf16[64,640]{1,0:T(8,128)(2,1)S(1)} %bitcast.15), channel_id=1, source_target_pairs={{0,1},{1,0},{2,3},{3,2},{4,5},{5,4},{6,7},{7,6},{8,9},{9,8},{10,11... | collective-permute-start | bytes 245768 | tf_op jit(solution)/shard_map/ppermute | solution.py:220
  9.3 0.1 pad_add_fusion.pos_ref
  9.4 0.0 collective-permute-done.1.odd_ref.near_ref.co_ref
  9.4 0.0 copy-done
  9.4 0.0 copy-done.1
  9.4 1.8 %input_grad.1 = (f32[64,640]{1,0:T(8,128)S(1)}, f32[64,640]{1,0:T(8,128)S(1)}, f32[64,640]{1,0:T(8,128)S(1)}, f32[64,640]{1,0:T(8,128)S(1)}, f32[8,128]{1,0:T(8,128)S(1)}) custom-call(s32[2]{0:T(128)S(1)} %pad_add_fusion.pos_ref, f32[8,128]{1,0:T(8,128)S(1)} %begin.1.begin_ref, bf16[64,640]{1,0:T(8,128)(2,1)S(1)} %bitcast.10, ...), custom_call_target="tpu_custom_call" | custom-call | flops 566231040 | tf_op jit(solution)/shard_map/input_grad/pallas_call | solution.py:181
  11.2 1.3 %collective-permute-start.5 = (f32[64,640]{1,0:T(8,128)S(1)}, f32[64,640]{1,0:T(8,128)S(1)}, u32[]{:S(2)}, u32[]{:S(2)}) collective-permute-start(f32[64,640]{1,0:T(8,128)S(1)} %get-tuple-element.21), channel_id=1, source_target_pairs={{0,1},{1,0},{2,3},{3,2},{4,5},{5,4},{6,7},{7,6},{8,9},{9,8},{10,11... | collective-permute-start | bytes 491528 | tf_op jit(solution)/shard_map/ppermute | solution.py:230
  12.5 2.9 %collective-permute-start.6 = (f32[64,640]{1,0:T(8,128)S(1)}, f32[64,640]{1,0:T(8,128)S(1)}, u32[]{:S(2)}, u32[]{:S(2)}) collective-permute-start(f32[64,640]{1,0:T(8,128)S(1)} %get-tuple-element.22), channel_id=1, source_target_pairs={{0,2},{1,3},{2,0},{3,1},{4,6},{5,7},{6,4},{7,5},{8,10},{9,11},{10,... | collective-permute-start | bytes 491528 | tf_op jit(solution)/shard_map/ppermute | solution.py:230
  15.4 0.0 collective-permute-done.4.refs_3_
  15.4 0.2 collective-permute-start.7
  15.7 0.6 %collective-permute-done.3.refs_2_ = bf16[64,640]{1,0:T(8,128)(2,1)S(1)} collective-permute-done((bf16[64,640]{1,0:T(8,128)(2,1)S(1)}, bf16[64,640]{1,0:T(8,128)(2,1)S(1)}, u32[]{:S(2)}, u32[]{:S(2)}) %collective-permute-start.3) | collective-permute-done | bytes 81952 | tf_op jit(solution)/shard_map/ppermute | solution.py:220
  16.3 0.0 collective-permute-done.2.refs_1_
  16.3 0.6 %gather.1 = (bf16[320,640]{1,0:T(8,128)(2,1)S(1)}, bf16[64,640]{1,0:T(8,128)(2,1)S(1)}) custom-call(s32[2]{0:T(128)S(1)} %pad_add_fusion.pos_ref, f32[8,128]{1,0:T(8,128)S(1)} %get-tuple-element.16.token_ref, bf16[64,640]{1,0:T(8,128)(2,1)S(1)} %bitcast.11, bf16[64,640]{1,0:T(8,128)(2,1)S(1)} %collective-permute-done.1.odd_ref.near_ref.co_ref, ...), custom_call_target="tpu_custom_call" | custom-call | tf_op jit(solution)/shard_map/gather/pallas_call | solution.py:181
  16.9 0.1 collective-permute-start.8
  17.0 0.7 %collective-permute-start.9 = (bf16[256,640]{1,0:T(8,128)(2,1)S(1)}, bf16[256,640]{1,0:T(8,128)(2,1)S(1)}, u32[]{:S(2)}, u32[]{:S(2)}) collective-permute-start(bf16[256,640]{1,0:T(8,128)(2,1)S(1)} %slice.3), channel_id=1, source_target_pairs={{0,12},{4,8},{8,4},{12,0},{1,13},{5,9},{9,5},{13,1},{2,14},{6,10},... | collective-permute-start | bytes 983048 | tf_op jit(solution)/shard_map/ppermute | solution.py:239
  17.7 1.2 %early.1 = (f32[64,640]{1,0:T(8,128)S(1)}, bf16[3,192,640]{2,1,0:T(8,128)(2,1)S(1)}, f32[8,128]{1,0:T(8,128)S(1)}) custom-call(s32[2]{0:T(128)S(1)} %pad_add_fusion.pos_ref, bf16[1728,256]{1,0:T(8,128)(2,1)S(1)} %bitcast.6, bf16[320,640]{1,0:T(8,128)(2,1)S(1)} %get-tuple-element.18.f_ref.refs_6_, bf16[64,640]{1,0:T(8,128)(2,1)S(1)} %bitcast.12, ...), custom_call_target="tpu_custom_call" | custom-call | tf_op jit(solution)/shard_map/early/pallas_call | solution.py:181
  18.9 2.6 %collective-permute-done.5.refs_2_.refs_1_ = f32[64,640]{1,0:T(8,128)S(1)} collective-permute-done((f32[64,640]{1,0:T(8,128)S(1)}, f32[64,640]{1,0:T(8,128)S(1)}, u32[]{:S(2)}, u32[]{:S(2)}) %collective-permute-start.5) | collective-permute-done | bytes 163872 | tf_op jit(solution)/shard_map/ppermute | solution.py:230
  21.5 0.5 %collective-permute-start.10 = (bf16[64,640]{1,0:T(8,128)(2,1)S(1)}, bf16[64,640]{1,0:T(8,128)(2,1)S(1)}, u32[]{:S(2)}, u32[]{:S(2)}) collective-permute-start(bf16[64,640]{1,0:T(8,128)(2,1)S(1)} %get-tuple-element.26), channel_id=1, source_target_pairs={{0,8},{4,12},{8,0},{12,4},{1,9},{5,13},{9,1},{13,5},{2,10},{6,14},... | collective-permute-start | bytes 245768 | tf_op jit(solution)/shard_map/ppermute | solution.py:242
  22.0 5.6 %collective-permute-done.6.refs_3_.refs_2_ = f32[64,640]{1,0:T(8,128)S(1)} collective-permute-done((f32[64,640]{1,0:T(8,128)S(1)}, f32[64,640]{1,0:T(8,128)S(1)}, u32[]{:S(2)}, u32[]{:S(2)}) %collective-permute-start.6) | collective-permute-done | bytes 163872 | tf_op jit(solution)/shard_map/ppermute | solution.py:230
  27.6 0.0 collective-permute-done.7.refs_4_.refs_3_
  27.6 1.3 %collective-permute-done.10.refs_9_ = bf16[64,640]{1,0:T(8,128)(2,1)S(1)} collective-permute-done((bf16[64,640]{1,0:T(8,128)(2,1)S(1)}, bf16[64,640]{1,0:T(8,128)(2,1)S(1)}, u32[]{:S(2)}, u32[]{:S(2)}) %collective-permute-start.10) | collective-permute-done | bytes 81952 | tf_op jit(solution)/shard_map/ppermute | solution.py:242
  28.9 0.0 collective-permute-done.9.refs_8_
  28.9 0.0 collective-permute-done.8.refs_7_
  28.9 3.2 %outputs.1 = (f32[64,1,640]{2,1,0:T(1,128)}, f32[64,1,640]{2,1,0:T(1,128)}, f32[27,64,64]{2,1,0:T(8,128)}) custom-call(s32[2]{0:T(128)S(1)} %pad_add_fusion.pos_ref, f32[8,128]{1,0:T(8,128)S(1)} %hold.1.last_ref, bf16[1728,256]{1,0:T(8,128)(2,1)S(1)} %bitcast.7, f32[64,640]{1,0:T(8,128)S(1)} %get-tuple-element.20.refs_1_.refs_0_, ...), custom_call_target="tpu_custom_call" | custom-call | tf_op jit(solution)/shard_map/outputs/pallas_call | solution.py:181
  (3 shorter events, 0.0 us)
Async XLA Ops:
  0.6 4.3 %copy-start.2 = (bf16[64,1,640]{2,0,1:T(8,128)(2,1)S(1)}, bf16[64,1,640]{2,0,1:T(8,128)(2,1)}, u32[]{:S(2)}) copy-start(bf16[64,1,640]{2,0,1:T(8,128)(2,1)} %param.3) | copy-start | bytes 245764
  0.6 8.7 %copy-start = (bf16[27,64,256]{2,1,0:T(8,128)(2,1)S(1)}, bf16[27,64,256]{2,1,0:T(8,128)(2,1)}, u32[]{:S(2)}) copy-start(bf16[27,64,256]{2,1,0:T(8,128)(2,1)} %param.4) | copy-start | bytes 2654212
  0.7 8.7 %copy-start.1 = (bf16[64,1,640]{2,0,1:T(8,128)(2,1)S(1)}, bf16[64,1,640]{2,0,1:T(8,128)(2,1)}, u32[]{:S(2)}) copy-start(bf16[64,1,640]{2,0,1:T(8,128)(2,1)} %param.5) | copy-start | bytes 245764
  0.7 8.7 %collective-permute-start.1 = (bf16[64,640]{1,0:T(8,128)(2,1)}, bf16[64,640]{1,0:T(8,128)(2,1)S(1)}, u32[]{:S(2)}, u32[]{:S(2)}) collective-permute-start(bf16[64,640]{1,0:T(8,128)(2,1)} %bitcast.8), channel_id=1, source_target_pairs={{0,12},{4,8},{8,4},{12,0},{1,13},{5,9},{9,5},{13,1},{2,14},{6,10},... | collective-permute-start | bytes 245768 | tf_op jit(solution)/shard_map/ppermute | solution.py:217
  3.1 1.8 %collective-permute-start = (bf16[64,640]{1,0:T(8,128)(2,1)}, bf16[64,640]{1,0:T(8,128)(2,1)S(1)}, u32[]{:S(2)}, u32[]{:S(2)}) collective-permute-start(bf16[64,640]{1,0:T(8,128)(2,1)} %bitcast.9), channel_id=1, source_target_pairs={{0,4},{4,0},{8,12},{12,8},{1,5},{5,1},{9,13},{13,9},{2,6},{6,2},{1... | collective-permute-start | bytes 245768 | tf_op jit(solution)/shard_map/ppermute | solution.py:216
  4.9 10.5 %collective-permute-start.4 = (bf16[64,640]{1,0:T(8,128)(2,1)S(1)}, bf16[64,640]{1,0:T(8,128)(2,1)S(1)}, u32[]{:S(2)}, u32[]{:S(2)}) collective-permute-start(bf16[64,640]{1,0:T(8,128)(2,1)S(1)} %bitcast.13), channel_id=1, source_target_pairs={{0,3},{1,2},{2,1},{3,0},{4,7},{5,6},{6,5},{7,4},{8,11},{9,10},{10,... | collective-permute-start | bytes 245768 | tf_op jit(solution)/shard_map/ppermute | solution.py:220
  8.5 7.8 %collective-permute-start.3 = (bf16[64,640]{1,0:T(8,128)(2,1)S(1)}, bf16[64,640]{1,0:T(8,128)(2,1)S(1)}, u32[]{:S(2)}, u32[]{:S(2)}) collective-permute-start(bf16[64,640]{1,0:T(8,128)(2,1)S(1)} %bitcast.14), channel_id=1, source_target_pairs={{0,2},{1,3},{2,0},{3,1},{4,6},{5,7},{6,4},{7,5},{8,10},{9,11},{10,... | collective-permute-start | bytes 245768 | tf_op jit(solution)/shard_map/ppermute | solution.py:220
  8.5 7.8 %collective-permute-start.2 = (bf16[64,640]{1,0:T(8,128)(2,1)S(1)}, bf16[64,640]{1,0:T(8,128)(2,1)S(1)}, u32[]{:S(2)}, u32[]{:S(2)}) collective-permute-start(bf16[64,640]{1,0:T(8,128)(2,1)S(1)} %bitcast.15), channel_id=1, source_target_pairs={{0,1},{1,0},{2,3},{3,2},{4,5},{5,4},{6,7},{7,6},{8,9},{9,8},{10,11... | collective-permute-start | bytes 245768 | tf_op jit(solution)/shard_map/ppermute | solution.py:220
  11.2 10.3 %collective-permute-start.5 = (f32[64,640]{1,0:T(8,128)S(1)}, f32[64,640]{1,0:T(8,128)S(1)}, u32[]{:S(2)}, u32[]{:S(2)}) collective-permute-start(f32[64,640]{1,0:T(8,128)S(1)} %get-tuple-element.21), channel_id=1, source_target_pairs={{0,1},{1,0},{2,3},{3,2},{4,5},{5,4},{6,7},{7,6},{8,9},{9,8},{10,11... | collective-permute-start | bytes 491528 | tf_op jit(solution)/shard_map/ppermute | solution.py:230
  12.5 15.1 %collective-permute-start.6 = (f32[64,640]{1,0:T(8,128)S(1)}, f32[64,640]{1,0:T(8,128)S(1)}, u32[]{:S(2)}, u32[]{:S(2)}) collective-permute-start(f32[64,640]{1,0:T(8,128)S(1)} %get-tuple-element.22), channel_id=1, source_target_pairs={{0,2},{1,3},{2,0},{3,1},{4,6},{5,7},{6,4},{7,5},{8,10},{9,11},{10,... | collective-permute-start | bytes 491528 | tf_op jit(solution)/shard_map/ppermute | solution.py:230
  15.4 12.1 %collective-permute-start.7 = (f32[64,640]{1,0:T(8,128)S(1)}, f32[64,640]{1,0:T(8,128)S(1)}, u32[]{:S(2)}, u32[]{:S(2)}) collective-permute-start(f32[64,640]{1,0:T(8,128)S(1)} %get-tuple-element.23), channel_id=1, source_target_pairs={{0,3},{1,2},{2,1},{3,0},{4,7},{5,6},{6,5},{7,4},{8,11},{9,10},{10,... | collective-permute-start | bytes 491528 | tf_op jit(solution)/shard_map/ppermute | solution.py:230
  16.9 12.0 %collective-permute-start.8 = (bf16[320,640]{1,0:T(8,128)(2,1)S(1)}, bf16[320,640]{1,0:T(8,128)(2,1)S(1)}, u32[]{:S(2)}, u32[]{:S(2)}) collective-permute-start(bf16[320,640]{1,0:T(8,128)(2,1)S(1)} %get-tuple-element.18.f_ref.refs_6_), channel_id=1, source_target_pairs={{0,4},{4,0},{8,12},{12,8},{1,5},{5,1},{9,13},{13,9},{2,6},{6,2},{1... | collective-permute-start | bytes 1228808 | tf_op jit(solution)/shard_map/ppermute | solution.py:240
  17.0 11.8 %collective-permute-start.9 = (bf16[256,640]{1,0:T(8,128)(2,1)S(1)}, bf16[256,640]{1,0:T(8,128)(2,1)S(1)}, u32[]{:S(2)}, u32[]{:S(2)}) collective-permute-start(bf16[256,640]{1,0:T(8,128)(2,1)S(1)} %slice.3), channel_id=1, source_target_pairs={{0,12},{4,8},{8,4},{12,0},{1,13},{5,9},{9,5},{13,1},{2,14},{6,10},... | collective-permute-start | bytes 983048 | tf_op jit(solution)/shard_map/ppermute | solution.py:239
  21.5 7.4 %collective-permute-start.10 = (bf16[64,640]{1,0:T(8,128)(2,1)S(1)}, bf16[64,640]{1,0:T(8,128)(2,1)S(1)}, u32[]{:S(2)}, u32[]{:S(2)}) collective-permute-start(bf16[64,640]{1,0:T(8,128)(2,1)S(1)} %get-tuple-element.26), channel_id=1, source_target_pairs={{0,8},{4,12},{8,0},{12,4},{1,9},{5,13},{9,1},{13,5},{2,10},{6,14},... | collective-permute-start | bytes 245768 | tf_op jit(solution)/shard_map/ppermute | solution.py:242

commit v8 on v7

--- a/solution.py
+++ b/solution.py
@@ -13,7 +13,7 @@
 CELLS = NX * NY
 F32 = jnp.float32
 BF16 = jnp.bfloat16
-W_BEGIN, W_GRAD, W_TOTAL, W_OUT = 8, 1, 5, 0
+W_BEGIN, W_GRAD, W_TOTAL, W_OUT = 8, 1, 0, 4
 VMEM_BYTES = 32 * 1024 * 1024
 
 
@@ -59,10 +59,6 @@
             cols_ref[tap * blocks : (tap + 1) * blocks, :] = shifted(plane, -dy, -dx).astype(BF16)
 
 
-def hold_kernel(*refs):
-    refs[-1][...] = jnp.zeros(refs[-1].shape, F32)
-
-
 def token_kernel(token_ref):
     token_ref[...] = jnp.zeros(token_ref.shape, F32)
 
@@ -115,24 +111,17 @@
     return jnp.concatenate([shifted(plane, -dy, 0).astype(BF16) for dy in (-1, 0, 1)], 0)
 
 
-def early_kernel(pos_ref, w_ref, f_ref, cot_ref, ce_ref, co_ref, out_ref, moved_ref, token_ref):
+def early_kernel(w_ref, f_ref, cot_ref, ce_ref, co_ref, out_ref, moved_ref):
     channels = w_ref.shape[1]
-    token_ref[...] = jnp.zeros(token_ref.shape, F32)
     out_ref[...] = moved_sum(conv_part(w_ref, f_ref[:channels, :], 0))
     for i, ref in enumerate((cot_ref, ce_ref, co_ref)):
         moved_ref[i] = moved_rows(ref[...])
 
 
-def output_kernel(nz, nc, scale, pos_ref, last_ref, w_ref, *refs):
-    terms = refs[:nc]
-    own_ref, moved_ref, f_ref, fe_ref, fo_ref = refs[nc : nc + 5]
-    packs = refs[nc + 5 : -5]
-    out_ref, back_ref, wg_ref, c_ref, g_ref = refs[-5:]
-    total = terms[0][...]
-    for term in terms[1:]:
-        total = total + term[...]
-    back_ref[:, 0, :] = total
-
+def output_kernel(nz, scale, pos_ref, w_ref, own_ref, moved_ref, f_ref, fe_ref, fo_ref, *refs):
+    packs = refs[:-5]
+    out_ref, wg_ref, token_ref, c_ref, g_ref = refs[-5:]
+    token_ref[...] = jnp.zeros(token_ref.shape, F32)
     channels = w_ref.shape[1]
     blocks = own_ref.shape[0]
     cols = g_ref.shape[1]
@@ -173,6 +162,13 @@
                 wg_ref[tap] = sums[dy * blocks : (dy + 1) * blocks, dx * cols : (dx + 1) * cols]
 
 
+def total_kernel(token_ref, *refs):
+    total = refs[0][...]
+    for ref in refs[1:-1]:
+        total = total + ref[...]
+    refs[-1][:, 0, :] = total
+
+
 VMEM = pl.BlockSpec(memory_space=pltpu.VMEM)
 SMEM = pl.BlockSpec(memory_space=pltpu.SMEM)
 
@@ -242,23 +238,23 @@
         lax.ppermute(packs[k - 2], "sp", [(i, (i + k) % nz) for i in range(nz)])
         for k in range(2, nz - 1)
     ]
-    out_own, moved, done = kernel_call(
+    out_own, moved = kernel_call(
         early_kernel,
         "early",
-        [of(blocks, F32), jax.ShapeDtypeStruct((3, 3 * blocks, plane), BF16), small],
-        [pos, w2, f_all, cot, cot_even, cot_odd],
+        [of(blocks, F32), jax.ShapeDtypeStruct((3, 3 * blocks, plane), BF16)],
+        [w2, f_all, cot, cot_even, cot_odd],
     )
 
     block = jax.ShapeDtypeStruct((blocks, 1, plane), F32)
-    (last,) = kernel_call(hold_kernel, "hold", [small], [done] + terms, weight=W_TOTAL * work)
-    output, back, weight_grad = kernel_call(
-        functools.partial(output_kernel, nz, nc, 1.0 / math.sqrt(nz * depth * plane)),
+    output, weight_grad, last = kernel_call(
+        functools.partial(output_kernel, nz, 1.0 / math.sqrt(nz * depth * plane)),
         "outputs",
-        [block, block, jax.ShapeDtypeStruct((27, blocks, cols), F32)],
-        [pos, last, w2, *terms, out_own, moved, f_all, f_even, f_odd, *far],
+        [block, jax.ShapeDtypeStruct((27, blocks, cols), F32), small],
+        [pos, w2, out_own, moved, f_all, f_even, f_odd, *far],
         [pltpu.VMEM((nz, 3 * blocks, plane), BF16), pltpu.VMEM((nz, cols, plane), BF16)],
         W_OUT * work,
     )
+    (back,) = kernel_call(total_kernel, "total", [block], [last] + terms, weight=W_TOTAL * work)
     return (output, back, weight_grad)
 
 

time: 32.2 us -> 36.8 us (1.14)
  waiting for transfers between devices: 11.2 us -> 13.6 us
  starting transfers between devices: 13.3 us -> 15.3 us
    ppermute x3, waiting for transfers between devices: 8.14 us -> 1.88 us  [per_device(): lax.ppermute(parts[k], 'ch', mixed(k))]
    ppermute x1, waiting for transfers between devices: 1.27 us -> 5.93 us  [per_device(): lax.ppermute(packs[k - 2], 'sp', [(i, (i + k) % nz) for i in range(nz)])]
    ppermute x3, waiting for transfers between devices: 0.63 us -> 4.69 us  [per_device(): pieces = [feat] + [lax.ppermute(feat, 'ch', mixed(k)) for k in range(1, nc)]]
    ppermute x3, starting transfers between devices: 4.47 us -> 5.51 us  [per_device(): lax.ppermute(parts[k], 'ch', mixed(k))]
    ppermute x1, starting transfers between devices: 0.51 us -> 1.49 us  [per_device(): lax.ppermute(packs[k - 2], 'sp', [(i, (i + k) % nz) for i in range(nz)])]
  transfers between devices with their start and end apart: 11 -> 11, of which waited for: 5 -> 5; matrix products, arithmetic and copies ran while one was open for 0% -> 0% of each run, Pallas kernels for 11% -> 15%
where the time goes in v8:
time: 36.8 us; the launch traced here: 36.7 us
  starting transfers between devices  15.3 us (42%)
  waiting for transfers between devices  13.6 us (37%)
  Pallas kernels  6.93 us (19%)
  between operations  0.71 us (2%)
    pallas_call x6, Pallas kernels, kernel_call(): pl.pallas_call(body, out_shape=outs, in_specs=[SMEM if a.dtype == jnp.int...  6.93 us
    ppermute x1, waiting for transfers between devices, per_device(): lax.ppermute(packs[k - 2], 'sp', [(i, (i + k) % nz) for i in range(nz)])  5.93 us
    ppermute x3, starting transfers between devices, per_device(): lax.ppermute(parts[k], 'ch', mixed(k))  5.51 us
    ppermute x3, waiting for transfers between devices, per_device(): pieces = [feat] + [lax.ppermute(feat, 'ch', mixed(k)) for k in range(1, nc)]  4.69 us
    ppermute x3, starting transfers between devices, per_device(): pieces = [feat] + [lax.ppermute(feat, 'ch', mixed(k)) for k in range(1, nc)]  4.39 us
    ppermute x1, starting transfers between devices, per_device(): cot_odd = lax.ppermute(cot, 'sp', odd_pairs)  2.44 us
    ppermute x3, waiting for transfers between devices, per_device(): lax.ppermute(parts[k], 'ch', mixed(k))  1.88 us
    ppermute x1, starting transfers between devices, per_device(): lax.ppermute(packs[k - 2], 'sp', [(i, (i + k) % nz) for i in range(nz)])  1.49 us
  transfers between devices with their start and end apart: 11, of which 5 were waited for; matrix products, arithmetic and copies ran while one was open for 0% of the time, Pallas kernels for 15%

profile of v8, /device:TPU:0, one launch (start us, length us, event | category | flops | bytes accessed | tf_op | source)
XLA Modules:
  0.0 36.7 jit_solution(7078151171437410411)
XLA Ops:
  0.6 0.0 copy-start.2
  0.6 0.0 copy-start
  0.7 0.0 copy-start.1
  0.7 2.4 %collective-permute-start.1 = (bf16[64,640]{1,0:T(8,128)(2,1)}, bf16[64,640]{1,0:T(8,128)(2,1)S(1)}, u32[]{:S(2)}, u32[]{:S(2)}) collective-permute-start(bf16[64,640]{1,0:T(8,128)(2,1)} %bitcast.8), channel_id=1, source_target_pairs={{0,12},{4,8},{8,4},{12,0},{1,13},{5,9},{9,5},{13,1},{2,14},{6,10},... | collective-permute-start | bytes 245768 | tf_op jit(solution)/shard_map/ppermute | solution.py:213
  3.1 0.7 %collective-permute-start = (bf16[64,640]{1,0:T(8,128)(2,1)}, bf16[64,640]{1,0:T(8,128)(2,1)S(1)}, u32[]{:S(2)}, u32[]{:S(2)}) collective-permute-start(bf16[64,640]{1,0:T(8,128)(2,1)} %bitcast.9), channel_id=1, source_target_pairs={{0,4},{4,0},{8,12},{12,8},{1,5},{5,1},{9,13},{13,9},{2,6},{6,2},{1... | collective-permute-start | bytes 245768 | tf_op jit(solution)/shard_map/ppermute | solution.py:212
  3.8 1.1 %collective-permute-done.even_ref.ce_ref = bf16[64,640]{1,0:T(8,128)(2,1)S(1)} collective-permute-done((bf16[64,640]{1,0:T(8,128)(2,1)}, bf16[64,640]{1,0:T(8,128)(2,1)S(1)}, u32[]{:S(2)}, u32[]{:S(2)}) %collective-permute-start) | collective-permute-done | bytes 81952 | tf_op jit(solution)/shard_map/ppermute | solution.py:212
  4.9 0.0 copy-done.2
  4.9 3.6 %collective-permute-start.4 = (bf16[64,640]{1,0:T(8,128)(2,1)S(1)}, bf16[64,640]{1,0:T(8,128)(2,1)S(1)}, u32[]{:S(2)}, u32[]{:S(2)}) collective-permute-start(bf16[64,640]{1,0:T(8,128)(2,1)S(1)} %bitcast.13), channel_id=1, source_target_pairs={{0,3},{1,2},{2,1},{3,0},{4,7},{5,6},{6,5},{7,4},{8,11},{9,10},{10,... | collective-permute-start | bytes 245768 | tf_op jit(solution)/shard_map/ppermute | solution.py:216
  8.5 0.0 collective-permute-start.3
  8.5 0.8 %collective-permute-start.2 = (bf16[64,640]{1,0:T(8,128)(2,1)S(1)}, bf16[64,640]{1,0:T(8,128)(2,1)S(1)}, u32[]{:S(2)}, u32[]{:S(2)}) collective-permute-start(bf16[64,640]{1,0:T(8,128)(2,1)S(1)} %bitcast.15), channel_id=1, source_target_pairs={{0,1},{1,0},{2,3},{3,2},{4,5},{5,4},{6,7},{7,6},{8,9},{9,8},{10,11... | collective-permute-start | bytes 245768 | tf_op jit(solution)/shard_map/ppermute | solution.py:216
  9.3 0.1 pad_add_fusion.pos_ref
  9.4 0.0 collective-permute-done.1.odd_ref.near_ref.co_ref
  9.4 0.0 copy-done
  9.4 0.0 copy-done.1
  9.4 1.8 %input_grad.1 = (f32[64,640]{1,0:T(8,128)S(1)}, f32[64,640]{1,0:T(8,128)S(1)}, f32[64,640]{1,0:T(8,128)S(1)}, f32[64,640]{1,0:T(8,128)S(1)}, f32[8,128]{1,0:T(8,128)S(1)}) custom-call(s32[2]{0:T(128)S(1)} %pad_add_fusion.pos_ref, f32[8,128]{1,0:T(8,128)S(1)} %begin.1.begin_ref, bf16[64,640]{1,0:T(8,128)(2,1)S(1)} %bitcast.10, ...), custom_call_target="tpu_custom_call" | custom-call | flops 566231040 | tf_op jit(solution)/shard_map/input_grad/pallas_call | solution.py:177
  11.2 0.9 %collective-permute-done.4.refs_3_ = bf16[64,640]{1,0:T(8,128)(2,1)S(1)} collective-permute-done((bf16[64,640]{1,0:T(8,128)(2,1)S(1)}, bf16[64,640]{1,0:T(8,128)(2,1)S(1)}, u32[]{:S(2)}, u32[]{:S(2)}) %collective-permute-start.4) | collective-permute-done | bytes 81952 | tf_op jit(solution)/shard_map/ppermute | solution.py:216
  12.1 3.8 %collective-permute-done.3.refs_2_ = bf16[64,640]{1,0:T(8,128)(2,1)S(1)} collective-permute-done((bf16[64,640]{1,0:T(8,128)(2,1)S(1)}, bf16[64,640]{1,0:T(8,128)(2,1)S(1)}, u32[]{:S(2)}, u32[]{:S(2)}) %collective-permute-start.3) | collective-permute-done | bytes 81952 | tf_op jit(solution)/shard_map/ppermute | solution.py:216
  15.9 0.0 collective-permute-done.2.refs_1_
  15.9 0.6 %gather.1 = (bf16[320,640]{1,0:T(8,128)(2,1)S(1)}, bf16[64,640]{1,0:T(8,128)(2,1)S(1)}) custom-call(s32[2]{0:T(128)S(1)} %pad_add_fusion.pos_ref, f32[8,128]{1,0:T(8,128)S(1)} %get-tuple-element.18.token_ref, bf16[64,640]{1,0:T(8,128)(2,1)S(1)} %bitcast.11, bf16[64,640]{1,0:T(8,128)(2,1)S(1)} %collective-permute-done.1.odd_ref.near_ref.co_ref, ...), custom_call_target="tpu_custom_call" | custom-call | tf_op jit(solution)/shard_map/gather/pallas_call | solution.py:177
  16.5 0.1 collective-permute-start.5
  16.6 0.7 %collective-permute-start.6 = (bf16[256,640]{1,0:T(8,128)(2,1)S(1)}, bf16[256,640]{1,0:T(8,128)(2,1)S(1)}, u32[]{:S(2)}, u32[]{:S(2)}) collective-permute-start(bf16[256,640]{1,0:T(8,128)(2,1)S(1)} %slice.3), channel_id=1, source_target_pairs={{0,12},{4,8},{8,4},{12,0},{1,13},{5,9},{9,5},{13,1},{2,14},{6,10},... | collective-permute-start | bytes 983048 | tf_op jit(solution)/shard_map/ppermute | solution.py:235
  17.3 1.5 %collective-permute-start.7 = (bf16[64,640]{1,0:T(8,128)(2,1)S(1)}, bf16[64,640]{1,0:T(8,128)(2,1)S(1)}, u32[]{:S(2)}, u32[]{:S(2)}) collective-permute-start(bf16[64,640]{1,0:T(8,128)(2,1)S(1)} %get-tuple-element.23), channel_id=1, source_target_pairs={{0,8},{4,12},{8,0},{12,4},{1,9},{5,13},{9,1},{13,5},{2,10},{6,14},... | collective-permute-start | bytes 245768 | tf_op jit(solution)/shard_map/ppermute | solution.py:238
  18.8 0.9 %collective-permute-start.8 = (f32[64,640]{1,0:T(8,128)S(1)}, f32[64,640]{1,0:T(8,128)S(1)}, u32[]{:S(2)}, u32[]{:S(2)}) collective-permute-start(f32[64,640]{1,0:T(8,128)S(1)} %get-tuple-element.27), channel_id=1, source_target_pairs={{0,1},{1,0},{2,3},{3,2},{4,5},{5,4},{6,7},{7,6},{8,9},{9,8},{10,11... | collective-permute-start | bytes 491528 | tf_op jit(solution)/shard_map/ppermute | solution.py:226
  19.7 2.2 %collective-permute-start.9 = (f32[64,640]{1,0:T(8,128)S(1)}, f32[64,640]{1,0:T(8,128)S(1)}, u32[]{:S(2)}, u32[]{:S(2)}) collective-permute-start(f32[64,640]{1,0:T(8,128)S(1)} %get-tuple-element.28), channel_id=1, source_target_pairs={{0,2},{1,3},{2,0},{3,1},{4,6},{5,7},{6,4},{7,5},{8,10},{9,11},{10,... | collective-permute-start | bytes 491528 | tf_op jit(solution)/shard_map/ppermute | solution.py:226
  21.8 0.7 %early.1 = (f32[64,640]{1,0:T(8,128)S(1)}, bf16[3,192,640]{2,1,0:T(8,128)(2,1)S(1)}) custom-call(bf16[1728,256]{1,0:T(8,128)(2,1)S(1)} %bitcast.6, bf16[320,640]{1,0:T(8,128)(2,1)S(1)} %get-tuple-element.20.f_ref, bf16[64,640]{1,0:T(8,128)(2,1)S(1)} %bitcast.12, bf16[64,640]{1,0:T(8,128)(2,1)S(1)} %collective-permute-done.even_ref.ce_ref, ...), custom_call_target="tpu_custom_call" | custom-call | tf_op jit(solution)/shard_map/early/pallas_call | solution.py:177
  22.5 5.9 %collective-permute-done.7.refs_0_ = bf16[64,640]{1,0:T(8,128)(2,1)S(1)} collective-permute-done((bf16[64,640]{1,0:T(8,128)(2,1)S(1)}, bf16[64,640]{1,0:T(8,128)(2,1)S(1)}, u32[]{:S(2)}, u32[]{:S(2)}) %collective-permute-start.7) | collective-permute-done | bytes 81952 | tf_op jit(solution)/shard_map/ppermute | solution.py:238
  28.4 2.5 %collective-permute-start.10 = (f32[64,640]{1,0:T(8,128)S(1)}, f32[64,640]{1,0:T(8,128)S(1)}, u32[]{:S(2)}, u32[]{:S(2)}) collective-permute-start(f32[64,640]{1,0:T(8,128)S(1)} %get-tuple-element.29), channel_id=1, source_target_pairs={{0,3},{1,2},{2,1},{3,0},{4,7},{5,6},{6,5},{7,4},{8,11},{9,10},{10,... | collective-permute-start | bytes 491528 | tf_op jit(solution)/shard_map/ppermute | solution.py:226
  30.9 0.0 collective-permute-done.6.fo_ref
  30.9 0.0 collective-permute-done.5.fe_ref
  30.9 3.1 %outputs.1 = (f32[64,1,640]{2,1,0:T(1,128)}, f32[27,64,64]{2,1,0:T(8,128)}, f32[8,128]{1,0:T(8,128)S(1)}) custom-call(s32[2]{0:T(128)S(1)} %pad_add_fusion.pos_ref, bf16[1728,256]{1,0:T(8,128)(2,1)S(1)} %bitcast.7, f32[64,640]{1,0:T(8,128)S(1)} %get-tuple-element.21.own_ref, bf16[3,192,640]{2,1,0:T(8,128)(2,1)S(1)} %get-tuple-element.22.moved_ref, ...), custom_call_target="tpu_custom_call" | custom-call | flops 2264924160 | tf_op jit(solution)/shard_map/outputs/pallas_call | solution.py:177
  34.1 0.0 collective-permute-done.8.refs_1_
  34.1 0.0 collective-permute-done.9.refs_2_
  34.1 1.9 %collective-permute-done.10.refs_3_ = f32[64,640]{1,0:T(8,128)S(1)} collective-permute-done((f32[64,640]{1,0:T(8,128)S(1)}, f32[64,640]{1,0:T(8,128)S(1)}, u32[]{:S(2)}, u32[]{:S(2)}) %collective-permute-start.10) | collective-permute-done | bytes 163872 | tf_op jit(solution)/shard_map/ppermute | solution.py:226
  35.9 0.7 %total.1 = f32[64,1,640]{2,1,0:T(1,128)} custom-call(f32[8,128]{1,0:T(8,128)S(1)} %get-tuple-element.25.token_ref, f32[64,640]{1,0:T(8,128)S(1)} %get-tuple-element.26.refs_0_, f32[64,640]{1,0:T(8,128)S(1)} %collective-permute-done.8.refs_1_, f32[64,640]{1,0:T(8,128)S(1)} %collective-permute-done.9.refs_2_, f32[64,640]{1,0:T(8,128)S(1)} %collective-permute-done.10.refs_3_), custom_call_target="tpu_custom_call" | custom-call | tf_op jit(solution)/shard_map/total/pallas_call | solution.py:177
  (2 shorter events, 0.0 us)
Async XLA Ops:
  0.6 4.3 %copy-start.2 = (bf16[64,1,640]{2,0,1:T(8,128)(2,1)S(1)}, bf16[64,1,640]{2,0,1:T(8,128)(2,1)}, u32[]{:S(2)}) copy-start(bf16[64,1,640]{2,0,1:T(8,128)(2,1)} %param.3) | copy-start | bytes 245764
  0.6 8.7 %copy-start = (bf16[27,64,256]{2,1,0:T(8,128)(2,1)S(1)}, bf16[27,64,256]{2,1,0:T(8,128)(2,1)}, u32[]{:S(2)}) copy-start(bf16[27,64,256]{2,1,0:T(8,128)(2,1)} %param.4) | copy-start | bytes 2654212
  0.7 8.7 %copy-start.1 = (bf16[64,1,640]{2,0,1:T(8,128)(2,1)S(1)}, bf16[64,1,640]{2,0,1:T(8,128)(2,1)}, u32[]{:S(2)}) copy-start(bf16[64,1,640]{2,0,1:T(8,128)(2,1)} %param.5) | copy-start | bytes 245764
  0.7 8.7 %collective-permute-start.1 = (bf16[64,640]{1,0:T(8,128)(2,1)}, bf16[64,640]{1,0:T(8,128)(2,1)S(1)}, u32[]{:S(2)}, u32[]{:S(2)}) collective-permute-start(bf16[64,640]{1,0:T(8,128)(2,1)} %bitcast.8), channel_id=1, source_target_pairs={{0,12},{4,8},{8,4},{12,0},{1,13},{5,9},{9,5},{13,1},{2,14},{6,10},... | collective-permute-start | bytes 245768 | tf_op jit(solution)/shard_map/ppermute | solution.py:213
  3.1 1.8 %collective-permute-start = (bf16[64,640]{1,0:T(8,128)(2,1)}, bf16[64,640]{1,0:T(8,128)(2,1)S(1)}, u32[]{:S(2)}, u32[]{:S(2)}) collective-permute-start(bf16[64,640]{1,0:T(8,128)(2,1)} %bitcast.9), channel_id=1, source_target_pairs={{0,4},{4,0},{8,12},{12,8},{1,5},{5,1},{9,13},{13,9},{2,6},{6,2},{1... | collective-permute-start | bytes 245768 | tf_op jit(solution)/shard_map/ppermute | solution.py:212
  4.9 7.2 %collective-permute-start.4 = (bf16[64,640]{1,0:T(8,128)(2,1)S(1)}, bf16[64,640]{1,0:T(8,128)(2,1)S(1)}, u32[]{:S(2)}, u32[]{:S(2)}) collective-permute-start(bf16[64,640]{1,0:T(8,128)(2,1)S(1)} %bitcast.13), channel_id=1, source_target_pairs={{0,3},{1,2},{2,1},{3,0},{4,7},{5,6},{6,5},{7,4},{8,11},{9,10},{10,... | collective-permute-start | bytes 245768 | tf_op jit(solution)/shard_map/ppermute | solution.py:216
  8.5 7.4 %collective-permute-start.3 = (bf16[64,640]{1,0:T(8,128)(2,1)S(1)}, bf16[64,640]{1,0:T(8,128)(2,1)S(1)}, u32[]{:S(2)}, u32[]{:S(2)}) collective-permute-start(bf16[64,640]{1,0:T(8,128)(2,1)S(1)} %bitcast.14), channel_id=1, source_target_pairs={{0,2},{1,3},{2,0},{3,1},{4,6},{5,7},{6,4},{7,5},{8,10},{9,11},{10,... | collective-permute-start | bytes 245768 | tf_op jit(solution)/shard_map/ppermute | solution.py:216
  8.5 7.4 %collective-permute-start.2 = (bf16[64,640]{1,0:T(8,128)(2,1)S(1)}, bf16[64,640]{1,0:T(8,128)(2,1)S(1)}, u32[]{:S(2)}, u32[]{:S(2)}) collective-permute-start(bf16[64,640]{1,0:T(8,128)(2,1)S(1)} %bitcast.15), channel_id=1, source_target_pairs={{0,1},{1,0},{2,3},{3,2},{4,5},{5,4},{6,7},{7,6},{8,9},{9,8},{10,11... | collective-permute-start | bytes 245768 | tf_op jit(solution)/shard_map/ppermute | solution.py:216
  16.5 14.4 %collective-permute-start.5 = (bf16[320,640]{1,0:T(8,128)(2,1)S(1)}, bf16[320,640]{1,0:T(8,128)(2,1)S(1)}, u32[]{:S(2)}, u32[]{:S(2)}) collective-permute-start(bf16[320,640]{1,0:T(8,128)(2,1)S(1)} %get-tuple-element.20.f_ref), channel_id=1, source_target_pairs={{0,4},{4,0},{8,12},{12,8},{1,5},{5,1},{9,13},{13,9},{2,6},{6,2},{1... | collective-permute-start | bytes 1228808 | tf_op jit(solution)/shard_map/ppermute | solution.py:236
  16.6 14.3 %collective-permute-start.6 = (bf16[256,640]{1,0:T(8,128)(2,1)S(1)}, bf16[256,640]{1,0:T(8,128)(2,1)S(1)}, u32[]{:S(2)}, u32[]{:S(2)}) collective-permute-start(bf16[256,640]{1,0:T(8,128)(2,1)S(1)} %slice.3), channel_id=1, source_target_pairs={{0,12},{4,8},{8,4},{12,0},{1,13},{5,9},{9,5},{13,1},{2,14},{6,10},... | collective-permute-start | bytes 983048 | tf_op jit(solution)/shard_map/ppermute | solution.py:235
  17.3 11.1 %collective-permute-start.7 = (bf16[64,640]{1,0:T(8,128)(2,1)S(1)}, bf16[64,640]{1,0:T(8,128)(2,1)S(1)}, u32[]{:S(2)}, u32[]{:S(2)}) collective-permute-start(bf16[64,640]{1,0:T(8,128)(2,1)S(1)} %get-tuple-element.23), channel_id=1, source_target_pairs={{0,8},{4,12},{8,0},{12,4},{1,9},{5,13},{9,1},{13,5},{2,10},{6,14},... | collective-permute-start | bytes 245768 | tf_op jit(solution)/shard_map/ppermute | solution.py:238
  18.8 15.3 %collective-permute-start.8 = (f32[64,640]{1,0:T(8,128)S(1)}, f32[64,640]{1,0:T(8,128)S(1)}, u32[]{:S(2)}, u32[]{:S(2)}) collective-permute-start(f32[64,640]{1,0:T(8,128)S(1)} %get-tuple-element.27), channel_id=1, source_target_pairs={{0,1},{1,0},{2,3},{3,2},{4,5},{5,4},{6,7},{7,6},{8,9},{9,8},{10,11... | collective-permute-start | bytes 491528 | tf_op jit(solution)/shard_map/ppermute | solution.py:226
  19.7 14.4 %collective-permute-start.9 = (f32[64,640]{1,0:T(8,128)S(1)}, f32[64,640]{1,0:T(8,128)S(1)}, u32[]{:S(2)}, u32[]{:S(2)}) collective-permute-start(f32[64,640]{1,0:T(8,128)S(1)} %get-tuple-element.28), channel_id=1, source_target_pairs={{0,2},{1,3},{2,0},{3,1},{4,6},{5,7},{6,4},{7,5},{8,10},{9,11},{10,... | collective-permute-start | bytes 491528 | tf_op jit(solution)/shard_map/ppermute | solution.py:226
  28.4 7.5 %collective-permute-start.10 = (f32[64,640]{1,0:T(8,128)S(1)}, f32[64,640]{1,0:T(8,128)S(1)}, u32[]{:S(2)}, u32[]{:S(2)}) collective-permute-start(f32[64,640]{1,0:T(8,128)S(1)} %get-tuple-element.29), channel_id=1, source_target_pairs={{0,3},{1,2},{2,1},{3,0},{4,7},{5,6},{6,5},{7,4},{8,11},{9,10},{10,... | collective-permute-start | bytes 491528 | tf_op jit(solution)/shard_map/ppermute | solution.py:226

commit v9 on v8

v9 whole, which is shorter than its diff:
```python
import functools
import math

import jax
import jax.numpy as jnp
from jax import lax
from jax.experimental import pallas as pl
from jax.experimental.pallas import tpu as pltpu
from jax.sharding import PartitionSpec as P

NX = 64
NY = 10
CELLS = NX * NY
F32 = jnp.float32
BF16 = jnp.bfloat16
W_BEGIN, W_GRAD, W_EARLY, W_TOTAL, W_OUT = 8, 1, 4, 0, 0
VMEM_BYTES = 32 * 1024 * 1024


def cell_mask(dy, dx):
    q = lax.broadcasted_iota(jnp.int32, (1, CELLS), 1)
    x = lax.rem(q, NX) + dx
    at = q + NX * dy
    return ((x >= 0) & (x < NX) & (at >= 0) & (at < CELLS)).astype(F32)


def shifted(value, dy, dx):
    if dy == 0 and dx == 0:
        return value
    return pltpu.roll(value, (-(dy * NX + dx)) % CELLS, 1) * cell_mask(dy, dx)


def odd_partner(s, nz):
    return lax.rem(((s + 1) ^ 1) + nz - 1, nz)


def gather_kernel(nz, nc, pos_ref, token_ref, cot_ref, near_ref, *refs):
    pieces, (f_ref, even_ref, odd_ref), packs = refs[:nc], refs[nc : nc + 3], refs[nc + 3 :]
    blocks = cot_ref.shape[0]
    cols = f_ref.shape[0] // nz
    s, c = pos_ref[0], pos_ref[1]

    def block_for(goal):
        return f_ref[pl.ds(pl.multiple_of(goal * cols, cols), cols), :]

    for k in range(nc):
        f_ref[pl.ds(pl.multiple_of((c ^ k) * blocks, blocks), blocks), :] = pieces[k][...]
    even_ref[:cols, :] = block_for(s ^ 1)
    even_ref[cols:, :] = near_ref[...]
    odd_ref[...] = block_for(odd_partner(s, nz))
    for k, pack in zip(range(2, nz - 1), packs):
        pack[:cols, :] = block_for(lax.rem(s + k, nz))
        if nz > 4:
            pack[cols:, :] = cot_ref[...]


def columns(cols_ref, first, plane):
    blocks = plane.shape[0]
    for dy in (-1, 0, 1):
        for dx in (-1, 0, 1):
            tap = first + 3 * (dy + 1) + dx + 1
            cols_ref[tap * blocks : (tap + 1) * blocks, :] = shifted(plane, -dy, -dx).astype(BF16)


def token_kernel(token_ref):
    token_ref[...] = jnp.zeros(token_ref.shape, F32)


def input_grad_kernel(nz, nc, pos_ref, begin_ref, cot_ref, even_ref, odd_ref, w_ref, *refs):
    parts = refs[:nc]
    token_ref, cols_ref, sum_ref = refs[nc:]
    blocks = even_ref.shape[0]
    s, c = pos_ref[0], pos_ref[1]
    token_ref[...] = jnp.zeros(token_ref.shape, F32)
    even, odd = even_ref[...].astype(F32), odd_ref[...].astype(F32)
    first = s % 2 == 0
    columns(cols_ref, 0, jnp.where(s < nz - 1, jnp.where(first, even, odd), 0.0))
    columns(cols_ref, 9, cot_ref[...].astype(F32))
    columns(cols_ref, 18, jnp.where(s > 0, jnp.where(first, odd, even), 0.0))
    sum_ref[...] = lax.dot_general(
        w_ref[...], cols_ref[...], (((0,), (0,)), ((), ())), preferred_element_type=F32
    )
    for k in range(nc):
        parts[k][...] = sum_ref[pl.ds(pl.multiple_of((c ^ k) * blocks, blocks), blocks), :]


def conv_part(w_ref, field, dz):
    taps = w_ref.shape[0] // 3
    rows = pl.ds(pl.multiple_of((dz + 1) * taps, taps), taps)
    return jnp.dot(w_ref[rows, :], field, preferred_element_type=F32)


def moved_sum(acc):
    blocks = acc.shape[0] // 9
    total = None
    for dx in (-1, 0, 1):
        for dy in (-1, 0, 1):
            at = (3 * (dy + 1) + dx + 1) * blocks
            term = shifted(acc[at : at + blocks], dy, dx)
            total = term if total is None else total + term
    return total


def moved_rows(plane):
    plane = plane.astype(F32)
    return jnp.concatenate([shifted(plane, -dy, 0).astype(BF16) for dy in (-1, 0, 1)], 0)


def early_kernel(pos_ref, w_ref, f_ref, cot_ref, ce_ref, co_ref, own_ref, even_ref, odd_ref, moved_ref):
    side = 1 - 2 * lax.rem(pos_ref[0], 2)
    for ref, dz in ((odd_ref, side), (even_ref, -side), (own_ref, 0)):
        ref[...] = moved_sum(conv_part(w_ref, f_ref[...], dz))
    for i, ref in enumerate((cot_ref, ce_ref, co_ref)):
        moved_ref[i] = moved_rows(ref[...])


def weight_grad_kernel(nz, scale, pos_ref, moved_ref, f_ref, ge_ref, go_ref, *refs):
    packs = refs[:-4]
    wg_ref, token_ref, c_ref, g_ref = refs[-4:]
    token_ref[...] = jnp.zeros(token_ref.shape, F32)
    blocks = c_ref.shape[1] // 3
    cols = go_ref.shape[0]
    s = pos_ref[0]

    empty = jnp.zeros(c_ref.shape[1:], BF16)
    c_ref[0] = empty
    c_ref[nz + 1] = empty
    mine = pl.ds(pl.multiple_of(s * cols, cols), cols)
    sources = (s, s ^ 1, odd_partner(s, nz))
    for i, (source, field) in enumerate(zip(sources, (f_ref[mine, :], ge_ref[:cols, :], go_ref[...]))):
        c_ref[source + 1] = moved_ref[i]
        g_ref[source] = field
    for k, pack in zip(range(2, nz - 1), packs):
        source = lax.rem(s + nz - k, nz)
        g_ref[source] = pack[:cols, :]
        c_ref[source + 1] = moved_rows(pack[cols:, :] if nz > 4 else ge_ref[cols:, :])

    sums = None
    for z in range(nz):
        field = g_ref[z].astype(F32)
        fields = jnp.concatenate([shifted(field, 0, dx).astype(BF16) for dx in (-1, 0, 1)], 0)
        term = lax.dot_general(
            c_ref[z : z + 3].reshape(9 * blocks, CELLS),
            fields,
            (((1,), (1,)), ((), ())),
            preferred_element_type=F32,
        )
        sums = term if sums is None else sums + term
    sums = sums * scale
    for tap in range(27):
        dz, dy, dx = tap // 9, tap // 3 % 3, tap % 3
        at = ((2 - dz) * 3 + dy) * blocks
        wg_ref[tap] = sums[at : at + blocks, dx * cols : (dx + 1) * cols]


def total_kernel(nz, pos_ref, token_ref, *refs):
    terms, (own_ref, even_ref, odd_ref, out_ref, back_ref) = refs[:-5], refs[-5:]
    s = pos_ref[0]
    inner = ((s > 0) & (s < nz - 1)).astype(F32)
    out_ref[:, 0, :] = own_ref[...] + even_ref[...] + inner * odd_ref[...]
    total = terms[0][...]
    for term in terms[1:]:
        total = total + term[...]
    back_ref[:, 0, :] = total


VMEM = pl.BlockSpec(memory_space=pltpu.VMEM)
SMEM = pl.BlockSpec(memory_space=pltpu.SMEM)


def kernel_call(body, name, outs, args, scratch=(), weight=0):
    return pl.pallas_call(
        body,
        out_shape=outs,
        in_specs=[SMEM if a.dtype == jnp.int32 else VMEM for a in args],
        out_specs=tuple(VMEM for _ in outs),
        scratch_shapes=list(scratch),
        compiler_params=pltpu.CompilerParams(vmem_limit_bytes=VMEM_BYTES),
        cost_estimate=pl.CostEstimate(flops=int(weight), bytes_accessed=0, transcendentals=0),
        name=name,
    )(*args)


def per_device(features, weights, cotangent):
    blocks, depth, plane = features.shape
    channels = weights.shape[2]
    nz = lax.axis_size("sp")
    nc = lax.axis_size("ch")
    cols = channels // nz
    w2 = weights.reshape(27 * blocks, channels)
    feat = features.reshape(blocks, plane)
    cot = cotangent.reshape(blocks, plane)
    pos = jnp.stack([lax.axis_index("sp"), lax.axis_index("ch")]).astype(jnp.int32)

    even_pairs = [(i, i ^ 1) for i in range(nz)]
    odd_pairs = [(i, (((i + 1) ^ 1) - 1) % nz) for i in range(nz)]

    def mixed(k):
        return [(i, i ^ k) for i in range(nc)]

    def of(rows, dtype):
        return jax.ShapeDtypeStruct((rows, plane), dtype)

    small = jax.ShapeDtypeStruct((8, 128), F32)
    work = 2 * 27 * blocks * channels * plane

    cot_even = lax.ppermute(cot, "sp", even_pairs)
    cot_odd = lax.ppermute(cot, "sp", odd_pairs)
    (begin,) = kernel_call(token_kernel, "begin", [small], [], weight=W_BEGIN * work)
    feat, cot_even = lax.optimization_barrier((feat, cot_even))
    pieces = [feat] + [lax.ppermute(feat, "ch", mixed(k)) for k in range(1, nc)]

    *parts, token = kernel_call(
        functools.partial(input_grad_kernel, nz, nc),
        "input_grad",
        [of(blocks, F32)] * nc + [small],
        [pos, begin, cot, cot_even, cot_odd, w2],
        [pltpu.VMEM((27 * blocks, plane), BF16), pltpu.VMEM((channels, plane), F32)],
        W_GRAD * work,
    )
    terms = [parts[0]] + [lax.ppermute(parts[k], "ch", mixed(k)) for k in (*range(2, nc), 1)]

    far_rows = cols if nz == 4 else cols + blocks
    f_all, to_even, to_odd, *packs = kernel_call(
        functools.partial(gather_kernel, nz, nc),
        "gather",
        [of(channels, BF16), of(cols + blocks, BF16), of(cols, BF16)]
        + [of(far_rows, BF16)] * (nz - 3),
        [pos, token, cot, cot_odd] + pieces,
    )
    g_odd = lax.ppermute(to_odd, "sp", odd_pairs)
    far = [
        lax.ppermute(packs[k - 2], "sp", [(i, (i + k) % nz) for i in range(nz)])
        for k in range(2, nz - 1)
    ]
    g_even = lax.ppermute(to_even, "sp", even_pairs)
    out_own, out_even, out_odd, moved = kernel_call(
        early_kernel,
        "early",
        [of(blocks, F32)] * 3 + [jax.ShapeDtypeStruct((3, 3 * blocks, plane), BF16)],
        [pos, w2, f_all, cot, cot_even, cot_odd],
        weight=W_EARLY * work,
    )
    out_odd = lax.ppermute(out_odd, "sp", odd_pairs)
    out_even = lax.ppermute(out_even, "sp", even_pairs)

    weight_grad, last = kernel_call(
        functools.partial(weight_grad_kernel, nz, 1.0 / math.sqrt(nz * depth * plane)),
        "weight_grad",
        [jax.ShapeDtypeStruct((27, blocks, cols), F32), small],
        [pos, moved, f_all, g_even, g_odd, *far],
        [pltpu.VMEM((nz + 2, 3 * blocks, plane), BF16), pltpu.VMEM((nz, cols, plane), BF16)],
        W_OUT * work,
    )
    block = jax.ShapeDtypeStruct((blocks, 1, plane), F32)
    output, back = kernel_call(
        functools.partial(total_kernel, nz),
        "total",
        [block, block],
        [pos, last, *terms, out_own, out_even, out_odd],
        weight=W_TOTAL * work,
    )
    return (output, back, weight_grad)


def solution(mesh):
    return jax.shard_map(
        per_device,
        mesh=mesh,
        in_specs=(P("ch", ("grp", "sp"), None), P(None, "ch", None), P("ch", ("grp", "sp"), None)),
        out_specs=(
            P("ch", ("grp", "sp"), None),
            P("ch", ("grp", "sp"), None),
            P("grp", "ch", "sp"),
        ),
        check_vma=False,
    )
```

time: 36.8 us -> 37.2 us (1.011)
  Pallas kernels: 6.93 us -> 8.56 us
  waiting for transfers between devices: 13.6 us -> 12.7 us
    ppermute x1, waiting for transfers between devices: 5.93 us -> 1.21 us  [per_device(): lax.ppermute(packs[k - 2], 'sp', [(i, (i + k) % nz) for i in range(nz)])]
    ppermute x3, waiting for transfers between devices: 4.69 us -> 8.52 us  [per_device(): pieces = [feat] + [lax.ppermute(feat, 'ch', mixed(k)) for k in range(1, nc)]]
    ppermute x2 -> x4, starting transfers between devices: 0.77 us -> 3.12 us  [the longest x1 1.69 us: per_device(): out_odd = lax.ppermute(out_odd, 'sp', odd_pairs)]
    ppermute x3, waiting for transfers between devices: 1.88 us -> 0.06 us  [per_device(): lax.ppermute(parts[k], 'ch', mixed(k))]
    ppermute x3, starting transfers between devices: 5.51 us -> 3.75 us  [per_device(): lax.ppermute(parts[k], 'ch', mixed(k))]
    ppermute x2 -> x4, waiting for transfers between devices: 0.01 us -> 1.75 us  [the longest x1 1.47 us: per_device(): out_odd = lax.ppermute(out_odd, 'sp', odd_pairs)]
    pallas_call x6, Pallas kernels: 6.93 us -> 8.56 us  [kernel_call(): pl.pallas_call(body, out_shape=outs, in_specs=[SMEM if a.dtype == jnp.int...]
    ppermute x1, starting transfers between devices: 1.49 us -> 0.6 us  [per_device(): lax.ppermute(packs[k - 2], 'sp', [(i, (i + k) % nz) for i in range(nz)])]
  transfers between devices with their start and end apart: 11 -> 13, of which waited for: 5 -> 6; matrix products, arithmetic and copies ran while one was open for 0% -> 0% of each run, Pallas kernels for 15% -> 20%
where the time goes in v9:
time: 37.2 us; the launch traced here: 37 us
  starting transfers between devices  15 us (40%)
  waiting for transfers between devices  12.7 us (34%)
  Pallas kernels  8.56 us (23%)
  between operations  0.7 us (2%)
    pallas_call x6, Pallas kernels, kernel_call(): pl.pallas_call(body, out_shape=outs, in_specs=[SMEM if a.dtype == jnp.int...  8.56 us
    ppermute x3, waiting for transfers between devices, per_device(): pieces = [feat] + [lax.ppermute(feat, 'ch', mixed(k)) for k in range(1, nc)]  8.52 us
    ppermute x3, starting transfers between devices, per_device(): pieces = [feat] + [lax.ppermute(feat, 'ch', mixed(k)) for k in range(1, nc)]  4.39 us
    ppermute x3, starting transfers between devices, per_device(): lax.ppermute(parts[k], 'ch', mixed(k))  3.75 us
    ppermute x1, starting transfers between devices, per_device(): cot_odd = lax.ppermute(cot, 'sp', odd_pairs)  2.44 us
    ppermute x1, starting transfers between devices, per_device(): out_odd = lax.ppermute(out_odd, 'sp', odd_pairs)  1.69 us
    ppermute x1, waiting for transfers between devices, per_device(): out_odd = lax.ppermute(out_odd, 'sp', odd_pairs)  1.47 us
    ppermute x1, starting transfers between devices, per_device(): g_even = lax.ppermute(to_even, 'sp', even_pairs)  1.25 us
  transfers between devices with their start and end apart: 13, of which 6 were waited for; matrix products, arithmetic and copies ran while one was open for 0% of the time, Pallas kernels for 20%

profile of v9, /device:TPU:0, one launch (start us, length us, event | category | flops | bytes accessed | tf_op | source)
XLA Modules:
  0.0 37.0 jit_solution(6386189350055737047)
XLA Ops:
  0.6 0.0 copy-start
  0.6 0.0 copy-start.1
  0.7 0.0 copy-start.2
  0.7 2.4 %collective-permute-start.1 = (bf16[64,640]{1,0:T(8,128)(2,1)}, bf16[64,640]{1,0:T(8,128)(2,1)S(1)}, u32[]{:S(2)}, u32[]{:S(2)}) collective-permute-start(bf16[64,640]{1,0:T(8,128)(2,1)} %bitcast.9), channel_id=1, source_target_pairs={{0,12},{4,8},{8,4},{12,0},{1,13},{5,9},{9,5},{13,1},{2,14},{6,10},... | collective-permute-start | bytes 245768 | tf_op jit(solution)/shard_map/ppermute | solution.py:208
  3.1 0.7 %collective-permute-start = (bf16[64,640]{1,0:T(8,128)(2,1)}, bf16[64,640]{1,0:T(8,128)(2,1)S(1)}, u32[]{:S(2)}, u32[]{:S(2)}) collective-permute-start(bf16[64,640]{1,0:T(8,128)(2,1)} %bitcast.10), channel_id=1, source_target_pairs={{0,4},{4,0},{8,12},{12,8},{1,5},{5,1},{9,13},{13,9},{2,6},{6,2},{1... | collective-permute-start | bytes 245768 | tf_op jit(solution)/shard_map/ppermute | solution.py:207
  3.8 1.1 %collective-permute-done.even_ref.ce_ref = bf16[64,640]{1,0:T(8,128)(2,1)S(1)} collective-permute-done((bf16[64,640]{1,0:T(8,128)(2,1)}, bf16[64,640]{1,0:T(8,128)(2,1)S(1)}, u32[]{:S(2)}, u32[]{:S(2)}) %collective-permute-start) | collective-permute-done | bytes 81952 | tf_op jit(solution)/shard_map/ppermute | solution.py:207
  4.9 0.0 copy-done
  4.9 3.6 %collective-permute-start.4 = (bf16[64,640]{1,0:T(8,128)(2,1)S(1)}, bf16[64,640]{1,0:T(8,128)(2,1)S(1)}, u32[]{:S(2)}, u32[]{:S(2)}) collective-permute-start(bf16[64,640]{1,0:T(8,128)(2,1)S(1)} %bitcast.5), channel_id=1, source_target_pairs={{0,3},{1,2},{2,1},{3,0},{4,7},{5,6},{6,5},{7,4},{8,11},{9,10},{10,... | collective-permute-start | bytes 245768 | tf_op jit(solution)/shard_map/ppermute | solution.py:211
  8.5 0.0 collective-permute-start.3
  8.5 0.8 %collective-permute-start.2 = (bf16[64,640]{1,0:T(8,128)(2,1)S(1)}, bf16[64,640]{1,0:T(8,128)(2,1)S(1)}, u32[]{:S(2)}, u32[]{:S(2)}) collective-permute-start(bf16[64,640]{1,0:T(8,128)(2,1)S(1)} %bitcast.7), channel_id=1, source_target_pairs={{0,1},{1,0},{2,3},{3,2},{4,5},{5,4},{6,7},{7,6},{8,9},{9,8},{10,11... | collective-permute-start | bytes 245768 | tf_op jit(solution)/shard_map/ppermute | solution.py:211
  9.3 0.1 pad_add_fusion.pos_ref
  9.4 0.0 collective-permute-done.1.odd_ref.near_ref.co_ref
  9.4 0.0 copy-done.1
  9.4 0.0 copy-done.2
  9.4 1.8 %input_grad.1 = (f32[64,640]{1,0:T(8,128)S(1)}, f32[64,640]{1,0:T(8,128)S(1)}, f32[64,640]{1,0:T(8,128)S(1)}, f32[64,640]{1,0:T(8,128)S(1)}, f32[8,128]{1,0:T(8,128)S(1)}) custom-call(s32[2]{0:T(128)S(1)} %pad_add_fusion.pos_ref, f32[8,128]{1,0:T(8,128)S(1)} %begin.1.begin_ref, bf16[64,640]{1,0:T(8,128)(2,1)S(1)} %bitcast.11, ...), custom_call_target="tpu_custom_call" | custom-call | flops 566231040 | tf_op jit(solution)/shard_map/input_grad/pallas_call | solution.py:172
  11.2 2.2 %collective-permute-start.8 = (f32[64,640]{1,0:T(8,128)S(1)}, f32[64,640]{1,0:T(8,128)S(1)}, u32[]{:S(2)}, u32[]{:S(2)}) collective-permute-start(f32[64,640]{1,0:T(8,128)S(1)} %get-tuple-element.32), channel_id=1, source_target_pairs={{0,2},{1,3},{2,0},{3,1},{4,6},{5,7},{6,4},{7,5},{8,10},{9,11},{10,... | collective-permute-start | bytes 491528 | tf_op jit(solution)/shard_map/ppermute | solution.py:221
  13.4 1.5 %collective-permute-start.9 = (f32[64,640]{1,0:T(8,128)S(1)}, f32[64,640]{1,0:T(8,128)S(1)}, u32[]{:S(2)}, u32[]{:S(2)}) collective-permute-start(f32[64,640]{1,0:T(8,128)S(1)} %get-tuple-element.33), channel_id=1, source_target_pairs={{0,3},{1,2},{2,1},{3,0},{4,7},{5,6},{6,5},{7,4},{8,11},{9,10},{10,... | collective-permute-start | bytes 491528 | tf_op jit(solution)/shard_map/ppermute | solution.py:221
  15.0 0.0 collective-permute-done.4.refs_3_
  15.0 8.5 %collective-permute-done.3.refs_2_ = bf16[64,640]{1,0:T(8,128)(2,1)S(1)} collective-permute-done((bf16[64,640]{1,0:T(8,128)(2,1)S(1)}, bf16[64,640]{1,0:T(8,128)(2,1)S(1)}, u32[]{:S(2)}, u32[]{:S(2)}) %collective-permute-start.3) | collective-permute-done | bytes 81952 | tf_op jit(solution)/shard_map/ppermute | solution.py:211
  23.5 0.0 collective-permute-done.2.refs_1_
  23.5 0.6 %gather.1 = (bf16[256,640]{1,0:T(8,128)(2,1)S(1)}, bf16[128,640]{1,0:T(8,128)(2,1)S(1)}, bf16[64,640]{1,0:T(8,128)(2,1)S(1)}, bf16[64,640]{1,0:T(8,128)(2,1)S(1)}) custom-call(s32[2]{0:T(128)S(1)} %pad_add_fusion.pos_ref, f32[8,128]{1,0:T(8,128)S(1)} %get-tuple-element.23.token_ref, bf16[64,640]{1,0:T(8,128)(2,1)S(1)} %bitcast.12, ...), custom_call_target="tpu_custom_call" | custom-call | tf_op jit(solution)/shard_map/gather/pallas_call | solution.py:172
  24.1 0.1 collective-permute-start.6
  24.2 0.6 %collective-permute-start.7 = (bf16[64,640]{1,0:T(8,128)(2,1)S(1)}, bf16[64,640]{1,0:T(8,128)(2,1)S(1)}, u32[]{:S(2)}, u32[]{:S(2)}) collective-permute-start(bf16[64,640]{1,0:T(8,128)(2,1)S(1)} %get-tuple-element.29), channel_id=1, source_target_pairs={{0,8},{4,12},{8,0},{12,4},{1,9},{5,13},{9,1},{13,5},{2,10},{6,14},... | collective-permute-start | bytes 245768 | tf_op jit(solution)/shard_map/ppermute | solution.py:233
  24.8 1.2 %collective-permute-start.5 = (bf16[128,640]{1,0:T(8,128)(2,1)S(1)}, bf16[128,640]{1,0:T(8,128)(2,1)S(1)}, u32[]{:S(2)}, u32[]{:S(2)}) collective-permute-start(bf16[128,640]{1,0:T(8,128)(2,1)S(1)} %get-tuple-element.27), channel_id=1, source_target_pairs={{0,4},{4,0},{8,12},{12,8},{1,5},{5,1},{9,13},{13,9},{2,6},{6,2},{1... | collective-permute-start | bytes 491528 | tf_op jit(solution)/shard_map/ppermute | solution.py:236
  26.0 2.0 %early.1 = (f32[64,640]{1,0:T(8,128)S(1)}, f32[64,640]{1,0:T(8,128)S(1)}, f32[64,640]{1,0:T(8,128)S(1)}, bf16[3,192,640]{2,1,0:T(8,128)(2,1)S(1)}) custom-call(s32[2]{0:T(128)S(1)} %pad_add_fusion.pos_ref, bf16[1728,256]{1,0:T(8,128)(2,1)S(1)} %bitcast.15, bf16[256,640]{1,0:T(8,128)(2,1)S(1)} %get-tuple-element.25.f_ref, bf16[64,640]{1,0:T(8,128)(2,1)S(1)} %bitcast.13, ...), custom_call_target="tpu_custom_call" | custom-call | flops 2264924160 | tf_op jit(solution)/shard_map/early/pallas_call | solution.py:172
  28.0 0.3 collective-permute-done.6.go_ref
  28.3 0.0 collective-permute-start.10
  28.3 1.2 %collective-permute-done.7.refs_0_ = bf16[64,640]{1,0:T(8,128)(2,1)S(1)} collective-permute-done((bf16[64,640]{1,0:T(8,128)(2,1)S(1)}, bf16[64,640]{1,0:T(8,128)(2,1)S(1)}, u32[]{:S(2)}, u32[]{:S(2)}) %collective-permute-start.7) | collective-permute-done | bytes 81952 | tf_op jit(solution)/shard_map/ppermute | solution.py:233
  29.5 0.1 collective-permute-start.11
  29.6 0.0 collective-permute-done.5.ge_ref
  29.6 1.7 %collective-permute-start.12 = (f32[64,640]{1,0:T(8,128)S(1)}, f32[64,640]{1,0:T(8,128)S(1)}, u32[]{:S(2)}, u32[]{:S(2)}) collective-permute-start(f32[64,640]{1,0:T(8,128)S(1)} %get-tuple-element.37), channel_id=1, source_target_pairs={{0,12},{4,8},{8,4},{12,0},{1,13},{5,9},{9,5},{13,1},{2,14},{6,10},... | collective-permute-start | bytes 491528 | tf_op jit(solution)/shard_map/ppermute | solution.py:244
  31.3 2.8 %weight_grad.1 = (f32[27,64,64]{2,1,0:T(8,128)}, f32[8,128]{1,0:T(8,128)S(1)}) custom-call(s32[2]{0:T(128)S(1)} %pad_add_fusion.pos_ref, bf16[3,192,640]{2,1,0:T(8,128)(2,1)S(1)} %get-tuple-element.26.moved_ref, bf16[256,640]{1,0:T(8,128)(2,1)S(1)} %get-tuple-element.25.f_ref, bf16[128,640]{1,0:T(8,128)(2,1)S(1)} %collective-permute-done.5.ge_ref, ...), custom_call_target="tpu_custom_call" | custom-call | tf_op jit(solution)/shard_map/weight_grad/pallas_call | solution.py:172
  34.1 0.0 collective-permute-done.8.refs_1_
  34.1 0.0 collective-permute-done.9.refs_2_
  34.2 0.1 collective-permute-done.10.refs_3_
  34.2 0.0 collective-permute-done.11.refs_5_
  34.2 1.5 %collective-permute-done.12.refs_6_ = f32[64,640]{1,0:T(8,128)S(1)} collective-permute-done((f32[64,640]{1,0:T(8,128)S(1)}, f32[64,640]{1,0:T(8,128)S(1)}, u32[]{:S(2)}, u32[]{:S(2)}) %collective-permute-start.12) | collective-permute-done | bytes 163872 | tf_op jit(solution)/shard_map/ppermute | solution.py:244
  35.7 1.3 %total.1 = (f32[64,1,640]{2,1,0:T(1,128)}, f32[64,1,640]{2,1,0:T(1,128)}) custom-call(s32[2]{0:T(128)S(1)} %pad_add_fusion.pos_ref, f32[8,128]{1,0:T(8,128)S(1)} %get-tuple-element.30.token_ref, f32[64,640]{1,0:T(8,128)S(1)} %get-tuple-element.31.refs_0_, f32[64,640]{1,0:T(8,128)S(1)} %collective-permute-done.8.refs_1_, ...), custom_call_target="tpu_custom_call" | custom-call | tf_op jit(solution)/shard_map/total/pallas_call | solution.py:172
  (1 shorter events, 0.0 us)
Async XLA Ops:
  0.6 4.3 %copy-start = (bf16[64,1,640]{2,0,1:T(8,128)(2,1)S(1)}, bf16[64,1,640]{2,0,1:T(8,128)(2,1)}, u32[]{:S(2)}) copy-start(bf16[64,1,640]{2,0,1:T(8,128)(2,1)} %param.3) | copy-start | bytes 245764
  0.6 8.7 %copy-start.1 = (bf16[64,1,640]{2,0,1:T(8,128)(2,1)S(1)}, bf16[64,1,640]{2,0,1:T(8,128)(2,1)}, u32[]{:S(2)}) copy-start(bf16[64,1,640]{2,0,1:T(8,128)(2,1)} %param.5) | copy-start | bytes 245764
  0.7 8.7 %copy-start.2 = (bf16[27,64,256]{2,1,0:T(8,128)(2,1)S(1)}, bf16[27,64,256]{2,1,0:T(8,128)(2,1)}, u32[]{:S(2)}) copy-start(bf16[27,64,256]{2,1,0:T(8,128)(2,1)} %param.4) | copy-start | bytes 2654212
  0.7 8.7 %collective-permute-start.1 = (bf16[64,640]{1,0:T(8,128)(2,1)}, bf16[64,640]{1,0:T(8,128)(2,1)S(1)}, u32[]{:S(2)}, u32[]{:S(2)}) collective-permute-start(bf16[64,640]{1,0:T(8,128)(2,1)} %bitcast.9), channel_id=1, source_target_pairs={{0,12},{4,8},{8,4},{12,0},{1,13},{5,9},{9,5},{13,1},{2,14},{6,10},... | collective-permute-start | bytes 245768 | tf_op jit(solution)/shard_map/ppermute | solution.py:208
  3.1 1.8 %collective-permute-start = (bf16[64,640]{1,0:T(8,128)(2,1)}, bf16[64,640]{1,0:T(8,128)(2,1)S(1)}, u32[]{:S(2)}, u32[]{:S(2)}) collective-permute-start(bf16[64,640]{1,0:T(8,128)(2,1)} %bitcast.10), channel_id=1, source_target_pairs={{0,4},{4,0},{8,12},{12,8},{1,5},{5,1},{9,13},{13,9},{2,6},{6,2},{1... | collective-permute-start | bytes 245768 | tf_op jit(solution)/shard_map/ppermute | solution.py:207
  4.9 10.0 %collective-permute-start.4 = (bf16[64,640]{1,0:T(8,128)(2,1)S(1)}, bf16[64,640]{1,0:T(8,128)(2,1)S(1)}, u32[]{:S(2)}, u32[]{:S(2)}) collective-permute-start(bf16[64,640]{1,0:T(8,128)(2,1)S(1)} %bitcast.5), channel_id=1, source_target_pairs={{0,3},{1,2},{2,1},{3,0},{4,7},{5,6},{6,5},{7,4},{8,11},{9,10},{10,... | collective-permute-start | bytes 245768 | tf_op jit(solution)/shard_map/ppermute | solution.py:211
  8.5 15.0 %collective-permute-start.3 = (bf16[64,640]{1,0:T(8,128)(2,1)S(1)}, bf16[64,640]{1,0:T(8,128)(2,1)S(1)}, u32[]{:S(2)}, u32[]{:S(2)}) collective-permute-start(bf16[64,640]{1,0:T(8,128)(2,1)S(1)} %bitcast.6), channel_id=1, source_target_pairs={{0,2},{1,3},{2,0},{3,1},{4,6},{5,7},{6,4},{7,5},{8,10},{9,11},{10,... | collective-permute-start | bytes 245768 | tf_op jit(solution)/shard_map/ppermute | solution.py:211
  8.5 15.0 %collective-permute-start.2 = (bf16[64,640]{1,0:T(8,128)(2,1)S(1)}, bf16[64,640]{1,0:T(8,128)(2,1)S(1)}, u32[]{:S(2)}, u32[]{:S(2)}) collective-permute-start(bf16[64,640]{1,0:T(8,128)(2,1)S(1)} %bitcast.7), channel_id=1, source_target_pairs={{0,1},{1,0},{2,3},{3,2},{4,5},{5,4},{6,7},{7,6},{8,9},{9,8},{10,11... | collective-permute-start | bytes 245768 | tf_op jit(solution)/shard_map/ppermute | solution.py:211
  11.2 22.9 %collective-permute-start.8 = (f32[64,640]{1,0:T(8,128)S(1)}, f32[64,640]{1,0:T(8,128)S(1)}, u32[]{:S(2)}, u32[]{:S(2)}) collective-permute-start(f32[64,640]{1,0:T(8,128)S(1)} %get-tuple-element.32), channel_id=1, source_target_pairs={{0,2},{1,3},{2,0},{3,1},{4,6},{5,7},{6,4},{7,5},{8,10},{9,11},{10,... | collective-permute-start | bytes 491528 | tf_op jit(solution)/shard_map/ppermute | solution.py:221
  13.4 20.7 %collective-permute-start.9 = (f32[64,640]{1,0:T(8,128)S(1)}, f32[64,640]{1,0:T(8,128)S(1)}, u32[]{:S(2)}, u32[]{:S(2)}) collective-permute-start(f32[64,640]{1,0:T(8,128)S(1)} %get-tuple-element.33), channel_id=1, source_target_pairs={{0,3},{1,2},{2,1},{3,0},{4,7},{5,6},{6,5},{7,4},{8,11},{9,10},{10,... | collective-permute-start | bytes 491528 | tf_op jit(solution)/shard_map/ppermute | solution.py:221
  24.1 4.2 %collective-permute-start.6 = (bf16[64,640]{1,0:T(8,128)(2,1)S(1)}, bf16[64,640]{1,0:T(8,128)(2,1)S(1)}, u32[]{:S(2)}, u32[]{:S(2)}) collective-permute-start(bf16[64,640]{1,0:T(8,128)(2,1)S(1)} %get-tuple-element.28), channel_id=1, source_target_pairs={{0,12},{4,8},{8,4},{12,0},{1,13},{5,9},{9,5},{13,1},{2,14},{6,10},... | collective-permute-start | bytes 245768 | tf_op jit(solution)/shard_map/ppermute | solution.py:231
  24.2 5.3 %collective-permute-start.7 = (bf16[64,640]{1,0:T(8,128)(2,1)S(1)}, bf16[64,640]{1,0:T(8,128)(2,1)S(1)}, u32[]{:S(2)}, u32[]{:S(2)}) collective-permute-start(bf16[64,640]{1,0:T(8,128)(2,1)S(1)} %get-tuple-element.29), channel_id=1, source_target_pairs={{0,8},{4,12},{8,0},{12,4},{1,9},{5,13},{9,1},{13,5},{2,10},{6,14},... | collective-permute-start | bytes 245768 | tf_op jit(solution)/shard_map/ppermute | solution.py:233
  24.8 4.9 %collective-permute-start.5 = (bf16[128,640]{1,0:T(8,128)(2,1)S(1)}, bf16[128,640]{1,0:T(8,128)(2,1)S(1)}, u32[]{:S(2)}, u32[]{:S(2)}) collective-permute-start(bf16[128,640]{1,0:T(8,128)(2,1)S(1)} %get-tuple-element.27), channel_id=1, source_target_pairs={{0,4},{4,0},{8,12},{12,8},{1,5},{5,1},{9,13},{13,9},{2,6},{6,2},{1... | collective-permute-start | bytes 491528 | tf_op jit(solution)/shard_map/ppermute | solution.py:236
  28.3 5.9 %collective-permute-start.10 = (f32[64,640]{1,0:T(8,128)S(1)}, f32[64,640]{1,0:T(8,128)S(1)}, u32[]{:S(2)}, u32[]{:S(2)}) collective-permute-start(f32[64,640]{1,0:T(8,128)S(1)} %get-tuple-element.34), channel_id=1, source_target_pairs={{0,1},{1,0},{2,3},{3,2},{4,5},{5,4},{6,7},{7,6},{8,9},{9,8},{10,11... | collective-permute-start | bytes 491528 | tf_op jit(solution)/shard_map/ppermute | solution.py:221
  29.5 4.7 %collective-permute-start.11 = (f32[64,640]{1,0:T(8,128)S(1)}, f32[64,640]{1,0:T(8,128)S(1)}, u32[]{:S(2)}, u32[]{:S(2)}) collective-permute-start(f32[64,640]{1,0:T(8,128)S(1)} %get-tuple-element.36), channel_id=1, source_target_pairs={{0,4},{4,0},{8,12},{12,8},{1,5},{5,1},{9,13},{13,9},{2,6},{6,2},{1... | collective-permute-start | bytes 491528 | tf_op jit(solution)/shard_map/ppermute | solution.py:245
  29.6 6.1 %collective-permute-start.12 = (f32[64,640]{1,0:T(8,128)S(1)}, f32[64,640]{1,0:T(8,128)S(1)}, u32[]{:S(2)}, u32[]{:S(2)}) collective-permute-start(f32[64,640]{1,0:T(8,128)S(1)} %get-tuple-element.37), channel_id=1, source_target_pairs={{0,12},{4,8},{8,4},{12,0},{1,13},{5,9},{9,5},{13,1},{2,14},{6,10},... | collective-permute-start | bytes 491528 | tf_op jit(solution)/shard_map/ppermute | solution.py:244

commit v10 on v7

--- a/solution.py
+++ b/solution.py
@@ -17,18 +17,17 @@
 VMEM_BYTES = 32 * 1024 * 1024
 
 
-def cell_mask(rows, dy, dx):
-    q = lax.broadcasted_iota(jnp.int32, (rows, CELLS), 1)
-    x = q % NX + dx
-    y = q // NX + dy
-    return (x >= 0) & (x < NX) & (y >= 0) & (y < NY)
+def cell_mask(dy, dx):
+    q = lax.broadcasted_iota(jnp.int32, (1, CELLS), 1)
+    x = lax.rem(q, NX) + dx
+    at = q + NX * dy
+    return ((x >= 0) & (x < NX) & (at >= 0) & (at < CELLS)).astype(F32)
 
 
 def shifted(value, dy, dx):
     if dy == 0 and dx == 0:
         return value
-    moved = pltpu.roll(value, (-(dy * NX + dx)) % CELLS, 1)
-    return jnp.where(cell_mask(value.shape[0], dy, dx), moved, 0.0)
+    return pltpu.roll(value, (-(dy * NX + dx)) % CELLS, 1) * cell_mask(dy, dx)
 
 
 def odd_partner(s, nz):
@@ -123,69 +122,86 @@
         moved_ref[i] = moved_rows(ref[...])
 
 
+def block_of(ref, goal, cols):
+    return ref[pl.ds(pl.multiple_of(goal * cols, cols), cols), :]
+
+
 def output_kernel(nz, nc, scale, pos_ref, last_ref, w_ref, *refs):
     terms = refs[:nc]
     own_ref, moved_ref, f_ref, fe_ref, fo_ref = refs[nc : nc + 5]
-    packs = refs[nc + 5 : -5]
-    out_ref, back_ref, wg_ref, c_ref, g_ref = refs[-5:]
+    packs = refs[nc + 5 : -9]
+    out_hbm, back_hbm, wg_hbm, out_ref, back_ref, wg_ref, c_ref, g_ref, sems = refs[-9:]
     total = terms[0][...]
     for term in terms[1:]:
         total = total + term[...]
     back_ref[:, 0, :] = total
+    copies = [pltpu.make_async_copy(back_ref, back_hbm, sems.at[0])]
+    copies[0].start()
 
     channels = w_ref.shape[1]
     blocks = own_ref.shape[0]
     cols = g_ref.shape[1]
     s = pos_ref[0]
+
+    empty = jnp.zeros(c_ref.shape[1:], BF16)
+    c_ref[0] = empty
+    c_ref[nz + 1] = empty
+    even, odd = s ^ 1, odd_partner(s, nz)
+    for i, (source, field) in enumerate(((s, f_ref), (even, fe_ref), (odd, fo_ref))):
+        c_ref[source + 1] = moved_ref[i]
+        g_ref[source] = block_of(field, s, cols)
+    for k, pack in zip(range(2, nz - 1), packs):
+        source = lax.rem(s + nz - k, nz)
+        g_ref[source] = pack[:cols, :]
+        c_ref[source + 1] = moved_rows(pack[cols:, :] if nz > 4 else fe_ref[channels:, :])
+
+    sums = None
+    for z in range(nz):
+        field = g_ref[z].astype(F32)
+        fields = jnp.concatenate([shifted(field, 0, dx).astype(BF16) for dx in (-1, 0, 1)], 0)
+        term = lax.dot_general(
+            c_ref[z : z + 3].reshape(9 * blocks, CELLS),
+            fields,
+            (((1,), (1,)), ((), ())),
+            preferred_element_type=F32,
+        )
+        sums = term if sums is None else sums + term
+    sums = sums * scale
+    for dz in range(3):
+        for dy in range(3):
+            at = ((2 - dz) * 3 + dy) * blocks
+            for dx in range(3):
+                wg_ref[9 * dz + 3 * dy + dx] = sums[at : at + blocks, dx * cols : (dx + 1) * cols]
+        taps = pl.ds(9 * dz, 9)
+        copies.append(pltpu.make_async_copy(wg_ref.at[taps], wg_hbm.at[taps], sems.at[dz + 1]))
+        copies[-1].start()
+
     first = s % 2 == 0
     even, odd = fe_ref[:channels, :], fo_ref[...]
     after = conv_part(w_ref, jnp.where(first, even, odd), 1)
     before = conv_part(w_ref, jnp.where(first, odd, even), -1)
     acc = jnp.where(s < nz - 1, after, 0.0) + jnp.where(s > 0, before, 0.0)
     out_ref[:, 0, :] = own_ref[...] + moved_sum(acc)
-
-    mine = pl.ds(pl.multiple_of(s * cols, cols), cols)
-    sources = (s, s ^ 1, odd_partner(s, nz))
-    for i, (source, field) in enumerate(zip(sources, (f_ref, fe_ref, fo_ref))):
-        c_ref[source] = moved_ref[i]
-        g_ref[source] = field[mine, :]
-    for k, pack in zip(range(2, nz - 1), packs):
-        source = lax.rem(s + nz - k, nz)
-        g_ref[source] = pack[:cols, :]
-        c_ref[source] = moved_rows(pack[cols:, :] if nz > 4 else fe_ref[channels:, :])
-
-    feats = []
-    for z in range(nz):
-        field = g_ref[z].astype(F32)
-        feats.append(jnp.concatenate([shifted(field, 0, dx).astype(BF16) for dx in (-1, 0, 1)], 0))
-    for dz in (-1, 0, 1):
-        sums = None
-        for z in range(nz):
-            if 0 <= z - dz < nz:
-                term = lax.dot_general(
-                    c_ref[z - dz], feats[z], (((1,), (1,)), ((), ())), preferred_element_type=F32
-                )
-                sums = term if sums is None else sums + term
-        sums = sums * scale
-        for dy in range(3):
-            for dx in range(3):
-                tap = 9 * (dz + 1) + 3 * dy + dx
-                wg_ref[tap] = sums[dy * blocks : (dy + 1) * blocks, dx * cols : (dx + 1) * cols]
+    copies.append(pltpu.make_async_copy(out_ref, out_hbm, sems.at[4]))
+    copies[-1].start()
+    for copy in copies:
+        copy.wait()
 
 
 VMEM = pl.BlockSpec(memory_space=pltpu.VMEM)
 SMEM = pl.BlockSpec(memory_space=pltpu.SMEM)
-
-
-def kernel_call(body, name, outs, args, scratch=(), weight=0):
+ANY = pl.BlockSpec(memory_space=pl.ANY)
+
+
+def kernel_call(body, name, outs, args, scratch=(), weight=0, far_outs=()):
     return pl.pallas_call(
         body,
         out_shape=outs,
         in_specs=[SMEM if a.dtype == jnp.int32 else VMEM for a in args],
-        out_specs=tuple(VMEM for _ in outs),
+        out_specs=tuple(ANY if i in far_outs else VMEM for i in range(len(outs))),
         scratch_shapes=list(scratch),
         compiler_params=pltpu.CompilerParams(vmem_limit_bytes=VMEM_BYTES),
-        cost_estimate=pl.CostEstimate(flops=int(weight), bytes_accessed=0, transcendentals=0),
+        cost_estimate=pl.CostEstimate(flops=weight, bytes_accessed=0, transcendentals=0),
         name=name,
     )(*args)
 
@@ -256,8 +272,16 @@
         "outputs",
         [block, block, jax.ShapeDtypeStruct((27, blocks, cols), F32)],
         [pos, last, w2, *terms, out_own, moved, f_all, f_even, f_odd, *far],
-        [pltpu.VMEM((nz, 3 * blocks, plane), BF16), pltpu.VMEM((nz, cols, plane), BF16)],
+        [
+            pltpu.VMEM((blocks, 1, plane), F32),
+            pltpu.VMEM((blocks, 1, plane), F32),
+            pltpu.VMEM((27, blocks, cols), F32),
+            pltpu.VMEM((nz + 2, 3 * blocks, plane), BF16),
+            pltpu.VMEM((nz, cols, plane), BF16),
+            pltpu.SemaphoreType.DMA((5,)),
+        ],
         W_OUT * work,
+        (0, 1, 2),
     )
     return (output, back, weight_grad)
 

time: 32.2 us -> 32.6 us (1.012)
  no operation moved by 1% of the time
where the time goes in v10:
time: 32.6 us; the launch traced here: 32.4 us
  starting transfers between devices  13.3 us (41%)
  waiting for transfers between devices  11.2 us (34%)
  Pallas kernels  7.13 us (22%)
  between operations  0.71 us (2%)
    ppermute x3, waiting for transfers between devices, per_device(): lax.ppermute(parts[k], 'ch', mixed(k))  8.15 us
    pallas_call x6, Pallas kernels, kernel_call(): pl.pallas_call(body, out_shape=outs, in_specs=[SMEM if a.dtype == jnp.int...  7.13 us
    ppermute x3, starting transfers between devices, per_device(): lax.ppermute(parts[k], 'ch', mixed(k))  4.47 us
    ppermute x3, starting transfers between devices, per_device(): pieces = [feat] + [lax.ppermute(feat, 'ch', mixed(k)) for k in range(1, nc)]  4.39 us
    ppermute x1, starting transfers between devices, per_device(): cot_odd = lax.ppermute(cot, 'sp', odd_pairs)  2.44 us
    ppermute x1, waiting for transfers between devices, per_device(): lax.ppermute(packs[k - 2], 'sp', [(i, (i + k) % nz) for i in range(nz)])  1.27 us
    ppermute x1, waiting for transfers between devices, per_device(): cot_even = lax.ppermute(cot, 'sp', even_pairs)  1.13 us
    ppermute x1, starting transfers between devices, per_device(): f_odd = lax.ppermute(f_all[:channels], 'sp', odd_pairs)  0.7 us
  transfers between devices with their start and end apart: 11, of which 5 were waited for; matrix products, arithmetic and copies ran while one was open for 0% of the time, Pallas kernels for 11%

profile of v10, /device:TPU:0, one launch (start us, length us, event | category | flops | bytes accessed | tf_op | source)
XLA Modules:
  0.0 32.4 jit_solution(3529716638499756808)
XLA Ops:
  0.6 0.0 copy-start.2
  0.6 0.0 copy-start
  0.7 0.0 copy-start.1
  0.7 2.4 %collective-permute-start.1 = (bf16[64,640]{1,0:T(8,128)(2,1)}, bf16[64,640]{1,0:T(8,128)(2,1)S(1)}, u32[]{:S(2)}, u32[]{:S(2)}) collective-permute-start(bf16[64,640]{1,0:T(8,128)(2,1)} %bitcast.8), channel_id=1, source_target_pairs={{0,12},{4,8},{8,4},{12,0},{1,13},{5,9},{9,5},{13,1},{2,14},{6,10},... | collective-permute-start | bytes 245768 | tf_op jit(solution)/shard_map/ppermute | solution.py:233
  3.1 0.7 %collective-permute-start = (bf16[64,640]{1,0:T(8,128)(2,1)}, bf16[64,640]{1,0:T(8,128)(2,1)S(1)}, u32[]{:S(2)}, u32[]{:S(2)}) collective-permute-start(bf16[64,640]{1,0:T(8,128)(2,1)} %bitcast.9), channel_id=1, source_target_pairs={{0,4},{4,0},{8,12},{12,8},{1,5},{5,1},{9,13},{13,9},{2,6},{6,2},{1... | collective-permute-start | bytes 245768 | tf_op jit(solution)/shard_map/ppermute | solution.py:232
  3.8 1.1 %collective-permute-done.even_ref.ce_ref = bf16[64,640]{1,0:T(8,128)(2,1)S(1)} collective-permute-done((bf16[64,640]{1,0:T(8,128)(2,1)}, bf16[64,640]{1,0:T(8,128)(2,1)S(1)}, u32[]{:S(2)}, u32[]{:S(2)}) %collective-permute-start) | collective-permute-done | bytes 81952 | tf_op jit(solution)/shard_map/ppermute | solution.py:232
  4.9 0.0 copy-done.2
  4.9 3.6 %collective-permute-start.4 = (bf16[64,640]{1,0:T(8,128)(2,1)S(1)}, bf16[64,640]{1,0:T(8,128)(2,1)S(1)}, u32[]{:S(2)}, u32[]{:S(2)}) collective-permute-start(bf16[64,640]{1,0:T(8,128)(2,1)S(1)} %bitcast.13), channel_id=1, source_target_pairs={{0,3},{1,2},{2,1},{3,0},{4,7},{5,6},{6,5},{7,4},{8,11},{9,10},{10,... | collective-permute-start | bytes 245768 | tf_op jit(solution)/shard_map/ppermute | solution.py:236
  8.5 0.0 collective-permute-start.3
  8.5 0.8 %collective-permute-start.2 = (bf16[64,640]{1,0:T(8,128)(2,1)S(1)}, bf16[64,640]{1,0:T(8,128)(2,1)S(1)}, u32[]{:S(2)}, u32[]{:S(2)}) collective-permute-start(bf16[64,640]{1,0:T(8,128)(2,1)S(1)} %bitcast.15), channel_id=1, source_target_pairs={{0,1},{1,0},{2,3},{3,2},{4,5},{5,4},{6,7},{7,6},{8,9},{9,8},{10,11... | collective-permute-start | bytes 245768 | tf_op jit(solution)/shard_map/ppermute | solution.py:236
  9.3 0.1 pad_add_fusion.pos_ref
  9.4 0.0 collective-permute-done.1.odd_ref.near_ref.co_ref
  9.4 0.0 copy-done
  9.4 0.0 copy-done.1
  9.4 1.8 %input_grad.1 = (f32[64,640]{1,0:T(8,128)S(1)}, f32[64,640]{1,0:T(8,128)S(1)}, f32[64,640]{1,0:T(8,128)S(1)}, f32[64,640]{1,0:T(8,128)S(1)}, f32[8,128]{1,0:T(8,128)S(1)}) custom-call(s32[2]{0:T(128)S(1)} %pad_add_fusion.pos_ref, f32[8,128]{1,0:T(8,128)S(1)} %begin.1.begin_ref, bf16[64,640]{1,0:T(8,128)(2,1)S(1)} %bitcast.10, ...), custom_call_target="tpu_custom_call" | custom-call | flops 566231040 | tf_op jit(solution)/shard_map/input_grad/pallas_call | solution.py:197
  11.2 1.3 %collective-permute-start.5 = (f32[64,640]{1,0:T(8,128)S(1)}, f32[64,640]{1,0:T(8,128)S(1)}, u32[]{:S(2)}, u32[]{:S(2)}) collective-permute-start(f32[64,640]{1,0:T(8,128)S(1)} %get-tuple-element.21), channel_id=1, source_target_pairs={{0,1},{1,0},{2,3},{3,2},{4,5},{5,4},{6,7},{7,6},{8,9},{9,8},{10,11... | collective-permute-start | bytes 491528 | tf_op jit(solution)/shard_map/ppermute | solution.py:246
  12.5 2.9 %collective-permute-start.6 = (f32[64,640]{1,0:T(8,128)S(1)}, f32[64,640]{1,0:T(8,128)S(1)}, u32[]{:S(2)}, u32[]{:S(2)}) collective-permute-start(f32[64,640]{1,0:T(8,128)S(1)} %get-tuple-element.22), channel_id=1, source_target_pairs={{0,2},{1,3},{2,0},{3,1},{4,6},{5,7},{6,4},{7,5},{8,10},{9,11},{10,... | collective-permute-start | bytes 491528 | tf_op jit(solution)/shard_map/ppermute | solution.py:246
  15.4 0.0 collective-permute-done.4.refs_3_
  15.4 0.2 collective-permute-start.7
  15.7 0.6 %collective-permute-done.3.refs_2_ = bf16[64,640]{1,0:T(8,128)(2,1)S(1)} collective-permute-done((bf16[64,640]{1,0:T(8,128)(2,1)S(1)}, bf16[64,640]{1,0:T(8,128)(2,1)S(1)}, u32[]{:S(2)}, u32[]{:S(2)}) %collective-permute-start.3) | collective-permute-done | bytes 81952 | tf_op jit(solution)/shard_map/ppermute | solution.py:236
  16.3 0.0 collective-permute-done.2.refs_1_
  16.3 0.6 %gather.1 = (bf16[320,640]{1,0:T(8,128)(2,1)S(1)}, bf16[64,640]{1,0:T(8,128)(2,1)S(1)}) custom-call(s32[2]{0:T(128)S(1)} %pad_add_fusion.pos_ref, f32[8,128]{1,0:T(8,128)S(1)} %get-tuple-element.16.token_ref, bf16[64,640]{1,0:T(8,128)(2,1)S(1)} %bitcast.11, bf16[64,640]{1,0:T(8,128)(2,1)S(1)} %collective-permute-done.1.odd_ref.near_ref.co_ref, ...), custom_call_target="tpu_custom_call" | custom-call | tf_op jit(solution)/shard_map/gather/pallas_call | solution.py:197
  16.9 0.1 collective-permute-start.8
  17.0 0.7 %collective-permute-start.9 = (bf16[256,640]{1,0:T(8,128)(2,1)S(1)}, bf16[256,640]{1,0:T(8,128)(2,1)S(1)}, u32[]{:S(2)}, u32[]{:S(2)}) collective-permute-start(bf16[256,640]{1,0:T(8,128)(2,1)S(1)} %slice.3), channel_id=1, source_target_pairs={{0,12},{4,8},{8,4},{12,0},{1,13},{5,9},{9,5},{13,1},{2,14},{6,10},... | collective-permute-start | bytes 983048 | tf_op jit(solution)/shard_map/ppermute | solution.py:255
  17.7 1.2 %early.1 = (f32[64,640]{1,0:T(8,128)S(1)}, bf16[3,192,640]{2,1,0:T(8,128)(2,1)S(1)}, f32[8,128]{1,0:T(8,128)S(1)}) custom-call(s32[2]{0:T(128)S(1)} %pad_add_fusion.pos_ref, bf16[1728,256]{1,0:T(8,128)(2,1)S(1)} %bitcast.6, bf16[320,640]{1,0:T(8,128)(2,1)S(1)} %get-tuple-element.18.f_ref.refs_6_, bf16[64,640]{1,0:T(8,128)(2,1)S(1)} %bitcast.12, ...), custom_call_target="tpu_custom_call" | custom-call | tf_op jit(solution)/shard_map/early/pallas_call | solution.py:197
  18.9 2.6 %collective-permute-done.5.refs_2_.refs_1_ = f32[64,640]{1,0:T(8,128)S(1)} collective-permute-done((f32[64,640]{1,0:T(8,128)S(1)}, f32[64,640]{1,0:T(8,128)S(1)}, u32[]{:S(2)}, u32[]{:S(2)}) %collective-permute-start.5) | collective-permute-done | bytes 163872 | tf_op jit(solution)/shard_map/ppermute | solution.py:246
  21.5 0.5 %collective-permute-start.10 = (bf16[64,640]{1,0:T(8,128)(2,1)S(1)}, bf16[64,640]{1,0:T(8,128)(2,1)S(1)}, u32[]{:S(2)}, u32[]{:S(2)}) collective-permute-start(bf16[64,640]{1,0:T(8,128)(2,1)S(1)} %get-tuple-element.26), channel_id=1, source_target_pairs={{0,8},{4,12},{8,0},{12,4},{1,9},{5,13},{9,1},{13,5},{2,10},{6,14},... | collective-permute-start | bytes 245768 | tf_op jit(solution)/shard_map/ppermute | solution.py:258
  22.0 5.5 %collective-permute-done.6.refs_3_.refs_2_ = f32[64,640]{1,0:T(8,128)S(1)} collective-permute-done((f32[64,640]{1,0:T(8,128)S(1)}, f32[64,640]{1,0:T(8,128)S(1)}, u32[]{:S(2)}, u32[]{:S(2)}) %collective-permute-start.6) | collective-permute-done | bytes 163872 | tf_op jit(solution)/shard_map/ppermute | solution.py:246
  27.6 0.0 collective-permute-done.7.refs_4_.refs_3_
  27.6 1.3 %collective-permute-done.10.refs_9_ = bf16[64,640]{1,0:T(8,128)(2,1)S(1)} collective-permute-done((bf16[64,640]{1,0:T(8,128)(2,1)S(1)}, bf16[64,640]{1,0:T(8,128)(2,1)S(1)}, u32[]{:S(2)}, u32[]{:S(2)}) %collective-permute-start.10) | collective-permute-done | bytes 81952 | tf_op jit(solution)/shard_map/ppermute | solution.py:258
  28.9 0.0 collective-permute-done.9.refs_8_
  28.9 0.0 collective-permute-done.8.refs_7_
  28.9 3.6 %outputs.1 = (f32[64,1,640]{2,1,0:T(1,128)}, f32[64,1,640]{2,1,0:T(1,128)}, f32[27,64,64]{2,1,0:T(8,128)}) custom-call(s32[2]{0:T(128)S(1)} %pad_add_fusion.pos_ref, f32[8,128]{1,0:T(8,128)S(1)} %hold.1.last_ref, bf16[1728,256]{1,0:T(8,128)(2,1)S(1)} %bitcast.7, f32[64,640]{1,0:T(8,128)S(1)} %get-tuple-element.20.refs_1_.refs_0_, ...), custom_call_target="tpu_custom_call" | custom-call | tf_op jit(solution)/shard_map/outputs/pallas_call | solution.py:197
  (3 shorter events, 0.0 us)
Async XLA Ops:
  0.6 4.3 %copy-start.2 = (bf16[64,1,640]{2,0,1:T(8,128)(2,1)S(1)}, bf16[64,1,640]{2,0,1:T(8,128)(2,1)}, u32[]{:S(2)}) copy-start(bf16[64,1,640]{2,0,1:T(8,128)(2,1)} %param.3) | copy-start | bytes 245764
  0.6 8.7 %copy-start = (bf16[27,64,256]{2,1,0:T(8,128)(2,1)S(1)}, bf16[27,64,256]{2,1,0:T(8,128)(2,1)}, u32[]{:S(2)}) copy-start(bf16[27,64,256]{2,1,0:T(8,128)(2,1)} %param.4) | copy-start | bytes 2654212
  0.7 8.7 %copy-start.1 = (bf16[64,1,640]{2,0,1:T(8,128)(2,1)S(1)}, bf16[64,1,640]{2,0,1:T(8,128)(2,1)}, u32[]{:S(2)}) copy-start(bf16[64,1,640]{2,0,1:T(8,128)(2,1)} %param.5) | copy-start | bytes 245764
  0.7 8.7 %collective-permute-start.1 = (bf16[64,640]{1,0:T(8,128)(2,1)}, bf16[64,640]{1,0:T(8,128)(2,1)S(1)}, u32[]{:S(2)}, u32[]{:S(2)}) collective-permute-start(bf16[64,640]{1,0:T(8,128)(2,1)} %bitcast.8), channel_id=1, source_target_pairs={{0,12},{4,8},{8,4},{12,0},{1,13},{5,9},{9,5},{13,1},{2,14},{6,10},... | collective-permute-start | bytes 245768 | tf_op jit(solution)/shard_map/ppermute | solution.py:233
  3.1 1.8 %collective-permute-start = (bf16[64,640]{1,0:T(8,128)(2,1)}, bf16[64,640]{1,0:T(8,128)(2,1)S(1)}, u32[]{:S(2)}, u32[]{:S(2)}) collective-permute-start(bf16[64,640]{1,0:T(8,128)(2,1)} %bitcast.9), channel_id=1, source_target_pairs={{0,4},{4,0},{8,12},{12,8},{1,5},{5,1},{9,13},{13,9},{2,6},{6,2},{1... | collective-permute-start | bytes 245768 | tf_op jit(solution)/shard_map/ppermute | solution.py:232
  4.9 10.5 %collective-permute-start.4 = (bf16[64,640]{1,0:T(8,128)(2,1)S(1)}, bf16[64,640]{1,0:T(8,128)(2,1)S(1)}, u32[]{:S(2)}, u32[]{:S(2)}) collective-permute-start(bf16[64,640]{1,0:T(8,128)(2,1)S(1)} %bitcast.13), channel_id=1, source_target_pairs={{0,3},{1,2},{2,1},{3,0},{4,7},{5,6},{6,5},{7,4},{8,11},{9,10},{10,... | collective-permute-start | bytes 245768 | tf_op jit(solution)/shard_map/ppermute | solution.py:236
  8.5 7.8 %collective-permute-start.3 = (bf16[64,640]{1,0:T(8,128)(2,1)S(1)}, bf16[64,640]{1,0:T(8,128)(2,1)S(1)}, u32[]{:S(2)}, u32[]{:S(2)}) collective-permute-start(bf16[64,640]{1,0:T(8,128)(2,1)S(1)} %bitcast.14), channel_id=1, source_target_pairs={{0,2},{1,3},{2,0},{3,1},{4,6},{5,7},{6,4},{7,5},{8,10},{9,11},{10,... | collective-permute-start | bytes 245768 | tf_op jit(solution)/shard_map/ppermute | solution.py:236
  8.5 7.8 %collective-permute-start.2 = (bf16[64,640]{1,0:T(8,128)(2,1)S(1)}, bf16[64,640]{1,0:T(8,128)(2,1)S(1)}, u32[]{:S(2)}, u32[]{:S(2)}) collective-permute-start(bf16[64,640]{1,0:T(8,128)(2,1)S(1)} %bitcast.15), channel_id=1, source_target_pairs={{0,1},{1,0},{2,3},{3,2},{4,5},{5,4},{6,7},{7,6},{8,9},{9,8},{10,11... | collective-permute-start | bytes 245768 | tf_op jit(solution)/shard_map/ppermute | solution.py:236
  11.2 10.3 %collective-permute-start.5 = (f32[64,640]{1,0:T(8,128)S(1)}, f32[64,640]{1,0:T(8,128)S(1)}, u32[]{:S(2)}, u32[]{:S(2)}) collective-permute-start(f32[64,640]{1,0:T(8,128)S(1)} %get-tuple-element.21), channel_id=1, source_target_pairs={{0,1},{1,0},{2,3},{3,2},{4,5},{5,4},{6,7},{7,6},{8,9},{9,8},{10,11... | collective-permute-start | bytes 491528 | tf_op jit(solution)/shard_map/ppermute | solution.py:246
  12.5 15.1 %collective-permute-start.6 = (f32[64,640]{1,0:T(8,128)S(1)}, f32[64,640]{1,0:T(8,128)S(1)}, u32[]{:S(2)}, u32[]{:S(2)}) collective-permute-start(f32[64,640]{1,0:T(8,128)S(1)} %get-tuple-element.22), channel_id=1, source_target_pairs={{0,2},{1,3},{2,0},{3,1},{4,6},{5,7},{6,4},{7,5},{8,10},{9,11},{10,... | collective-permute-start | bytes 491528 | tf_op jit(solution)/shard_map/ppermute | solution.py:246
  15.4 12.1 %collective-permute-start.7 = (f32[64,640]{1,0:T(8,128)S(1)}, f32[64,640]{1,0:T(8,128)S(1)}, u32[]{:S(2)}, u32[]{:S(2)}) collective-permute-start(f32[64,640]{1,0:T(8,128)S(1)} %get-tuple-element.23), channel_id=1, source_target_pairs={{0,3},{1,2},{2,1},{3,0},{4,7},{5,6},{6,5},{7,4},{8,11},{9,10},{10,... | collective-permute-start | bytes 491528 | tf_op jit(solution)/shard_map/ppermute | solution.py:246
  16.9 12.0 %collective-permute-start.8 = (bf16[320,640]{1,0:T(8,128)(2,1)S(1)}, bf16[320,640]{1,0:T(8,128)(2,1)S(1)}, u32[]{:S(2)}, u32[]{:S(2)}) collective-permute-start(bf16[320,640]{1,0:T(8,128)(2,1)S(1)} %get-tuple-element.18.f_ref.refs_6_), channel_id=1, source_target_pairs={{0,4},{4,0},{8,12},{12,8},{1,5},{5,1},{9,13},{13,9},{2,6},{6,2},{1... | collective-permute-start | bytes 1228808 | tf_op jit(solution)/shard_map/ppermute | solution.py:256
  17.0 11.8 %collective-permute-start.9 = (bf16[256,640]{1,0:T(8,128)(2,1)S(1)}, bf16[256,640]{1,0:T(8,128)(2,1)S(1)}, u32[]{:S(2)}, u32[]{:S(2)}) collective-permute-start(bf16[256,640]{1,0:T(8,128)(2,1)S(1)} %slice.3), channel_id=1, source_target_pairs={{0,12},{4,8},{8,4},{12,0},{1,13},{5,9},{9,5},{13,1},{2,14},{6,10},... | collective-permute-start | bytes 983048 | tf_op jit(solution)/shard_map/ppermute | solution.py:255
  21.5 7.4 %collective-permute-start.10 = (bf16[64,640]{1,0:T(8,128)(2,1)S(1)}, bf16[64,640]{1,0:T(8,128)(2,1)S(1)}, u32[]{:S(2)}, u32[]{:S(2)}) collective-permute-start(bf16[64,640]{1,0:T(8,128)(2,1)S(1)} %get-tuple-element.26), channel_id=1, source_target_pairs={{0,8},{4,12},{8,0},{12,4},{1,9},{5,13},{9,1},{13,5},{2,10},{6,14},... | collective-permute-start | bytes 245768 | tf_op jit(solution)/shard_map/ppermute | solution.py:258

commit v11 on v7

--- a/solution.py
+++ b/solution.py
@@ -13,22 +13,21 @@
 CELLS = NX * NY
 F32 = jnp.float32
 BF16 = jnp.bfloat16
-W_BEGIN, W_GRAD, W_TOTAL, W_OUT = 8, 1, 5, 0
+W_GATHER, W_EARLY, W_BEGIN, W_GRAD, W_FOLD, W_TOTAL, W_OUT = 2, 0, 8, 1, 0, 3, 0
 VMEM_BYTES = 32 * 1024 * 1024
 
 
-def cell_mask(rows, dy, dx):
-    q = lax.broadcasted_iota(jnp.int32, (rows, CELLS), 1)
-    x = q % NX + dx
-    y = q // NX + dy
-    return (x >= 0) & (x < NX) & (y >= 0) & (y < NY)
+def cell_mask(dy, dx):
+    q = lax.broadcasted_iota(jnp.int32, (1, CELLS), 1)
+    x = lax.rem(q, NX) + dx
+    at = q + NX * dy
+    return ((x >= 0) & (x < NX) & (at >= 0) & (at < CELLS)).astype(F32)
 
 
 def shifted(value, dy, dx):
     if dy == 0 and dx == 0:
         return value
-    moved = pltpu.roll(value, (-(dy * NX + dx)) % CELLS, 1)
-    return jnp.where(cell_mask(value.shape[0], dy, dx), moved, 0.0)
+    return pltpu.roll(value, (-(dy * NX + dx)) % CELLS, 1) * cell_mask(dy, dx)
 
 
 def odd_partner(s, nz):
@@ -36,14 +35,15 @@
 
 
 def gather_kernel(nz, nc, pos_ref, token_ref, cot_ref, near_ref, *refs):
-    pieces, f_ref, packs = refs[:nc], refs[nc], refs[nc + 1 :]
+    pieces, (f_ref, even_ref), packs = refs[:nc], refs[nc : nc + 2], refs[nc + 2 :]
     blocks = cot_ref.shape[0]
     channels = nc * blocks
     cols = channels // nz
     s, c = pos_ref[0], pos_ref[1]
     for k in range(nc):
         f_ref[pl.ds(pl.multiple_of((c ^ k) * blocks, blocks), blocks), :] = pieces[k][...]
-    f_ref[channels:, :] = near_ref[...]
+    even_ref[:cols, :] = f_ref[pl.ds(pl.multiple_of((s ^ 1) * cols, cols), cols), :]
+    even_ref[cols:, :] = near_ref[...]
     for k, pack in zip(range(2, nz - 1), packs):
         goal = lax.rem(s + k, nz)
         pack[:cols, :] = f_ref[pl.ds(pl.multiple_of(goal * cols, cols), cols), :]
@@ -57,6 +57,10 @@
         for dx in (-1, 0, 1):
             tap = first + 3 * (dy + 1) + dx + 1
             cols_ref[tap * blocks : (tap + 1) * blocks, :] = shifted(plane, -dy, -dx).astype(BF16)
+
+
+def fold_kernel(own_ref, got_ref, both_ref):
+    both_ref[...] = own_ref[...] + got_ref[...]
 
 
 def hold_kernel(*refs):
@@ -87,16 +91,8 @@
 
 def conv_part(w_ref, field, dz):
     taps = w_ref.shape[0] // 3
-    return jnp.dot(
-        w_ref[(dz + 1) * taps : (dz + 2) * taps, :], field, preferred_element_type=F32
-    )
-
-
-def conv_part(w_ref, field, dz):
-    taps = w_ref.shape[0] // 3
-    return jnp.dot(
-        w_ref[(dz + 1) * taps : (dz + 2) * taps, :], field, preferred_element_type=F32
-    )
+    rows = pl.ds(pl.multiple_of((dz + 1) * taps, taps), taps)
+    return jnp.dot(w_ref[rows, :], field, preferred_element_type=F32)
 
 
 def moved_sum(acc):
@@ -115,44 +111,44 @@
     return jnp.concatenate([shifted(plane, -dy, 0).astype(BF16) for dy in (-1, 0, 1)], 0)
 
 
-def early_kernel(pos_ref, w_ref, f_ref, cot_ref, ce_ref, co_ref, out_ref, moved_ref, token_ref):
-    channels = w_ref.shape[1]
+def side_of(s):
+    return 1 - 2 * lax.rem(s, 2)
+
+
+def early_kernel(pos_ref, w_ref, f_ref, cot_ref, ce_ref, co_ref, own_ref, even_ref, moved_ref, token_ref):
     token_ref[...] = jnp.zeros(token_ref.shape, F32)
-    out_ref[...] = moved_sum(conv_part(w_ref, f_ref[:channels, :], 0))
+    even_ref[...] = moved_sum(conv_part(w_ref, f_ref[...], -side_of(pos_ref[0])))
+    own_ref[...] = moved_sum(conv_part(w_ref, f_ref[...], 0))
     for i, ref in enumerate((cot_ref, ce_ref, co_ref)):
         moved_ref[i] = moved_rows(ref[...])
 
 
-def output_kernel(nz, nc, scale, pos_ref, last_ref, w_ref, *refs):
-    terms = refs[:nc]
-    own_ref, moved_ref, f_ref, fe_ref, fo_ref = refs[nc : nc + 5]
-    packs = refs[nc + 5 : -5]
+def output_kernel(nz, count, scale, pos_ref, last_ref, w_ref, *refs):
+    terms = refs[:count]
+    own_ref, part_ref, moved_ref, f_ref, ge_ref, fo_ref = refs[count : count + 6]
+    packs = refs[count + 6 : -5]
     out_ref, back_ref, wg_ref, c_ref, g_ref = refs[-5:]
     total = terms[0][...]
     for term in terms[1:]:
         total = total + term[...]
     back_ref[:, 0, :] = total
 
-    channels = w_ref.shape[1]
     blocks = own_ref.shape[0]
     cols = g_ref.shape[1]
     s = pos_ref[0]
-    first = s % 2 == 0
-    even, odd = fe_ref[:channels, :], fo_ref[...]
-    after = conv_part(w_ref, jnp.where(first, even, odd), 1)
-    before = conv_part(w_ref, jnp.where(first, odd, even), -1)
-    acc = jnp.where(s < nz - 1, after, 0.0) + jnp.where(s > 0, before, 0.0)
-    out_ref[:, 0, :] = own_ref[...] + moved_sum(acc)
+    inner = ((s > 0) & (s < nz - 1)).astype(F32)
+    beyond = moved_sum(conv_part(w_ref, fo_ref[...], -side_of(s)))
+    out_ref[:, 0, :] = own_ref[...] + part_ref[...] + inner * beyond
 
     mine = pl.ds(pl.multiple_of(s * cols, cols), cols)
     sources = (s, s ^ 1, odd_partner(s, nz))
-    for i, (source, field) in enumerate(zip(sources, (f_ref, fe_ref, fo_ref))):
+    for i, (source, field) in enumerate(zip(sources, (f_ref[mine, :], ge_ref[:cols, :], fo_ref[mine, :]))):
         c_ref[source] = moved_ref[i]
-        g_ref[source] = field[mine, :]
+        g_ref[source] = field
     for k, pack in zip(range(2, nz - 1), packs):
         source = lax.rem(s + nz - k, nz)
         g_ref[source] = pack[:cols, :]
-        c_ref[source] = moved_rows(pack[cols:, :] if nz > 4 else fe_ref[channels:, :])
+        c_ref[source] = moved_rows(pack[cols:, :] if nz > 4 else ge_ref[cols:, :])
 
     feats = []
     for z in range(nz):
@@ -227,35 +223,43 @@
         [pltpu.VMEM((27 * blocks, plane), BF16), pltpu.VMEM((channels, plane), F32)],
         W_GRAD * work,
     )
-    terms = [parts[0]] + [lax.ppermute(parts[k], "ch", mixed(k)) for k in range(1, nc)]
+    terms = [parts[0]]
+    for k in range(2, nc, 2):
+        got = lax.ppermute(parts[k + 1], "ch", mixed(1))
+        (both,) = kernel_call(fold_kernel, "fold", [of(blocks, F32)], [parts[k], got], weight=W_FOLD * work)
+        terms.append(lax.ppermute(both, "ch", mixed(k)))
+    terms.append(lax.ppermute(parts[1], "ch", mixed(1)))
 
     far_rows = cols if nz == 4 else cols + blocks
-    f_all, *packs = kernel_call(
+    f_all, to_even, *packs = kernel_call(
         functools.partial(gather_kernel, nz, nc),
         "gather",
-        [of(channels + blocks, BF16)] + [of(far_rows, BF16)] * (nz - 3),
+        [of(channels, BF16), of(cols + blocks, BF16)] + [of(far_rows, BF16)] * (nz - 3),
         [pos, token, cot, cot_odd] + pieces,
-    )
-    f_odd = lax.ppermute(f_all[:channels], "sp", odd_pairs)
-    f_even = lax.ppermute(f_all, "sp", even_pairs)
+        weight=W_GATHER * work,
+    )
+    f_odd = lax.ppermute(f_all, "sp", odd_pairs)
+    g_even = lax.ppermute(to_even, "sp", even_pairs)
     far = [
         lax.ppermute(packs[k - 2], "sp", [(i, (i + k) % nz) for i in range(nz)])
         for k in range(2, nz - 1)
     ]
-    out_own, moved, done = kernel_call(
+    out_own, out_even, moved, done = kernel_call(
         early_kernel,
         "early",
-        [of(blocks, F32), jax.ShapeDtypeStruct((3, 3 * blocks, plane), BF16), small],
+        [of(blocks, F32)] * 2 + [jax.ShapeDtypeStruct((3, 3 * blocks, plane), BF16), small],
         [pos, w2, f_all, cot, cot_even, cot_odd],
-    )
+        weight=W_EARLY * work,
+    )
+    out_even = lax.ppermute(out_even, "sp", even_pairs)
 
     block = jax.ShapeDtypeStruct((blocks, 1, plane), F32)
     (last,) = kernel_call(hold_kernel, "hold", [small], [done] + terms, weight=W_TOTAL * work)
     output, back, weight_grad = kernel_call(
-        functools.partial(output_kernel, nz, nc, 1.0 / math.sqrt(nz * depth * plane)),
+        functools.partial(output_kernel, nz, len(terms), 1.0 / math.sqrt(nz * depth * plane)),
         "outputs",
         [block, block, jax.ShapeDtypeStruct((27, blocks, cols), F32)],
-        [pos, last, w2, *terms, out_own, moved, f_all, f_even, f_odd, *far],
+        [pos, last, w2, *terms, out_own, out_even, moved, f_all, g_even, f_odd, *far],
         [pltpu.VMEM((nz, 3 * blocks, plane), BF16), pltpu.VMEM((nz, cols, plane), BF16)],
         W_OUT * work,
     )

time: 32.2 us -> 33.2 us (1.031)
  waiting for transfers between devices: 11.2 us -> 12.3 us
    ppermute x3, waiting for transfers between devices: 0.63 us -> 3.57 us  [per_device(): pieces = [feat] + [lax.ppermute(feat, 'ch', mixed(k)) for k in range(1, nc)]]
    ppermute x5 -> x6, waiting for transfers between devices: 8.14 us -> 6.62 us  [the longest x1 3.62 us: per_device(): terms.append(lax.ppermute(parts[1], 'ch', mixed(1)))]
    ppermute x5 -> x6, starting transfers between devices: 5.23 us -> 4.57 us  [the longest x1 1.39 us: per_device(): terms.append(lax.ppermute(parts[1], 'ch', mixed(1)))]
    ppermute x1, starting transfers between devices: 0.51 us -> 0.92 us  [per_device(): lax.ppermute(packs[k - 2], 'sp', [(i, (i + k) % nz) for i in range(nz)])]
    pallas_call x6 -> x7, Pallas kernels: 6.83 us -> 6.94 us  [kernel_call(): pl.pallas_call(body, out_shape=outs, in_specs=[SMEM if a.dtype == jnp.int...]
  transfers between devices with their start and end apart: 11 -> 12, of which waited for: 5 -> 6; matrix products, arithmetic and copies ran while one was open for 0% -> 0% of each run, Pallas kernels for 11% -> 12%
where the time goes in v11:
time: 33.2 us; the launch traced here: 33 us
  starting transfers between devices  13 us (39%)
  waiting for transfers between devices  12.3 us (37%)
  Pallas kernels  6.94 us (21%)
  between operations  0.7 us (2%)
    pallas_call x7, Pallas kernels, kernel_call(): pl.pallas_call(body, out_shape=outs, in_specs=[SMEM if a.dtype == jnp.int...  6.94 us
    ppermute x3, starting transfers between devices, per_device(): pieces = [feat] + [lax.ppermute(feat, 'ch', mixed(k)) for k in range(1, nc)]  4.39 us
    ppermute x1, waiting for transfers between devices, per_device(): terms.append(lax.ppermute(parts[1], 'ch', mixed(1)))  3.62 us
    ppermute x3, waiting for transfers between devices, per_device(): pieces = [feat] + [lax.ppermute(feat, 'ch', mixed(k)) for k in range(1, nc)]  3.57 us
    ppermute x1, starting transfers between devices, per_device(): cot_odd = lax.ppermute(cot, 'sp', odd_pairs)  2.44 us
    ppermute x1, waiting for transfers between devices, per_device(): terms.append(lax.ppermute(both, 'ch', mixed(k)))  2.42 us
    ppermute x1, starting transfers between devices, per_device(): terms.append(lax.ppermute(parts[1], 'ch', mixed(1)))  1.39 us
    ppermute x1, starting transfers between devices, per_device(): got = lax.ppermute(parts[k + 1], 'ch', mixed(1))  1.3 us
  transfers between devices with their start and end apart: 12, of which 6 were waited for; matrix products, arithmetic and copies ran while one was open for 0% of the time, Pallas kernels for 12%

profile of v11, /device:TPU:0, one launch (start us, length us, event | category | flops | bytes accessed | tf_op | source)
XLA Modules:
  0.0 33.0 jit_solution(11644050204737297708)
XLA Ops:
  0.6 2.4 %collective-permute-start.1 = (bf16[64,640]{1,0:T(8,128)(2,1)}, bf16[64,640]{1,0:T(8,128)(2,1)S(1)}, u32[]{:S(2)}, u32[]{:S(2)}) collective-permute-start(bf16[64,640]{1,0:T(8,128)(2,1)} %bitcast.8), channel_id=1, source_target_pairs={{0,12},{4,8},{8,4},{12,0},{1,13},{5,9},{9,5},{13,1},{2,14},{6,10},... | collective-permute-start | bytes 245768 | tf_op jit(solution)/shard_map/ppermute | solution.py:213
  3.1 0.7 %collective-permute-start = (bf16[64,640]{1,0:T(8,128)(2,1)}, bf16[64,640]{1,0:T(8,128)(2,1)S(1)}, u32[]{:S(2)}, u32[]{:S(2)}) collective-permute-start(bf16[64,640]{1,0:T(8,128)(2,1)} %bitcast.9), channel_id=1, source_target_pairs={{0,4},{4,0},{8,12},{12,8},{1,5},{5,1},{9,13},{13,9},{2,6},{6,2},{1... | collective-permute-start | bytes 245768 | tf_op jit(solution)/shard_map/ppermute | solution.py:212
  3.8 0.0 copy-start.2
  3.8 0.0 copy-start
  3.8 0.0 copy-start.1
  3.8 0.1 pad_add_fusion.pos_ref
  3.8 1.0 %collective-permute-done.even_ref.ce_ref = bf16[64,640]{1,0:T(8,128)(2,1)S(1)} collective-permute-done((bf16[64,640]{1,0:T(8,128)(2,1)}, bf16[64,640]{1,0:T(8,128)(2,1)S(1)}, u32[]{:S(2)}, u32[]{:S(2)}) %collective-permute-start) | collective-permute-done | bytes 81952 | tf_op jit(solution)/shard_map/ppermute | solution.py:212
  4.9 0.0 copy-done.2
  4.9 3.6 %collective-permute-start.4 = (bf16[64,640]{1,0:T(8,128)(2,1)S(1)}, bf16[64,640]{1,0:T(8,128)(2,1)S(1)}, u32[]{:S(2)}, u32[]{:S(2)}) collective-permute-start(bf16[64,640]{1,0:T(8,128)(2,1)S(1)} %bitcast.13), channel_id=1, source_target_pairs={{0,3},{1,2},{2,1},{3,0},{4,7},{5,6},{6,5},{7,4},{8,11},{9,10},{10,... | collective-permute-start | bytes 245768 | tf_op jit(solution)/shard_map/ppermute | solution.py:216
  8.5 0.0 collective-permute-start.3
  8.5 0.8 %collective-permute-start.2 = (bf16[64,640]{1,0:T(8,128)(2,1)S(1)}, bf16[64,640]{1,0:T(8,128)(2,1)S(1)}, u32[]{:S(2)}, u32[]{:S(2)}) collective-permute-start(bf16[64,640]{1,0:T(8,128)(2,1)S(1)} %bitcast.15), channel_id=1, source_target_pairs={{0,1},{1,0},{2,3},{3,2},{4,5},{5,4},{6,7},{7,6},{8,9},{9,8},{10,11... | collective-permute-start | bytes 245768 | tf_op jit(solution)/shard_map/ppermute | solution.py:216
  9.3 0.0 collective-permute-done.1.odd_ref.near_ref.co_ref
  9.3 0.0 copy-done
  9.3 0.0 copy-done.1
  9.3 1.8 %input_grad.1 = (f32[64,640]{1,0:T(8,128)S(1)}, f32[64,640]{1,0:T(8,128)S(1)}, f32[64,640]{1,0:T(8,128)S(1)}, f32[64,640]{1,0:T(8,128)S(1)}, f32[8,128]{1,0:T(8,128)S(1)}) custom-call(s32[2]{0:T(128)S(1)} %pad_add_fusion.pos_ref, f32[8,128]{1,0:T(8,128)S(1)} %begin.1.begin_ref, bf16[64,640]{1,0:T(8,128)(2,1)S(1)} %bitcast.10, ...), custom_call_target="tpu_custom_call" | custom-call | flops 566231040 | tf_op jit(solution)/shard_map/input_grad/pallas_call | solution.py:177
  11.1 1.3 %collective-permute-start.5 = (f32[64,640]{1,0:T(8,128)S(1)}, f32[64,640]{1,0:T(8,128)S(1)}, u32[]{:S(2)}, u32[]{:S(2)}) collective-permute-start(f32[64,640]{1,0:T(8,128)S(1)} %get-tuple-element.24), channel_id=1, source_target_pairs={{0,1},{1,0},{2,3},{3,2},{4,5},{5,4},{6,7},{7,6},{8,9},{9,8},{10,11... | collective-permute-start | bytes 491528 | tf_op jit(solution)/shard_map/ppermute | solution.py:228
  12.4 0.0 collective-permute-done.4.refs_3_
  12.4 3.6 %collective-permute-done.3.refs_2_ = bf16[64,640]{1,0:T(8,128)(2,1)S(1)} collective-permute-done((bf16[64,640]{1,0:T(8,128)(2,1)S(1)}, bf16[64,640]{1,0:T(8,128)(2,1)S(1)}, u32[]{:S(2)}, u32[]{:S(2)}) %collective-permute-start.3) | collective-permute-done | bytes 81952 | tf_op jit(solution)/shard_map/ppermute | solution.py:216
  16.0 0.0 collective-permute-done.2.refs_1_
  16.0 0.6 %gather.1 = (bf16[256,640]{1,0:T(8,128)(2,1)S(1)}, bf16[128,640]{1,0:T(8,128)(2,1)S(1)}, bf16[64,640]{1,0:T(8,128)(2,1)S(1)}) custom-call(s32[2]{0:T(128)S(1)} %pad_add_fusion.pos_ref, f32[8,128]{1,0:T(8,128)S(1)} %get-tuple-element.18.token_ref, bf16[64,640]{1,0:T(8,128)(2,1)S(1)} %bitcast.11, ...), custom_call_target="tpu_custom_call" | custom-call | flops 1132462080 | tf_op jit(solution)/shard_map/gather/pallas_call | solution.py:177
  16.6 0.1 collective-permute-start.10
  16.7 1.4 %collective-permute-start.7 = (f32[64,640]{1,0:T(8,128)S(1)}, f32[64,640]{1,0:T(8,128)S(1)}, u32[]{:S(2)}, u32[]{:S(2)}) collective-permute-start(f32[64,640]{1,0:T(8,128)S(1)} %get-tuple-element.25), channel_id=1, source_target_pairs={{0,1},{1,0},{2,3},{3,2},{4,5},{5,4},{6,7},{7,6},{8,9},{9,8},{10,11... | collective-permute-start | bytes 491528 | tf_op jit(solution)/shard_map/ppermute | solution.py:231
  18.1 0.6 %collective-permute-done.5.got_ref = f32[64,640]{1,0:T(8,128)S(1)} collective-permute-done((f32[64,640]{1,0:T(8,128)S(1)}, f32[64,640]{1,0:T(8,128)S(1)}, u32[]{:S(2)}, u32[]{:S(2)}) %collective-permute-start.5) | collective-permute-done | bytes 163872 | tf_op jit(solution)/shard_map/ppermute | solution.py:228
  18.6 1.2 %collective-permute-start.6 = (f32[64,640]{1,0:T(8,128)S(1)}, f32[64,640]{1,0:T(8,128)S(1)}, u32[]{:S(2)}, u32[]{:S(2)}) collective-permute-start(f32[64,640]{1,0:T(8,128)S(1)} %fold.1), channel_id=1, source_target_pairs={{0,2},{1,3},{2,0},{3,1},{4,6},{5,7},{6,4},{7,5},{8,10},{9,11},{10,... | collective-permute-start | bytes 491528 | tf_op jit(solution)/shard_map/ppermute | solution.py:230
  19.9 0.0 collective-permute-start.9
  19.9 1.6 %early.1 = (f32[64,640]{1,0:T(8,128)S(1)}, f32[64,640]{1,0:T(8,128)S(1)}, bf16[3,192,640]{2,1,0:T(8,128)(2,1)S(1)}, f32[8,128]{1,0:T(8,128)S(1)}) custom-call(s32[2]{0:T(128)S(1)} %pad_add_fusion.pos_ref, bf16[1728,256]{1,0:T(8,128)(2,1)S(1)} %bitcast.6, bf16[256,640]{1,0:T(8,128)(2,1)S(1)} %get-tuple-element.20.f_ref.refs_6_, bf16[64,640]{1,0:T(8,128)(2,1)S(1)} %bitcast.12, ...), custom_call_target="tpu_custom_call" | custom-call | tf_op jit(solution)/shard_map/early/pallas_call | solution.py:177
  21.5 0.6 %collective-permute-start.8 = (f32[64,640]{1,0:T(8,128)S(1)}, f32[64,640]{1,0:T(8,128)S(1)}, u32[]{:S(2)}, u32[]{:S(2)}) collective-permute-start(f32[64,640]{1,0:T(8,128)S(1)} %get-tuple-element.27), channel_id=1, source_target_pairs={{0,4},{4,0},{8,12},{12,8},{1,5},{5,1},{9,13},{13,9},{2,6},{6,2},{1... | collective-permute-start | bytes 491528 | tf_op jit(solution)/shard_map/ppermute | solution.py:254
  22.0 3.6 %collective-permute-done.7.refs_3_.refs_2_ = f32[64,640]{1,0:T(8,128)S(1)} collective-permute-done((f32[64,640]{1,0:T(8,128)S(1)}, f32[64,640]{1,0:T(8,128)S(1)}, u32[]{:S(2)}, u32[]{:S(2)}) %collective-permute-start.7) | collective-permute-done | bytes 163872 | tf_op jit(solution)/shard_map/ppermute | solution.py:231
  25.7 0.9 %collective-permute-start.11 = (bf16[64,640]{1,0:T(8,128)(2,1)S(1)}, bf16[64,640]{1,0:T(8,128)(2,1)S(1)}, u32[]{:S(2)}, u32[]{:S(2)}) collective-permute-start(bf16[64,640]{1,0:T(8,128)(2,1)S(1)} %get-tuple-element.30), channel_id=1, source_target_pairs={{0,8},{4,12},{8,0},{12,4},{1,9},{5,13},{9,1},{13,5},{2,10},{6,14},... | collective-permute-start | bytes 245768 | tf_op jit(solution)/shard_map/ppermute | solution.py:244
  26.6 2.4 %collective-permute-done.6.refs_2_.refs_1_ = f32[64,640]{1,0:T(8,128)S(1)} collective-permute-done((f32[64,640]{1,0:T(8,128)S(1)}, f32[64,640]{1,0:T(8,128)S(1)}, u32[]{:S(2)}, u32[]{:S(2)}) %collective-permute-start.6) | collective-permute-done | bytes 163872 | tf_op jit(solution)/shard_map/ppermute | solution.py:230
  29.0 1.1 %collective-permute-done.11.refs_9_ = bf16[64,640]{1,0:T(8,128)(2,1)S(1)} collective-permute-done((bf16[64,640]{1,0:T(8,128)(2,1)S(1)}, bf16[64,640]{1,0:T(8,128)(2,1)S(1)}, u32[]{:S(2)}, u32[]{:S(2)}) %collective-permute-start.11) | collective-permute-done | bytes 81952 | tf_op jit(solution)/shard_map/ppermute | solution.py:244
  30.1 0.0 collective-permute-done.9.refs_7_
  30.1 0.0 collective-permute-done.8.refs_4_
  30.1 0.0 collective-permute-done.10.refs_8_
  30.1 2.9 %outputs.1 = (f32[64,1,640]{2,1,0:T(1,128)}, f32[64,1,640]{2,1,0:T(1,128)}, f32[27,64,64]{2,1,0:T(8,128)}) custom-call(s32[2]{0:T(128)S(1)} %pad_add_fusion.pos_ref, f32[8,128]{1,0:T(8,128)S(1)} %hold.1.last_ref, bf16[1728,256]{1,0:T(8,128)(2,1)S(1)} %bitcast.7, f32[64,640]{1,0:T(8,128)S(1)} %get-tuple-element.22.refs_1_.refs_0_, ...), custom_call_target="tpu_custom_call" | custom-call | tf_op jit(solution)/shard_map/outputs/pallas_call | solution.py:177
  (3 shorter events, 0.0 us)
Async XLA Ops:
  0.6 8.6 %collective-permute-start.1 = (bf16[64,640]{1,0:T(8,128)(2,1)}, bf16[64,640]{1,0:T(8,128)(2,1)S(1)}, u32[]{:S(2)}, u32[]{:S(2)}) collective-permute-start(bf16[64,640]{1,0:T(8,128)(2,1)} %bitcast.8), channel_id=1, source_target_pairs={{0,12},{4,8},{8,4},{12,0},{1,13},{5,9},{9,5},{13,1},{2,14},{6,10},... | collective-permute-start | bytes 245768 | tf_op jit(solution)/shard_map/ppermute | solution.py:213
  3.1 1.8 %collective-permute-start = (bf16[64,640]{1,0:T(8,128)(2,1)}, bf16[64,640]{1,0:T(8,128)(2,1)S(1)}, u32[]{:S(2)}, u32[]{:S(2)}) collective-permute-start(bf16[64,640]{1,0:T(8,128)(2,1)} %bitcast.9), channel_id=1, source_target_pairs={{0,4},{4,0},{8,12},{12,8},{1,5},{5,1},{9,13},{13,9},{2,6},{6,2},{1... | collective-permute-start | bytes 245768 | tf_op jit(solution)/shard_map/ppermute | solution.py:212
  3.8 1.1 %copy-start.2 = (bf16[64,1,640]{2,0,1:T(8,128)(2,1)S(1)}, bf16[64,1,640]{2,0,1:T(8,128)(2,1)}, u32[]{:S(2)}) copy-start(bf16[64,1,640]{2,0,1:T(8,128)(2,1)} %param.3) | copy-start | bytes 245764
  3.8 5.5 %copy-start = (bf16[27,64,256]{2,1,0:T(8,128)(2,1)S(1)}, bf16[27,64,256]{2,1,0:T(8,128)(2,1)}, u32[]{:S(2)}) copy-start(bf16[27,64,256]{2,1,0:T(8,128)(2,1)} %param.4) | copy-start | bytes 2654212
  3.8 5.5 %copy-start.1 = (bf16[64,1,640]{2,0,1:T(8,128)(2,1)S(1)}, bf16[64,1,640]{2,0,1:T(8,128)(2,1)}, u32[]{:S(2)}) copy-start(bf16[64,1,640]{2,0,1:T(8,128)(2,1)} %param.5) | copy-start | bytes 245764
  4.9 7.5 %collective-permute-start.4 = (bf16[64,640]{1,0:T(8,128)(2,1)S(1)}, bf16[64,640]{1,0:T(8,128)(2,1)S(1)}, u32[]{:S(2)}, u32[]{:S(2)}) collective-permute-start(bf16[64,640]{1,0:T(8,128)(2,1)S(1)} %bitcast.13), channel_id=1, source_target_pairs={{0,3},{1,2},{2,1},{3,0},{4,7},{5,6},{6,5},{7,4},{8,11},{9,10},{10,... | collective-permute-start | bytes 245768 | tf_op jit(solution)/shard_map/ppermute | solution.py:216
  8.5 7.5 %collective-permute-start.3 = (bf16[64,640]{1,0:T(8,128)(2,1)S(1)}, bf16[64,640]{1,0:T(8,128)(2,1)S(1)}, u32[]{:S(2)}, u32[]{:S(2)}) collective-permute-start(bf16[64,640]{1,0:T(8,128)(2,1)S(1)} %bitcast.14), channel_id=1, source_target_pairs={{0,2},{1,3},{2,0},{3,1},{4,6},{5,7},{6,4},{7,5},{8,10},{9,11},{10,... | collective-permute-start | bytes 245768 | tf_op jit(solution)/shard_map/ppermute | solution.py:216
  8.5 7.5 %collective-permute-start.2 = (bf16[64,640]{1,0:T(8,128)(2,1)S(1)}, bf16[64,640]{1,0:T(8,128)(2,1)S(1)}, u32[]{:S(2)}, u32[]{:S(2)}) collective-permute-start(bf16[64,640]{1,0:T(8,128)(2,1)S(1)} %bitcast.15), channel_id=1, source_target_pairs={{0,1},{1,0},{2,3},{3,2},{4,5},{5,4},{6,7},{7,6},{8,9},{9,8},{10,11... | collective-permute-start | bytes 245768 | tf_op jit(solution)/shard_map/ppermute | solution.py:216
  11.1 7.5 %collective-permute-start.5 = (f32[64,640]{1,0:T(8,128)S(1)}, f32[64,640]{1,0:T(8,128)S(1)}, u32[]{:S(2)}, u32[]{:S(2)}) collective-permute-start(f32[64,640]{1,0:T(8,128)S(1)} %get-tuple-element.24), channel_id=1, source_target_pairs={{0,1},{1,0},{2,3},{3,2},{4,5},{5,4},{6,7},{7,6},{8,9},{9,8},{10,11... | collective-permute-start | bytes 491528 | tf_op jit(solution)/shard_map/ppermute | solution.py:228
  16.6 13.5 %collective-permute-start.10 = (bf16[256,640]{1,0:T(8,128)(2,1)S(1)}, bf16[256,640]{1,0:T(8,128)(2,1)S(1)}, u32[]{:S(2)}, u32[]{:S(2)}) collective-permute-start(bf16[256,640]{1,0:T(8,128)(2,1)S(1)} %get-tuple-element.20.f_ref.refs_6_), channel_id=1, source_target_pairs={{0,12},{4,8},{8,4},{12,0},{1,13},{5,9},{9,5},{13,1},{2,14},{6,10},... | collective-permute-start | bytes 983048 | tf_op jit(solution)/shard_map/ppermute | solution.py:241
  16.7 9.0 %collective-permute-start.7 = (f32[64,640]{1,0:T(8,128)S(1)}, f32[64,640]{1,0:T(8,128)S(1)}, u32[]{:S(2)}, u32[]{:S(2)}) collective-permute-start(f32[64,640]{1,0:T(8,128)S(1)} %get-tuple-element.25), channel_id=1, source_target_pairs={{0,1},{1,0},{2,3},{3,2},{4,5},{5,4},{6,7},{7,6},{8,9},{9,8},{10,11... | collective-permute-start | bytes 491528 | tf_op jit(solution)/shard_map/ppermute | solution.py:231
  18.6 10.4 %collective-permute-start.6 = (f32[64,640]{1,0:T(8,128)S(1)}, f32[64,640]{1,0:T(8,128)S(1)}, u32[]{:S(2)}, u32[]{:S(2)}) collective-permute-start(f32[64,640]{1,0:T(8,128)S(1)} %fold.1), channel_id=1, source_target_pairs={{0,2},{1,3},{2,0},{3,1},{4,6},{5,7},{6,4},{7,5},{8,10},{9,11},{10,... | collective-permute-start | bytes 491528 | tf_op jit(solution)/shard_map/ppermute | solution.py:230
  19.9 10.2 %collective-permute-start.9 = (bf16[128,640]{1,0:T(8,128)(2,1)S(1)}, bf16[128,640]{1,0:T(8,128)(2,1)S(1)}, u32[]{:S(2)}, u32[]{:S(2)}) collective-permute-start(bf16[128,640]{1,0:T(8,128)(2,1)S(1)} %get-tuple-element.29), channel_id=1, source_target_pairs={{0,4},{4,0},{8,12},{12,8},{1,5},{5,1},{9,13},{13,9},{2,6},{6,2},{1... | collective-permute-start | bytes 491528 | tf_op jit(solution)/shard_map/ppermute | solution.py:242
  21.5 8.6 %collective-permute-start.8 = (f32[64,640]{1,0:T(8,128)S(1)}, f32[64,640]{1,0:T(8,128)S(1)}, u32[]{:S(2)}, u32[]{:S(2)}) collective-permute-start(f32[64,640]{1,0:T(8,128)S(1)} %get-tuple-element.27), channel_id=1, source_target_pairs={{0,4},{4,0},{8,12},{12,8},{1,5},{5,1},{9,13},{13,9},{2,6},{6,2},{1... | collective-permute-start | bytes 491528 | tf_op jit(solution)/shard_map/ppermute | solution.py:254
  25.7 4.4 %collective-permute-start.11 = (bf16[64,640]{1,0:T(8,128)(2,1)S(1)}, bf16[64,640]{1,0:T(8,128)(2,1)S(1)}, u32[]{:S(2)}, u32[]{:S(2)}) collective-permute-start(bf16[64,640]{1,0:T(8,128)(2,1)S(1)} %get-tuple-element.30), channel_id=1, source_target_pairs={{0,8},{4,12},{8,0},{12,4},{1,9},{5,13},{9,1},{13,5},{2,10},{6,14},... | collective-permute-start | bytes 245768 | tf_op jit(solution)/shard_map/ppermute | solution.py:244

commit v12 on v9

--- a/solution.py
+++ b/solution.py
@@ -13,7 +13,7 @@
 CELLS = NX * NY
 F32 = jnp.float32
 BF16 = jnp.bfloat16
-W_BEGIN, W_GRAD, W_EARLY, W_TOTAL, W_OUT = 8, 1, 4, 0, 0
+W_GATHER, W_EARLY, W_BEGIN, W_GRAD, W_FOLD, W_TOTAL, W_OUT = 2, 0, 8, 1, 0, 1, 0
 VMEM_BYTES = 32 * 1024 * 1024
 
 
@@ -153,15 +153,23 @@
         wg_ref[tap] = sums[at : at + blocks, dx * cols : (dx + 1) * cols]
 
 
-def total_kernel(nz, pos_ref, token_ref, *refs):
-    terms, (own_ref, even_ref, odd_ref, out_ref, back_ref) = refs[:-5], refs[-5:]
-    s = pos_ref[0]
-    inner = ((s > 0) & (s < nz - 1)).astype(F32)
-    out_ref[:, 0, :] = own_ref[...] + even_ref[...] + inner * odd_ref[...]
+def fold_kernel(own_ref, got_ref, both_ref):
+    both_ref[...] = own_ref[...] + got_ref[...]
+
+
+def input_total_kernel(token_ref, *refs):
+    terms, back_ref, done_ref = refs[:-2], refs[-2], refs[-1]
+    done_ref[...] = jnp.zeros(done_ref.shape, F32)
     total = terms[0][...]
     for term in terms[1:]:
         total = total + term[...]
     back_ref[:, 0, :] = total
+
+
+def output_total_kernel(nz, pos_ref, token_ref, own_ref, odd_ref, even_ref, out_ref):
+    s = pos_ref[0]
+    inner = ((s > 0) & (s < nz - 1)).astype(F32)
+    out_ref[:, 0, :] = own_ref[...] + even_ref[...] + inner * odd_ref[...]
 
 
 VMEM = pl.BlockSpec(memory_space=pltpu.VMEM)
@@ -218,7 +226,12 @@
         [pltpu.VMEM((27 * blocks, plane), BF16), pltpu.VMEM((channels, plane), F32)],
         W_GRAD * work,
     )
-    terms = [parts[0]] + [lax.ppermute(parts[k], "ch", mixed(k)) for k in (*range(2, nc), 1)]
+    terms = [parts[0]]
+    for k in range(2, nc, 2):
+        got = lax.ppermute(parts[k + 1], "ch", mixed(1))
+        (both,) = kernel_call(fold_kernel, "fold", [of(blocks, F32)], [parts[k], got], weight=W_FOLD * work)
+        terms.append(lax.ppermute(both, "ch", mixed(k)))
+    terms.append(lax.ppermute(parts[1], "ch", mixed(1)))
 
     far_rows = cols if nz == 4 else cols + blocks
     f_all, to_even, to_odd, *packs = kernel_call(
@@ -227,6 +240,7 @@
         [of(channels, BF16), of(cols + blocks, BF16), of(cols, BF16)]
         + [of(far_rows, BF16)] * (nz - 3),
         [pos, token, cot, cot_odd] + pieces,
+        weight=W_GATHER * work,
     )
     g_odd = lax.ppermute(to_odd, "sp", odd_pairs)
     far = [
@@ -253,12 +267,14 @@
         W_OUT * work,
     )
     block = jax.ShapeDtypeStruct((blocks, 1, plane), F32)
-    output, back = kernel_call(
-        functools.partial(total_kernel, nz),
-        "total",
-        [block, block],
-        [pos, last, *terms, out_own, out_even, out_odd],
-        weight=W_TOTAL * work,
+    back, done = kernel_call(
+        input_total_kernel, "input_total", [block, small], [last] + terms, weight=W_TOTAL * work
+    )
+    (output,) = kernel_call(
+        functools.partial(output_total_kernel, nz),
+        "output_total",
+        [block],
+        [pos, done, out_own, out_odd, out_even],
     )
     return (output, back, weight_grad)
 

time: 37.2 us -> 32.4 us (0.87)
  waiting for transfers between devices: 12.7 us -> 7.91 us
  Pallas kernels: 8.56 us -> 9.27 us
  starting transfers between devices: 15 us -> 14.3 us
    ppermute x3, waiting for transfers between devices: 8.52 us -> 3.57 us  [per_device(): pieces = [feat] + [lax.ppermute(feat, 'ch', mixed(k)) for k in range(1, nc)]]
    ppermute x3, waiting for transfers between devices: 0.06 us -> 3.28 us  [the longest x1 3.28 us: per_device(): terms.append(lax.ppermute(both, 'ch', mixed(k)))]
    ppermute x1, waiting for transfers between devices: 1.47 us -> 0.01 us  [per_device(): out_odd = lax.ppermute(out_odd, 'sp', odd_pairs)]
    ppermute x1, starting transfers between devices: 1.69 us -> 0.42 us  [per_device(): out_odd = lax.ppermute(out_odd, 'sp', odd_pairs)]
    ppermute x1, waiting for transfers between devices: 1.21 us -> 0.01 us  [per_device(): lax.ppermute(packs[k - 2], 'sp', [(i, (i + k) % nz) for i in range(nz)])]
    pallas_call x6 -> x8, Pallas kernels: 8.56 us -> 9.27 us  [kernel_call(): pl.pallas_call(body, out_shape=outs, in_specs=[SMEM if a.dtype == jnp.int...]
    ppermute x1, starting transfers between devices: 0.6 us -> 1.06 us  [per_device(): lax.ppermute(packs[k - 2], 'sp', [(i, (i + k) % nz) for i in range(nz)])]
  transfers between devices with their start and end apart: 13 -> 13, of which waited for: 6 -> 3; matrix products, arithmetic and copies ran while one was open for 0% -> 0% of each run, Pallas kernels for 20% -> 25%
where the time goes in v12:
time: 32.4 us; the launch traced here: 32.2 us
  starting transfers between devices  14.3 us (44%)
  Pallas kernels  9.27 us (29%)
  waiting for transfers between devices  7.91 us (24%)
  between operations  0.7 us (2%)
    pallas_call x8, Pallas kernels, kernel_call(): pl.pallas_call(body, out_shape=outs, in_specs=[SMEM if a.dtype == jnp.int...  9.27 us
    ppermute x3, starting transfers between devices, per_device(): pieces = [feat] + [lax.ppermute(feat, 'ch', mixed(k)) for k in range(1, nc)]  4.39 us
    ppermute x3, waiting for transfers between devices, per_device(): pieces = [feat] + [lax.ppermute(feat, 'ch', mixed(k)) for k in range(1, nc)]  3.57 us
    ppermute x1, waiting for transfers between devices, per_device(): terms.append(lax.ppermute(both, 'ch', mixed(k)))  3.28 us
    ppermute x1, starting transfers between devices, per_device(): cot_odd = lax.ppermute(cot, 'sp', odd_pairs)  2.44 us
    ppermute x1, starting transfers between devices, per_device(): terms.append(lax.ppermute(both, 'ch', mixed(k)))  1.77 us
    ppermute x1, starting transfers between devices, per_device(): got = lax.ppermute(parts[k + 1], 'ch', mixed(1))  1.3 us
    ppermute x1, starting transfers between devices, per_device(): lax.ppermute(packs[k - 2], 'sp', [(i, (i + k) % nz) for i in range(nz)])  1.06 us
  transfers between devices with their start and end apart: 13, of which 3 were waited for; matrix products, arithmetic and copies ran while one was open for 0% of the time, Pallas kernels for 25%

profile of v12, /device:TPU:0, one launch (start us, length us, event | category | flops | bytes accessed | tf_op | source)
XLA Modules:
  0.0 32.2 jit_solution(12794509661470153103)
XLA Ops:
  0.6 2.4 %collective-permute-start.1 = (bf16[64,640]{1,0:T(8,128)(2,1)}, bf16[64,640]{1,0:T(8,128)(2,1)S(1)}, u32[]{:S(2)}, u32[]{:S(2)}) collective-permute-start(bf16[64,640]{1,0:T(8,128)(2,1)} %bitcast.7), channel_id=1, source_target_pairs={{0,12},{4,8},{8,4},{12,0},{1,13},{5,9},{9,5},{13,1},{2,14},{6,10},... | collective-permute-start | bytes 245768 | tf_op jit(solution)/shard_map/ppermute | solution.py:216
  3.1 0.7 %collective-permute-start = (bf16[64,640]{1,0:T(8,128)(2,1)}, bf16[64,640]{1,0:T(8,128)(2,1)S(1)}, u32[]{:S(2)}, u32[]{:S(2)}) collective-permute-start(bf16[64,640]{1,0:T(8,128)(2,1)} %bitcast.8), channel_id=1, source_target_pairs={{0,4},{4,0},{8,12},{12,8},{1,5},{5,1},{9,13},{13,9},{2,6},{6,2},{1... | collective-permute-start | bytes 245768 | tf_op jit(solution)/shard_map/ppermute | solution.py:215
  3.8 0.0 copy-start.2
  3.8 0.0 copy-start
  3.8 0.0 copy-start.1
  3.8 0.1 pad_add_fusion.pos_ref
  3.8 1.0 %collective-permute-done.even_ref.ce_ref = bf16[64,640]{1,0:T(8,128)(2,1)S(1)} collective-permute-done((bf16[64,640]{1,0:T(8,128)(2,1)}, bf16[64,640]{1,0:T(8,128)(2,1)S(1)}, u32[]{:S(2)}, u32[]{:S(2)}) %collective-permute-start) | collective-permute-done | bytes 81952 | tf_op jit(solution)/shard_map/ppermute | solution.py:215
  4.9 0.0 copy-done.2
  4.9 3.6 %collective-permute-start.4 = (bf16[64,640]{1,0:T(8,128)(2,1)S(1)}, bf16[64,640]{1,0:T(8,128)(2,1)S(1)}, u32[]{:S(2)}, u32[]{:S(2)}) collective-permute-start(bf16[64,640]{1,0:T(8,128)(2,1)S(1)} %bitcast.12), channel_id=1, source_target_pairs={{0,3},{1,2},{2,1},{3,0},{4,7},{5,6},{6,5},{7,4},{8,11},{9,10},{10,... | collective-permute-start | bytes 245768 | tf_op jit(solution)/shard_map/ppermute | solution.py:219
  8.5 0.0 collective-permute-start.3
  8.5 0.8 %collective-permute-start.2 = (bf16[64,640]{1,0:T(8,128)(2,1)S(1)}, bf16[64,640]{1,0:T(8,128)(2,1)S(1)}, u32[]{:S(2)}, u32[]{:S(2)}) collective-permute-start(bf16[64,640]{1,0:T(8,128)(2,1)S(1)} %bitcast.14), channel_id=1, source_target_pairs={{0,1},{1,0},{2,3},{3,2},{4,5},{5,4},{6,7},{7,6},{8,9},{9,8},{10,11... | collective-permute-start | bytes 245768 | tf_op jit(solution)/shard_map/ppermute | solution.py:219
  9.3 0.0 collective-permute-done.1.odd_ref.near_ref.co_ref
  9.3 0.0 copy-done
  9.3 0.0 copy-done.1
  9.3 1.8 %input_grad.1 = (f32[64,640]{1,0:T(8,128)S(1)}, f32[64,640]{1,0:T(8,128)S(1)}, f32[64,640]{1,0:T(8,128)S(1)}, f32[64,640]{1,0:T(8,128)S(1)}, f32[8,128]{1,0:T(8,128)S(1)}) custom-call(s32[2]{0:T(128)S(1)} %pad_add_fusion.pos_ref, f32[8,128]{1,0:T(8,128)S(1)} %begin.1.begin_ref, bf16[64,640]{1,0:T(8,128)(2,1)S(1)} %bitcast.9, ...), custom_call_target="tpu_custom_call" | custom-call | flops 566231040 | tf_op jit(solution)/shard_map/input_grad/pallas_call | solution.py:180
  11.1 1.3 %collective-permute-start.8 = (f32[64,640]{1,0:T(8,128)S(1)}, f32[64,640]{1,0:T(8,128)S(1)}, u32[]{:S(2)}, u32[]{:S(2)}) collective-permute-start(f32[64,640]{1,0:T(8,128)S(1)} %get-tuple-element.33), channel_id=1, source_target_pairs={{0,1},{1,0},{2,3},{3,2},{4,5},{5,4},{6,7},{7,6},{8,9},{9,8},{10,11... | collective-permute-start | bytes 491528 | tf_op jit(solution)/shard_map/ppermute | solution.py:231
  12.4 0.0 collective-permute-done.4.refs_3_
  12.4 3.6 %collective-permute-done.3.refs_2_ = bf16[64,640]{1,0:T(8,128)(2,1)S(1)} collective-permute-done((bf16[64,640]{1,0:T(8,128)(2,1)S(1)}, bf16[64,640]{1,0:T(8,128)(2,1)S(1)}, u32[]{:S(2)}, u32[]{:S(2)}) %collective-permute-start.3) | collective-permute-done | bytes 81952 | tf_op jit(solution)/shard_map/ppermute | solution.py:219
  16.0 0.0 collective-permute-done.2.refs_1_
  16.0 0.6 %gather.1 = (bf16[256,640]{1,0:T(8,128)(2,1)S(1)}, bf16[128,640]{1,0:T(8,128)(2,1)S(1)}, bf16[64,640]{1,0:T(8,128)(2,1)S(1)}, bf16[64,640]{1,0:T(8,128)(2,1)S(1)}) custom-call(s32[2]{0:T(128)S(1)} %pad_add_fusion.pos_ref, f32[8,128]{1,0:T(8,128)S(1)} %get-tuple-element.23.token_ref, bf16[64,640]{1,0:T(8,128)(2,1)S(1)} %bitcast.10, ...), custom_call_target="tpu_custom_call" | custom-call | flops 1132462080 | tf_op jit(solution)/shard_map/gather/pallas_call | solution.py:180
  16.6 0.1 collective-permute-start.6
  16.7 1.1 %collective-permute-start.7 = (bf16[64,640]{1,0:T(8,128)(2,1)S(1)}, bf16[64,640]{1,0:T(8,128)(2,1)S(1)}, u32[]{:S(2)}, u32[]{:S(2)}) collective-permute-start(bf16[64,640]{1,0:T(8,128)(2,1)S(1)} %get-tuple-element.29), channel_id=1, source_target_pairs={{0,8},{4,12},{8,0},{12,4},{1,9},{5,13},{9,1},{13,5},{2,10},{6,14},... | collective-permute-start | bytes 245768 | tf_op jit(solution)/shard_map/ppermute | solution.py:247
  17.7 0.9 %collective-permute-start.10 = (f32[64,640]{1,0:T(8,128)S(1)}, f32[64,640]{1,0:T(8,128)S(1)}, u32[]{:S(2)}, u32[]{:S(2)}) collective-permute-start(f32[64,640]{1,0:T(8,128)S(1)} %get-tuple-element.34), channel_id=1, source_target_pairs={{0,1},{1,0},{2,3},{3,2},{4,5},{5,4},{6,7},{7,6},{8,9},{9,8},{10,11... | collective-permute-start | bytes 491528 | tf_op jit(solution)/shard_map/ppermute | solution.py:234
  18.6 1.0 %collective-permute-start.5 = (bf16[128,640]{1,0:T(8,128)(2,1)S(1)}, bf16[128,640]{1,0:T(8,128)(2,1)S(1)}, u32[]{:S(2)}, u32[]{:S(2)}) collective-permute-start(bf16[128,640]{1,0:T(8,128)(2,1)S(1)} %get-tuple-element.27), channel_id=1, source_target_pairs={{0,4},{4,0},{8,12},{12,8},{1,5},{5,1},{9,13},{13,9},{2,6},{6,2},{1... | collective-permute-start | bytes 491528 | tf_op jit(solution)/shard_map/ppermute | solution.py:250
  19.6 0.0 collective-permute-done.8.got_ref
  19.6 1.8 %collective-permute-start.9 = (f32[64,640]{1,0:T(8,128)S(1)}, f32[64,640]{1,0:T(8,128)S(1)}, u32[]{:S(2)}, u32[]{:S(2)}) collective-permute-start(f32[64,640]{1,0:T(8,128)S(1)} %fold.1), channel_id=1, source_target_pairs={{0,2},{1,3},{2,0},{3,1},{4,6},{5,7},{6,4},{7,5},{8,10},{9,11},{10,... | collective-permute-start | bytes 491528 | tf_op jit(solution)/shard_map/ppermute | solution.py:233
  21.4 2.0 %early.1 = (f32[64,640]{1,0:T(8,128)S(1)}, f32[64,640]{1,0:T(8,128)S(1)}, f32[64,640]{1,0:T(8,128)S(1)}, bf16[3,192,640]{2,1,0:T(8,128)(2,1)S(1)}) custom-call(s32[2]{0:T(128)S(1)} %pad_add_fusion.pos_ref, bf16[1728,256]{1,0:T(8,128)(2,1)S(1)} %bitcast.6, bf16[256,640]{1,0:T(8,128)(2,1)S(1)} %get-tuple-element.25.f_ref, bf16[64,640]{1,0:T(8,128)(2,1)S(1)} %bitcast.11, ...), custom_call_target="tpu_custom_call" | custom-call | tf_op jit(solution)/shard_map/early/pallas_call | solution.py:180
  23.4 0.0 collective-permute-done.6.go_ref
  23.4 0.4 %collective-permute-start.11 = (f32[64,640]{1,0:T(8,128)S(1)}, f32[64,640]{1,0:T(8,128)S(1)}, u32[]{:S(2)}, u32[]{:S(2)}) collective-permute-start(f32[64,640]{1,0:T(8,128)S(1)} %get-tuple-element.37), channel_id=1, source_target_pairs={{0,12},{4,8},{8,4},{12,0},{1,13},{5,9},{9,5},{13,1},{2,14},{6,10},... | collective-permute-start | bytes 491528 | tf_op jit(solution)/shard_map/ppermute | solution.py:258
  23.8 0.0 collective-permute-done.7.refs_0_
  23.8 0.3 collective-permute-start.12
  24.1 0.0 collective-permute-done.5.ge_ref
  24.1 2.8 %weight_grad.1 = (f32[27,64,64]{2,1,0:T(8,128)}, f32[8,128]{1,0:T(8,128)S(1)}) custom-call(s32[2]{0:T(128)S(1)} %pad_add_fusion.pos_ref, bf16[3,192,640]{2,1,0:T(8,128)(2,1)S(1)} %get-tuple-element.26.moved_ref, bf16[256,640]{1,0:T(8,128)(2,1)S(1)} %get-tuple-element.25.f_ref, bf16[128,640]{1,0:T(8,128)(2,1)S(1)} %collective-permute-done.5.ge_ref, ...), custom_call_target="tpu_custom_call" | custom-call | tf_op jit(solution)/shard_map/weight_grad/pallas_call | solution.py:180
  26.9 0.0 collective-permute-done.10.refs_2_
  26.9 3.3 %collective-permute-done.9.refs_1_ = f32[64,640]{1,0:T(8,128)S(1)} collective-permute-done((f32[64,640]{1,0:T(8,128)S(1)}, f32[64,640]{1,0:T(8,128)S(1)}, u32[]{:S(2)}, u32[]{:S(2)}) %collective-permute-start.9) | collective-permute-done | bytes 163872 | tf_op jit(solution)/shard_map/ppermute | solution.py:233
  30.2 0.7 %input_total.1 = (f32[64,1,640]{2,1,0:T(1,128)}, f32[8,128]{1,0:T(8,128)S(1)}) custom-call(f32[8,128]{1,0:T(8,128)S(1)} %get-tuple-element.30.token_ref, f32[64,640]{1,0:T(8,128)S(1)} %get-tuple-element.31.refs_0_, f32[64,640]{1,0:T(8,128)S(1)} %collective-permute-done.9.refs_1_, f32[64,640]{1,0:T(8,128)S(1)} %collective-permute-done.10.refs_2_), custom_call_target="tpu_custom_call" | custom-call | flops 566231040 | tf_op jit(solution)/shard_map/input_total/pallas_call | solution.py:180
  30.9 0.0 collective-permute-done.11.odd_ref
  30.9 0.0 collective-permute-done.12.even_ref
  31.0 1.3 %output_total.1 = f32[64,1,640]{2,1,0:T(1,128)} custom-call(s32[2]{0:T(128)S(1)} %pad_add_fusion.pos_ref, f32[8,128]{1,0:T(8,128)S(1)} %get-tuple-element.35.token_ref, f32[64,640]{1,0:T(8,128)S(1)} %get-tuple-element.36.own_ref, f32[64,640]{1,0:T(8,128)S(1)} %collective-permute-done.11.odd_ref, f32[64,640]{1,0:T(8,128)S(1)} %collective-permute-done.12.even_ref), custom_call_target="tpu_custom_call" | custom-call | tf_op jit(solution)/shard_map/output_total/pallas_call | solution.py:180
  (2 shorter events, 0.0 us)
Async XLA Ops:
  0.6 8.6 %collective-permute-start.1 = (bf16[64,640]{1,0:T(8,128)(2,1)}, bf16[64,640]{1,0:T(8,128)(2,1)S(1)}, u32[]{:S(2)}, u32[]{:S(2)}) collective-permute-start(bf16[64,640]{1,0:T(8,128)(2,1)} %bitcast.7), channel_id=1, source_target_pairs={{0,12},{4,8},{8,4},{12,0},{1,13},{5,9},{9,5},{13,1},{2,14},{6,10},... | collective-permute-start | bytes 245768 | tf_op jit(solution)/shard_map/ppermute | solution.py:216
  3.1 1.8 %collective-permute-start = (bf16[64,640]{1,0:T(8,128)(2,1)}, bf16[64,640]{1,0:T(8,128)(2,1)S(1)}, u32[]{:S(2)}, u32[]{:S(2)}) collective-permute-start(bf16[64,640]{1,0:T(8,128)(2,1)} %bitcast.8), channel_id=1, source_target_pairs={{0,4},{4,0},{8,12},{12,8},{1,5},{5,1},{9,13},{13,9},{2,6},{6,2},{1... | collective-permute-start | bytes 245768 | tf_op jit(solution)/shard_map/ppermute | solution.py:215
  3.8 1.1 %copy-start.2 = (bf16[64,1,640]{2,0,1:T(8,128)(2,1)S(1)}, bf16[64,1,640]{2,0,1:T(8,128)(2,1)}, u32[]{:S(2)}) copy-start(bf16[64,1,640]{2,0,1:T(8,128)(2,1)} %param.3) | copy-start | bytes 245764
  3.8 5.5 %copy-start = (bf16[27,64,256]{2,1,0:T(8,128)(2,1)S(1)}, bf16[27,64,256]{2,1,0:T(8,128)(2,1)}, u32[]{:S(2)}) copy-start(bf16[27,64,256]{2,1,0:T(8,128)(2,1)} %param.4) | copy-start | bytes 2654212
  3.8 5.5 %copy-start.1 = (bf16[64,1,640]{2,0,1:T(8,128)(2,1)S(1)}, bf16[64,1,640]{2,0,1:T(8,128)(2,1)}, u32[]{:S(2)}) copy-start(bf16[64,1,640]{2,0,1:T(8,128)(2,1)} %param.5) | copy-start | bytes 245764
  4.9 7.5 %collective-permute-start.4 = (bf16[64,640]{1,0:T(8,128)(2,1)S(1)}, bf16[64,640]{1,0:T(8,128)(2,1)S(1)}, u32[]{:S(2)}, u32[]{:S(2)}) collective-permute-start(bf16[64,640]{1,0:T(8,128)(2,1)S(1)} %bitcast.12), channel_id=1, source_target_pairs={{0,3},{1,2},{2,1},{3,0},{4,7},{5,6},{6,5},{7,4},{8,11},{9,10},{10,... | collective-permute-start | bytes 245768 | tf_op jit(solution)/shard_map/ppermute | solution.py:219
  8.5 7.5 %collective-permute-start.3 = (bf16[64,640]{1,0:T(8,128)(2,1)S(1)}, bf16[64,640]{1,0:T(8,128)(2,1)S(1)}, u32[]{:S(2)}, u32[]{:S(2)}) collective-permute-start(bf16[64,640]{1,0:T(8,128)(2,1)S(1)} %bitcast.13), channel_id=1, source_target_pairs={{0,2},{1,3},{2,0},{3,1},{4,6},{5,7},{6,4},{7,5},{8,10},{9,11},{10,... | collective-permute-start | bytes 245768 | tf_op jit(solution)/shard_map/ppermute | solution.py:219
  8.5 7.5 %collective-permute-start.2 = (bf16[64,640]{1,0:T(8,128)(2,1)S(1)}, bf16[64,640]{1,0:T(8,128)(2,1)S(1)}, u32[]{:S(2)}, u32[]{:S(2)}) collective-permute-start(bf16[64,640]{1,0:T(8,128)(2,1)S(1)} %bitcast.14), channel_id=1, source_target_pairs={{0,1},{1,0},{2,3},{3,2},{4,5},{5,4},{6,7},{7,6},{8,9},{9,8},{10,11... | collective-permute-start | bytes 245768 | tf_op jit(solution)/shard_map/ppermute | solution.py:219
  11.1 8.5 %collective-permute-start.8 = (f32[64,640]{1,0:T(8,128)S(1)}, f32[64,640]{1,0:T(8,128)S(1)}, u32[]{:S(2)}, u32[]{:S(2)}) collective-permute-start(f32[64,640]{1,0:T(8,128)S(1)} %get-tuple-element.33), channel_id=1, source_target_pairs={{0,1},{1,0},{2,3},{3,2},{4,5},{5,4},{6,7},{7,6},{8,9},{9,8},{10,11... | collective-permute-start | bytes 491528 | tf_op jit(solution)/shard_map/ppermute | solution.py:231
  16.6 6.8 %collective-permute-start.6 = (bf16[64,640]{1,0:T(8,128)(2,1)S(1)}, bf16[64,640]{1,0:T(8,128)(2,1)S(1)}, u32[]{:S(2)}, u32[]{:S(2)}) collective-permute-start(bf16[64,640]{1,0:T(8,128)(2,1)S(1)} %get-tuple-element.28), channel_id=1, source_target_pairs={{0,12},{4,8},{8,4},{12,0},{1,13},{5,9},{9,5},{13,1},{2,14},{6,10},... | collective-permute-start | bytes 245768 | tf_op jit(solution)/shard_map/ppermute | solution.py:245
  16.7 7.1 %collective-permute-start.7 = (bf16[64,640]{1,0:T(8,128)(2,1)S(1)}, bf16[64,640]{1,0:T(8,128)(2,1)S(1)}, u32[]{:S(2)}, u32[]{:S(2)}) collective-permute-start(bf16[64,640]{1,0:T(8,128)(2,1)S(1)} %get-tuple-element.29), channel_id=1, source_target_pairs={{0,8},{4,12},{8,0},{12,4},{1,9},{5,13},{9,1},{13,5},{2,10},{6,14},... | collective-permute-start | bytes 245768 | tf_op jit(solution)/shard_map/ppermute | solution.py:247
  17.7 9.2 %collective-permute-start.10 = (f32[64,640]{1,0:T(8,128)S(1)}, f32[64,640]{1,0:T(8,128)S(1)}, u32[]{:S(2)}, u32[]{:S(2)}) collective-permute-start(f32[64,640]{1,0:T(8,128)S(1)} %get-tuple-element.34), channel_id=1, source_target_pairs={{0,1},{1,0},{2,3},{3,2},{4,5},{5,4},{6,7},{7,6},{8,9},{9,8},{10,11... | collective-permute-start | bytes 491528 | tf_op jit(solution)/shard_map/ppermute | solution.py:234
  18.6 5.5 %collective-permute-start.5 = (bf16[128,640]{1,0:T(8,128)(2,1)S(1)}, bf16[128,640]{1,0:T(8,128)(2,1)S(1)}, u32[]{:S(2)}, u32[]{:S(2)}) collective-permute-start(bf16[128,640]{1,0:T(8,128)(2,1)S(1)} %get-tuple-element.27), channel_id=1, source_target_pairs={{0,4},{4,0},{8,12},{12,8},{1,5},{5,1},{9,13},{13,9},{2,6},{6,2},{1... | collective-permute-start | bytes 491528 | tf_op jit(solution)/shard_map/ppermute | solution.py:250
  19.6 10.6 %collective-permute-start.9 = (f32[64,640]{1,0:T(8,128)S(1)}, f32[64,640]{1,0:T(8,128)S(1)}, u32[]{:S(2)}, u32[]{:S(2)}) collective-permute-start(f32[64,640]{1,0:T(8,128)S(1)} %fold.1), channel_id=1, source_target_pairs={{0,2},{1,3},{2,0},{3,1},{4,6},{5,7},{6,4},{7,5},{8,10},{9,11},{10,... | collective-permute-start | bytes 491528 | tf_op jit(solution)/shard_map/ppermute | solution.py:233
  23.4 7.6 %collective-permute-start.11 = (f32[64,640]{1,0:T(8,128)S(1)}, f32[64,640]{1,0:T(8,128)S(1)}, u32[]{:S(2)}, u32[]{:S(2)}) collective-permute-start(f32[64,640]{1,0:T(8,128)S(1)} %get-tuple-element.37), channel_id=1, source_target_pairs={{0,12},{4,8},{8,4},{12,0},{1,13},{5,9},{9,5},{13,1},{2,14},{6,10},... | collective-permute-start | bytes 491528 | tf_op jit(solution)/shard_map/ppermute | solution.py:258
  23.8 7.1 %collective-permute-start.12 = (f32[64,640]{1,0:T(8,128)S(1)}, f32[64,640]{1,0:T(8,128)S(1)}, u32[]{:S(2)}, u32[]{:S(2)}) collective-permute-start(f32[64,640]{1,0:T(8,128)S(1)} %get-tuple-element.38), channel_id=1, source_target_pairs={{0,4},{4,0},{8,12},{12,8},{1,5},{5,1},{9,13},{13,9},{2,6},{6,2},{1... | collective-permute-start | bytes 491528 | tf_op jit(solution)/shard_map/ppermute | solution.py:259

commit v13 on v12

--- a/solution.py
+++ b/solution.py
@@ -34,11 +34,11 @@
     return lax.rem(((s + 1) ^ 1) + nz - 1, nz)
 
 
-def gather_kernel(nz, nc, pos_ref, token_ref, cot_ref, near_ref, *refs):
+def gather_kernel(nz, nc, token_ref, cot_ref, near_ref, *refs):
     pieces, (f_ref, even_ref, odd_ref), packs = refs[:nc], refs[nc : nc + 3], refs[nc + 3 :]
     blocks = cot_ref.shape[0]
     cols = f_ref.shape[0] // nz
-    s, c = pos_ref[0], pos_ref[1]
+    s, c = lax.axis_index("sp"), lax.axis_index("ch")
 
     def block_for(goal):
         return f_ref[pl.ds(pl.multiple_of(goal * cols, cols), cols), :]
@@ -66,11 +66,11 @@
     token_ref[...] = jnp.zeros(token_ref.shape, F32)
 
 
-def input_grad_kernel(nz, nc, pos_ref, begin_ref, cot_ref, even_ref, odd_ref, w_ref, *refs):
+def input_grad_kernel(nz, nc, begin_ref, cot_ref, even_ref, odd_ref, w_ref, *refs):
     parts = refs[:nc]
     token_ref, cols_ref, sum_ref = refs[nc:]
     blocks = even_ref.shape[0]
-    s, c = pos_ref[0], pos_ref[1]
+    s, c = lax.axis_index("sp"), lax.axis_index("ch")
     token_ref[...] = jnp.zeros(token_ref.shape, F32)
     even, odd = even_ref[...].astype(F32), odd_ref[...].astype(F32)
     first = s % 2 == 0
@@ -106,21 +106,21 @@
     return jnp.concatenate([shifted(plane, -dy, 0).astype(BF16) for dy in (-1, 0, 1)], 0)
 
 
-def early_kernel(pos_ref, w_ref, f_ref, cot_ref, ce_ref, co_ref, own_ref, even_ref, odd_ref, moved_ref):
-    side = 1 - 2 * lax.rem(pos_ref[0], 2)
+def early_kernel(w_ref, f_ref, cot_ref, ce_ref, co_ref, own_ref, even_ref, odd_ref, moved_ref):
+    side = 1 - 2 * lax.rem(lax.axis_index("sp"), 2)
     for ref, dz in ((odd_ref, side), (even_ref, -side), (own_ref, 0)):
         ref[...] = moved_sum(conv_part(w_ref, f_ref[...], dz))
     for i, ref in enumerate((cot_ref, ce_ref, co_ref)):
         moved_ref[i] = moved_rows(ref[...])
 
 
-def weight_grad_kernel(nz, scale, pos_ref, moved_ref, f_ref, ge_ref, go_ref, *refs):
+def weight_grad_kernel(nz, scale, moved_ref, f_ref, ge_ref, go_ref, *refs):
     packs = refs[:-4]
     wg_ref, token_ref, c_ref, g_ref = refs[-4:]
     token_ref[...] = jnp.zeros(token_ref.shape, F32)
     blocks = c_ref.shape[1] // 3
     cols = go_ref.shape[0]
-    s = pos_ref[0]
+    s = lax.axis_index("sp")
 
     empty = jnp.zeros(c_ref.shape[1:], BF16)
     c_ref[0] = empty
@@ -166,8 +166,8 @@
     back_ref[:, 0, :] = total
 
 
-def output_total_kernel(nz, pos_ref, token_ref, own_ref, odd_ref, even_ref, out_ref):
-    s = pos_ref[0]
+def output_total_kernel(nz, token_ref, own_ref, odd_ref, even_ref, out_ref):
+    s = lax.axis_index("sp")
     inner = ((s > 0) & (s < nz - 1)).astype(F32)
     out_ref[:, 0, :] = own_ref[...] + even_ref[...] + inner * odd_ref[...]
 
@@ -198,7 +198,6 @@
     w2 = weights.reshape(27 * blocks, channels)
     feat = features.reshape(blocks, plane)
     cot = cotangent.reshape(blocks, plane)
-    pos = jnp.stack([lax.axis_index("sp"), lax.axis_index("ch")]).astype(jnp.int32)
 
     even_pairs = [(i, i ^ 1) for i in range(nz)]
     odd_pairs = [(i, (((i + 1) ^ 1) - 1) % nz) for i in range(nz)]
@@ -222,7 +221,7 @@
         functools.partial(input_grad_kernel, nz, nc),
         "input_grad",
         [of(blocks, F32)] * nc + [small],
-        [pos, begin, cot, cot_even, cot_odd, w2],
+        [begin, cot, cot_even, cot_odd, w2],
         [pltpu.VMEM((27 * blocks, plane), BF16), pltpu.VMEM((channels, plane), F32)],
         W_GRAD * work,
     )
@@ -239,7 +238,7 @@
         "gather",
         [of(channels, BF16), of(cols + blocks, BF16), of(cols, BF16)]
         + [of(far_rows, BF16)] * (nz - 3),
-        [pos, token, cot, cot_odd] + pieces,
+        [token, cot, cot_odd] + pieces,
         weight=W_GATHER * work,
     )
     g_odd = lax.ppermute(to_odd, "sp", odd_pairs)
@@ -252,7 +251,7 @@
         early_kernel,
         "early",
         [of(blocks, F32)] * 3 + [jax.ShapeDtypeStruct((3, 3 * blocks, plane), BF16)],
-        [pos, w2, f_all, cot, cot_even, cot_odd],
+        [w2, f_all, cot, cot_even, cot_odd],
         weight=W_EARLY * work,
     )
     out_odd = lax.ppermute(out_odd, "sp", odd_pairs)
@@ -262,7 +261,7 @@
         functools.partial(weight_grad_kernel, nz, 1.0 / math.sqrt(nz * depth * plane)),
         "weight_grad",
         [jax.ShapeDtypeStruct((27, blocks, cols), F32), small],
-        [pos, moved, f_all, g_even, g_odd, *far],
+        [moved, f_all, g_even, g_odd, *far],
         [pltpu.VMEM((nz + 2, 3 * blocks, plane), BF16), pltpu.VMEM((nz, cols, plane), BF16)],
         W_OUT * work,
     )
@@ -274,7 +273,7 @@
         functools.partial(output_total_kernel, nz),
         "output_total",
         [block],
-        [pos, done, out_own, out_odd, out_even],
+        [done, out_own, out_odd, out_even],
     )
     return (output, back, weight_grad)
 

time: 32.4 us -> 31.3 us (0.966)
  Pallas kernels: 9.27 us -> 6.53 us
  waiting for transfers between devices: 7.91 us -> 9.64 us
    pallas_call x8, Pallas kernels: 9.27 us -> 6.53 us  [kernel_call(): pl.pallas_call(body, out_shape=outs, in_specs=[SMEM if a.dtype == jnp.int...]
    ppermute x1, waiting for transfers between devices: 0.01 us -> 0.97 us  [per_device(): terms.append(lax.ppermute(parts[1], 'ch', mixed(1)))]
    ppermute x3, waiting for transfers between devices: 3.57 us -> 4.07 us  [per_device(): pieces = [feat] + [lax.ppermute(feat, 'ch', mixed(k)) for k in range(1, nc)]]
  transfers between devices with their start and end apart: 13 -> 13, of which waited for: 3 -> 5; matrix products, arithmetic and copies ran while one was open for 0% -> 0% of each run, Pallas kernels for 25% -> 19%
where the time goes in v13:
time: 31.3 us; the launch traced here: 31.2 us
  starting transfers between devices  14.3 us (46%)
  waiting for transfers between devices  9.64 us (31%)
  Pallas kernels  6.53 us (21%)
  between operations  0.71 us (2%)
    pallas_call x8, Pallas kernels, kernel_call(): pl.pallas_call(body, out_shape=outs, in_specs=[SMEM if a.dtype == jnp.int...  6.53 us
    ppermute x3, starting transfers between devices, per_device(): pieces = [feat] + [lax.ppermute(feat, 'ch', mixed(k)) for k in range(1, nc)]  4.39 us
    ppermute x3, waiting for transfers between devices, per_device(): pieces = [feat] + [lax.ppermute(feat, 'ch', mixed(k)) for k in range(1, nc)]  4.07 us
    ppermute x1, waiting for transfers between devices, per_device(): terms.append(lax.ppermute(both, 'ch', mixed(k)))  3.44 us
    ppermute x1, starting transfers between devices, per_device(): cot_odd = lax.ppermute(cot, 'sp', odd_pairs)  2.44 us
    ppermute x1, starting transfers between devices, per_device(): terms.append(lax.ppermute(both, 'ch', mixed(k)))  1.77 us
    ppermute x1, starting transfers between devices, per_device(): got = lax.ppermute(parts[k + 1], 'ch', mixed(1))  1.31 us
    ppermute x1, waiting for transfers between devices, per_device(): cot_even = lax.ppermute(cot, 'sp', even_pairs)  1.13 us
  transfers between devices with their start and end apart: 13, of which 5 were waited for; matrix products, arithmetic and copies ran while one was open for 0% of the time, Pallas kernels for 19%

profile of v13, /device:TPU:0, one launch (start us, length us, event | category | flops | bytes accessed | tf_op | source)
XLA Modules:
  0.0 31.2 jit_solution(3463355655823752837)
XLA Ops:
  0.6 0.0 copy-start.2
  0.6 0.0 copy-start
  0.7 0.0 copy-start.1
  0.7 2.4 %collective-permute-start.1 = (bf16[64,640]{1,0:T(8,128)(2,1)}, bf16[64,640]{1,0:T(8,128)(2,1)S(1)}, u32[]{:S(2)}, u32[]{:S(2)}) collective-permute-start(bf16[64,640]{1,0:T(8,128)(2,1)} %bitcast.5), channel_id=1, source_target_pairs={{0,12},{4,8},{8,4},{12,0},{1,13},{5,9},{9,5},{13,1},{2,14},{6,10},... | collective-permute-start | bytes 245768 | tf_op jit(solution)/shard_map/ppermute | solution.py:215
  3.1 0.7 %collective-permute-start = (bf16[64,640]{1,0:T(8,128)(2,1)}, bf16[64,640]{1,0:T(8,128)(2,1)S(1)}, u32[]{:S(2)}, u32[]{:S(2)}) collective-permute-start(bf16[64,640]{1,0:T(8,128)(2,1)} %bitcast.6), channel_id=1, source_target_pairs={{0,4},{4,0},{8,12},{12,8},{1,5},{5,1},{9,13},{13,9},{2,6},{6,2},{1... | collective-permute-start | bytes 245768 | tf_op jit(solution)/shard_map/ppermute | solution.py:214
  3.8 1.1 %collective-permute-done.even_ref.ce_ref = bf16[64,640]{1,0:T(8,128)(2,1)S(1)} collective-permute-done((bf16[64,640]{1,0:T(8,128)(2,1)}, bf16[64,640]{1,0:T(8,128)(2,1)S(1)}, u32[]{:S(2)}, u32[]{:S(2)}) %collective-permute-start) | collective-permute-done | bytes 81952 | tf_op jit(solution)/shard_map/ppermute | solution.py:214
  4.9 0.0 copy-done.2
  4.9 3.6 %collective-permute-start.4 = (bf16[64,640]{1,0:T(8,128)(2,1)S(1)}, bf16[64,640]{1,0:T(8,128)(2,1)S(1)}, u32[]{:S(2)}, u32[]{:S(2)}) collective-permute-start(bf16[64,640]{1,0:T(8,128)(2,1)S(1)} %bitcast.10), channel_id=1, source_target_pairs={{0,3},{1,2},{2,1},{3,0},{4,7},{5,6},{6,5},{7,4},{8,11},{9,10},{10,... | collective-permute-start | bytes 245768 | tf_op jit(solution)/shard_map/ppermute | solution.py:218
  8.5 0.0 collective-permute-start.3
  8.5 0.8 %collective-permute-start.2 = (bf16[64,640]{1,0:T(8,128)(2,1)S(1)}, bf16[64,640]{1,0:T(8,128)(2,1)S(1)}, u32[]{:S(2)}, u32[]{:S(2)}) collective-permute-start(bf16[64,640]{1,0:T(8,128)(2,1)S(1)} %bitcast.12), channel_id=1, source_target_pairs={{0,1},{1,0},{2,3},{3,2},{4,5},{5,4},{6,7},{7,6},{8,9},{9,8},{10,11... | collective-permute-start | bytes 245768 | tf_op jit(solution)/shard_map/ppermute | solution.py:218
  9.3 0.0 collective-permute-done.1.odd_ref.near_ref.co_ref
  9.3 0.0 copy-done
  9.3 0.0 copy-done.1
  9.3 1.3 %input_grad.1 = (f32[64,640]{1,0:T(8,128)S(1)}, f32[64,640]{1,0:T(8,128)S(1)}, f32[64,640]{1,0:T(8,128)S(1)}, f32[64,640]{1,0:T(8,128)S(1)}, f32[8,128]{1,0:T(8,128)S(1)}) custom-call(f32[8,128]{1,0:T(8,128)S(1)} %begin.1.begin_ref, bf16[64,640]{1,0:T(8,128)(2,1)S(1)} %bitcast.7, bf16[64,640]{1,0:T(8,128)(2,1)S(1)} %collective-permute-done.even_ref.ce_ref, ...), custom_call_target="tpu_custom_call" | custom-call | flops 566231040 | tf_op jit(solution)/shard_map/input_grad/pallas_call | solution.py:180
  10.6 1.3 %collective-permute-start.8 = (f32[64,640]{1,0:T(8,128)S(1)}, f32[64,640]{1,0:T(8,128)S(1)}, u32[]{:S(2)}, u32[]{:S(2)}) collective-permute-start(f32[64,640]{1,0:T(8,128)S(1)} %get-tuple-element.33), channel_id=1, source_target_pairs={{0,1},{1,0},{2,3},{3,2},{4,5},{5,4},{6,7},{7,6},{8,9},{9,8},{10,11... | collective-permute-start | bytes 491528 | tf_op jit(solution)/shard_map/ppermute | solution.py:230
  11.9 0.1 collective-permute-done.4.refs_3_
  12.1 3.9 %collective-permute-done.3.refs_2_ = bf16[64,640]{1,0:T(8,128)(2,1)S(1)} collective-permute-done((bf16[64,640]{1,0:T(8,128)(2,1)S(1)}, bf16[64,640]{1,0:T(8,128)(2,1)S(1)}, u32[]{:S(2)}, u32[]{:S(2)}) %collective-permute-start.3) | collective-permute-done | bytes 81952 | tf_op jit(solution)/shard_map/ppermute | solution.py:218
  16.0 0.0 collective-permute-done.2.refs_1_
  16.0 0.1 gather.1
  16.1 0.1 collective-permute-start.6
  16.2 1.1 %collective-permute-start.7 = (bf16[64,640]{1,0:T(8,128)(2,1)S(1)}, bf16[64,640]{1,0:T(8,128)(2,1)S(1)}, u32[]{:S(2)}, u32[]{:S(2)}) collective-permute-start(bf16[64,640]{1,0:T(8,128)(2,1)S(1)} %get-tuple-element.29), channel_id=1, source_target_pairs={{0,8},{4,12},{8,0},{12,4},{1,9},{5,13},{9,1},{13,5},{2,10},{6,14},... | collective-permute-start | bytes 245768 | tf_op jit(solution)/shard_map/ppermute | solution.py:246
  17.2 0.9 %collective-permute-start.10 = (f32[64,640]{1,0:T(8,128)S(1)}, f32[64,640]{1,0:T(8,128)S(1)}, u32[]{:S(2)}, u32[]{:S(2)}) collective-permute-start(f32[64,640]{1,0:T(8,128)S(1)} %get-tuple-element.34), channel_id=1, source_target_pairs={{0,1},{1,0},{2,3},{3,2},{4,5},{5,4},{6,7},{7,6},{8,9},{9,8},{10,11... | collective-permute-start | bytes 491528 | tf_op jit(solution)/shard_map/ppermute | solution.py:233
  18.1 1.0 %collective-permute-start.5 = (bf16[128,640]{1,0:T(8,128)(2,1)S(1)}, bf16[128,640]{1,0:T(8,128)(2,1)S(1)}, u32[]{:S(2)}, u32[]{:S(2)}) collective-permute-start(bf16[128,640]{1,0:T(8,128)(2,1)S(1)} %get-tuple-element.27), channel_id=1, source_target_pairs={{0,4},{4,0},{8,12},{12,8},{1,5},{5,1},{9,13},{13,9},{2,6},{6,2},{1... | collective-permute-start | bytes 491528 | tf_op jit(solution)/shard_map/ppermute | solution.py:249
  19.1 0.0 collective-permute-done.8.got_ref
  19.1 1.8 %collective-permute-start.9 = (f32[64,640]{1,0:T(8,128)S(1)}, f32[64,640]{1,0:T(8,128)S(1)}, u32[]{:S(2)}, u32[]{:S(2)}) collective-permute-start(f32[64,640]{1,0:T(8,128)S(1)} %fold.1), channel_id=1, source_target_pairs={{0,2},{1,3},{2,0},{3,1},{4,6},{5,7},{6,4},{7,5},{8,10},{9,11},{10,... | collective-permute-start | bytes 491528 | tf_op jit(solution)/shard_map/ppermute | solution.py:232
  20.9 1.4 %early.1 = (f32[64,640]{1,0:T(8,128)S(1)}, f32[64,640]{1,0:T(8,128)S(1)}, f32[64,640]{1,0:T(8,128)S(1)}, bf16[3,192,640]{2,1,0:T(8,128)(2,1)S(1)}) custom-call(bf16[1728,256]{1,0:T(8,128)(2,1)S(1)} %bitcast.4, bf16[256,640]{1,0:T(8,128)(2,1)S(1)} %get-tuple-element.25.f_ref, bf16[64,640]{1,0:T(8,128)(2,1)S(1)} %bitcast.9, ...), custom_call_target="tpu_custom_call" | custom-call | tf_op jit(solution)/shard_map/early/pallas_call | solution.py:180
  22.3 0.0 collective-permute-done.6.go_ref
  22.3 0.4 %collective-permute-start.11 = (f32[64,640]{1,0:T(8,128)S(1)}, f32[64,640]{1,0:T(8,128)S(1)}, u32[]{:S(2)}, u32[]{:S(2)}) collective-permute-start(f32[64,640]{1,0:T(8,128)S(1)} %get-tuple-element.37), channel_id=1, source_target_pairs={{0,12},{4,8},{8,4},{12,0},{1,13},{5,9},{9,5},{13,1},{2,14},{6,10},... | collective-permute-start | bytes 491528 | tf_op jit(solution)/shard_map/ppermute | solution.py:257
  22.7 0.0 collective-permute-done.7.refs_0_
  22.7 0.3 collective-permute-start.12
  23.0 0.0 collective-permute-done.5.ge_ref
  23.0 2.3 %weight_grad.1 = (f32[27,64,64]{2,1,0:T(8,128)}, f32[8,128]{1,0:T(8,128)S(1)}) custom-call(bf16[3,192,640]{2,1,0:T(8,128)(2,1)S(1)} %get-tuple-element.26.moved_ref, bf16[256,640]{1,0:T(8,128)(2,1)S(1)} %get-tuple-element.25.f_ref, bf16[128,640]{1,0:T(8,128)(2,1)S(1)} %collective-permute-done.5.ge_ref, bf16[64,640]{1,0:T(8,128)(2,1)S(1)} %collective-permute-done.6.go_ref, ...), custom_call_target="tpu_custom_call" | custom-call | tf_op jit(solution)/shard_map/weight_grad/pallas_call | solution.py:180
  25.3 1.0 %collective-permute-done.10.refs_2_ = f32[64,640]{1,0:T(8,128)S(1)} collective-permute-done((f32[64,640]{1,0:T(8,128)S(1)}, f32[64,640]{1,0:T(8,128)S(1)}, u32[]{:S(2)}, u32[]{:S(2)}) %collective-permute-start.10) | collective-permute-done | bytes 163872 | tf_op jit(solution)/shard_map/ppermute | solution.py:233
  26.3 3.4 %collective-permute-done.9.refs_1_ = f32[64,640]{1,0:T(8,128)S(1)} collective-permute-done((f32[64,640]{1,0:T(8,128)S(1)}, f32[64,640]{1,0:T(8,128)S(1)}, u32[]{:S(2)}, u32[]{:S(2)}) %collective-permute-start.9) | collective-permute-done | bytes 163872 | tf_op jit(solution)/shard_map/ppermute | solution.py:232
  29.7 0.7 %input_total.1 = (f32[64,1,640]{2,1,0:T(1,128)}, f32[8,128]{1,0:T(8,128)S(1)}) custom-call(f32[8,128]{1,0:T(8,128)S(1)} %get-tuple-element.30.token_ref, f32[64,640]{1,0:T(8,128)S(1)} %get-tuple-element.31.refs_0_, f32[64,640]{1,0:T(8,128)S(1)} %collective-permute-done.9.refs_1_, f32[64,640]{1,0:T(8,128)S(1)} %collective-permute-done.10.refs_2_), custom_call_target="tpu_custom_call" | custom-call | flops 566231040 | tf_op jit(solution)/shard_map/input_total/pallas_call | solution.py:180
  30.4 0.0 collective-permute-done.11.odd_ref
  30.4 0.0 collective-permute-done.12.even_ref
  30.4 0.7 %output_total.1 = f32[64,1,640]{2,1,0:T(1,128)} custom-call(f32[8,128]{1,0:T(8,128)S(1)} %get-tuple-element.35.token_ref, f32[64,640]{1,0:T(8,128)S(1)} %get-tuple-element.36.own_ref, f32[64,640]{1,0:T(8,128)S(1)} %collective-permute-done.11.odd_ref, f32[64,640]{1,0:T(8,128)S(1)} %collective-permute-done.12.even_ref), custom_call_target="tpu_custom_call" | custom-call | tf_op jit(solution)/shard_map/output_total/pallas_call | solution.py:180
  (2 shorter events, 0.0 us)
Async XLA Ops:
  0.6 4.3 %copy-start.2 = (bf16[64,1,640]{2,0,1:T(8,128)(2,1)S(1)}, bf16[64,1,640]{2,0,1:T(8,128)(2,1)}, u32[]{:S(2)}) copy-start(bf16[64,1,640]{2,0,1:T(8,128)(2,1)} %param.3) | copy-start | bytes 245764
  0.6 8.7 %copy-start = (bf16[27,64,256]{2,1,0:T(8,128)(2,1)S(1)}, bf16[27,64,256]{2,1,0:T(8,128)(2,1)}, u32[]{:S(2)}) copy-start(bf16[27,64,256]{2,1,0:T(8,128)(2,1)} %param.4) | copy-start | bytes 2654212
  0.7 8.7 %copy-start.1 = (bf16[64,1,640]{2,0,1:T(8,128)(2,1)S(1)}, bf16[64,1,640]{2,0,1:T(8,128)(2,1)}, u32[]{:S(2)}) copy-start(bf16[64,1,640]{2,0,1:T(8,128)(2,1)} %param.5) | copy-start | bytes 245764
  0.7 8.6 %collective-permute-start.1 = (bf16[64,640]{1,0:T(8,128)(2,1)}, bf16[64,640]{1,0:T(8,128)(2,1)S(1)}, u32[]{:S(2)}, u32[]{:S(2)}) collective-permute-start(bf16[64,640]{1,0:T(8,128)(2,1)} %bitcast.5), channel_id=1, source_target_pairs={{0,12},{4,8},{8,4},{12,0},{1,13},{5,9},{9,5},{13,1},{2,14},{6,10},... | collective-permute-start | bytes 245768 | tf_op jit(solution)/shard_map/ppermute | solution.py:215
  3.1 1.8 %collective-permute-start = (bf16[64,640]{1,0:T(8,128)(2,1)}, bf16[64,640]{1,0:T(8,128)(2,1)S(1)}, u32[]{:S(2)}, u32[]{:S(2)}) collective-permute-start(bf16[64,640]{1,0:T(8,128)(2,1)} %bitcast.6), channel_id=1, source_target_pairs={{0,4},{4,0},{8,12},{12,8},{1,5},{5,1},{9,13},{13,9},{2,6},{6,2},{1... | collective-permute-start | bytes 245768 | tf_op jit(solution)/shard_map/ppermute | solution.py:214
  4.9 7.2 %collective-permute-start.4 = (bf16[64,640]{1,0:T(8,128)(2,1)S(1)}, bf16[64,640]{1,0:T(8,128)(2,1)S(1)}, u32[]{:S(2)}, u32[]{:S(2)}) collective-permute-start(bf16[64,640]{1,0:T(8,128)(2,1)S(1)} %bitcast.10), channel_id=1, source_target_pairs={{0,3},{1,2},{2,1},{3,0},{4,7},{5,6},{6,5},{7,4},{8,11},{9,10},{10,... | collective-permute-start | bytes 245768 | tf_op jit(solution)/shard_map/ppermute | solution.py:218
  8.5 7.5 %collective-permute-start.3 = (bf16[64,640]{1,0:T(8,128)(2,1)S(1)}, bf16[64,640]{1,0:T(8,128)(2,1)S(1)}, u32[]{:S(2)}, u32[]{:S(2)}) collective-permute-start(bf16[64,640]{1,0:T(8,128)(2,1)S(1)} %bitcast.11), channel_id=1, source_target_pairs={{0,2},{1,3},{2,0},{3,1},{4,6},{5,7},{6,4},{7,5},{8,10},{9,11},{10,... | collective-permute-start | bytes 245768 | tf_op jit(solution)/shard_map/ppermute | solution.py:218
  8.5 7.5 %collective-permute-start.2 = (bf16[64,640]{1,0:T(8,128)(2,1)S(1)}, bf16[64,640]{1,0:T(8,128)(2,1)S(1)}, u32[]{:S(2)}, u32[]{:S(2)}) collective-permute-start(bf16[64,640]{1,0:T(8,128)(2,1)S(1)} %bitcast.12), channel_id=1, source_target_pairs={{0,1},{1,0},{2,3},{3,2},{4,5},{5,4},{6,7},{7,6},{8,9},{9,8},{10,11... | collective-permute-start | bytes 245768 | tf_op jit(solution)/shard_map/ppermute | solution.py:218
  10.6 8.4 %collective-permute-start.8 = (f32[64,640]{1,0:T(8,128)S(1)}, f32[64,640]{1,0:T(8,128)S(1)}, u32[]{:S(2)}, u32[]{:S(2)}) collective-permute-start(f32[64,640]{1,0:T(8,128)S(1)} %get-tuple-element.33), channel_id=1, source_target_pairs={{0,1},{1,0},{2,3},{3,2},{4,5},{5,4},{6,7},{7,6},{8,9},{9,8},{10,11... | collective-permute-start | bytes 491528 | tf_op jit(solution)/shard_map/ppermute | solution.py:230
  16.1 6.2 %collective-permute-start.6 = (bf16[64,640]{1,0:T(8,128)(2,1)S(1)}, bf16[64,640]{1,0:T(8,128)(2,1)S(1)}, u32[]{:S(2)}, u32[]{:S(2)}) collective-permute-start(bf16[64,640]{1,0:T(8,128)(2,1)S(1)} %get-tuple-element.28), channel_id=1, source_target_pairs={{0,12},{4,8},{8,4},{12,0},{1,13},{5,9},{9,5},{13,1},{2,14},{6,10},... | collective-permute-start | bytes 245768 | tf_op jit(solution)/shard_map/ppermute | solution.py:244
  16.2 6.6 %collective-permute-start.7 = (bf16[64,640]{1,0:T(8,128)(2,1)S(1)}, bf16[64,640]{1,0:T(8,128)(2,1)S(1)}, u32[]{:S(2)}, u32[]{:S(2)}) collective-permute-start(bf16[64,640]{1,0:T(8,128)(2,1)S(1)} %get-tuple-element.29), channel_id=1, source_target_pairs={{0,8},{4,12},{8,0},{12,4},{1,9},{5,13},{9,1},{13,5},{2,10},{6,14},... | collective-permute-start | bytes 245768 | tf_op jit(solution)/shard_map/ppermute | solution.py:246
  17.2 9.0 %collective-permute-start.10 = (f32[64,640]{1,0:T(8,128)S(1)}, f32[64,640]{1,0:T(8,128)S(1)}, u32[]{:S(2)}, u32[]{:S(2)}) collective-permute-start(f32[64,640]{1,0:T(8,128)S(1)} %get-tuple-element.34), channel_id=1, source_target_pairs={{0,1},{1,0},{2,3},{3,2},{4,5},{5,4},{6,7},{7,6},{8,9},{9,8},{10,11... | collective-permute-start | bytes 491528 | tf_op jit(solution)/shard_map/ppermute | solution.py:233
  18.1 4.9 %collective-permute-start.5 = (bf16[128,640]{1,0:T(8,128)(2,1)S(1)}, bf16[128,640]{1,0:T(8,128)(2,1)S(1)}, u32[]{:S(2)}, u32[]{:S(2)}) collective-permute-start(bf16[128,640]{1,0:T(8,128)(2,1)S(1)} %get-tuple-element.27), channel_id=1, source_target_pairs={{0,4},{4,0},{8,12},{12,8},{1,5},{5,1},{9,13},{13,9},{2,6},{6,2},{1... | collective-permute-start | bytes 491528 | tf_op jit(solution)/shard_map/ppermute | solution.py:249
  19.1 10.6 %collective-permute-start.9 = (f32[64,640]{1,0:T(8,128)S(1)}, f32[64,640]{1,0:T(8,128)S(1)}, u32[]{:S(2)}, u32[]{:S(2)}) collective-permute-start(f32[64,640]{1,0:T(8,128)S(1)} %fold.1), channel_id=1, source_target_pairs={{0,2},{1,3},{2,0},{3,1},{4,6},{5,7},{6,4},{7,5},{8,10},{9,11},{10,... | collective-permute-start | bytes 491528 | tf_op jit(solution)/shard_map/ppermute | solution.py:232
  22.3 8.1 %collective-permute-start.11 = (f32[64,640]{1,0:T(8,128)S(1)}, f32[64,640]{1,0:T(8,128)S(1)}, u32[]{:S(2)}, u32[]{:S(2)}) collective-permute-start(f32[64,640]{1,0:T(8,128)S(1)} %get-tuple-element.37), channel_id=1, source_target_pairs={{0,12},{4,8},{8,4},{12,0},{1,13},{5,9},{9,5},{13,1},{2,14},{6,10},... | collective-permute-start | bytes 491528 | tf_op jit(solution)/shard_map/ppermute | solution.py:257
  22.7 7.7 %collective-permute-start.12 = (f32[64,640]{1,0:T(8,128)S(1)}, f32[64,640]{1,0:T(8,128)S(1)}, u32[]{:S(2)}, u32[]{:S(2)}) collective-permute-start(f32[64,640]{1,0:T(8,128)S(1)} %get-tuple-element.38), channel_id=1, source_target_pairs={{0,4},{4,0},{8,12},{12,8},{1,5},{5,1},{9,13},{13,9},{2,6},{6,2},{1... | collective-permute-start | bytes 491528 | tf_op jit(solution)/shard_map/ppermute | solution.py:258

commit v14 on v13

--- a/solution.py
+++ b/solution.py
@@ -13,7 +13,7 @@
 CELLS = NX * NY
 F32 = jnp.float32
 BF16 = jnp.bfloat16
-W_GATHER, W_EARLY, W_BEGIN, W_GRAD, W_FOLD, W_TOTAL, W_OUT = 2, 0, 8, 1, 0, 1, 0
+W_GATHER, W_EARLY, W_BEGIN, W_GRAD, W_FOLD, W_TOTAL, W_OUT = 2, 0, 8, 1, 0, 2, 0
 VMEM_BYTES = 32 * 1024 * 1024
 
 

time: 31.3 us -> 31.5 us (level)
  waiting for transfers between devices: 9.64 us -> 11.6 us
  starting transfers between devices: 14.3 us -> 12.5 us
    ppermute x1, waiting for transfers between devices: 3.44 us -> 0.33 us  [per_device(): terms.append(lax.ppermute(both, 'ch', mixed(k)))]
    ppermute x1, waiting for transfers between devices: 0.01 us -> 3.09 us  [per_device(): got = lax.ppermute(parts[k + 1], 'ch', mixed(1))]
    ppermute x1, waiting for transfers between devices: 0.01 us -> 2.43 us  [per_device(): g_odd = lax.ppermute(to_odd, 'sp', odd_pairs)]
    ppermute x1, waiting for transfers between devices: 0.01 us -> 1.04 us  [per_device(): out_odd = lax.ppermute(out_odd, 'sp', odd_pairs)]
    ppermute x1, waiting for transfers between devices: 0.97 us -> 0.01 us  [per_device(): terms.append(lax.ppermute(parts[1], 'ch', mixed(1)))]
    ppermute x1, starting transfers between devices: 0.96 us -> 0.07 us  [per_device(): g_even = lax.ppermute(to_even, 'sp', even_pairs)]
    ppermute x1, starting transfers between devices: 1.77 us -> 0.95 us  [per_device(): terms.append(lax.ppermute(both, 'ch', mixed(k)))]
    ppermute x3, waiting for transfers between devices: 4.07 us -> 3.29 us  [per_device(): pieces = [feat] + [lax.ppermute(feat, 'ch', mixed(k)) for k in range(1, nc)]]
  transfers between devices with their start and end apart: 13 -> 13, of which waited for: 5 -> 7; matrix products, arithmetic and copies ran while one was open for 0% -> 0% of each run, Pallas kernels for 19% -> 19%
where the time goes in v14:
time: 31.5 us; the launch traced here: 31.3 us
  starting transfers between devices  12.5 us (40%)
  waiting for transfers between devices  11.6 us (37%)
  Pallas kernels  6.53 us (21%)
  between operations  0.7 us (2%)
    pallas_call x8, Pallas kernels, kernel_call(): pl.pallas_call(body, out_shape=outs, in_specs=[SMEM if a.dtype == jnp.int...  6.53 us
    ppermute x3, starting transfers between devices, per_device(): pieces = [feat] + [lax.ppermute(feat, 'ch', mixed(k)) for k in range(1, nc)]  4.39 us
    ppermute x3, waiting for transfers between devices, per_device(): pieces = [feat] + [lax.ppermute(feat, 'ch', mixed(k)) for k in range(1, nc)]  3.29 us
    ppermute x1, waiting for transfers between devices, per_device(): got = lax.ppermute(parts[k + 1], 'ch', mixed(1))  3.09 us
    ppermute x1, starting transfers between devices, per_device(): cot_odd = lax.ppermute(cot, 'sp', odd_pairs)  2.44 us
    ppermute x1, waiting for transfers between devices, per_device(): g_odd = lax.ppermute(to_odd, 'sp', odd_pairs)  2.43 us
    ppermute x1, starting transfers between devices, per_device(): got = lax.ppermute(parts[k + 1], 'ch', mixed(1))  1.31 us
    ppermute x1, waiting for transfers between devices, per_device(): cot_even = lax.ppermute(cot, 'sp', even_pairs)  1.13 us
  transfers between devices with their start and end apart: 13, of which 7 were waited for; matrix products, arithmetic and copies ran while one was open for 0% of the time, Pallas kernels for 19%

profile of v14, /device:TPU:0, one launch (start us, length us, event | category | flops | bytes accessed | tf_op | source)
XLA Modules:
  0.0 31.3 jit_solution(17083945604471048037)
XLA Ops:
  0.6 0.0 copy-start.2
  0.6 0.0 copy-start
  0.7 0.0 copy-start.1
  0.7 2.4 %collective-permute-start.1 = (bf16[64,640]{1,0:T(8,128)(2,1)}, bf16[64,640]{1,0:T(8,128)(2,1)S(1)}, u32[]{:S(2)}, u32[]{:S(2)}) collective-permute-start(bf16[64,640]{1,0:T(8,128)(2,1)} %bitcast.5), channel_id=1, source_target_pairs={{0,12},{4,8},{8,4},{12,0},{1,13},{5,9},{9,5},{13,1},{2,14},{6,10},... | collective-permute-start | bytes 245768 | tf_op jit(solution)/shard_map/ppermute | solution.py:215
  3.1 0.7 %collective-permute-start = (bf16[64,640]{1,0:T(8,128)(2,1)}, bf16[64,640]{1,0:T(8,128)(2,1)S(1)}, u32[]{:S(2)}, u32[]{:S(2)}) collective-permute-start(bf16[64,640]{1,0:T(8,128)(2,1)} %bitcast.6), channel_id=1, source_target_pairs={{0,4},{4,0},{8,12},{12,8},{1,5},{5,1},{9,13},{13,9},{2,6},{6,2},{1... | collective-permute-start | bytes 245768 | tf_op jit(solution)/shard_map/ppermute | solution.py:214
  3.8 1.1 %collective-permute-done.even_ref.ce_ref = bf16[64,640]{1,0:T(8,128)(2,1)S(1)} collective-permute-done((bf16[64,640]{1,0:T(8,128)(2,1)}, bf16[64,640]{1,0:T(8,128)(2,1)S(1)}, u32[]{:S(2)}, u32[]{:S(2)}) %collective-permute-start) | collective-permute-done | bytes 81952 | tf_op jit(solution)/shard_map/ppermute | solution.py:214
  4.9 0.0 copy-done.2
  4.9 3.6 %collective-permute-start.4 = (bf16[64,640]{1,0:T(8,128)(2,1)S(1)}, bf16[64,640]{1,0:T(8,128)(2,1)S(1)}, u32[]{:S(2)}, u32[]{:S(2)}) collective-permute-start(bf16[64,640]{1,0:T(8,128)(2,1)S(1)} %bitcast.10), channel_id=1, source_target_pairs={{0,3},{1,2},{2,1},{3,0},{4,7},{5,6},{6,5},{7,4},{8,11},{9,10},{10,... | collective-permute-start | bytes 245768 | tf_op jit(solution)/shard_map/ppermute | solution.py:218
  8.5 0.0 collective-permute-start.3
  8.5 0.8 %collective-permute-start.2 = (bf16[64,640]{1,0:T(8,128)(2,1)S(1)}, bf16[64,640]{1,0:T(8,128)(2,1)S(1)}, u32[]{:S(2)}, u32[]{:S(2)}) collective-permute-start(bf16[64,640]{1,0:T(8,128)(2,1)S(1)} %bitcast.12), channel_id=1, source_target_pairs={{0,1},{1,0},{2,3},{3,2},{4,5},{5,4},{6,7},{7,6},{8,9},{9,8},{10,11... | collective-permute-start | bytes 245768 | tf_op jit(solution)/shard_map/ppermute | solution.py:218
  9.3 0.0 collective-permute-done.1.odd_ref.near_ref.co_ref
  9.3 0.0 copy-done
  9.3 0.0 copy-done.1
  9.3 1.3 %input_grad.1 = (f32[64,640]{1,0:T(8,128)S(1)}, f32[64,640]{1,0:T(8,128)S(1)}, f32[64,640]{1,0:T(8,128)S(1)}, f32[64,640]{1,0:T(8,128)S(1)}, f32[8,128]{1,0:T(8,128)S(1)}) custom-call(f32[8,128]{1,0:T(8,128)S(1)} %begin.1.begin_ref, bf16[64,640]{1,0:T(8,128)(2,1)S(1)} %bitcast.7, bf16[64,640]{1,0:T(8,128)(2,1)S(1)} %collective-permute-done.even_ref.ce_ref, ...), custom_call_target="tpu_custom_call" | custom-call | flops 566231040 | tf_op jit(solution)/shard_map/input_grad/pallas_call | solution.py:180
  10.6 1.3 %collective-permute-start.8 = (f32[64,640]{1,0:T(8,128)S(1)}, f32[64,640]{1,0:T(8,128)S(1)}, u32[]{:S(2)}, u32[]{:S(2)}) collective-permute-start(f32[64,640]{1,0:T(8,128)S(1)} %get-tuple-element.33), channel_id=1, source_target_pairs={{0,1},{1,0},{2,3},{3,2},{4,5},{5,4},{6,7},{7,6},{8,9},{9,8},{10,11... | collective-permute-start | bytes 491528 | tf_op jit(solution)/shard_map/ppermute | solution.py:230
  11.9 0.8 %collective-permute-start.10 = (f32[64,640]{1,0:T(8,128)S(1)}, f32[64,640]{1,0:T(8,128)S(1)}, u32[]{:S(2)}, u32[]{:S(2)}) collective-permute-start(f32[64,640]{1,0:T(8,128)S(1)} %get-tuple-element.34), channel_id=1, source_target_pairs={{0,1},{1,0},{2,3},{3,2},{4,5},{5,4},{6,7},{7,6},{8,9},{9,8},{10,11... | collective-permute-start | bytes 491528 | tf_op jit(solution)/shard_map/ppermute | solution.py:233
  12.7 0.0 collective-permute-done.4.refs_3_
  12.7 3.3 %collective-permute-done.3.refs_2_ = bf16[64,640]{1,0:T(8,128)(2,1)S(1)} collective-permute-done((bf16[64,640]{1,0:T(8,128)(2,1)S(1)}, bf16[64,640]{1,0:T(8,128)(2,1)S(1)}, u32[]{:S(2)}, u32[]{:S(2)}) %collective-permute-start.3) | collective-permute-done | bytes 81952 | tf_op jit(solution)/shard_map/ppermute | solution.py:218
  16.0 0.0 collective-permute-done.2.refs_1_
  16.0 0.1 gather.1
  16.1 0.1 collective-permute-start.5
  16.2 3.1 %collective-permute-done.8.got_ref = f32[64,640]{1,0:T(8,128)S(1)} collective-permute-done((f32[64,640]{1,0:T(8,128)S(1)}, f32[64,640]{1,0:T(8,128)S(1)}, u32[]{:S(2)}, u32[]{:S(2)}) %collective-permute-start.8) | collective-permute-done | bytes 163872 | tf_op jit(solution)/shard_map/ppermute | solution.py:230
  19.3 0.9 %collective-permute-start.9 = (f32[64,640]{1,0:T(8,128)S(1)}, f32[64,640]{1,0:T(8,128)S(1)}, u32[]{:S(2)}, u32[]{:S(2)}) collective-permute-start(f32[64,640]{1,0:T(8,128)S(1)} %fold.1), channel_id=1, source_target_pairs={{0,2},{1,3},{2,0},{3,1},{4,6},{5,7},{6,4},{7,5},{8,10},{9,11},{10,... | collective-permute-start | bytes 491528 | tf_op jit(solution)/shard_map/ppermute | solution.py:232
  20.2 0.0 collective-permute-start.6
  20.2 0.8 %collective-permute-start.7 = (bf16[64,640]{1,0:T(8,128)(2,1)S(1)}, bf16[64,640]{1,0:T(8,128)(2,1)S(1)}, u32[]{:S(2)}, u32[]{:S(2)}) collective-permute-start(bf16[64,640]{1,0:T(8,128)(2,1)S(1)} %get-tuple-element.29), channel_id=1, source_target_pairs={{0,8},{4,12},{8,0},{12,4},{1,9},{5,13},{9,1},{13,5},{2,10},{6,14},... | collective-permute-start | bytes 245768 | tf_op jit(solution)/shard_map/ppermute | solution.py:246
  21.1 1.4 %early.1 = (f32[64,640]{1,0:T(8,128)S(1)}, f32[64,640]{1,0:T(8,128)S(1)}, f32[64,640]{1,0:T(8,128)S(1)}, bf16[3,192,640]{2,1,0:T(8,128)(2,1)S(1)}) custom-call(bf16[1728,256]{1,0:T(8,128)(2,1)S(1)} %bitcast.4, bf16[256,640]{1,0:T(8,128)(2,1)S(1)} %get-tuple-element.25.f_ref, bf16[64,640]{1,0:T(8,128)(2,1)S(1)} %bitcast.9, ...), custom_call_target="tpu_custom_call" | custom-call | tf_op jit(solution)/shard_map/early/pallas_call | solution.py:180
  22.5 2.4 %collective-permute-done.6.go_ref = bf16[64,640]{1,0:T(8,128)(2,1)S(1)} collective-permute-done((bf16[64,640]{1,0:T(8,128)(2,1)S(1)}, bf16[64,640]{1,0:T(8,128)(2,1)S(1)}, u32[]{:S(2)}, u32[]{:S(2)}) %collective-permute-start.6) | collective-permute-done | bytes 81952 | tf_op jit(solution)/shard_map/ppermute | solution.py:244
  24.9 0.3 %collective-permute-start.11 = (f32[64,640]{1,0:T(8,128)S(1)}, f32[64,640]{1,0:T(8,128)S(1)}, u32[]{:S(2)}, u32[]{:S(2)}) collective-permute-start(f32[64,640]{1,0:T(8,128)S(1)} %get-tuple-element.37), channel_id=1, source_target_pairs={{0,12},{4,8},{8,4},{12,0},{1,13},{5,9},{9,5},{13,1},{2,14},{6,10},... | collective-permute-start | bytes 491528 | tf_op jit(solution)/shard_map/ppermute | solution.py:257
  25.3 0.3 collective-permute-done.7.refs_0_
  25.5 0.7 %collective-permute-start.12 = (f32[64,640]{1,0:T(8,128)S(1)}, f32[64,640]{1,0:T(8,128)S(1)}, u32[]{:S(2)}, u32[]{:S(2)}) collective-permute-start(f32[64,640]{1,0:T(8,128)S(1)} %get-tuple-element.38), channel_id=1, source_target_pairs={{0,4},{4,0},{8,12},{12,8},{1,5},{5,1},{9,13},{13,9},{2,6},{6,2},{1... | collective-permute-start | bytes 491528 | tf_op jit(solution)/shard_map/ppermute | solution.py:258
  26.2 0.0 collective-permute-done.5.ge_ref
  26.2 2.3 %weight_grad.1 = (f32[27,64,64]{2,1,0:T(8,128)}, f32[8,128]{1,0:T(8,128)S(1)}) custom-call(bf16[3,192,640]{2,1,0:T(8,128)(2,1)S(1)} %get-tuple-element.26.moved_ref, bf16[256,640]{1,0:T(8,128)(2,1)S(1)} %get-tuple-element.25.f_ref, bf16[128,640]{1,0:T(8,128)(2,1)S(1)} %collective-permute-done.5.ge_ref, bf16[64,640]{1,0:T(8,128)(2,1)S(1)} %collective-permute-done.6.go_ref, ...), custom_call_target="tpu_custom_call" | custom-call | tf_op jit(solution)/shard_map/weight_grad/pallas_call | solution.py:180
  28.5 0.0 collective-permute-done.10.refs_2_
  28.5 0.3 %collective-permute-done.9.refs_1_ = f32[64,640]{1,0:T(8,128)S(1)} collective-permute-done((f32[64,640]{1,0:T(8,128)S(1)}, f32[64,640]{1,0:T(8,128)S(1)}, u32[]{:S(2)}, u32[]{:S(2)}) %collective-permute-start.9) | collective-permute-done | bytes 163872 | tf_op jit(solution)/shard_map/ppermute | solution.py:232
  28.8 0.7 %input_total.1 = (f32[64,1,640]{2,1,0:T(1,128)}, f32[8,128]{1,0:T(8,128)S(1)}) custom-call(f32[8,128]{1,0:T(8,128)S(1)} %get-tuple-element.30.token_ref, f32[64,640]{1,0:T(8,128)S(1)} %get-tuple-element.31.refs_0_, f32[64,640]{1,0:T(8,128)S(1)} %collective-permute-done.9.refs_1_, f32[64,640]{1,0:T(8,128)S(1)} %collective-permute-done.10.refs_2_), custom_call_target="tpu_custom_call" | custom-call | flops 1132462080 | tf_op jit(solution)/shard_map/input_total/pallas_call | solution.py:180
  29.5 1.0 %collective-permute-done.11.odd_ref = f32[64,640]{1,0:T(8,128)S(1)} collective-permute-done((f32[64,640]{1,0:T(8,128)S(1)}, f32[64,640]{1,0:T(8,128)S(1)}, u32[]{:S(2)}, u32[]{:S(2)}) %collective-permute-start.11) | collective-permute-done | bytes 163872 | tf_op jit(solution)/shard_map/ppermute | solution.py:257
  30.6 0.0 collective-permute-done.12.even_ref
  30.6 0.7 %output_total.1 = f32[64,1,640]{2,1,0:T(1,128)} custom-call(f32[8,128]{1,0:T(8,128)S(1)} %get-tuple-element.35.token_ref, f32[64,640]{1,0:T(8,128)S(1)} %get-tuple-element.36.own_ref, f32[64,640]{1,0:T(8,128)S(1)} %collective-permute-done.11.odd_ref, f32[64,640]{1,0:T(8,128)S(1)} %collective-permute-done.12.even_ref), custom_call_target="tpu_custom_call" | custom-call | tf_op jit(solution)/shard_map/output_total/pallas_call | solution.py:180
  (2 shorter events, 0.0 us)
Async XLA Ops:
  0.6 4.3 %copy-start.2 = (bf16[64,1,640]{2,0,1:T(8,128)(2,1)S(1)}, bf16[64,1,640]{2,0,1:T(8,128)(2,1)}, u32[]{:S(2)}) copy-start(bf16[64,1,640]{2,0,1:T(8,128)(2,1)} %param.3) | copy-start | bytes 245764
  0.6 8.7 %copy-start = (bf16[27,64,256]{2,1,0:T(8,128)(2,1)S(1)}, bf16[27,64,256]{2,1,0:T(8,128)(2,1)}, u32[]{:S(2)}) copy-start(bf16[27,64,256]{2,1,0:T(8,128)(2,1)} %param.4) | copy-start | bytes 2654212
  0.7 8.7 %copy-start.1 = (bf16[64,1,640]{2,0,1:T(8,128)(2,1)S(1)}, bf16[64,1,640]{2,0,1:T(8,128)(2,1)}, u32[]{:S(2)}) copy-start(bf16[64,1,640]{2,0,1:T(8,128)(2,1)} %param.5) | copy-start | bytes 245764
  0.7 8.6 %collective-permute-start.1 = (bf16[64,640]{1,0:T(8,128)(2,1)}, bf16[64,640]{1,0:T(8,128)(2,1)S(1)}, u32[]{:S(2)}, u32[]{:S(2)}) collective-permute-start(bf16[64,640]{1,0:T(8,128)(2,1)} %bitcast.5), channel_id=1, source_target_pairs={{0,12},{4,8},{8,4},{12,0},{1,13},{5,9},{9,5},{13,1},{2,14},{6,10},... | collective-permute-start | bytes 245768 | tf_op jit(solution)/shard_map/ppermute | solution.py:215
  3.1 1.8 %collective-permute-start = (bf16[64,640]{1,0:T(8,128)(2,1)}, bf16[64,640]{1,0:T(8,128)(2,1)S(1)}, u32[]{:S(2)}, u32[]{:S(2)}) collective-permute-start(bf16[64,640]{1,0:T(8,128)(2,1)} %bitcast.6), channel_id=1, source_target_pairs={{0,4},{4,0},{8,12},{12,8},{1,5},{5,1},{9,13},{13,9},{2,6},{6,2},{1... | collective-permute-start | bytes 245768 | tf_op jit(solution)/shard_map/ppermute | solution.py:214
  4.9 7.8 %collective-permute-start.4 = (bf16[64,640]{1,0:T(8,128)(2,1)S(1)}, bf16[64,640]{1,0:T(8,128)(2,1)S(1)}, u32[]{:S(2)}, u32[]{:S(2)}) collective-permute-start(bf16[64,640]{1,0:T(8,128)(2,1)S(1)} %bitcast.10), channel_id=1, source_target_pairs={{0,3},{1,2},{2,1},{3,0},{4,7},{5,6},{6,5},{7,4},{8,11},{9,10},{10,... | collective-permute-start | bytes 245768 | tf_op jit(solution)/shard_map/ppermute | solution.py:218
  8.5 7.5 %collective-permute-start.3 = (bf16[64,640]{1,0:T(8,128)(2,1)S(1)}, bf16[64,640]{1,0:T(8,128)(2,1)S(1)}, u32[]{:S(2)}, u32[]{:S(2)}) collective-permute-start(bf16[64,640]{1,0:T(8,128)(2,1)S(1)} %bitcast.11), channel_id=1, source_target_pairs={{0,2},{1,3},{2,0},{3,1},{4,6},{5,7},{6,4},{7,5},{8,10},{9,11},{10,... | collective-permute-start | bytes 245768 | tf_op jit(solution)/shard_map/ppermute | solution.py:218
  8.5 7.5 %collective-permute-start.2 = (bf16[64,640]{1,0:T(8,128)(2,1)S(1)}, bf16[64,640]{1,0:T(8,128)(2,1)S(1)}, u32[]{:S(2)}, u32[]{:S(2)}) collective-permute-start(bf16[64,640]{1,0:T(8,128)(2,1)S(1)} %bitcast.12), channel_id=1, source_target_pairs={{0,1},{1,0},{2,3},{3,2},{4,5},{5,4},{6,7},{7,6},{8,9},{9,8},{10,11... | collective-permute-start | bytes 245768 | tf_op jit(solution)/shard_map/ppermute | solution.py:218
  10.6 8.6 %collective-permute-start.8 = (f32[64,640]{1,0:T(8,128)S(1)}, f32[64,640]{1,0:T(8,128)S(1)}, u32[]{:S(2)}, u32[]{:S(2)}) collective-permute-start(f32[64,640]{1,0:T(8,128)S(1)} %get-tuple-element.33), channel_id=1, source_target_pairs={{0,1},{1,0},{2,3},{3,2},{4,5},{5,4},{6,7},{7,6},{8,9},{9,8},{10,11... | collective-permute-start | bytes 491528 | tf_op jit(solution)/shard_map/ppermute | solution.py:230
  11.9 16.5 %collective-permute-start.10 = (f32[64,640]{1,0:T(8,128)S(1)}, f32[64,640]{1,0:T(8,128)S(1)}, u32[]{:S(2)}, u32[]{:S(2)}) collective-permute-start(f32[64,640]{1,0:T(8,128)S(1)} %get-tuple-element.34), channel_id=1, source_target_pairs={{0,1},{1,0},{2,3},{3,2},{4,5},{5,4},{6,7},{7,6},{8,9},{9,8},{10,11... | collective-permute-start | bytes 491528 | tf_op jit(solution)/shard_map/ppermute | solution.py:233
  16.1 10.1 %collective-permute-start.5 = (bf16[128,640]{1,0:T(8,128)(2,1)S(1)}, bf16[128,640]{1,0:T(8,128)(2,1)S(1)}, u32[]{:S(2)}, u32[]{:S(2)}) collective-permute-start(bf16[128,640]{1,0:T(8,128)(2,1)S(1)} %get-tuple-element.27), channel_id=1, source_target_pairs={{0,4},{4,0},{8,12},{12,8},{1,5},{5,1},{9,13},{13,9},{2,6},{6,2},{1... | collective-permute-start | bytes 491528 | tf_op jit(solution)/shard_map/ppermute | solution.py:249
  19.3 9.6 %collective-permute-start.9 = (f32[64,640]{1,0:T(8,128)S(1)}, f32[64,640]{1,0:T(8,128)S(1)}, u32[]{:S(2)}, u32[]{:S(2)}) collective-permute-start(f32[64,640]{1,0:T(8,128)S(1)} %fold.1), channel_id=1, source_target_pairs={{0,2},{1,3},{2,0},{3,1},{4,6},{5,7},{6,4},{7,5},{8,10},{9,11},{10,... | collective-permute-start | bytes 491528 | tf_op jit(solution)/shard_map/ppermute | solution.py:232
  20.2 4.7 %collective-permute-start.6 = (bf16[64,640]{1,0:T(8,128)(2,1)S(1)}, bf16[64,640]{1,0:T(8,128)(2,1)S(1)}, u32[]{:S(2)}, u32[]{:S(2)}) collective-permute-start(bf16[64,640]{1,0:T(8,128)(2,1)S(1)} %get-tuple-element.28), channel_id=1, source_target_pairs={{0,12},{4,8},{8,4},{12,0},{1,13},{5,9},{9,5},{13,1},{2,14},{6,10},... | collective-permute-start | bytes 245768 | tf_op jit(solution)/shard_map/ppermute | solution.py:244
  20.2 5.3 %collective-permute-start.7 = (bf16[64,640]{1,0:T(8,128)(2,1)S(1)}, bf16[64,640]{1,0:T(8,128)(2,1)S(1)}, u32[]{:S(2)}, u32[]{:S(2)}) collective-permute-start(bf16[64,640]{1,0:T(8,128)(2,1)S(1)} %get-tuple-element.29), channel_id=1, source_target_pairs={{0,8},{4,12},{8,0},{12,4},{1,9},{5,13},{9,1},{13,5},{2,10},{6,14},... | collective-permute-start | bytes 245768 | tf_op jit(solution)/shard_map/ppermute | solution.py:246
  24.9 5.6 %collective-permute-start.11 = (f32[64,640]{1,0:T(8,128)S(1)}, f32[64,640]{1,0:T(8,128)S(1)}, u32[]{:S(2)}, u32[]{:S(2)}) collective-permute-start(f32[64,640]{1,0:T(8,128)S(1)} %get-tuple-element.37), channel_id=1, source_target_pairs={{0,12},{4,8},{8,4},{12,0},{1,13},{5,9},{9,5},{13,1},{2,14},{6,10},... | collective-permute-start | bytes 491528 | tf_op jit(solution)/shard_map/ppermute | solution.py:257
  25.5 5.1 %collective-permute-start.12 = (f32[64,640]{1,0:T(8,128)S(1)}, f32[64,640]{1,0:T(8,128)S(1)}, u32[]{:S(2)}, u32[]{:S(2)}) collective-permute-start(f32[64,640]{1,0:T(8,128)S(1)} %get-tuple-element.38), channel_id=1, source_target_pairs={{0,4},{4,0},{8,12},{12,8},{1,5},{5,1},{9,13},{13,9},{2,6},{6,2},{1... | collective-permute-start | bytes 491528 | tf_op jit(solution)/shard_map/ppermute | solution.py:258

commit v15 on v13

--- a/solution.py
+++ b/solution.py
@@ -106,7 +106,7 @@
     return jnp.concatenate([shifted(plane, -dy, 0).astype(BF16) for dy in (-1, 0, 1)], 0)
 
 
-def early_kernel(w_ref, f_ref, cot_ref, ce_ref, co_ref, own_ref, even_ref, odd_ref, moved_ref):
+def early_kernel(token_ref, w_ref, f_ref, cot_ref, ce_ref, co_ref, own_ref, even_ref, odd_ref, moved_ref):
     side = 1 - 2 * lax.rem(lax.axis_index("sp"), 2)
     for ref, dz in ((odd_ref, side), (even_ref, -side), (own_ref, 0)):
         ref[...] = moved_sum(conv_part(w_ref, f_ref[...], dz))
@@ -230,7 +230,6 @@
         got = lax.ppermute(parts[k + 1], "ch", mixed(1))
         (both,) = kernel_call(fold_kernel, "fold", [of(blocks, F32)], [parts[k], got], weight=W_FOLD * work)
         terms.append(lax.ppermute(both, "ch", mixed(k)))
-    terms.append(lax.ppermute(parts[1], "ch", mixed(1)))
 
     far_rows = cols if nz == 4 else cols + blocks
     f_all, to_even, to_odd, *packs = kernel_call(
@@ -251,9 +250,11 @@
         early_kernel,
         "early",
         [of(blocks, F32)] * 3 + [jax.ShapeDtypeStruct((3, 3 * blocks, plane), BF16)],
-        [w2, f_all, cot, cot_even, cot_odd],
+        [both, w2, f_all, cot, cot_even, cot_odd],
         weight=W_EARLY * work,
     )
+    near, out_own = lax.optimization_barrier((parts[1], out_own))
+    terms.append(lax.ppermute(near, "ch", mixed(1)))
     out_odd = lax.ppermute(out_odd, "sp", odd_pairs)
     out_even = lax.ppermute(out_even, "sp", even_pairs)
 

time: 31.3 us -> 31.7 us (1.013)
  starting transfers between devices: 14.3 us -> 15.2 us
  waiting for transfers between devices: 9.64 us -> 9.13 us
    ppermute x1, starting transfers between devices: 0.88 us -> 2.55 us  [per_device(): terms.append(lax.ppermute(near, 'ch', mixed(1)))]
    ppermute x1, waiting for transfers between devices: 3.44 us -> 2.06 us  [per_device(): terms.append(lax.ppermute(both, 'ch', mixed(k)))]
    ppermute x1, waiting for transfers between devices: 0.01 us -> 0.65 us  [per_device(): got = lax.ppermute(parts[k + 1], 'ch', mixed(1))]
    ppermute x1, starting transfers between devices: 1.77 us -> 1.23 us  [per_device(): terms.append(lax.ppermute(both, 'ch', mixed(k)))]
    ppermute x1, starting transfers between devices: 0.42 us -> 0.01 us  [per_device(): out_odd = lax.ppermute(out_odd, 'sp', odd_pairs)]
    ppermute x1, starting transfers between devices: 0.3 us -> 0.65 us  [per_device(): out_even = lax.ppermute(out_even, 'sp', even_pairs)]
  transfers between devices with their start and end apart: 13 -> 13, of which waited for: 5 -> 6; matrix products, arithmetic and copies ran while one was open for 0% -> 0% of each run, Pallas kernels for 19% -> 18%
where the time goes in v15:
time: 31.7 us; the launch traced here: 31.5 us
  starting transfers between devices  15.2 us (48%)
  waiting for transfers between devices  9.13 us (29%)
  Pallas kernels  6.53 us (21%)
  between operations  0.71 us (2%)
    pallas_call x8, Pallas kernels, kernel_call(): pl.pallas_call(body, out_shape=outs, in_specs=[SMEM if a.dtype == jnp.int...  6.53 us
    ppermute x3, starting transfers between devices, per_device(): pieces = [feat] + [lax.ppermute(feat, 'ch', mixed(k)) for k in range(1, nc)]  4.39 us
    ppermute x3, waiting for transfers between devices, per_device(): pieces = [feat] + [lax.ppermute(feat, 'ch', mixed(k)) for k in range(1, nc)]  4.07 us
    ppermute x1, starting transfers between devices, per_device(): terms.append(lax.ppermute(near, 'ch', mixed(1)))  2.55 us
    ppermute x1, starting transfers between devices, per_device(): cot_odd = lax.ppermute(cot, 'sp', odd_pairs)  2.44 us
    ppermute x1, waiting for transfers between devices, per_device(): terms.append(lax.ppermute(both, 'ch', mixed(k)))  2.06 us
    ppermute x1, starting transfers between devices, per_device(): got = lax.ppermute(parts[k + 1], 'ch', mixed(1))  1.31 us
    ppermute x1, starting transfers between devices, per_device(): terms.append(lax.ppermute(both, 'ch', mixed(k)))  1.23 us
  transfers between devices with their start and end apart: 13, of which 6 were waited for; matrix products, arithmetic and copies ran while one was open for 0% of the time, Pallas kernels for 18%

profile of v15, /device:TPU:0, one launch (start us, length us, event | category | flops | bytes accessed | tf_op | source)
XLA Modules:
  0.0 31.5 jit_solution(6620491088764101609)
XLA Ops:
  0.6 0.0 copy-start.2
  0.6 0.0 copy-start
  0.7 0.0 copy-start.1
  0.7 2.4 %collective-permute-start.1 = (bf16[64,640]{1,0:T(8,128)(2,1)}, bf16[64,640]{1,0:T(8,128)(2,1)S(1)}, u32[]{:S(2)}, u32[]{:S(2)}) collective-permute-start(bf16[64,640]{1,0:T(8,128)(2,1)} %bitcast.5), channel_id=1, source_target_pairs={{0,12},{4,8},{8,4},{12,0},{1,13},{5,9},{9,5},{13,1},{2,14},{6,10},... | collective-permute-start | bytes 245768 | tf_op jit(solution)/shard_map/ppermute | solution.py:215
  3.1 0.7 %collective-permute-start = (bf16[64,640]{1,0:T(8,128)(2,1)}, bf16[64,640]{1,0:T(8,128)(2,1)S(1)}, u32[]{:S(2)}, u32[]{:S(2)}) collective-permute-start(bf16[64,640]{1,0:T(8,128)(2,1)} %bitcast.6), channel_id=1, source_target_pairs={{0,4},{4,0},{8,12},{12,8},{1,5},{5,1},{9,13},{13,9},{2,6},{6,2},{1... | collective-permute-start | bytes 245768 | tf_op jit(solution)/shard_map/ppermute | solution.py:214
  3.8 1.1 %collective-permute-done.even_ref.ce_ref = bf16[64,640]{1,0:T(8,128)(2,1)S(1)} collective-permute-done((bf16[64,640]{1,0:T(8,128)(2,1)}, bf16[64,640]{1,0:T(8,128)(2,1)S(1)}, u32[]{:S(2)}, u32[]{:S(2)}) %collective-permute-start) | collective-permute-done | bytes 81952 | tf_op jit(solution)/shard_map/ppermute | solution.py:214
  4.9 0.0 copy-done.2
  4.9 3.6 %collective-permute-start.5 = (bf16[64,640]{1,0:T(8,128)(2,1)S(1)}, bf16[64,640]{1,0:T(8,128)(2,1)S(1)}, u32[]{:S(2)}, u32[]{:S(2)}) collective-permute-start(bf16[64,640]{1,0:T(8,128)(2,1)S(1)} %bitcast.10), channel_id=1, source_target_pairs={{0,3},{1,2},{2,1},{3,0},{4,7},{5,6},{6,5},{7,4},{8,11},{9,10},{10,... | collective-permute-start | bytes 245768 | tf_op jit(solution)/shard_map/ppermute | solution.py:218
  8.5 0.0 collective-permute-start.4
  8.5 0.8 %collective-permute-start.3 = (bf16[64,640]{1,0:T(8,128)(2,1)S(1)}, bf16[64,640]{1,0:T(8,128)(2,1)S(1)}, u32[]{:S(2)}, u32[]{:S(2)}) collective-permute-start(bf16[64,640]{1,0:T(8,128)(2,1)S(1)} %bitcast.12), channel_id=1, source_target_pairs={{0,1},{1,0},{2,3},{3,2},{4,5},{5,4},{6,7},{7,6},{8,9},{9,8},{10,11... | collective-permute-start | bytes 245768 | tf_op jit(solution)/shard_map/ppermute | solution.py:218
  9.3 0.0 collective-permute-done.1.odd_ref.near_ref.co_ref
  9.3 0.0 copy-done
  9.3 0.0 copy-done.1
  9.3 1.3 %input_grad.1 = (f32[64,640]{1,0:T(8,128)S(1)}, f32[64,640]{1,0:T(8,128)S(1)}, f32[64,640]{1,0:T(8,128)S(1)}, f32[64,640]{1,0:T(8,128)S(1)}, f32[8,128]{1,0:T(8,128)S(1)}) custom-call(f32[8,128]{1,0:T(8,128)S(1)} %begin.1.begin_ref, bf16[64,640]{1,0:T(8,128)(2,1)S(1)} %bitcast.7, bf16[64,640]{1,0:T(8,128)(2,1)S(1)} %collective-permute-done.even_ref.ce_ref, ...), custom_call_target="tpu_custom_call" | custom-call | flops 566231040 | tf_op jit(solution)/shard_map/input_grad/pallas_call | solution.py:180
  10.6 1.3 %collective-permute-start.2 = (f32[64,640]{1,0:T(8,128)S(1)}, f32[64,640]{1,0:T(8,128)S(1)}, u32[]{:S(2)}, u32[]{:S(2)}) collective-permute-start(f32[64,640]{1,0:T(8,128)S(1)} %get-tuple-element.26), channel_id=1, source_target_pairs={{0,1},{1,0},{2,3},{3,2},{4,5},{5,4},{6,7},{7,6},{8,9},{9,8},{10,11... | collective-permute-start | bytes 491528 | tf_op jit(solution)/shard_map/ppermute | solution.py:230
  11.9 0.1 collective-permute-done.5.refs_3_
  12.1 3.9 %collective-permute-done.4.refs_2_ = bf16[64,640]{1,0:T(8,128)(2,1)S(1)} collective-permute-done((bf16[64,640]{1,0:T(8,128)(2,1)S(1)}, bf16[64,640]{1,0:T(8,128)(2,1)S(1)}, u32[]{:S(2)}, u32[]{:S(2)}) %collective-permute-start.4) | collective-permute-done | bytes 81952 | tf_op jit(solution)/shard_map/ppermute | solution.py:218
  16.0 0.0 collective-permute-done.3.refs_1_
  16.0 0.1 gather.1
  16.1 0.1 collective-permute-start.7
  16.2 1.1 %collective-permute-start.8 = (bf16[64,640]{1,0:T(8,128)(2,1)S(1)}, bf16[64,640]{1,0:T(8,128)(2,1)S(1)}, u32[]{:S(2)}, u32[]{:S(2)}) collective-permute-start(bf16[64,640]{1,0:T(8,128)(2,1)S(1)} %get-tuple-element.33), channel_id=1, source_target_pairs={{0,8},{4,12},{8,0},{12,4},{1,9},{5,13},{9,1},{13,5},{2,10},{6,14},... | collective-permute-start | bytes 245768 | tf_op jit(solution)/shard_map/ppermute | solution.py:245
  17.2 0.8 %collective-permute-start.6 = (bf16[128,640]{1,0:T(8,128)(2,1)S(1)}, bf16[128,640]{1,0:T(8,128)(2,1)S(1)}, u32[]{:S(2)}, u32[]{:S(2)}) collective-permute-start(bf16[128,640]{1,0:T(8,128)(2,1)S(1)} %get-tuple-element.31), channel_id=1, source_target_pairs={{0,4},{4,0},{8,12},{12,8},{1,5},{5,1},{9,13},{13,9},{2,6},{6,2},{1... | collective-permute-start | bytes 491528 | tf_op jit(solution)/shard_map/ppermute | solution.py:248
  18.0 0.6 %collective-permute-done.2.got_ref = f32[64,640]{1,0:T(8,128)S(1)} collective-permute-done((f32[64,640]{1,0:T(8,128)S(1)}, f32[64,640]{1,0:T(8,128)S(1)}, u32[]{:S(2)}, u32[]{:S(2)}) %collective-permute-start.2) | collective-permute-done | bytes 163872 | tf_op jit(solution)/shard_map/ppermute | solution.py:230
  18.7 1.2 %collective-permute-start.9 = (f32[64,640]{1,0:T(8,128)S(1)}, f32[64,640]{1,0:T(8,128)S(1)}, u32[]{:S(2)}, u32[]{:S(2)}) collective-permute-start(f32[64,640]{1,0:T(8,128)S(1)} %fold.1.token_ref), channel_id=1, source_target_pairs={{0,2},{1,3},{2,0},{3,1},{4,6},{5,7},{6,4},{7,5},{8,10},{9,11},{10,... | collective-permute-start | bytes 491528 | tf_op jit(solution)/shard_map/ppermute | solution.py:232
  19.9 1.4 %early.1 = (f32[64,640]{1,0:T(8,128)S(1)}, f32[64,640]{1,0:T(8,128)S(1)}, f32[64,640]{1,0:T(8,128)S(1)}, bf16[3,192,640]{2,1,0:T(8,128)(2,1)S(1)}) custom-call(f32[64,640]{1,0:T(8,128)S(1)} %fold.1.token_ref, bf16[1728,256]{1,0:T(8,128)(2,1)S(1)} %bitcast.4, bf16[256,640]{1,0:T(8,128)(2,1)S(1)} %get-tuple-element.29.f_ref, bf16[64,640]{1,0:T(8,128)(2,1)S(1)} %bitcast.9, ...), custom_call_target="tpu_custom_call" | custom-call | tf_op jit(solution)/shard_map/early/pallas_call | solution.py:180
  21.3 2.5 %collective-permute-start.10 = (f32[64,640]{1,0:T(8,128)S(1)}, f32[64,640]{1,0:T(8,128)S(1)}, u32[]{:S(2)}, u32[]{:S(2)}) collective-permute-start(f32[64,640]{1,0:T(8,128)S(1)} %get-tuple-element.38), channel_id=1, source_target_pairs={{0,1},{1,0},{2,3},{3,2},{4,5},{5,4},{6,7},{7,6},{8,9},{9,8},{10,11... | collective-permute-start | bytes 491528 | tf_op jit(solution)/shard_map/ppermute | solution.py:257
  23.9 0.0 collective-permute-done.7.go_ref
  23.9 0.0 collective-permute-start.11
  23.9 0.0 collective-permute-done.8.refs_0_
  23.9 0.6 %collective-permute-start.12 = (f32[64,640]{1,0:T(8,128)S(1)}, f32[64,640]{1,0:T(8,128)S(1)}, u32[]{:S(2)}, u32[]{:S(2)}) collective-permute-start(f32[64,640]{1,0:T(8,128)S(1)} %get-tuple-element.42), channel_id=1, source_target_pairs={{0,4},{4,0},{8,12},{12,8},{1,5},{5,1},{9,13},{13,9},{2,6},{6,2},{1... | collective-permute-start | bytes 491528 | tf_op jit(solution)/shard_map/ppermute | solution.py:259
  24.6 0.0 collective-permute-done.6.ge_ref
  24.6 2.3 %weight_grad.1 = (f32[27,64,64]{2,1,0:T(8,128)}, f32[8,128]{1,0:T(8,128)S(1)}) custom-call(bf16[3,192,640]{2,1,0:T(8,128)(2,1)S(1)} %get-tuple-element.30.moved_ref, bf16[256,640]{1,0:T(8,128)(2,1)S(1)} %get-tuple-element.29.f_ref, bf16[128,640]{1,0:T(8,128)(2,1)S(1)} %collective-permute-done.6.ge_ref, bf16[64,640]{1,0:T(8,128)(2,1)S(1)} %collective-permute-done.7.go_ref, ...), custom_call_target="tpu_custom_call" | custom-call | tf_op jit(solution)/shard_map/weight_grad/pallas_call | solution.py:180
  26.8 2.1 %collective-permute-done.9.refs_1_ = f32[64,640]{1,0:T(8,128)S(1)} collective-permute-done((f32[64,640]{1,0:T(8,128)S(1)}, f32[64,640]{1,0:T(8,128)S(1)}, u32[]{:S(2)}, u32[]{:S(2)}) %collective-permute-start.9) | collective-permute-done | bytes 163872 | tf_op jit(solution)/shard_map/ppermute | solution.py:232
  28.9 1.2 %collective-permute-done.10.refs_2_ = f32[64,640]{1,0:T(8,128)S(1)} collective-permute-done((f32[64,640]{1,0:T(8,128)S(1)}, f32[64,640]{1,0:T(8,128)S(1)}, u32[]{:S(2)}, u32[]{:S(2)}) %collective-permute-start.10) | collective-permute-done | bytes 163872 | tf_op jit(solution)/shard_map/ppermute | solution.py:257
  30.1 0.7 %input_total.1 = (f32[64,1,640]{2,1,0:T(1,128)}, f32[8,128]{1,0:T(8,128)S(1)}) custom-call(f32[8,128]{1,0:T(8,128)S(1)} %get-tuple-element.34.token_ref, f32[64,640]{1,0:T(8,128)S(1)} %get-tuple-element.35.refs_0_, f32[64,640]{1,0:T(8,128)S(1)} %collective-permute-done.9.refs_1_, f32[64,640]{1,0:T(8,128)S(1)} %collective-permute-done.10.refs_2_), custom_call_target="tpu_custom_call" | custom-call | flops 566231040 | tf_op jit(solution)/shard_map/input_total/pallas_call | solution.py:180
  30.8 0.0 collective-permute-done.11.odd_ref
  30.8 0.0 collective-permute-done.12.even_ref
  30.8 0.7 %output_total.1 = f32[64,1,640]{2,1,0:T(1,128)} custom-call(f32[8,128]{1,0:T(8,128)S(1)} %get-tuple-element.39.token_ref, f32[64,640]{1,0:T(8,128)S(1)} %get-tuple-element.40.own_ref, f32[64,640]{1,0:T(8,128)S(1)} %collective-permute-done.11.odd_ref, f32[64,640]{1,0:T(8,128)S(1)} %collective-permute-done.12.even_ref), custom_call_target="tpu_custom_call" | custom-call | tf_op jit(solution)/shard_map/output_total/pallas_call | solution.py:180
  (2 shorter events, 0.0 us)
Async XLA Ops:
  0.6 4.3 %copy-start.2 = (bf16[64,1,640]{2,0,1:T(8,128)(2,1)S(1)}, bf16[64,1,640]{2,0,1:T(8,128)(2,1)}, u32[]{:S(2)}) copy-start(bf16[64,1,640]{2,0,1:T(8,128)(2,1)} %param.3) | copy-start | bytes 245764
  0.6 8.7 %copy-start = (bf16[27,64,256]{2,1,0:T(8,128)(2,1)S(1)}, bf16[27,64,256]{2,1,0:T(8,128)(2,1)}, u32[]{:S(2)}) copy-start(bf16[27,64,256]{2,1,0:T(8,128)(2,1)} %param.4) | copy-start | bytes 2654212
  0.7 8.7 %copy-start.1 = (bf16[64,1,640]{2,0,1:T(8,128)(2,1)S(1)}, bf16[64,1,640]{2,0,1:T(8,128)(2,1)}, u32[]{:S(2)}) copy-start(bf16[64,1,640]{2,0,1:T(8,128)(2,1)} %param.5) | copy-start | bytes 245764
  0.7 8.6 %collective-permute-start.1 = (bf16[64,640]{1,0:T(8,128)(2,1)}, bf16[64,640]{1,0:T(8,128)(2,1)S(1)}, u32[]{:S(2)}, u32[]{:S(2)}) collective-permute-start(bf16[64,640]{1,0:T(8,128)(2,1)} %bitcast.5), channel_id=1, source_target_pairs={{0,12},{4,8},{8,4},{12,0},{1,13},{5,9},{9,5},{13,1},{2,14},{6,10},... | collective-permute-start | bytes 245768 | tf_op jit(solution)/shard_map/ppermute | solution.py:215
  3.1 1.8 %collective-permute-start = (bf16[64,640]{1,0:T(8,128)(2,1)}, bf16[64,640]{1,0:T(8,128)(2,1)S(1)}, u32[]{:S(2)}, u32[]{:S(2)}) collective-permute-start(bf16[64,640]{1,0:T(8,128)(2,1)} %bitcast.6), channel_id=1, source_target_pairs={{0,4},{4,0},{8,12},{12,8},{1,5},{5,1},{9,13},{13,9},{2,6},{6,2},{1... | collective-permute-start | bytes 245768 | tf_op jit(solution)/shard_map/ppermute | solution.py:214
  4.9 7.2 %collective-permute-start.5 = (bf16[64,640]{1,0:T(8,128)(2,1)S(1)}, bf16[64,640]{1,0:T(8,128)(2,1)S(1)}, u32[]{:S(2)}, u32[]{:S(2)}) collective-permute-start(bf16[64,640]{1,0:T(8,128)(2,1)S(1)} %bitcast.10), channel_id=1, source_target_pairs={{0,3},{1,2},{2,1},{3,0},{4,7},{5,6},{6,5},{7,4},{8,11},{9,10},{10,... | collective-permute-start | bytes 245768 | tf_op jit(solution)/shard_map/ppermute | solution.py:218
  8.5 7.5 %collective-permute-start.4 = (bf16[64,640]{1,0:T(8,128)(2,1)S(1)}, bf16[64,640]{1,0:T(8,128)(2,1)S(1)}, u32[]{:S(2)}, u32[]{:S(2)}) collective-permute-start(bf16[64,640]{1,0:T(8,128)(2,1)S(1)} %bitcast.11), channel_id=1, source_target_pairs={{0,2},{1,3},{2,0},{3,1},{4,6},{5,7},{6,4},{7,5},{8,10},{9,11},{10,... | collective-permute-start | bytes 245768 | tf_op jit(solution)/shard_map/ppermute | solution.py:218
  8.5 7.5 %collective-permute-start.3 = (bf16[64,640]{1,0:T(8,128)(2,1)S(1)}, bf16[64,640]{1,0:T(8,128)(2,1)S(1)}, u32[]{:S(2)}, u32[]{:S(2)}) collective-permute-start(bf16[64,640]{1,0:T(8,128)(2,1)S(1)} %bitcast.12), channel_id=1, source_target_pairs={{0,1},{1,0},{2,3},{3,2},{4,5},{5,4},{6,7},{7,6},{8,9},{9,8},{10,11... | collective-permute-start | bytes 245768 | tf_op jit(solution)/shard_map/ppermute | solution.py:218
  10.6 8.0 %collective-permute-start.2 = (f32[64,640]{1,0:T(8,128)S(1)}, f32[64,640]{1,0:T(8,128)S(1)}, u32[]{:S(2)}, u32[]{:S(2)}) collective-permute-start(f32[64,640]{1,0:T(8,128)S(1)} %get-tuple-element.26), channel_id=1, source_target_pairs={{0,1},{1,0},{2,3},{3,2},{4,5},{5,4},{6,7},{7,6},{8,9},{9,8},{10,11... | collective-permute-start | bytes 491528 | tf_op jit(solution)/shard_map/ppermute | solution.py:230
  16.1 7.8 %collective-permute-start.7 = (bf16[64,640]{1,0:T(8,128)(2,1)S(1)}, bf16[64,640]{1,0:T(8,128)(2,1)S(1)}, u32[]{:S(2)}, u32[]{:S(2)}) collective-permute-start(bf16[64,640]{1,0:T(8,128)(2,1)S(1)} %get-tuple-element.32), channel_id=1, source_target_pairs={{0,12},{4,8},{8,4},{12,0},{1,13},{5,9},{9,5},{13,1},{2,14},{6,10},... | collective-permute-start | bytes 245768 | tf_op jit(solution)/shard_map/ppermute | solution.py:243
  16.2 7.7 %collective-permute-start.8 = (bf16[64,640]{1,0:T(8,128)(2,1)S(1)}, bf16[64,640]{1,0:T(8,128)(2,1)S(1)}, u32[]{:S(2)}, u32[]{:S(2)}) collective-permute-start(bf16[64,640]{1,0:T(8,128)(2,1)S(1)} %get-tuple-element.33), channel_id=1, source_target_pairs={{0,8},{4,12},{8,0},{12,4},{1,9},{5,13},{9,1},{13,5},{2,10},{6,14},... | collective-permute-start | bytes 245768 | tf_op jit(solution)/shard_map/ppermute | solution.py:245
  17.2 7.3 %collective-permute-start.6 = (bf16[128,640]{1,0:T(8,128)(2,1)S(1)}, bf16[128,640]{1,0:T(8,128)(2,1)S(1)}, u32[]{:S(2)}, u32[]{:S(2)}) collective-permute-start(bf16[128,640]{1,0:T(8,128)(2,1)S(1)} %get-tuple-element.31), channel_id=1, source_target_pairs={{0,4},{4,0},{8,12},{12,8},{1,5},{5,1},{9,13},{13,9},{2,6},{6,2},{1... | collective-permute-start | bytes 491528 | tf_op jit(solution)/shard_map/ppermute | solution.py:248
  18.7 10.2 %collective-permute-start.9 = (f32[64,640]{1,0:T(8,128)S(1)}, f32[64,640]{1,0:T(8,128)S(1)}, u32[]{:S(2)}, u32[]{:S(2)}) collective-permute-start(f32[64,640]{1,0:T(8,128)S(1)} %fold.1.token_ref), channel_id=1, source_target_pairs={{0,2},{1,3},{2,0},{3,1},{4,6},{5,7},{6,4},{7,5},{8,10},{9,11},{10,... | collective-permute-start | bytes 491528 | tf_op jit(solution)/shard_map/ppermute | solution.py:232
  21.3 8.7 %collective-permute-start.10 = (f32[64,640]{1,0:T(8,128)S(1)}, f32[64,640]{1,0:T(8,128)S(1)}, u32[]{:S(2)}, u32[]{:S(2)}) collective-permute-start(f32[64,640]{1,0:T(8,128)S(1)} %get-tuple-element.38), channel_id=1, source_target_pairs={{0,1},{1,0},{2,3},{3,2},{4,5},{5,4},{6,7},{7,6},{8,9},{9,8},{10,11... | collective-permute-start | bytes 491528 | tf_op jit(solution)/shard_map/ppermute | solution.py:257
  23.9 6.9 %collective-permute-start.11 = (f32[64,640]{1,0:T(8,128)S(1)}, f32[64,640]{1,0:T(8,128)S(1)}, u32[]{:S(2)}, u32[]{:S(2)}) collective-permute-start(f32[64,640]{1,0:T(8,128)S(1)} %get-tuple-element.41), channel_id=1, source_target_pairs={{0,12},{4,8},{8,4},{12,0},{1,13},{5,9},{9,5},{13,1},{2,14},{6,10},... | collective-permute-start | bytes 491528 | tf_op jit(solution)/shard_map/ppermute | solution.py:258
  23.9 6.9 %collective-permute-start.12 = (f32[64,640]{1,0:T(8,128)S(1)}, f32[64,640]{1,0:T(8,128)S(1)}, u32[]{:S(2)}, u32[]{:S(2)}) collective-permute-start(f32[64,640]{1,0:T(8,128)S(1)} %get-tuple-element.42), channel_id=1, source_target_pairs={{0,4},{4,0},{8,12},{12,8},{1,5},{5,1},{9,13},{13,9},{2,6},{6,2},{1... | collective-permute-start | bytes 491528 | tf_op jit(solution)/shard_map/ppermute | solution.py:259

commit v16 on v13

--- a/solution.py
+++ b/solution.py
@@ -214,7 +214,7 @@
     cot_even = lax.ppermute(cot, "sp", even_pairs)
     cot_odd = lax.ppermute(cot, "sp", odd_pairs)
     (begin,) = kernel_call(token_kernel, "begin", [small], [], weight=W_BEGIN * work)
-    feat, cot_even = lax.optimization_barrier((feat, cot_even))
+    feat, begin = lax.optimization_barrier((feat, begin))
     pieces = [feat] + [lax.ppermute(feat, "ch", mixed(k)) for k in range(1, nc)]
 
     *parts, token = kernel_call(

time: 31.3 us -> 30.2 us (0.965)
  waiting for transfers between devices: 9.64 us -> 8.4 us
    ppermute x1, waiting for transfers between devices: 1.13 us -> 0.01 us  [per_device(): cot_even = lax.ppermute(cot, 'sp', even_pairs)]
    ppermute x1, waiting for transfers between devices: 3.44 us -> 4.35 us  [per_device(): terms.append(lax.ppermute(both, 'ch', mixed(k)))]
    ppermute x1, waiting for transfers between devices: 0.97 us -> 0.26 us  [per_device(): terms.append(lax.ppermute(parts[1], 'ch', mixed(1)))]
    ppermute x1, starting transfers between devices: 0.88 us -> 1.55 us  [per_device(): terms.append(lax.ppermute(parts[1], 'ch', mixed(1)))]
    ppermute x1, starting transfers between devices: 1.77 us -> 1.43 us  [per_device(): terms.append(lax.ppermute(both, 'ch', mixed(k)))]
  transfers between devices with their start and end apart: 13 -> 13, of which waited for: 5 -> 3; matrix products, arithmetic and copies ran while one was open for 0% -> 0% of each run, Pallas kernels for 19% -> 19%
where the time goes in v16:
time: 30.2 us; the launch traced here: 30.1 us
  starting transfers between devices  14.4 us (48%)
  waiting for transfers between devices  8.4 us (28%)
  Pallas kernels  6.54 us (22%)
  between operations  0.72 us (2%)
    pallas_call x8, Pallas kernels, kernel_call(): pl.pallas_call(body, out_shape=outs, in_specs=[SMEM if a.dtype == jnp.int...  6.54 us
    ppermute x3, starting transfers between devices, per_device(): pieces = [feat] + [lax.ppermute(feat, 'ch', mixed(k)) for k in range(1, nc)]  4.39 us
    ppermute x1, waiting for transfers between devices, per_device(): terms.append(lax.ppermute(both, 'ch', mixed(k)))  4.35 us
    ppermute x3, waiting for transfers between devices, per_device(): pieces = [feat] + [lax.ppermute(feat, 'ch', mixed(k)) for k in range(1, nc)]  3.77 us
    ppermute x1, starting transfers between devices, per_device(): cot_odd = lax.ppermute(cot, 'sp', odd_pairs)  2.44 us
    ppermute x1, starting transfers between devices, per_device(): terms.append(lax.ppermute(parts[1], 'ch', mixed(1)))  1.55 us
    ppermute x1, starting transfers between devices, per_device(): terms.append(lax.ppermute(both, 'ch', mixed(k)))  1.43 us
    ppermute x1, starting transfers between devices, per_device(): got = lax.ppermute(parts[k + 1], 'ch', mixed(1))  1.3 us
  transfers between devices with their start and end apart: 13, of which 3 were waited for; matrix products, arithmetic and copies ran while one was open for 0% of the time, Pallas kernels for 19%

profile of v16, /device:TPU:0, one launch (start us, length us, event | category | flops | bytes accessed | tf_op | source)
XLA Modules:
  0.0 30.1 jit_solution(7361071358386343291)
XLA Ops:
  0.6 0.0 copy-start.2
  0.6 0.0 copy-start
  0.7 0.0 copy-start.1
  0.7 2.4 %collective-permute-start.1 = (bf16[64,640]{1,0:T(8,128)(2,1)}, bf16[64,640]{1,0:T(8,128)(2,1)S(1)}, u32[]{:S(2)}, u32[]{:S(2)}) collective-permute-start(bf16[64,640]{1,0:T(8,128)(2,1)} %bitcast.5), channel_id=1, source_target_pairs={{0,12},{4,8},{8,4},{12,0},{1,13},{5,9},{9,5},{13,1},{2,14},{6,10},... | collective-permute-start | bytes 245768 | tf_op jit(solution)/shard_map/ppermute | solution.py:215
  3.1 0.7 %collective-permute-start = (bf16[64,640]{1,0:T(8,128)(2,1)}, bf16[64,640]{1,0:T(8,128)(2,1)S(1)}, u32[]{:S(2)}, u32[]{:S(2)}) collective-permute-start(bf16[64,640]{1,0:T(8,128)(2,1)} %bitcast.6), channel_id=1, source_target_pairs={{0,4},{4,0},{8,12},{12,8},{1,5},{5,1},{9,13},{13,9},{2,6},{6,2},{1... | collective-permute-start | bytes 245768 | tf_op jit(solution)/shard_map/ppermute | solution.py:214
  3.8 0.0 copy-done.2
  3.8 3.6 %collective-permute-start.4 = (bf16[64,640]{1,0:T(8,128)(2,1)S(1)}, bf16[64,640]{1,0:T(8,128)(2,1)S(1)}, u32[]{:S(2)}, u32[]{:S(2)}) collective-permute-start(bf16[64,640]{1,0:T(8,128)(2,1)S(1)} %bitcast.10), channel_id=1, source_target_pairs={{0,3},{1,2},{2,1},{3,0},{4,7},{5,6},{6,5},{7,4},{8,11},{9,10},{10,... | collective-permute-start | bytes 245768 | tf_op jit(solution)/shard_map/ppermute | solution.py:218
  7.4 0.0 collective-permute-start.3
  7.4 0.8 %collective-permute-start.2 = (bf16[64,640]{1,0:T(8,128)(2,1)S(1)}, bf16[64,640]{1,0:T(8,128)(2,1)S(1)}, u32[]{:S(2)}, u32[]{:S(2)}) collective-permute-start(bf16[64,640]{1,0:T(8,128)(2,1)S(1)} %bitcast.12), channel_id=1, source_target_pairs={{0,1},{1,0},{2,3},{3,2},{4,5},{5,4},{6,7},{7,6},{8,9},{9,8},{10,11... | collective-permute-start | bytes 245768 | tf_op jit(solution)/shard_map/ppermute | solution.py:218
  8.2 0.0 collective-permute-done.1.odd_ref.near_ref.co_ref
  8.2 0.0 collective-permute-done.even_ref.ce_ref
  8.2 0.0 copy-done
  8.2 0.0 copy-done.1
  8.2 1.3 %input_grad.1 = (f32[64,640]{1,0:T(8,128)S(1)}, f32[64,640]{1,0:T(8,128)S(1)}, f32[64,640]{1,0:T(8,128)S(1)}, f32[64,640]{1,0:T(8,128)S(1)}, f32[8,128]{1,0:T(8,128)S(1)}) custom-call(f32[8,128]{1,0:T(8,128)S(1)} %begin.1.begin_ref, bf16[64,640]{1,0:T(8,128)(2,1)S(1)} %bitcast.7, bf16[64,640]{1,0:T(8,128)(2,1)S(1)} %collective-permute-done.even_ref.ce_ref, ...), custom_call_target="tpu_custom_call" | custom-call | flops 566231040 | tf_op jit(solution)/shard_map/input_grad/pallas_call | solution.py:180
  9.5 1.3 %collective-permute-start.8 = (f32[64,640]{1,0:T(8,128)S(1)}, f32[64,640]{1,0:T(8,128)S(1)}, u32[]{:S(2)}, u32[]{:S(2)}) collective-permute-start(f32[64,640]{1,0:T(8,128)S(1)} %get-tuple-element.33), channel_id=1, source_target_pairs={{0,1},{1,0},{2,3},{3,2},{4,5},{5,4},{6,7},{7,6},{8,9},{9,8},{10,11... | collective-permute-start | bytes 491528 | tf_op jit(solution)/shard_map/ppermute | solution.py:230
  10.8 0.0 collective-permute-done.4.refs_3_
  10.8 3.8 %collective-permute-done.3.refs_2_ = bf16[64,640]{1,0:T(8,128)(2,1)S(1)} collective-permute-done((bf16[64,640]{1,0:T(8,128)(2,1)S(1)}, bf16[64,640]{1,0:T(8,128)(2,1)S(1)}, u32[]{:S(2)}, u32[]{:S(2)}) %collective-permute-start.3) | collective-permute-done | bytes 81952 | tf_op jit(solution)/shard_map/ppermute | solution.py:218
  14.6 0.0 collective-permute-done.2.refs_1_
  14.6 0.1 gather.1
  14.7 0.1 collective-permute-start.6
  14.7 0.8 %collective-permute-start.7 = (bf16[64,640]{1,0:T(8,128)(2,1)S(1)}, bf16[64,640]{1,0:T(8,128)(2,1)S(1)}, u32[]{:S(2)}, u32[]{:S(2)}) collective-permute-start(bf16[64,640]{1,0:T(8,128)(2,1)S(1)} %get-tuple-element.29), channel_id=1, source_target_pairs={{0,8},{4,12},{8,0},{12,4},{1,9},{5,13},{9,1},{13,5},{2,10},{6,14},... | collective-permute-start | bytes 245768 | tf_op jit(solution)/shard_map/ppermute | solution.py:246
  15.5 1.6 %collective-permute-start.10 = (f32[64,640]{1,0:T(8,128)S(1)}, f32[64,640]{1,0:T(8,128)S(1)}, u32[]{:S(2)}, u32[]{:S(2)}) collective-permute-start(f32[64,640]{1,0:T(8,128)S(1)} %get-tuple-element.34), channel_id=1, source_target_pairs={{0,1},{1,0},{2,3},{3,2},{4,5},{5,4},{6,7},{7,6},{8,9},{9,8},{10,11... | collective-permute-start | bytes 491528 | tf_op jit(solution)/shard_map/ppermute | solution.py:233
  17.1 0.9 %collective-permute-start.5 = (bf16[128,640]{1,0:T(8,128)(2,1)S(1)}, bf16[128,640]{1,0:T(8,128)(2,1)S(1)}, u32[]{:S(2)}, u32[]{:S(2)}) collective-permute-start(bf16[128,640]{1,0:T(8,128)(2,1)S(1)} %get-tuple-element.27), channel_id=1, source_target_pairs={{0,4},{4,0},{8,12},{12,8},{1,5},{5,1},{9,13},{13,9},{2,6},{6,2},{1... | collective-permute-start | bytes 491528 | tf_op jit(solution)/shard_map/ppermute | solution.py:249
  18.0 0.0 collective-permute-done.8.got_ref
  18.0 1.4 %collective-permute-start.9 = (f32[64,640]{1,0:T(8,128)S(1)}, f32[64,640]{1,0:T(8,128)S(1)}, u32[]{:S(2)}, u32[]{:S(2)}) collective-permute-start(f32[64,640]{1,0:T(8,128)S(1)} %fold.1), channel_id=1, source_target_pairs={{0,2},{1,3},{2,0},{3,1},{4,6},{5,7},{6,4},{7,5},{8,10},{9,11},{10,... | collective-permute-start | bytes 491528 | tf_op jit(solution)/shard_map/ppermute | solution.py:232
  19.4 1.4 %early.1 = (f32[64,640]{1,0:T(8,128)S(1)}, f32[64,640]{1,0:T(8,128)S(1)}, f32[64,640]{1,0:T(8,128)S(1)}, bf16[3,192,640]{2,1,0:T(8,128)(2,1)S(1)}) custom-call(bf16[1728,256]{1,0:T(8,128)(2,1)S(1)} %bitcast.4, bf16[256,640]{1,0:T(8,128)(2,1)S(1)} %get-tuple-element.25.f_ref, bf16[64,640]{1,0:T(8,128)(2,1)S(1)} %bitcast.9, ...), custom_call_target="tpu_custom_call" | custom-call | tf_op jit(solution)/shard_map/early/pallas_call | solution.py:180
  20.9 0.0 collective-permute-done.6.go_ref
  20.9 0.4 %collective-permute-start.11 = (f32[64,640]{1,0:T(8,128)S(1)}, f32[64,640]{1,0:T(8,128)S(1)}, u32[]{:S(2)}, u32[]{:S(2)}) collective-permute-start(f32[64,640]{1,0:T(8,128)S(1)} %get-tuple-element.37), channel_id=1, source_target_pairs={{0,12},{4,8},{8,4},{12,0},{1,13},{5,9},{9,5},{13,1},{2,14},{6,10},... | collective-permute-start | bytes 491528 | tf_op jit(solution)/shard_map/ppermute | solution.py:257
  21.3 0.0 collective-permute-done.7.refs_0_
  21.3 0.4 %collective-permute-start.12 = (f32[64,640]{1,0:T(8,128)S(1)}, f32[64,640]{1,0:T(8,128)S(1)}, u32[]{:S(2)}, u32[]{:S(2)}) collective-permute-start(f32[64,640]{1,0:T(8,128)S(1)} %get-tuple-element.38), channel_id=1, source_target_pairs={{0,4},{4,0},{8,12},{12,8},{1,5},{5,1},{9,13},{13,9},{2,6},{6,2},{1... | collective-permute-start | bytes 491528 | tf_op jit(solution)/shard_map/ppermute | solution.py:258
  21.7 0.0 collective-permute-done.5.ge_ref
  21.7 2.3 %weight_grad.1 = (f32[27,64,64]{2,1,0:T(8,128)}, f32[8,128]{1,0:T(8,128)S(1)}) custom-call(bf16[3,192,640]{2,1,0:T(8,128)(2,1)S(1)} %get-tuple-element.26.moved_ref, bf16[256,640]{1,0:T(8,128)(2,1)S(1)} %get-tuple-element.25.f_ref, bf16[128,640]{1,0:T(8,128)(2,1)S(1)} %collective-permute-done.5.ge_ref, bf16[64,640]{1,0:T(8,128)(2,1)S(1)} %collective-permute-done.6.go_ref, ...), custom_call_target="tpu_custom_call" | custom-call | tf_op jit(solution)/shard_map/weight_grad/pallas_call | solution.py:180
  24.0 0.3 collective-permute-done.10.refs_2_
  24.3 4.3 %collective-permute-done.9.refs_1_ = f32[64,640]{1,0:T(8,128)S(1)} collective-permute-done((f32[64,640]{1,0:T(8,128)S(1)}, f32[64,640]{1,0:T(8,128)S(1)}, u32[]{:S(2)}, u32[]{:S(2)}) %collective-permute-start.9) | collective-permute-done | bytes 163872 | tf_op jit(solution)/shard_map/ppermute | solution.py:232
  28.6 0.7 %input_total.1 = (f32[64,1,640]{2,1,0:T(1,128)}, f32[8,128]{1,0:T(8,128)S(1)}) custom-call(f32[8,128]{1,0:T(8,128)S(1)} %get-tuple-element.30.token_ref, f32[64,640]{1,0:T(8,128)S(1)} %get-tuple-element.31.refs_0_, f32[64,640]{1,0:T(8,128)S(1)} %collective-permute-done.9.refs_1_, f32[64,640]{1,0:T(8,128)S(1)} %collective-permute-done.10.refs_2_), custom_call_target="tpu_custom_call" | custom-call | flops 566231040 | tf_op jit(solution)/shard_map/input_total/pallas_call | solution.py:180
  29.3 0.0 collective-permute-done.11.odd_ref
  29.3 0.0 collective-permute-done.12.even_ref
  29.3 0.7 %output_total.1 = f32[64,1,640]{2,1,0:T(1,128)} custom-call(f32[8,128]{1,0:T(8,128)S(1)} %get-tuple-element.35.token_ref, f32[64,640]{1,0:T(8,128)S(1)} %get-tuple-element.36.own_ref, f32[64,640]{1,0:T(8,128)S(1)} %collective-permute-done.11.odd_ref, f32[64,640]{1,0:T(8,128)S(1)} %collective-permute-done.12.even_ref), custom_call_target="tpu_custom_call" | custom-call | tf_op jit(solution)/shard_map/output_total/pallas_call | solution.py:180
  (2 shorter events, 0.0 us)
Async XLA Ops:
  0.6 3.2 %copy-start.2 = (bf16[64,1,640]{2,0,1:T(8,128)(2,1)S(1)}, bf16[64,1,640]{2,0,1:T(8,128)(2,1)}, u32[]{:S(2)}) copy-start(bf16[64,1,640]{2,0,1:T(8,128)(2,1)} %param.3) | copy-start | bytes 245764
  0.6 7.5 %copy-start = (bf16[27,64,256]{2,1,0:T(8,128)(2,1)S(1)}, bf16[27,64,256]{2,1,0:T(8,128)(2,1)}, u32[]{:S(2)}) copy-start(bf16[27,64,256]{2,1,0:T(8,128)(2,1)} %param.4) | copy-start | bytes 2654212
  0.7 7.5 %copy-start.1 = (bf16[64,1,640]{2,0,1:T(8,128)(2,1)S(1)}, bf16[64,1,640]{2,0,1:T(8,128)(2,1)}, u32[]{:S(2)}) copy-start(bf16[64,1,640]{2,0,1:T(8,128)(2,1)} %param.5) | copy-start | bytes 245764
  0.7 7.5 %collective-permute-start.1 = (bf16[64,640]{1,0:T(8,128)(2,1)}, bf16[64,640]{1,0:T(8,128)(2,1)S(1)}, u32[]{:S(2)}, u32[]{:S(2)}) collective-permute-start(bf16[64,640]{1,0:T(8,128)(2,1)} %bitcast.5), channel_id=1, source_target_pairs={{0,12},{4,8},{8,4},{12,0},{1,13},{5,9},{9,5},{13,1},{2,14},{6,10},... | collective-permute-start | bytes 245768 | tf_op jit(solution)/shard_map/ppermute | solution.py:215
  3.1 5.1 %collective-permute-start = (bf16[64,640]{1,0:T(8,128)(2,1)}, bf16[64,640]{1,0:T(8,128)(2,1)S(1)}, u32[]{:S(2)}, u32[]{:S(2)}) collective-permute-start(bf16[64,640]{1,0:T(8,128)(2,1)} %bitcast.6), channel_id=1, source_target_pairs={{0,4},{4,0},{8,12},{12,8},{1,5},{5,1},{9,13},{13,9},{2,6},{6,2},{1... | collective-permute-start | bytes 245768 | tf_op jit(solution)/shard_map/ppermute | solution.py:214
  3.8 7.0 %collective-permute-start.4 = (bf16[64,640]{1,0:T(8,128)(2,1)S(1)}, bf16[64,640]{1,0:T(8,128)(2,1)S(1)}, u32[]{:S(2)}, u32[]{:S(2)}) collective-permute-start(bf16[64,640]{1,0:T(8,128)(2,1)S(1)} %bitcast.10), channel_id=1, source_target_pairs={{0,3},{1,2},{2,1},{3,0},{4,7},{5,6},{6,5},{7,4},{8,11},{9,10},{10,... | collective-permute-start | bytes 245768 | tf_op jit(solution)/shard_map/ppermute | solution.py:218
  7.4 7.2 %collective-permute-start.3 = (bf16[64,640]{1,0:T(8,128)(2,1)S(1)}, bf16[64,640]{1,0:T(8,128)(2,1)S(1)}, u32[]{:S(2)}, u32[]{:S(2)}) collective-permute-start(bf16[64,640]{1,0:T(8,128)(2,1)S(1)} %bitcast.11), channel_id=1, source_target_pairs={{0,2},{1,3},{2,0},{3,1},{4,6},{5,7},{6,4},{7,5},{8,10},{9,11},{10,... | collective-permute-start | bytes 245768 | tf_op jit(solution)/shard_map/ppermute | solution.py:218
  7.4 7.2 %collective-permute-start.2 = (bf16[64,640]{1,0:T(8,128)(2,1)S(1)}, bf16[64,640]{1,0:T(8,128)(2,1)S(1)}, u32[]{:S(2)}, u32[]{:S(2)}) collective-permute-start(bf16[64,640]{1,0:T(8,128)(2,1)S(1)} %bitcast.12), channel_id=1, source_target_pairs={{0,1},{1,0},{2,3},{3,2},{4,5},{5,4},{6,7},{7,6},{8,9},{9,8},{10,11... | collective-permute-start | bytes 245768 | tf_op jit(solution)/shard_map/ppermute | solution.py:218
  9.5 8.5 %collective-permute-start.8 = (f32[64,640]{1,0:T(8,128)S(1)}, f32[64,640]{1,0:T(8,128)S(1)}, u32[]{:S(2)}, u32[]{:S(2)}) collective-permute-start(f32[64,640]{1,0:T(8,128)S(1)} %get-tuple-element.33), channel_id=1, source_target_pairs={{0,1},{1,0},{2,3},{3,2},{4,5},{5,4},{6,7},{7,6},{8,9},{9,8},{10,11... | collective-permute-start | bytes 491528 | tf_op jit(solution)/shard_map/ppermute | solution.py:230
  14.7 6.2 %collective-permute-start.6 = (bf16[64,640]{1,0:T(8,128)(2,1)S(1)}, bf16[64,640]{1,0:T(8,128)(2,1)S(1)}, u32[]{:S(2)}, u32[]{:S(2)}) collective-permute-start(bf16[64,640]{1,0:T(8,128)(2,1)S(1)} %get-tuple-element.28), channel_id=1, source_target_pairs={{0,12},{4,8},{8,4},{12,0},{1,13},{5,9},{9,5},{13,1},{2,14},{6,10},... | collective-permute-start | bytes 245768 | tf_op jit(solution)/shard_map/ppermute | solution.py:244
  14.7 6.6 %collective-permute-start.7 = (bf16[64,640]{1,0:T(8,128)(2,1)S(1)}, bf16[64,640]{1,0:T(8,128)(2,1)S(1)}, u32[]{:S(2)}, u32[]{:S(2)}) collective-permute-start(bf16[64,640]{1,0:T(8,128)(2,1)S(1)} %get-tuple-element.29), channel_id=1, source_target_pairs={{0,8},{4,12},{8,0},{12,4},{1,9},{5,13},{9,1},{13,5},{2,10},{6,14},... | collective-permute-start | bytes 245768 | tf_op jit(solution)/shard_map/ppermute | solution.py:246
  15.5 8.7 %collective-permute-start.10 = (f32[64,640]{1,0:T(8,128)S(1)}, f32[64,640]{1,0:T(8,128)S(1)}, u32[]{:S(2)}, u32[]{:S(2)}) collective-permute-start(f32[64,640]{1,0:T(8,128)S(1)} %get-tuple-element.34), channel_id=1, source_target_pairs={{0,1},{1,0},{2,3},{3,2},{4,5},{5,4},{6,7},{7,6},{8,9},{9,8},{10,11... | collective-permute-start | bytes 491528 | tf_op jit(solution)/shard_map/ppermute | solution.py:233
  17.1 4.6 %collective-permute-start.5 = (bf16[128,640]{1,0:T(8,128)(2,1)S(1)}, bf16[128,640]{1,0:T(8,128)(2,1)S(1)}, u32[]{:S(2)}, u32[]{:S(2)}) collective-permute-start(bf16[128,640]{1,0:T(8,128)(2,1)S(1)} %get-tuple-element.27), channel_id=1, source_target_pairs={{0,4},{4,0},{8,12},{12,8},{1,5},{5,1},{9,13},{13,9},{2,6},{6,2},{1... | collective-permute-start | bytes 491528 | tf_op jit(solution)/shard_map/ppermute | solution.py:249
  18.0 10.6 %collective-permute-start.9 = (f32[64,640]{1,0:T(8,128)S(1)}, f32[64,640]{1,0:T(8,128)S(1)}, u32[]{:S(2)}, u32[]{:S(2)}) collective-permute-start(f32[64,640]{1,0:T(8,128)S(1)} %fold.1), channel_id=1, source_target_pairs={{0,2},{1,3},{2,0},{3,1},{4,6},{5,7},{6,4},{7,5},{8,10},{9,11},{10,... | collective-permute-start | bytes 491528 | tf_op jit(solution)/shard_map/ppermute | solution.py:232
  20.9 8.5 %collective-permute-start.11 = (f32[64,640]{1,0:T(8,128)S(1)}, f32[64,640]{1,0:T(8,128)S(1)}, u32[]{:S(2)}, u32[]{:S(2)}) collective-permute-start(f32[64,640]{1,0:T(8,128)S(1)} %get-tuple-element.37), channel_id=1, source_target_pairs={{0,12},{4,8},{8,4},{12,0},{1,13},{5,9},{9,5},{13,1},{2,14},{6,10},... | collective-permute-start | bytes 491528 | tf_op jit(solution)/shard_map/ppermute | solution.py:257
  21.3 8.1 %collective-permute-start.12 = (f32[64,640]{1,0:T(8,128)S(1)}, f32[64,640]{1,0:T(8,128)S(1)}, u32[]{:S(2)}, u32[]{:S(2)}) collective-permute-start(f32[64,640]{1,0:T(8,128)S(1)} %get-tuple-element.38), channel_id=1, source_target_pairs={{0,4},{4,0},{8,12},{12,8},{1,5},{5,1},{9,13},{13,9},{2,6},{6,2},{1... | collective-permute-start | bytes 491528 | tf_op jit(solution)/shard_map/ppermute | solution.py:258

commit v17 on v16

--- a/solution.py
+++ b/solution.py
@@ -13,7 +13,7 @@
 CELLS = NX * NY
 F32 = jnp.float32
 BF16 = jnp.bfloat16
-W_GATHER, W_EARLY, W_BEGIN, W_GRAD, W_FOLD, W_TOTAL, W_OUT = 2, 0, 8, 1, 0, 1, 0
+W_GATHER, W_EARLY, W_BEGIN, W_GRAD, W_FOLD, W_TOTAL, W_OUT = 2, 2, 8, 1, 0, 1, 0
 VMEM_BYTES = 32 * 1024 * 1024
 
 

time: 30.2 us -> 28.9 us (0.957)
  starting transfers between devices: 14.4 us -> 13.5 us
  waiting for transfers between devices: 8.4 us -> 7.96 us
    ppermute x1, waiting for transfers between devices: 0.01 us -> 1.28 us  [per_device(): got = lax.ppermute(parts[k + 1], 'ch', mixed(1))]
    ppermute x3, waiting for transfers between devices: 3.77 us -> 2.98 us  [per_device(): pieces = [feat] + [lax.ppermute(feat, 'ch', mixed(k)) for k in range(1, nc)]]
    ppermute x1, starting transfers between devices: 1.55 us -> 0.78 us  [per_device(): terms.append(lax.ppermute(parts[1], 'ch', mixed(1)))]
    ppermute x1, waiting for transfers between devices: 4.35 us -> 3.68 us  [per_device(): terms.append(lax.ppermute(both, 'ch', mixed(k)))]
    ppermute x1, starting transfers between devices: 0.42 us -> 0.07 us  [per_device(): out_odd = lax.ppermute(out_odd, 'sp', odd_pairs)]
  transfers between devices with their start and end apart: 13 -> 13, of which waited for: 3 -> 3; matrix products, arithmetic and copies ran while one was open for 0% -> 0% of each run, Pallas kernels for 19% -> 20%
where the time goes in v17:
time: 28.9 us; the launch traced here: 28.8 us
  starting transfers between devices  13.5 us (47%)
  waiting for transfers between devices  7.96 us (28%)
  Pallas kernels  6.55 us (23%)
  between operations  0.73 us (3%)
    pallas_call x8, Pallas kernels, kernel_call(): pl.pallas_call(body, out_shape=outs, in_specs=[SMEM if a.dtype == jnp.int...  6.55 us
    ppermute x3, starting transfers between devices, per_device(): pieces = [feat] + [lax.ppermute(feat, 'ch', mixed(k)) for k in range(1, nc)]  4.39 us
    ppermute x1, waiting for transfers between devices, per_device(): terms.append(lax.ppermute(both, 'ch', mixed(k)))  3.68 us
    ppermute x3, waiting for transfers between devices, per_device(): pieces = [feat] + [lax.ppermute(feat, 'ch', mixed(k)) for k in range(1, nc)]  2.98 us
    ppermute x1, starting transfers between devices, per_device(): cot_odd = lax.ppermute(cot, 'sp', odd_pairs)  2.44 us
    ppermute x1, starting transfers between devices, per_device(): terms.append(lax.ppermute(both, 'ch', mixed(k)))  1.35 us
    ppermute x1, starting transfers between devices, per_device(): got = lax.ppermute(parts[k + 1], 'ch', mixed(1))  1.32 us
    ppermute x1, waiting for transfers between devices, per_device(): got = lax.ppermute(parts[k + 1], 'ch', mixed(1))  1.28 us
  transfers between devices with their start and end apart: 13, of which 3 were waited for; matrix products, arithmetic and copies ran while one was open for 0% of the time, Pallas kernels for 20%

profile of v17, /device:TPU:0, one launch (start us, length us, event | category | flops | bytes accessed | tf_op | source)
XLA Modules:
  0.0 28.8 jit_solution(6418455279021062248)
XLA Ops:
  0.6 0.0 copy-start.1
  0.6 0.0 copy-start
  0.7 0.0 copy-start.2
  0.7 2.4 %collective-permute-start.1 = (bf16[64,640]{1,0:T(8,128)(2,1)}, bf16[64,640]{1,0:T(8,128)(2,1)S(1)}, u32[]{:S(2)}, u32[]{:S(2)}) collective-permute-start(bf16[64,640]{1,0:T(8,128)(2,1)} %bitcast.9), channel_id=1, source_target_pairs={{0,12},{4,8},{8,4},{12,0},{1,13},{5,9},{9,5},{13,1},{2,14},{6,10},... | collective-permute-start | bytes 245768 | tf_op jit(solution)/shard_map/ppermute | solution.py:215
  3.1 0.7 %collective-permute-start = (bf16[64,640]{1,0:T(8,128)(2,1)}, bf16[64,640]{1,0:T(8,128)(2,1)S(1)}, u32[]{:S(2)}, u32[]{:S(2)}) collective-permute-start(bf16[64,640]{1,0:T(8,128)(2,1)} %bitcast.10), channel_id=1, source_target_pairs={{0,4},{4,0},{8,12},{12,8},{1,5},{5,1},{9,13},{13,9},{2,6},{6,2},{1... | collective-permute-start | bytes 245768 | tf_op jit(solution)/shard_map/ppermute | solution.py:214
  3.8 0.0 copy-done.1
  3.8 3.6 %collective-permute-start.4 = (bf16[64,640]{1,0:T(8,128)(2,1)S(1)}, bf16[64,640]{1,0:T(8,128)(2,1)S(1)}, u32[]{:S(2)}, u32[]{:S(2)}) collective-permute-start(bf16[64,640]{1,0:T(8,128)(2,1)S(1)} %bitcast.5), channel_id=1, source_target_pairs={{0,3},{1,2},{2,1},{3,0},{4,7},{5,6},{6,5},{7,4},{8,11},{9,10},{10,... | collective-permute-start | bytes 245768 | tf_op jit(solution)/shard_map/ppermute | solution.py:218
  7.4 0.0 collective-permute-start.3
  7.4 0.8 %collective-permute-start.2 = (bf16[64,640]{1,0:T(8,128)(2,1)S(1)}, bf16[64,640]{1,0:T(8,128)(2,1)S(1)}, u32[]{:S(2)}, u32[]{:S(2)}) collective-permute-start(bf16[64,640]{1,0:T(8,128)(2,1)S(1)} %bitcast.7), channel_id=1, source_target_pairs={{0,1},{1,0},{2,3},{3,2},{4,5},{5,4},{6,7},{7,6},{8,9},{9,8},{10,11... | collective-permute-start | bytes 245768 | tf_op jit(solution)/shard_map/ppermute | solution.py:218
  8.2 0.0 collective-permute-done.1.odd_ref.near_ref.co_ref
  8.2 0.0 collective-permute-done.even_ref.ce_ref
  8.2 0.0 copy-done
  8.2 0.0 copy-done.2
  8.2 1.3 %input_grad.1 = (f32[64,640]{1,0:T(8,128)S(1)}, f32[64,640]{1,0:T(8,128)S(1)}, f32[64,640]{1,0:T(8,128)S(1)}, f32[64,640]{1,0:T(8,128)S(1)}, f32[8,128]{1,0:T(8,128)S(1)}) custom-call(f32[8,128]{1,0:T(8,128)S(1)} %begin.1.begin_ref, bf16[64,640]{1,0:T(8,128)(2,1)S(1)} %bitcast.11, bf16[64,640]{1,0:T(8,128)(2,1)S(1)} %collective-permute-done.even_ref.ce_ref, ...), custom_call_target="tpu_custom_call" | custom-call | flops 566231040 | tf_op jit(solution)/shard_map/input_grad/pallas_call | solution.py:180
  9.5 1.3 %collective-permute-start.8 = (f32[64,640]{1,0:T(8,128)S(1)}, f32[64,640]{1,0:T(8,128)S(1)}, u32[]{:S(2)}, u32[]{:S(2)}) collective-permute-start(f32[64,640]{1,0:T(8,128)S(1)} %get-tuple-element.33), channel_id=1, source_target_pairs={{0,1},{1,0},{2,3},{3,2},{4,5},{5,4},{6,7},{7,6},{8,9},{9,8},{10,11... | collective-permute-start | bytes 491528 | tf_op jit(solution)/shard_map/ppermute | solution.py:230
  10.8 0.8 %collective-permute-start.10 = (f32[64,640]{1,0:T(8,128)S(1)}, f32[64,640]{1,0:T(8,128)S(1)}, u32[]{:S(2)}, u32[]{:S(2)}) collective-permute-start(f32[64,640]{1,0:T(8,128)S(1)} %get-tuple-element.34), channel_id=1, source_target_pairs={{0,1},{1,0},{2,3},{3,2},{4,5},{5,4},{6,7},{7,6},{8,9},{9,8},{10,11... | collective-permute-start | bytes 491528 | tf_op jit(solution)/shard_map/ppermute | solution.py:233
  11.6 0.0 collective-permute-done.4.refs_3_
  11.6 3.0 %collective-permute-done.3.refs_2_ = bf16[64,640]{1,0:T(8,128)(2,1)S(1)} collective-permute-done((bf16[64,640]{1,0:T(8,128)(2,1)S(1)}, bf16[64,640]{1,0:T(8,128)(2,1)S(1)}, u32[]{:S(2)}, u32[]{:S(2)}) %collective-permute-start.3) | collective-permute-done | bytes 81952 | tf_op jit(solution)/shard_map/ppermute | solution.py:218
  14.6 0.0 collective-permute-done.2.refs_1_
  14.6 0.1 gather.1
  14.7 0.1 collective-permute-start.6
  14.7 0.8 %collective-permute-start.7 = (bf16[64,640]{1,0:T(8,128)(2,1)S(1)}, bf16[64,640]{1,0:T(8,128)(2,1)S(1)}, u32[]{:S(2)}, u32[]{:S(2)}) collective-permute-start(bf16[64,640]{1,0:T(8,128)(2,1)S(1)} %get-tuple-element.29), channel_id=1, source_target_pairs={{0,8},{4,12},{8,0},{12,4},{1,9},{5,13},{9,1},{13,5},{2,10},{6,14},... | collective-permute-start | bytes 245768 | tf_op jit(solution)/shard_map/ppermute | solution.py:246
  15.5 1.0 %collective-permute-start.5 = (bf16[128,640]{1,0:T(8,128)(2,1)S(1)}, bf16[128,640]{1,0:T(8,128)(2,1)S(1)}, u32[]{:S(2)}, u32[]{:S(2)}) collective-permute-start(bf16[128,640]{1,0:T(8,128)(2,1)S(1)} %get-tuple-element.27), channel_id=1, source_target_pairs={{0,4},{4,0},{8,12},{12,8},{1,5},{5,1},{9,13},{13,9},{2,6},{6,2},{1... | collective-permute-start | bytes 491528 | tf_op jit(solution)/shard_map/ppermute | solution.py:249
  16.6 1.3 %collective-permute-done.8.got_ref = f32[64,640]{1,0:T(8,128)S(1)} collective-permute-done((f32[64,640]{1,0:T(8,128)S(1)}, f32[64,640]{1,0:T(8,128)S(1)}, u32[]{:S(2)}, u32[]{:S(2)}) %collective-permute-start.8) | collective-permute-done | bytes 163872 | tf_op jit(solution)/shard_map/ppermute | solution.py:230
  17.9 1.3 %collective-permute-start.9 = (f32[64,640]{1,0:T(8,128)S(1)}, f32[64,640]{1,0:T(8,128)S(1)}, u32[]{:S(2)}, u32[]{:S(2)}) collective-permute-start(f32[64,640]{1,0:T(8,128)S(1)} %fold.1), channel_id=1, source_target_pairs={{0,2},{1,3},{2,0},{3,1},{4,6},{5,7},{6,4},{7,5},{8,10},{9,11},{10,... | collective-permute-start | bytes 491528 | tf_op jit(solution)/shard_map/ppermute | solution.py:232
  19.2 1.4 %early.1 = (f32[64,640]{1,0:T(8,128)S(1)}, f32[64,640]{1,0:T(8,128)S(1)}, f32[64,640]{1,0:T(8,128)S(1)}, bf16[3,192,640]{2,1,0:T(8,128)(2,1)S(1)}) custom-call(bf16[1728,256]{1,0:T(8,128)(2,1)S(1)} %bitcast.4, bf16[256,640]{1,0:T(8,128)(2,1)S(1)} %get-tuple-element.25.f_ref, bf16[64,640]{1,0:T(8,128)(2,1)S(1)} %bitcast.13, ...), custom_call_target="tpu_custom_call" | custom-call | flops 1132462080 | tf_op jit(solution)/shard_map/early/pallas_call | solution.py:180
  20.7 0.0 collective-permute-done.6.go_ref
  20.7 0.1 collective-permute-start.11
  20.8 0.0 collective-permute-done.7.refs_0_
  20.8 0.6 %collective-permute-start.12 = (f32[64,640]{1,0:T(8,128)S(1)}, f32[64,640]{1,0:T(8,128)S(1)}, u32[]{:S(2)}, u32[]{:S(2)}) collective-permute-start(f32[64,640]{1,0:T(8,128)S(1)} %get-tuple-element.38), channel_id=1, source_target_pairs={{0,4},{4,0},{8,12},{12,8},{1,5},{5,1},{9,13},{13,9},{2,6},{6,2},{1... | collective-permute-start | bytes 491528 | tf_op jit(solution)/shard_map/ppermute | solution.py:258
  21.4 0.0 collective-permute-done.5.ge_ref
  21.4 2.3 %weight_grad.1 = (f32[27,64,64]{2,1,0:T(8,128)}, f32[8,128]{1,0:T(8,128)S(1)}) custom-call(bf16[3,192,640]{2,1,0:T(8,128)(2,1)S(1)} %get-tuple-element.26.moved_ref, bf16[256,640]{1,0:T(8,128)(2,1)S(1)} %get-tuple-element.25.f_ref, bf16[128,640]{1,0:T(8,128)(2,1)S(1)} %collective-permute-done.5.ge_ref, bf16[64,640]{1,0:T(8,128)(2,1)S(1)} %collective-permute-done.6.go_ref, ...), custom_call_target="tpu_custom_call" | custom-call | tf_op jit(solution)/shard_map/weight_grad/pallas_call | solution.py:180
  23.6 0.0 collective-permute-done.10.refs_2_
  23.6 3.7 %collective-permute-done.9.refs_1_ = f32[64,640]{1,0:T(8,128)S(1)} collective-permute-done((f32[64,640]{1,0:T(8,128)S(1)}, f32[64,640]{1,0:T(8,128)S(1)}, u32[]{:S(2)}, u32[]{:S(2)}) %collective-permute-start.9) | collective-permute-done | bytes 163872 | tf_op jit(solution)/shard_map/ppermute | solution.py:232
  27.3 0.7 %input_total.1 = (f32[64,1,640]{2,1,0:T(1,128)}, f32[8,128]{1,0:T(8,128)S(1)}) custom-call(f32[8,128]{1,0:T(8,128)S(1)} %get-tuple-element.30.token_ref, f32[64,640]{1,0:T(8,128)S(1)} %get-tuple-element.31.refs_0_, f32[64,640]{1,0:T(8,128)S(1)} %collective-permute-done.9.refs_1_, f32[64,640]{1,0:T(8,128)S(1)} %collective-permute-done.10.refs_2_), custom_call_target="tpu_custom_call" | custom-call | flops 566231040 | tf_op jit(solution)/shard_map/input_total/pallas_call | solution.py:180
  28.0 0.0 collective-permute-done.11.odd_ref
  28.0 0.0 collective-permute-done.12.even_ref
  28.0 0.7 %output_total.1 = f32[64,1,640]{2,1,0:T(1,128)} custom-call(f32[8,128]{1,0:T(8,128)S(1)} %get-tuple-element.35.token_ref, f32[64,640]{1,0:T(8,128)S(1)} %get-tuple-element.36.own_ref, f32[64,640]{1,0:T(8,128)S(1)} %collective-permute-done.11.odd_ref, f32[64,640]{1,0:T(8,128)S(1)} %collective-permute-done.12.even_ref), custom_call_target="tpu_custom_call" | custom-call | tf_op jit(solution)/shard_map/output_total/pallas_call | solution.py:180
  (2 shorter events, 0.0 us)
Async XLA Ops:
  0.6 3.2 %copy-start.1 = (bf16[64,1,640]{2,0,1:T(8,128)(2,1)S(1)}, bf16[64,1,640]{2,0,1:T(8,128)(2,1)}, u32[]{:S(2)}) copy-start(bf16[64,1,640]{2,0,1:T(8,128)(2,1)} %param.3) | copy-start | bytes 245764
  0.6 7.5 %copy-start = (bf16[27,64,256]{2,1,0:T(8,128)(2,1)S(1)}, bf16[27,64,256]{2,1,0:T(8,128)(2,1)}, u32[]{:S(2)}) copy-start(bf16[27,64,256]{2,1,0:T(8,128)(2,1)} %param.4) | copy-start | bytes 2654212
  0.7 7.5 %copy-start.2 = (bf16[64,1,640]{2,0,1:T(8,128)(2,1)S(1)}, bf16[64,1,640]{2,0,1:T(8,128)(2,1)}, u32[]{:S(2)}) copy-start(bf16[64,1,640]{2,0,1:T(8,128)(2,1)} %param.5) | copy-start | bytes 245764
  0.7 7.5 %collective-permute-start.1 = (bf16[64,640]{1,0:T(8,128)(2,1)}, bf16[64,640]{1,0:T(8,128)(2,1)S(1)}, u32[]{:S(2)}, u32[]{:S(2)}) collective-permute-start(bf16[64,640]{1,0:T(8,128)(2,1)} %bitcast.9), channel_id=1, source_target_pairs={{0,12},{4,8},{8,4},{12,0},{1,13},{5,9},{9,5},{13,1},{2,14},{6,10},... | collective-permute-start | bytes 245768 | tf_op jit(solution)/shard_map/ppermute | solution.py:215
  3.1 5.1 %collective-permute-start = (bf16[64,640]{1,0:T(8,128)(2,1)}, bf16[64,640]{1,0:T(8,128)(2,1)S(1)}, u32[]{:S(2)}, u32[]{:S(2)}) collective-permute-start(bf16[64,640]{1,0:T(8,128)(2,1)} %bitcast.10), channel_id=1, source_target_pairs={{0,4},{4,0},{8,12},{12,8},{1,5},{5,1},{9,13},{13,9},{2,6},{6,2},{1... | collective-permute-start | bytes 245768 | tf_op jit(solution)/shard_map/ppermute | solution.py:214
  3.8 7.8 %collective-permute-start.4 = (bf16[64,640]{1,0:T(8,128)(2,1)S(1)}, bf16[64,640]{1,0:T(8,128)(2,1)S(1)}, u32[]{:S(2)}, u32[]{:S(2)}) collective-permute-start(bf16[64,640]{1,0:T(8,128)(2,1)S(1)} %bitcast.5), channel_id=1, source_target_pairs={{0,3},{1,2},{2,1},{3,0},{4,7},{5,6},{6,5},{7,4},{8,11},{9,10},{10,... | collective-permute-start | bytes 245768 | tf_op jit(solution)/shard_map/ppermute | solution.py:218
  7.4 7.2 %collective-permute-start.3 = (bf16[64,640]{1,0:T(8,128)(2,1)S(1)}, bf16[64,640]{1,0:T(8,128)(2,1)S(1)}, u32[]{:S(2)}, u32[]{:S(2)}) collective-permute-start(bf16[64,640]{1,0:T(8,128)(2,1)S(1)} %bitcast.6), channel_id=1, source_target_pairs={{0,2},{1,3},{2,0},{3,1},{4,6},{5,7},{6,4},{7,5},{8,10},{9,11},{10,... | collective-permute-start | bytes 245768 | tf_op jit(solution)/shard_map/ppermute | solution.py:218
  7.4 7.2 %collective-permute-start.2 = (bf16[64,640]{1,0:T(8,128)(2,1)S(1)}, bf16[64,640]{1,0:T(8,128)(2,1)S(1)}, u32[]{:S(2)}, u32[]{:S(2)}) collective-permute-start(bf16[64,640]{1,0:T(8,128)(2,1)S(1)} %bitcast.7), channel_id=1, source_target_pairs={{0,1},{1,0},{2,3},{3,2},{4,5},{5,4},{6,7},{7,6},{8,9},{9,8},{10,11... | collective-permute-start | bytes 245768 | tf_op jit(solution)/shard_map/ppermute | solution.py:218
  9.5 8.3 %collective-permute-start.8 = (f32[64,640]{1,0:T(8,128)S(1)}, f32[64,640]{1,0:T(8,128)S(1)}, u32[]{:S(2)}, u32[]{:S(2)}) collective-permute-start(f32[64,640]{1,0:T(8,128)S(1)} %get-tuple-element.33), channel_id=1, source_target_pairs={{0,1},{1,0},{2,3},{3,2},{4,5},{5,4},{6,7},{7,6},{8,9},{9,8},{10,11... | collective-permute-start | bytes 491528 | tf_op jit(solution)/shard_map/ppermute | solution.py:230
  10.8 12.8 %collective-permute-start.10 = (f32[64,640]{1,0:T(8,128)S(1)}, f32[64,640]{1,0:T(8,128)S(1)}, u32[]{:S(2)}, u32[]{:S(2)}) collective-permute-start(f32[64,640]{1,0:T(8,128)S(1)} %get-tuple-element.34), channel_id=1, source_target_pairs={{0,1},{1,0},{2,3},{3,2},{4,5},{5,4},{6,7},{7,6},{8,9},{9,8},{10,11... | collective-permute-start | bytes 491528 | tf_op jit(solution)/shard_map/ppermute | solution.py:233
  14.7 6.0 %collective-permute-start.6 = (bf16[64,640]{1,0:T(8,128)(2,1)S(1)}, bf16[64,640]{1,0:T(8,128)(2,1)S(1)}, u32[]{:S(2)}, u32[]{:S(2)}) collective-permute-start(bf16[64,640]{1,0:T(8,128)(2,1)S(1)} %get-tuple-element.28), channel_id=1, source_target_pairs={{0,12},{4,8},{8,4},{12,0},{1,13},{5,9},{9,5},{13,1},{2,14},{6,10},... | collective-permute-start | bytes 245768 | tf_op jit(solution)/shard_map/ppermute | solution.py:244
  14.7 6.0 %collective-permute-start.7 = (bf16[64,640]{1,0:T(8,128)(2,1)S(1)}, bf16[64,640]{1,0:T(8,128)(2,1)S(1)}, u32[]{:S(2)}, u32[]{:S(2)}) collective-permute-start(bf16[64,640]{1,0:T(8,128)(2,1)S(1)} %get-tuple-element.29), channel_id=1, source_target_pairs={{0,8},{4,12},{8,0},{12,4},{1,9},{5,13},{9,1},{13,5},{2,10},{6,14},... | collective-permute-start | bytes 245768 | tf_op jit(solution)/shard_map/ppermute | solution.py:246
  15.5 5.8 %collective-permute-start.5 = (bf16[128,640]{1,0:T(8,128)(2,1)S(1)}, bf16[128,640]{1,0:T(8,128)(2,1)S(1)}, u32[]{:S(2)}, u32[]{:S(2)}) collective-permute-start(bf16[128,640]{1,0:T(8,128)(2,1)S(1)} %get-tuple-element.27), channel_id=1, source_target_pairs={{0,4},{4,0},{8,12},{12,8},{1,5},{5,1},{9,13},{13,9},{2,6},{6,2},{1... | collective-permute-start | bytes 491528 | tf_op jit(solution)/shard_map/ppermute | solution.py:249
  17.9 9.4 %collective-permute-start.9 = (f32[64,640]{1,0:T(8,128)S(1)}, f32[64,640]{1,0:T(8,128)S(1)}, u32[]{:S(2)}, u32[]{:S(2)}) collective-permute-start(f32[64,640]{1,0:T(8,128)S(1)} %fold.1), channel_id=1, source_target_pairs={{0,2},{1,3},{2,0},{3,1},{4,6},{5,7},{6,4},{7,5},{8,10},{9,11},{10,... | collective-permute-start | bytes 491528 | tf_op jit(solution)/shard_map/ppermute | solution.py:232
  20.7 7.4 %collective-permute-start.11 = (f32[64,640]{1,0:T(8,128)S(1)}, f32[64,640]{1,0:T(8,128)S(1)}, u32[]{:S(2)}, u32[]{:S(2)}) collective-permute-start(f32[64,640]{1,0:T(8,128)S(1)} %get-tuple-element.37), channel_id=1, source_target_pairs={{0,12},{4,8},{8,4},{12,0},{1,13},{5,9},{9,5},{13,1},{2,14},{6,10},... | collective-permute-start | bytes 491528 | tf_op jit(solution)/shard_map/ppermute | solution.py:257
  20.8 7.3 %collective-permute-start.12 = (f32[64,640]{1,0:T(8,128)S(1)}, f32[64,640]{1,0:T(8,128)S(1)}, u32[]{:S(2)}, u32[]{:S(2)}) collective-permute-start(f32[64,640]{1,0:T(8,128)S(1)} %get-tuple-element.38), channel_id=1, source_target_pairs={{0,4},{4,0},{8,12},{12,8},{1,5},{5,1},{9,13},{13,9},{2,6},{6,2},{1... | collective-permute-start | bytes 491528 | tf_op jit(solution)/shard_map/ppermute | solution.py:258

commit v18 on v17

--- a/solution.py
+++ b/solution.py
@@ -157,19 +157,19 @@
     both_ref[...] = own_ref[...] + got_ref[...]
 
 
-def input_total_kernel(token_ref, *refs):
-    terms, back_ref, done_ref = refs[:-2], refs[-2], refs[-1]
-    done_ref[...] = jnp.zeros(done_ref.shape, F32)
+def hold_kernel(*refs):
+    refs[-1][...] = jnp.zeros(refs[-1].shape, F32)
+
+
+def total_kernel(nz, token_ref, own_ref, odd_ref, even_ref, *refs):
+    terms, (out_ref, back_ref) = refs[:-2], refs[-2:]
+    s = lax.axis_index("sp")
+    inner = ((s > 0) & (s < nz - 1)).astype(F32)
+    out_ref[:, 0, :] = own_ref[...] + even_ref[...] + inner * odd_ref[...]
     total = terms[0][...]
     for term in terms[1:]:
         total = total + term[...]
     back_ref[:, 0, :] = total
-
-
-def output_total_kernel(nz, token_ref, own_ref, odd_ref, even_ref, out_ref):
-    s = lax.axis_index("sp")
-    inner = ((s > 0) & (s < nz - 1)).astype(F32)
-    out_ref[:, 0, :] = own_ref[...] + even_ref[...] + inner * odd_ref[...]
 
 
 VMEM = pl.BlockSpec(memory_space=pltpu.VMEM)
@@ -266,14 +266,12 @@
         W_OUT * work,
     )
     block = jax.ShapeDtypeStruct((blocks, 1, plane), F32)
-    back, done = kernel_call(
-        input_total_kernel, "input_total", [block, small], [last] + terms, weight=W_TOTAL * work
-    )
-    (output,) = kernel_call(
-        functools.partial(output_total_kernel, nz),
-        "output_total",
-        [block],
-        [done, out_own, out_odd, out_even],
+    (done,) = kernel_call(hold_kernel, "hold", [small], [last] + terms, weight=W_TOTAL * work)
+    output, back = kernel_call(
+        functools.partial(total_kernel, nz),
+        "total",
+        [block, block],
+        [done, out_own, out_odd, out_even, *terms],
     )
     return (output, back, weight_grad)
 

time: 28.9 us -> 28.3 us (0.979)
  Pallas kernels: 6.55 us -> 5.87 us
    pallas_call x8, Pallas kernels: 6.55 us -> 5.87 us  [kernel_call(): pl.pallas_call(body, out_shape=outs, in_specs=[SMEM if a.dtype == jnp.int...]
  transfers between devices with their start and end apart: 13 -> 13, of which waited for: 3 -> 3; matrix products, arithmetic and copies ran while one was open for 0% -> 0% of each run, Pallas kernels for 20% -> 18%
where the time goes in v18:
time: 28.3 us; the launch traced here: 28.1 us
  starting transfers between devices  13.5 us (48%)
  waiting for transfers between devices  7.98 us (28%)
  Pallas kernels  5.87 us (21%)
  between operations  0.74 us (3%)
    pallas_call x8, Pallas kernels, kernel_call(): pl.pallas_call(body, out_shape=outs, in_specs=[SMEM if a.dtype == jnp.int...  5.87 us
    ppermute x3, starting transfers between devices, per_device(): pieces = [feat] + [lax.ppermute(feat, 'ch', mixed(k)) for k in range(1, nc)]  4.39 us
    ppermute x1, waiting for transfers between devices, per_device(): terms.append(lax.ppermute(both, 'ch', mixed(k)))  3.7 us
    ppermute x3, waiting for transfers between devices, per_device(): pieces = [feat] + [lax.ppermute(feat, 'ch', mixed(k)) for k in range(1, nc)]  2.99 us
    ppermute x1, starting transfers between devices, per_device(): cot_odd = lax.ppermute(cot, 'sp', odd_pairs)  2.44 us
    ppermute x1, starting transfers between devices, per_device(): terms.append(lax.ppermute(both, 'ch', mixed(k)))  1.35 us
    ppermute x1, starting transfers between devices, per_device(): got = lax.ppermute(parts[k + 1], 'ch', mixed(1))  1.31 us
    ppermute x1, waiting for transfers between devices, per_device(): got = lax.ppermute(parts[k + 1], 'ch', mixed(1))  1.27 us
  transfers between devices with their start and end apart: 13, of which 3 were waited for; matrix products, arithmetic and copies ran while one was open for 0% of the time, Pallas kernels for 18%

profile of v18, /device:TPU:0, one launch (start us, length us, event | category | flops | bytes accessed | tf_op | source)
XLA Modules:
  0.0 28.1 jit_solution(13596527452627704986)
XLA Ops:
  0.6 0.0 copy-start.1
  0.6 0.0 copy-start
  0.7 0.0 copy-start.2
  0.7 2.4 %collective-permute-start.1 = (bf16[64,640]{1,0:T(8,128)(2,1)}, bf16[64,640]{1,0:T(8,128)(2,1)S(1)}, u32[]{:S(2)}, u32[]{:S(2)}) collective-permute-start(bf16[64,640]{1,0:T(8,128)(2,1)} %bitcast.9), channel_id=1, source_target_pairs={{0,12},{4,8},{8,4},{12,0},{1,13},{5,9},{9,5},{13,1},{2,14},{6,10},... | collective-permute-start | bytes 245768 | tf_op jit(solution)/shard_map/ppermute | solution.py:215
  3.1 0.7 %collective-permute-start = (bf16[64,640]{1,0:T(8,128)(2,1)}, bf16[64,640]{1,0:T(8,128)(2,1)S(1)}, u32[]{:S(2)}, u32[]{:S(2)}) collective-permute-start(bf16[64,640]{1,0:T(8,128)(2,1)} %bitcast.10), channel_id=1, source_target_pairs={{0,4},{4,0},{8,12},{12,8},{1,5},{5,1},{9,13},{13,9},{2,6},{6,2},{1... | collective-permute-start | bytes 245768 | tf_op jit(solution)/shard_map/ppermute | solution.py:214
  3.8 0.0 copy-done.1
  3.8 3.6 %collective-permute-start.4 = (bf16[64,640]{1,0:T(8,128)(2,1)S(1)}, bf16[64,640]{1,0:T(8,128)(2,1)S(1)}, u32[]{:S(2)}, u32[]{:S(2)}) collective-permute-start(bf16[64,640]{1,0:T(8,128)(2,1)S(1)} %bitcast.5), channel_id=1, source_target_pairs={{0,3},{1,2},{2,1},{3,0},{4,7},{5,6},{6,5},{7,4},{8,11},{9,10},{10,... | collective-permute-start | bytes 245768 | tf_op jit(solution)/shard_map/ppermute | solution.py:218
  7.4 0.0 collective-permute-start.3
  7.4 0.8 %collective-permute-start.2 = (bf16[64,640]{1,0:T(8,128)(2,1)S(1)}, bf16[64,640]{1,0:T(8,128)(2,1)S(1)}, u32[]{:S(2)}, u32[]{:S(2)}) collective-permute-start(bf16[64,640]{1,0:T(8,128)(2,1)S(1)} %bitcast.7), channel_id=1, source_target_pairs={{0,1},{1,0},{2,3},{3,2},{4,5},{5,4},{6,7},{7,6},{8,9},{9,8},{10,11... | collective-permute-start | bytes 245768 | tf_op jit(solution)/shard_map/ppermute | solution.py:218
  8.2 0.0 collective-permute-done.1.odd_ref.near_ref.co_ref
  8.2 0.0 collective-permute-done.even_ref.ce_ref
  8.2 0.0 copy-done
  8.2 0.0 copy-done.2
  8.2 1.3 %input_grad.1 = (f32[64,640]{1,0:T(8,128)S(1)}, f32[64,640]{1,0:T(8,128)S(1)}, f32[64,640]{1,0:T(8,128)S(1)}, f32[64,640]{1,0:T(8,128)S(1)}, f32[8,128]{1,0:T(8,128)S(1)}) custom-call(f32[8,128]{1,0:T(8,128)S(1)} %begin.1.begin_ref, bf16[64,640]{1,0:T(8,128)(2,1)S(1)} %bitcast.11, bf16[64,640]{1,0:T(8,128)(2,1)S(1)} %collective-permute-done.even_ref.ce_ref, ...), custom_call_target="tpu_custom_call" | custom-call | flops 566231040 | tf_op jit(solution)/shard_map/input_grad/pallas_call | solution.py:180
  9.5 1.3 %collective-permute-start.8 = (f32[64,640]{1,0:T(8,128)S(1)}, f32[64,640]{1,0:T(8,128)S(1)}, u32[]{:S(2)}, u32[]{:S(2)}) collective-permute-start(f32[64,640]{1,0:T(8,128)S(1)} %get-tuple-element.33), channel_id=1, source_target_pairs={{0,1},{1,0},{2,3},{3,2},{4,5},{5,4},{6,7},{7,6},{8,9},{9,8},{10,11... | collective-permute-start | bytes 491528 | tf_op jit(solution)/shard_map/ppermute | solution.py:230
  10.8 0.8 %collective-permute-start.10 = (f32[64,640]{1,0:T(8,128)S(1)}, f32[64,640]{1,0:T(8,128)S(1)}, u32[]{:S(2)}, u32[]{:S(2)}) collective-permute-start(f32[64,640]{1,0:T(8,128)S(1)} %get-tuple-element.34), channel_id=1, source_target_pairs={{0,1},{1,0},{2,3},{3,2},{4,5},{5,4},{6,7},{7,6},{8,9},{9,8},{10,11... | collective-permute-start | bytes 491528 | tf_op jit(solution)/shard_map/ppermute | solution.py:233
  11.6 0.0 collective-permute-done.4.refs_3_
  11.6 3.0 %collective-permute-done.3.refs_2_ = bf16[64,640]{1,0:T(8,128)(2,1)S(1)} collective-permute-done((bf16[64,640]{1,0:T(8,128)(2,1)S(1)}, bf16[64,640]{1,0:T(8,128)(2,1)S(1)}, u32[]{:S(2)}, u32[]{:S(2)}) %collective-permute-start.3) | collective-permute-done | bytes 81952 | tf_op jit(solution)/shard_map/ppermute | solution.py:218
  14.6 0.0 collective-permute-done.2.refs_1_
  14.6 0.1 gather.1
  14.7 0.1 collective-permute-start.6
  14.7 0.8 %collective-permute-start.7 = (bf16[64,640]{1,0:T(8,128)(2,1)S(1)}, bf16[64,640]{1,0:T(8,128)(2,1)S(1)}, u32[]{:S(2)}, u32[]{:S(2)}) collective-permute-start(bf16[64,640]{1,0:T(8,128)(2,1)S(1)} %get-tuple-element.29), channel_id=1, source_target_pairs={{0,8},{4,12},{8,0},{12,4},{1,9},{5,13},{9,1},{13,5},{2,10},{6,14},... | collective-permute-start | bytes 245768 | tf_op jit(solution)/shard_map/ppermute | solution.py:246
  15.5 1.0 %collective-permute-start.5 = (bf16[128,640]{1,0:T(8,128)(2,1)S(1)}, bf16[128,640]{1,0:T(8,128)(2,1)S(1)}, u32[]{:S(2)}, u32[]{:S(2)}) collective-permute-start(bf16[128,640]{1,0:T(8,128)(2,1)S(1)} %get-tuple-element.27), channel_id=1, source_target_pairs={{0,4},{4,0},{8,12},{12,8},{1,5},{5,1},{9,13},{13,9},{2,6},{6,2},{1... | collective-permute-start | bytes 491528 | tf_op jit(solution)/shard_map/ppermute | solution.py:249
  16.6 1.3 %collective-permute-done.8.got_ref = f32[64,640]{1,0:T(8,128)S(1)} collective-permute-done((f32[64,640]{1,0:T(8,128)S(1)}, f32[64,640]{1,0:T(8,128)S(1)}, u32[]{:S(2)}, u32[]{:S(2)}) %collective-permute-start.8) | collective-permute-done | bytes 163872 | tf_op jit(solution)/shard_map/ppermute | solution.py:230
  17.9 1.4 %collective-permute-start.9 = (f32[64,640]{1,0:T(8,128)S(1)}, f32[64,640]{1,0:T(8,128)S(1)}, u32[]{:S(2)}, u32[]{:S(2)}) collective-permute-start(f32[64,640]{1,0:T(8,128)S(1)} %fold.1), channel_id=1, source_target_pairs={{0,2},{1,3},{2,0},{3,1},{4,6},{5,7},{6,4},{7,5},{8,10},{9,11},{10,... | collective-permute-start | bytes 491528 | tf_op jit(solution)/shard_map/ppermute | solution.py:232
  19.2 1.4 %early.1 = (f32[64,640]{1,0:T(8,128)S(1)}, f32[64,640]{1,0:T(8,128)S(1)}, f32[64,640]{1,0:T(8,128)S(1)}, bf16[3,192,640]{2,1,0:T(8,128)(2,1)S(1)}) custom-call(bf16[1728,256]{1,0:T(8,128)(2,1)S(1)} %bitcast.4, bf16[256,640]{1,0:T(8,128)(2,1)S(1)} %get-tuple-element.25.f_ref, bf16[64,640]{1,0:T(8,128)(2,1)S(1)} %bitcast.13, ...), custom_call_target="tpu_custom_call" | custom-call | flops 1132462080 | tf_op jit(solution)/shard_map/early/pallas_call | solution.py:180
  20.7 0.0 collective-permute-done.6.go_ref
  20.7 0.1 collective-permute-start.11
  20.8 0.0 collective-permute-done.7.refs_0_
  20.8 0.6 %collective-permute-start.12 = (f32[64,640]{1,0:T(8,128)S(1)}, f32[64,640]{1,0:T(8,128)S(1)}, u32[]{:S(2)}, u32[]{:S(2)}) collective-permute-start(f32[64,640]{1,0:T(8,128)S(1)} %get-tuple-element.37), channel_id=1, source_target_pairs={{0,4},{4,0},{8,12},{12,8},{1,5},{5,1},{9,13},{13,9},{2,6},{6,2},{1... | collective-permute-start | bytes 491528 | tf_op jit(solution)/shard_map/ppermute | solution.py:258
  21.4 0.0 collective-permute-done.5.ge_ref
  21.4 2.3 %weight_grad.1 = (f32[27,64,64]{2,1,0:T(8,128)}, f32[8,128]{1,0:T(8,128)S(1)}) custom-call(bf16[3,192,640]{2,1,0:T(8,128)(2,1)S(1)} %get-tuple-element.26.moved_ref, bf16[256,640]{1,0:T(8,128)(2,1)S(1)} %get-tuple-element.25.f_ref, bf16[128,640]{1,0:T(8,128)(2,1)S(1)} %collective-permute-done.5.ge_ref, bf16[64,640]{1,0:T(8,128)(2,1)S(1)} %collective-permute-done.6.go_ref, ...), custom_call_target="tpu_custom_call" | custom-call | tf_op jit(solution)/shard_map/weight_grad/pallas_call | solution.py:180
  23.6 0.0 collective-permute-done.10.refs_3_.refs_2_
  23.6 3.7 %collective-permute-done.9.refs_2_.refs_1_ = f32[64,640]{1,0:T(8,128)S(1)} collective-permute-done((f32[64,640]{1,0:T(8,128)S(1)}, f32[64,640]{1,0:T(8,128)S(1)}, u32[]{:S(2)}, u32[]{:S(2)}) %collective-permute-start.9) | collective-permute-done | bytes 163872 | tf_op jit(solution)/shard_map/ppermute | solution.py:232
  27.3 0.0 collective-permute-done.11.odd_ref
  27.3 0.0 collective-permute-done.12.even_ref
  27.3 0.8 %total.1 = (f32[64,1,640]{2,1,0:T(1,128)}, f32[64,1,640]{2,1,0:T(1,128)}) custom-call(f32[8,128]{1,0:T(8,128)S(1)} %hold.1.token_ref, f32[64,640]{1,0:T(8,128)S(1)} %get-tuple-element.35.own_ref, f32[64,640]{1,0:T(8,128)S(1)} %collective-permute-done.11.odd_ref, f32[64,640]{1,0:T(8,128)S(1)} %collective-permute-done.12.even_ref, ...), custom_call_target="tpu_custom_call" | custom-call | tf_op jit(solution)/shard_map/total/pallas_call | solution.py:180
  (3 shorter events, 0.0 us)
Async XLA Ops:
  0.6 3.2 %copy-start.1 = (bf16[64,1,640]{2,0,1:T(8,128)(2,1)S(1)}, bf16[64,1,640]{2,0,1:T(8,128)(2,1)}, u32[]{:S(2)}) copy-start(bf16[64,1,640]{2,0,1:T(8,128)(2,1)} %param.3) | copy-start | bytes 245764
  0.6 7.5 %copy-start = (bf16[27,64,256]{2,1,0:T(8,128)(2,1)S(1)}, bf16[27,64,256]{2,1,0:T(8,128)(2,1)}, u32[]{:S(2)}) copy-start(bf16[27,64,256]{2,1,0:T(8,128)(2,1)} %param.4) | copy-start | bytes 2654212
  0.7 7.5 %copy-start.2 = (bf16[64,1,640]{2,0,1:T(8,128)(2,1)S(1)}, bf16[64,1,640]{2,0,1:T(8,128)(2,1)}, u32[]{:S(2)}) copy-start(bf16[64,1,640]{2,0,1:T(8,128)(2,1)} %param.5) | copy-start | bytes 245764
  0.7 7.5 %collective-permute-start.1 = (bf16[64,640]{1,0:T(8,128)(2,1)}, bf16[64,640]{1,0:T(8,128)(2,1)S(1)}, u32[]{:S(2)}, u32[]{:S(2)}) collective-permute-start(bf16[64,640]{1,0:T(8,128)(2,1)} %bitcast.9), channel_id=1, source_target_pairs={{0,12},{4,8},{8,4},{12,0},{1,13},{5,9},{9,5},{13,1},{2,14},{6,10},... | collective-permute-start | bytes 245768 | tf_op jit(solution)/shard_map/ppermute | solution.py:215
  3.1 5.1 %collective-permute-start = (bf16[64,640]{1,0:T(8,128)(2,1)}, bf16[64,640]{1,0:T(8,128)(2,1)S(1)}, u32[]{:S(2)}, u32[]{:S(2)}) collective-permute-start(bf16[64,640]{1,0:T(8,128)(2,1)} %bitcast.10), channel_id=1, source_target_pairs={{0,4},{4,0},{8,12},{12,8},{1,5},{5,1},{9,13},{13,9},{2,6},{6,2},{1... | collective-permute-start | bytes 245768 | tf_op jit(solution)/shard_map/ppermute | solution.py:214
  3.8 7.8 %collective-permute-start.4 = (bf16[64,640]{1,0:T(8,128)(2,1)S(1)}, bf16[64,640]{1,0:T(8,128)(2,1)S(1)}, u32[]{:S(2)}, u32[]{:S(2)}) collective-permute-start(bf16[64,640]{1,0:T(8,128)(2,1)S(1)} %bitcast.5), channel_id=1, source_target_pairs={{0,3},{1,2},{2,1},{3,0},{4,7},{5,6},{6,5},{7,4},{8,11},{9,10},{10,... | collective-permute-start | bytes 245768 | tf_op jit(solution)/shard_map/ppermute | solution.py:218
  7.4 7.2 %collective-permute-start.3 = (bf16[64,640]{1,0:T(8,128)(2,1)S(1)}, bf16[64,640]{1,0:T(8,128)(2,1)S(1)}, u32[]{:S(2)}, u32[]{:S(2)}) collective-permute-start(bf16[64,640]{1,0:T(8,128)(2,1)S(1)} %bitcast.6), channel_id=1, source_target_pairs={{0,2},{1,3},{2,0},{3,1},{4,6},{5,7},{6,4},{7,5},{8,10},{9,11},{10,... | collective-permute-start | bytes 245768 | tf_op jit(solution)/shard_map/ppermute | solution.py:218
  7.4 7.2 %collective-permute-start.2 = (bf16[64,640]{1,0:T(8,128)(2,1)S(1)}, bf16[64,640]{1,0:T(8,128)(2,1)S(1)}, u32[]{:S(2)}, u32[]{:S(2)}) collective-permute-start(bf16[64,640]{1,0:T(8,128)(2,1)S(1)} %bitcast.7), channel_id=1, source_target_pairs={{0,1},{1,0},{2,3},{3,2},{4,5},{5,4},{6,7},{7,6},{8,9},{9,8},{10,11... | collective-permute-start | bytes 245768 | tf_op jit(solution)/shard_map/ppermute | solution.py:218
  9.5 8.4 %collective-permute-start.8 = (f32[64,640]{1,0:T(8,128)S(1)}, f32[64,640]{1,0:T(8,128)S(1)}, u32[]{:S(2)}, u32[]{:S(2)}) collective-permute-start(f32[64,640]{1,0:T(8,128)S(1)} %get-tuple-element.33), channel_id=1, source_target_pairs={{0,1},{1,0},{2,3},{3,2},{4,5},{5,4},{6,7},{7,6},{8,9},{9,8},{10,11... | collective-permute-start | bytes 491528 | tf_op jit(solution)/shard_map/ppermute | solution.py:230
  10.8 12.8 %collective-permute-start.10 = (f32[64,640]{1,0:T(8,128)S(1)}, f32[64,640]{1,0:T(8,128)S(1)}, u32[]{:S(2)}, u32[]{:S(2)}) collective-permute-start(f32[64,640]{1,0:T(8,128)S(1)} %get-tuple-element.34), channel_id=1, source_target_pairs={{0,1},{1,0},{2,3},{3,2},{4,5},{5,4},{6,7},{7,6},{8,9},{9,8},{10,11... | collective-permute-start | bytes 491528 | tf_op jit(solution)/shard_map/ppermute | solution.py:233
  14.7 6.0 %collective-permute-start.6 = (bf16[64,640]{1,0:T(8,128)(2,1)S(1)}, bf16[64,640]{1,0:T(8,128)(2,1)S(1)}, u32[]{:S(2)}, u32[]{:S(2)}) collective-permute-start(bf16[64,640]{1,0:T(8,128)(2,1)S(1)} %get-tuple-element.28), channel_id=1, source_target_pairs={{0,12},{4,8},{8,4},{12,0},{1,13},{5,9},{9,5},{13,1},{2,14},{6,10},... | collective-permute-start | bytes 245768 | tf_op jit(solution)/shard_map/ppermute | solution.py:244
  14.7 6.0 %collective-permute-start.7 = (bf16[64,640]{1,0:T(8,128)(2,1)S(1)}, bf16[64,640]{1,0:T(8,128)(2,1)S(1)}, u32[]{:S(2)}, u32[]{:S(2)}) collective-permute-start(bf16[64,640]{1,0:T(8,128)(2,1)S(1)} %get-tuple-element.29), channel_id=1, source_target_pairs={{0,8},{4,12},{8,0},{12,4},{1,9},{5,13},{9,1},{13,5},{2,10},{6,14},... | collective-permute-start | bytes 245768 | tf_op jit(solution)/shard_map/ppermute | solution.py:246
  15.5 5.8 %collective-permute-start.5 = (bf16[128,640]{1,0:T(8,128)(2,1)S(1)}, bf16[128,640]{1,0:T(8,128)(2,1)S(1)}, u32[]{:S(2)}, u32[]{:S(2)}) collective-permute-start(bf16[128,640]{1,0:T(8,128)(2,1)S(1)} %get-tuple-element.27), channel_id=1, source_target_pairs={{0,4},{4,0},{8,12},{12,8},{1,5},{5,1},{9,13},{13,9},{2,6},{6,2},{1... | collective-permute-start | bytes 491528 | tf_op jit(solution)/shard_map/ppermute | solution.py:249
  17.9 9.4 %collective-permute-start.9 = (f32[64,640]{1,0:T(8,128)S(1)}, f32[64,640]{1,0:T(8,128)S(1)}, u32[]{:S(2)}, u32[]{:S(2)}) collective-permute-start(f32[64,640]{1,0:T(8,128)S(1)} %fold.1), channel_id=1, source_target_pairs={{0,2},{1,3},{2,0},{3,1},{4,6},{5,7},{6,4},{7,5},{8,10},{9,11},{10,... | collective-permute-start | bytes 491528 | tf_op jit(solution)/shard_map/ppermute | solution.py:232
  20.7 6.6 %collective-permute-start.11 = (f32[64,640]{1,0:T(8,128)S(1)}, f32[64,640]{1,0:T(8,128)S(1)}, u32[]{:S(2)}, u32[]{:S(2)}) collective-permute-start(f32[64,640]{1,0:T(8,128)S(1)} %get-tuple-element.36), channel_id=1, source_target_pairs={{0,12},{4,8},{8,4},{12,0},{1,13},{5,9},{9,5},{13,1},{2,14},{6,10},... | collective-permute-start | bytes 491528 | tf_op jit(solution)/shard_map/ppermute | solution.py:257
  20.8 6.5 %collective-permute-start.12 = (f32[64,640]{1,0:T(8,128)S(1)}, f32[64,640]{1,0:T(8,128)S(1)}, u32[]{:S(2)}, u32[]{:S(2)}) collective-permute-start(f32[64,640]{1,0:T(8,128)S(1)} %get-tuple-element.37), channel_id=1, source_target_pairs={{0,4},{4,0},{8,12},{12,8},{1,5},{5,1},{9,13},{13,9},{2,6},{6,2},{1... | collective-permute-start | bytes 491528 | tf_op jit(solution)/shard_map/ppermute | solution.py:258

commit v19 on v18

--- a/solution.py
+++ b/solution.py
@@ -34,7 +34,7 @@
     return lax.rem(((s + 1) ^ 1) + nz - 1, nz)
 
 
-def gather_kernel(nz, nc, token_ref, cot_ref, near_ref, *refs):
+def gather_kernel(nz, nc, steps, token_ref, cot_ref, near_ref, *refs):
     pieces, (f_ref, even_ref, odd_ref), packs = refs[:nc], refs[nc : nc + 3], refs[nc + 3 :]
     blocks = cot_ref.shape[0]
     cols = f_ref.shape[0] // nz
@@ -43,8 +43,8 @@
     def block_for(goal):
         return f_ref[pl.ds(pl.multiple_of(goal * cols, cols), cols), :]
 
-    for k in range(nc):
-        f_ref[pl.ds(pl.multiple_of((c ^ k) * blocks, blocks), blocks), :] = pieces[k][...]
+    for k, piece in zip(steps, pieces):
+        f_ref[pl.ds(pl.multiple_of((c ^ k) * blocks, blocks), blocks), :] = piece[...]
     even_ref[:cols, :] = block_for(s ^ 1)
     even_ref[cols:, :] = near_ref[...]
     odd_ref[...] = block_for(odd_partner(s, nz))
@@ -215,7 +215,11 @@
     cot_odd = lax.ppermute(cot, "sp", odd_pairs)
     (begin,) = kernel_call(token_kernel, "begin", [small], [], weight=W_BEGIN * work)
     feat, begin = lax.optimization_barrier((feat, begin))
-    pieces = [feat] + [lax.ppermute(feat, "ch", mixed(k)) for k in range(1, nc)]
+    pieces = {0: feat}
+    for k in range(2, nc, 2):
+        pieces[k] = lax.ppermute(feat, "ch", mixed(k))
+    for k in range(0, nc, 2):
+        pieces[k + 1] = lax.ppermute(pieces[k], "ch", mixed(1))
 
     *parts, token = kernel_call(
         functools.partial(input_grad_kernel, nz, nc),
@@ -234,11 +238,11 @@
 
     far_rows = cols if nz == 4 else cols + blocks
     f_all, to_even, to_odd, *packs = kernel_call(
-        functools.partial(gather_kernel, nz, nc),
+        functools.partial(gather_kernel, nz, nc, tuple(pieces)),
         "gather",
         [of(channels, BF16), of(cols + blocks, BF16), of(cols, BF16)]
         + [of(far_rows, BF16)] * (nz - 3),
-        [token, cot, cot_odd] + pieces,
+        [token, cot, cot_odd, *pieces.values()],
         weight=W_GATHER * work,
     )
     g_odd = lax.ppermute(to_odd, "sp", odd_pairs)

time: 28.3 us -> 31.5 us (1.11)
  starting transfers between devices: 13.5 us -> 17.2 us
  waiting for transfers between devices: 7.98 us -> 6.67 us
  local copies, waits for them, and re-layouts: 0.01 us -> 0.86 us
    ppermute x1, waiting for transfers between devices: 3.7 us -> 0.56 us  [per_device(): terms.append(lax.ppermute(both, 'ch', mixed(k)))]
    ppermute x1, starting transfers between devices: 1.35 us -> 3.55 us  [per_device(): terms.append(lax.ppermute(both, 'ch', mixed(k)))]
    ppermute x1, waiting for transfers between devices: 0.01 us -> 2.01 us  [per_device(): out_odd = lax.ppermute(out_odd, 'sp', odd_pairs)]
    ppermute x3, starting transfers between devices: 4.39 us -> 6.38 us  [the longest x1 4.04 us: per_device(): pieces[k] = lax.ppermute(feat, 'ch', mixed(k))]
    ppermute x1, starting transfers between devices: 2.44 us -> 0.65 us  [per_device(): cot_odd = lax.ppermute(cot, 'sp', odd_pairs)]
    ppermute x3, waiting for transfers between devices: 2.99 us -> 1.27 us  [the longest x1 1.01 us: per_device(): pieces[k] = lax.ppermute(feat, 'ch', mixed(k))]
    ppermute x1, waiting for transfers between devices: 1.27 us -> 2.81 us  [per_device(): got = lax.ppermute(parts[k + 1], 'ch', mixed(1))]
    ppermute x1, starting transfers between devices: 0.58 us -> 1.59 us  [per_device(): out_even = lax.ppermute(out_even, 'sp', even_pairs)]
  transfers between devices with their start and end apart: 13 -> 13, of which waited for: 3 -> 5; matrix products, arithmetic and copies ran while one was open for 0% -> 0% of each run, Pallas kernels for 18% -> 16%
where the time goes in v19:
time: 31.5 us; the launch traced here: 31.3 us
  starting transfers between devices  17.2 us (55%)
  waiting for transfers between devices  6.67 us (21%)
  Pallas kernels  5.87 us (19%)
  local copies, waits for them, and re-layouts  0.86 us (3%)
  between operations  0.73 us (2%)
    pallas_call x8, Pallas kernels, kernel_call(): pl.pallas_call(body, out_shape=outs, in_specs=[SMEM if a.dtype == jnp.int...  5.87 us
    ppermute x1, starting transfers between devices, per_device(): pieces[k] = lax.ppermute(feat, 'ch', mixed(k))  4.04 us
    ppermute x1, starting transfers between devices, per_device(): terms.append(lax.ppermute(both, 'ch', mixed(k)))  3.55 us
    ppermute x1, waiting for transfers between devices, per_device(): got = lax.ppermute(parts[k + 1], 'ch', mixed(1))  2.81 us
    ppermute x2, starting transfers between devices, per_device(): pieces[k + 1] = lax.ppermute(pieces[k], 'ch', mixed(1))  2.35 us
    ppermute x1, waiting for transfers between devices, per_device(): out_odd = lax.ppermute(out_odd, 'sp', odd_pairs)  2.01 us
    ppermute x1, starting transfers between devices, per_device(): out_even = lax.ppermute(out_even, 'sp', even_pairs)  1.59 us
    ppermute x1, starting transfers between devices, per_device(): lax.ppermute(packs[k - 2], 'sp', [(i, (i + k) % nz) for i in range(nz)])  1.54 us
  transfers between devices with their start and end apart: 13, of which 5 were waited for; matrix products, arithmetic and copies ran while one was open for 0% of the time, Pallas kernels for 16%

profile of v19, /device:TPU:0, one launch (start us, length us, event | category | flops | bytes accessed | tf_op | source)
XLA Modules:
  0.0 31.3 jit_solution(10229644977227926072)
XLA Ops:
  0.6 0.0 copy-start.1
  0.6 0.0 copy-start.2
  0.7 0.0 copy-start
  0.7 0.8 %copy-done.1 = bf16[64,1,640]{2,0,1:T(8,128)(2,1)S(1)} copy-done((bf16[64,1,640]{2,0,1:T(8,128)(2,1)S(1)}, bf16[64,1,640]{2,0,1:T(8,128)(2,1)}, u32[]{:S(2)}) %copy-start.1) | copy-done | bytes 81944
  1.5 4.0 %collective-permute-start.2 = (bf16[64,640]{1,0:T(8,128)(2,1)S(1)}, bf16[64,640]{1,0:T(8,128)(2,1)S(1)}, u32[]{:S(2)}, u32[]{:S(2)}) collective-permute-start(bf16[64,640]{1,0:T(8,128)(2,1)S(1)} %bitcast.5), channel_id=1, source_target_pairs={{0,2},{1,3},{2,0},{3,1},{4,6},{5,7},{6,4},{7,5},{8,10},{9,11},{10,... | collective-permute-start | bytes 245768 | tf_op jit(solution)/shard_map/ppermute | solution.py:220
  5.6 0.0 copy-done.2
  5.6 0.7 %collective-permute-start.1 = (bf16[64,640]{1,0:T(8,128)(2,1)S(1)}, bf16[64,640]{1,0:T(8,128)(2,1)S(1)}, u32[]{:S(2)}, u32[]{:S(2)}) collective-permute-start(bf16[64,640]{1,0:T(8,128)(2,1)S(1)} %bitcast.8), channel_id=1, source_target_pairs={{0,12},{4,8},{8,4},{12,0},{1,13},{5,9},{9,5},{13,1},{2,14},{6,10},... | collective-permute-start | bytes 245768 | tf_op jit(solution)/shard_map/ppermute | solution.py:215
  6.2 1.0 %collective-permute-start = (bf16[64,640]{1,0:T(8,128)(2,1)S(1)}, bf16[64,640]{1,0:T(8,128)(2,1)S(1)}, u32[]{:S(2)}, u32[]{:S(2)}) collective-permute-start(bf16[64,640]{1,0:T(8,128)(2,1)S(1)} %bitcast.9), channel_id=1, source_target_pairs={{0,4},{4,0},{8,12},{12,8},{1,5},{5,1},{9,13},{13,9},{2,6},{6,2},{1... | collective-permute-start | bytes 245768 | tf_op jit(solution)/shard_map/ppermute | solution.py:214
  7.2 1.6 %collective-permute-start.3 = (bf16[64,640]{1,0:T(8,128)(2,1)S(1)}, bf16[64,640]{1,0:T(8,128)(2,1)S(1)}, u32[]{:S(2)}, u32[]{:S(2)}) collective-permute-start(bf16[64,640]{1,0:T(8,128)(2,1)S(1)} %bitcast.6), channel_id=1, source_target_pairs={{0,1},{1,0},{2,3},{3,2},{4,5},{5,4},{6,7},{7,6},{8,9},{9,8},{10,11... | collective-permute-start | bytes 245768 | tf_op jit(solution)/shard_map/ppermute | solution.py:222
  8.7 1.0 %collective-permute-done.2.refs_1_ = bf16[64,640]{1,0:T(8,128)(2,1)S(1)} collective-permute-done((bf16[64,640]{1,0:T(8,128)(2,1)S(1)}, bf16[64,640]{1,0:T(8,128)(2,1)S(1)}, u32[]{:S(2)}, u32[]{:S(2)}) %collective-permute-start.2) | collective-permute-done | bytes 81952 | tf_op jit(solution)/shard_map/ppermute | solution.py:220
  9.8 0.8 %collective-permute-start.4 = (bf16[64,640]{1,0:T(8,128)(2,1)S(1)}, bf16[64,640]{1,0:T(8,128)(2,1)S(1)}, u32[]{:S(2)}, u32[]{:S(2)}) collective-permute-start(bf16[64,640]{1,0:T(8,128)(2,1)S(1)} %collective-permute-done.2.refs_1_), channel_id=1, source_target_pairs={{0,1},{1,0},{2,3},{3,2},{4,5},{5,4},{6,7},{7,6},{8,9},{9,8},{10,11... | collective-permute-start | bytes 245768 | tf_op jit(solution)/shard_map/ppermute | solution.py:222
  10.5 0.0 collective-permute-done.1.odd_ref.near_ref.co_ref
  10.5 0.0 collective-permute-done.even_ref.ce_ref
  10.5 0.0 copy-done
  10.5 1.3 %input_grad.1 = (f32[64,640]{1,0:T(8,128)S(1)}, f32[64,640]{1,0:T(8,128)S(1)}, f32[64,640]{1,0:T(8,128)S(1)}, f32[64,640]{1,0:T(8,128)S(1)}, f32[8,128]{1,0:T(8,128)S(1)}) custom-call(f32[8,128]{1,0:T(8,128)S(1)} %begin.1.begin_ref, bf16[64,640]{1,0:T(8,128)(2,1)S(1)} %bitcast.10, bf16[64,640]{1,0:T(8,128)(2,1)S(1)} %collective-permute-done.even_ref.ce_ref, ...), custom_call_target="tpu_custom_call" | custom-call | flops 566231040 | tf_op jit(solution)/shard_map/input_grad/pallas_call | solution.py:180
  11.8 1.4 %collective-permute-start.8 = (f32[64,640]{1,0:T(8,128)S(1)}, f32[64,640]{1,0:T(8,128)S(1)}, u32[]{:S(2)}, u32[]{:S(2)}) collective-permute-start(f32[64,640]{1,0:T(8,128)S(1)} %get-tuple-element.33), channel_id=1, source_target_pairs={{0,1},{1,0},{2,3},{3,2},{4,5},{5,4},{6,7},{7,6},{8,9},{9,8},{10,11... | collective-permute-start | bytes 491528 | tf_op jit(solution)/shard_map/ppermute | solution.py:234
  13.2 0.7 %collective-permute-start.10 = (f32[64,640]{1,0:T(8,128)S(1)}, f32[64,640]{1,0:T(8,128)S(1)}, u32[]{:S(2)}, u32[]{:S(2)}) collective-permute-start(f32[64,640]{1,0:T(8,128)S(1)} %get-tuple-element.34), channel_id=1, source_target_pairs={{0,1},{1,0},{2,3},{3,2},{4,5},{5,4},{6,7},{7,6},{8,9},{9,8},{10,11... | collective-permute-start | bytes 491528 | tf_op jit(solution)/shard_map/ppermute | solution.py:237
  13.9 0.0 collective-permute-done.3.refs_2_
  13.9 0.3 collective-permute-done.4.refs_3_
  14.2 0.1 gather.1
  14.3 0.1 collective-permute-start.6
  14.3 1.5 %collective-permute-start.7 = (bf16[64,640]{1,0:T(8,128)(2,1)S(1)}, bf16[64,640]{1,0:T(8,128)(2,1)S(1)}, u32[]{:S(2)}, u32[]{:S(2)}) collective-permute-start(bf16[64,640]{1,0:T(8,128)(2,1)S(1)} %get-tuple-element.29), channel_id=1, source_target_pairs={{0,8},{4,12},{8,0},{12,4},{1,9},{5,13},{9,1},{13,5},{2,10},{6,14},... | collective-permute-start | bytes 245768 | tf_op jit(solution)/shard_map/ppermute | solution.py:250
  15.9 0.3 collective-permute-start.5
  16.2 2.8 %collective-permute-done.8.got_ref = f32[64,640]{1,0:T(8,128)S(1)} collective-permute-done((f32[64,640]{1,0:T(8,128)S(1)}, f32[64,640]{1,0:T(8,128)S(1)}, u32[]{:S(2)}, u32[]{:S(2)}) %collective-permute-start.8) | collective-permute-done | bytes 163872 | tf_op jit(solution)/shard_map/ppermute | solution.py:234
  19.0 3.5 %collective-permute-start.9 = (f32[64,640]{1,0:T(8,128)S(1)}, f32[64,640]{1,0:T(8,128)S(1)}, u32[]{:S(2)}, u32[]{:S(2)}) collective-permute-start(f32[64,640]{1,0:T(8,128)S(1)} %fold.1), channel_id=1, source_target_pairs={{0,2},{1,3},{2,0},{3,1},{4,6},{5,7},{6,4},{7,5},{8,10},{9,11},{10,... | collective-permute-start | bytes 491528 | tf_op jit(solution)/shard_map/ppermute | solution.py:236
  22.6 1.4 %early.1 = (f32[64,640]{1,0:T(8,128)S(1)}, f32[64,640]{1,0:T(8,128)S(1)}, f32[64,640]{1,0:T(8,128)S(1)}, bf16[3,192,640]{2,1,0:T(8,128)(2,1)S(1)}) custom-call(bf16[1728,256]{1,0:T(8,128)(2,1)S(1)} %bitcast.4, bf16[256,640]{1,0:T(8,128)(2,1)S(1)} %get-tuple-element.25.f_ref, bf16[64,640]{1,0:T(8,128)(2,1)S(1)} %bitcast.12, ...), custom_call_target="tpu_custom_call" | custom-call | flops 1132462080 | tf_op jit(solution)/shard_map/early/pallas_call | solution.py:180
  24.0 0.0 collective-permute-done.6.go_ref
  24.0 0.1 collective-permute-start.11
  24.1 0.0 collective-permute-done.7.refs_0_
  24.1 1.6 %collective-permute-start.12 = (f32[64,640]{1,0:T(8,128)S(1)}, f32[64,640]{1,0:T(8,128)S(1)}, u32[]{:S(2)}, u32[]{:S(2)}) collective-permute-start(f32[64,640]{1,0:T(8,128)S(1)} %get-tuple-element.37), channel_id=1, source_target_pairs={{0,4},{4,0},{8,12},{12,8},{1,5},{5,1},{9,13},{13,9},{2,6},{6,2},{1... | collective-permute-start | bytes 491528 | tf_op jit(solution)/shard_map/ppermute | solution.py:262
  25.7 0.0 collective-permute-done.5.ge_ref
  25.7 2.3 %weight_grad.1 = (f32[27,64,64]{2,1,0:T(8,128)}, f32[8,128]{1,0:T(8,128)S(1)}) custom-call(bf16[3,192,640]{2,1,0:T(8,128)(2,1)S(1)} %get-tuple-element.26.moved_ref, bf16[256,640]{1,0:T(8,128)(2,1)S(1)} %get-tuple-element.25.f_ref, bf16[128,640]{1,0:T(8,128)(2,1)S(1)} %collective-permute-done.5.ge_ref, bf16[64,640]{1,0:T(8,128)(2,1)S(1)} %collective-permute-done.6.go_ref, ...), custom_call_target="tpu_custom_call" | custom-call | tf_op jit(solution)/shard_map/weight_grad/pallas_call | solution.py:180
  28.0 0.0 collective-permute-done.10.refs_3_.refs_2_
  28.0 0.6 %collective-permute-done.9.refs_2_.refs_1_ = f32[64,640]{1,0:T(8,128)S(1)} collective-permute-done((f32[64,640]{1,0:T(8,128)S(1)}, f32[64,640]{1,0:T(8,128)S(1)}, u32[]{:S(2)}, u32[]{:S(2)}) %collective-permute-start.9) | collective-permute-done | bytes 163872 | tf_op jit(solution)/shard_map/ppermute | solution.py:236
  28.5 2.0 %collective-permute-done.11.odd_ref = f32[64,640]{1,0:T(8,128)S(1)} collective-permute-done((f32[64,640]{1,0:T(8,128)S(1)}, f32[64,640]{1,0:T(8,128)S(1)}, u32[]{:S(2)}, u32[]{:S(2)}) %collective-permute-start.11) | collective-permute-done | bytes 163872 | tf_op jit(solution)/shard_map/ppermute | solution.py:261
  30.5 0.0 collective-permute-done.12.even_ref
  30.5 0.8 %total.1 = (f32[64,1,640]{2,1,0:T(1,128)}, f32[64,1,640]{2,1,0:T(1,128)}) custom-call(f32[8,128]{1,0:T(8,128)S(1)} %hold.1.token_ref, f32[64,640]{1,0:T(8,128)S(1)} %get-tuple-element.35.own_ref, f32[64,640]{1,0:T(8,128)S(1)} %collective-permute-done.11.odd_ref, f32[64,640]{1,0:T(8,128)S(1)} %collective-permute-done.12.even_ref, ...), custom_call_target="tpu_custom_call" | custom-call | tf_op jit(solution)/shard_map/total/pallas_call | solution.py:180
  (3 shorter events, 0.0 us)
Async XLA Ops:
  0.6 0.9 %copy-start.1 = (bf16[64,1,640]{2,0,1:T(8,128)(2,1)S(1)}, bf16[64,1,640]{2,0,1:T(8,128)(2,1)}, u32[]{:S(2)}) copy-start(bf16[64,1,640]{2,0,1:T(8,128)(2,1)} %param.3) | copy-start | bytes 245764
  0.6 4.9 %copy-start.2 = (bf16[64,1,640]{2,0,1:T(8,128)(2,1)S(1)}, bf16[64,1,640]{2,0,1:T(8,128)(2,1)}, u32[]{:S(2)}) copy-start(bf16[64,1,640]{2,0,1:T(8,128)(2,1)} %param.5) | copy-start | bytes 245764
  0.7 9.9 %copy-start = (bf16[27,64,256]{2,1,0:T(8,128)(2,1)S(1)}, bf16[27,64,256]{2,1,0:T(8,128)(2,1)}, u32[]{:S(2)}) copy-start(bf16[27,64,256]{2,1,0:T(8,128)(2,1)} %param.4) | copy-start | bytes 2654212
  1.5 8.2 %collective-permute-start.2 = (bf16[64,640]{1,0:T(8,128)(2,1)S(1)}, bf16[64,640]{1,0:T(8,128)(2,1)S(1)}, u32[]{:S(2)}, u32[]{:S(2)}) collective-permute-start(bf16[64,640]{1,0:T(8,128)(2,1)S(1)} %bitcast.5), channel_id=1, source_target_pairs={{0,2},{1,3},{2,0},{3,1},{4,6},{5,7},{6,4},{7,5},{8,10},{9,11},{10,... | collective-permute-start | bytes 245768 | tf_op jit(solution)/shard_map/ppermute | solution.py:220
  5.6 5.0 %collective-permute-start.1 = (bf16[64,640]{1,0:T(8,128)(2,1)S(1)}, bf16[64,640]{1,0:T(8,128)(2,1)S(1)}, u32[]{:S(2)}, u32[]{:S(2)}) collective-permute-start(bf16[64,640]{1,0:T(8,128)(2,1)S(1)} %bitcast.8), channel_id=1, source_target_pairs={{0,12},{4,8},{8,4},{12,0},{1,13},{5,9},{9,5},{13,1},{2,14},{6,10},... | collective-permute-start | bytes 245768 | tf_op jit(solution)/shard_map/ppermute | solution.py:215
  6.2 4.3 %collective-permute-start = (bf16[64,640]{1,0:T(8,128)(2,1)S(1)}, bf16[64,640]{1,0:T(8,128)(2,1)S(1)}, u32[]{:S(2)}, u32[]{:S(2)}) collective-permute-start(bf16[64,640]{1,0:T(8,128)(2,1)S(1)} %bitcast.9), channel_id=1, source_target_pairs={{0,4},{4,0},{8,12},{12,8},{1,5},{5,1},{9,13},{13,9},{2,6},{6,2},{1... | collective-permute-start | bytes 245768 | tf_op jit(solution)/shard_map/ppermute | solution.py:214
  7.2 6.8 %collective-permute-start.3 = (bf16[64,640]{1,0:T(8,128)(2,1)S(1)}, bf16[64,640]{1,0:T(8,128)(2,1)S(1)}, u32[]{:S(2)}, u32[]{:S(2)}) collective-permute-start(bf16[64,640]{1,0:T(8,128)(2,1)S(1)} %bitcast.6), channel_id=1, source_target_pairs={{0,1},{1,0},{2,3},{3,2},{4,5},{5,4},{6,7},{7,6},{8,9},{9,8},{10,11... | collective-permute-start | bytes 245768 | tf_op jit(solution)/shard_map/ppermute | solution.py:222
  9.8 4.4 %collective-permute-start.4 = (bf16[64,640]{1,0:T(8,128)(2,1)S(1)}, bf16[64,640]{1,0:T(8,128)(2,1)S(1)}, u32[]{:S(2)}, u32[]{:S(2)}) collective-permute-start(bf16[64,640]{1,0:T(8,128)(2,1)S(1)} %collective-permute-done.2.refs_1_), channel_id=1, source_target_pairs={{0,1},{1,0},{2,3},{3,2},{4,5},{5,4},{6,7},{7,6},{8,9},{9,8},{10,11... | collective-permute-start | bytes 245768 | tf_op jit(solution)/shard_map/ppermute | solution.py:222
  11.8 7.2 %collective-permute-start.8 = (f32[64,640]{1,0:T(8,128)S(1)}, f32[64,640]{1,0:T(8,128)S(1)}, u32[]{:S(2)}, u32[]{:S(2)}) collective-permute-start(f32[64,640]{1,0:T(8,128)S(1)} %get-tuple-element.33), channel_id=1, source_target_pairs={{0,1},{1,0},{2,3},{3,2},{4,5},{5,4},{6,7},{7,6},{8,9},{9,8},{10,11... | collective-permute-start | bytes 491528 | tf_op jit(solution)/shard_map/ppermute | solution.py:234
  13.2 14.7 %collective-permute-start.10 = (f32[64,640]{1,0:T(8,128)S(1)}, f32[64,640]{1,0:T(8,128)S(1)}, u32[]{:S(2)}, u32[]{:S(2)}) collective-permute-start(f32[64,640]{1,0:T(8,128)S(1)} %get-tuple-element.34), channel_id=1, source_target_pairs={{0,1},{1,0},{2,3},{3,2},{4,5},{5,4},{6,7},{7,6},{8,9},{9,8},{10,11... | collective-permute-start | bytes 491528 | tf_op jit(solution)/shard_map/ppermute | solution.py:237
  14.3 9.8 %collective-permute-start.6 = (bf16[64,640]{1,0:T(8,128)(2,1)S(1)}, bf16[64,640]{1,0:T(8,128)(2,1)S(1)}, u32[]{:S(2)}, u32[]{:S(2)}) collective-permute-start(bf16[64,640]{1,0:T(8,128)(2,1)S(1)} %get-tuple-element.28), channel_id=1, source_target_pairs={{0,12},{4,8},{8,4},{12,0},{1,13},{5,9},{9,5},{13,1},{2,14},{6,10},... | collective-permute-start | bytes 245768 | tf_op jit(solution)/shard_map/ppermute | solution.py:248
  14.3 9.8 %collective-permute-start.7 = (bf16[64,640]{1,0:T(8,128)(2,1)S(1)}, bf16[64,640]{1,0:T(8,128)(2,1)S(1)}, u32[]{:S(2)}, u32[]{:S(2)}) collective-permute-start(bf16[64,640]{1,0:T(8,128)(2,1)S(1)} %get-tuple-element.29), channel_id=1, source_target_pairs={{0,8},{4,12},{8,0},{12,4},{1,9},{5,13},{9,1},{13,5},{2,10},{6,14},... | collective-permute-start | bytes 245768 | tf_op jit(solution)/shard_map/ppermute | solution.py:250
  15.9 9.8 %collective-permute-start.5 = (bf16[128,640]{1,0:T(8,128)(2,1)S(1)}, bf16[128,640]{1,0:T(8,128)(2,1)S(1)}, u32[]{:S(2)}, u32[]{:S(2)}) collective-permute-start(bf16[128,640]{1,0:T(8,128)(2,1)S(1)} %get-tuple-element.27), channel_id=1, source_target_pairs={{0,4},{4,0},{8,12},{12,8},{1,5},{5,1},{9,13},{13,9},{2,6},{6,2},{1... | collective-permute-start | bytes 491528 | tf_op jit(solution)/shard_map/ppermute | solution.py:253
  19.0 9.5 %collective-permute-start.9 = (f32[64,640]{1,0:T(8,128)S(1)}, f32[64,640]{1,0:T(8,128)S(1)}, u32[]{:S(2)}, u32[]{:S(2)}) collective-permute-start(f32[64,640]{1,0:T(8,128)S(1)} %fold.1), channel_id=1, source_target_pairs={{0,2},{1,3},{2,0},{3,1},{4,6},{5,7},{6,4},{7,5},{8,10},{9,11},{10,... | collective-permute-start | bytes 491528 | tf_op jit(solution)/shard_map/ppermute | solution.py:236
  24.0 6.5 %collective-permute-start.11 = (f32[64,640]{1,0:T(8,128)S(1)}, f32[64,640]{1,0:T(8,128)S(1)}, u32[]{:S(2)}, u32[]{:S(2)}) collective-permute-start(f32[64,640]{1,0:T(8,128)S(1)} %get-tuple-element.36), channel_id=1, source_target_pairs={{0,12},{4,8},{8,4},{12,0},{1,13},{5,9},{9,5},{13,1},{2,14},{6,10},... | collective-permute-start | bytes 491528 | tf_op jit(solution)/shard_map/ppermute | solution.py:261
  24.1 6.4 %collective-permute-start.12 = (f32[64,640]{1,0:T(8,128)S(1)}, f32[64,640]{1,0:T(8,128)S(1)}, u32[]{:S(2)}, u32[]{:S(2)}) collective-permute-start(f32[64,640]{1,0:T(8,128)S(1)} %get-tuple-element.37), channel_id=1, source_target_pairs={{0,4},{4,0},{8,12},{12,8},{1,5},{5,1},{9,13},{13,9},{2,6},{6,2},{1... | collective-permute-start | bytes 491528 | tf_op jit(solution)/shard_map/ppermute | solution.py:262

commit v20 on v19

--- a/solution.py
+++ b/solution.py
@@ -13,7 +13,7 @@
 CELLS = NX * NY
 F32 = jnp.float32
 BF16 = jnp.bfloat16
-W_GATHER, W_EARLY, W_BEGIN, W_GRAD, W_FOLD, W_TOTAL, W_OUT = 2, 2, 8, 1, 0, 1, 0
+W_GATHER, W_EARLY, W_BEGIN, W_GRAD, W_FOLD, W_TOTAL, W_OUT = 0, 2, 8, 1, 0, 1, 0
 VMEM_BYTES = 32 * 1024 * 1024
 
 

time: 31.5 us -> 32.8 us (1.041)
  waiting for transfers between devices: 6.67 us -> 9.16 us
  local copies, waits for them, and re-layouts: 0.86 us -> 0.01 us
    ppermute x2, waiting for transfers between devices: 0.26 us -> 5.64 us  [per_device(): pieces[k + 1] = lax.ppermute(pieces[k], 'ch', mixed(1))]
    ppermute x1, waiting for transfers between devices: 2.81 us -> 0.01 us  [per_device(): got = lax.ppermute(parts[k + 1], 'ch', mixed(1))]
    ppermute x1, waiting for transfers between devices: 0.56 us -> 2.74 us  [per_device(): terms.append(lax.ppermute(both, 'ch', mixed(k)))]
    ppermute x1, waiting for transfers between devices: 2.01 us -> 0.01 us  [per_device(): out_odd = lax.ppermute(out_odd, 'sp', odd_pairs)]
    ppermute x1, starting transfers between devices: 0.65 us -> 2.44 us  [per_device(): cot_odd = lax.ppermute(cot, 'sp', odd_pairs)]
    ppermute x1, starting transfers between devices: 4.04 us -> 2.59 us  [per_device(): pieces[k] = lax.ppermute(feat, 'ch', mixed(k))]
    ppermute x2, starting transfers between devices: 2.35 us -> 1.27 us  [per_device(): pieces[k + 1] = lax.ppermute(pieces[k], 'ch', mixed(1))]
    ppermute x1, starting transfers between devices: 1.38 us -> 2.34 us  [per_device(): got = lax.ppermute(parts[k + 1], 'ch', mixed(1))]
  transfers between devices with their start and end apart: 13 -> 13, of which waited for: 5 -> 4; matrix products, arithmetic and copies ran while one was open for 0% -> 0% of each run, Pallas kernels for 16% -> 16%
where the time goes in v20:
time: 32.8 us; the launch traced here: 32.7 us
  starting transfers between devices  16.9 us (52%)
  waiting for transfers between devices  9.16 us (28%)
  Pallas kernels  5.87 us (18%)
  between operations  0.71 us (2%)
    pallas_call x8, Pallas kernels, kernel_call(): pl.pallas_call(body, out_shape=outs, in_specs=[SMEM if a.dtype == jnp.int...  5.87 us
    ppermute x2, waiting for transfers between devices, per_device(): pieces[k + 1] = lax.ppermute(pieces[k], 'ch', mixed(1))  5.64 us
    ppermute x1, starting transfers between devices, per_device(): terms.append(lax.ppermute(both, 'ch', mixed(k)))  2.87 us
    ppermute x1, waiting for transfers between devices, per_device(): terms.append(lax.ppermute(both, 'ch', mixed(k)))  2.74 us
    ppermute x1, starting transfers between devices, per_device(): pieces[k] = lax.ppermute(feat, 'ch', mixed(k))  2.59 us
    ppermute x1, starting transfers between devices, per_device(): cot_odd = lax.ppermute(cot, 'sp', odd_pairs)  2.44 us
    ppermute x1, starting transfers between devices, per_device(): got = lax.ppermute(parts[k + 1], 'ch', mixed(1))  2.34 us
    ppermute x1, starting transfers between devices, per_device(): lax.ppermute(packs[k - 2], 'sp', [(i, (i + k) % nz) for i in range(nz)])  2.01 us
  transfers between devices with their start and end apart: 13, of which 4 were waited for; matrix products, arithmetic and copies ran while one was open for 0% of the time, Pallas kernels for 16%

profile of v20, /device:TPU:0, one launch (start us, length us, event | category | flops | bytes accessed | tf_op | source)
XLA Modules:
  0.0 32.7 jit_solution(10569332072936243994)
XLA Ops:
  0.6 0.0 copy-start
  0.6 0.0 copy-start.1
  0.7 0.0 copy-start.2
  0.7 2.4 %collective-permute-start.1 = (bf16[64,640]{1,0:T(8,128)(2,1)}, bf16[64,640]{1,0:T(8,128)(2,1)S(1)}, u32[]{:S(2)}, u32[]{:S(2)}) collective-permute-start(bf16[64,640]{1,0:T(8,128)(2,1)} %bitcast.6), channel_id=1, source_target_pairs={{0,12},{4,8},{8,4},{12,0},{1,13},{5,9},{9,5},{13,1},{2,14},{6,10},... | collective-permute-start | bytes 245768 | tf_op jit(solution)/shard_map/ppermute | solution.py:215
  3.1 0.7 %collective-permute-start = (bf16[64,640]{1,0:T(8,128)(2,1)}, bf16[64,640]{1,0:T(8,128)(2,1)S(1)}, u32[]{:S(2)}, u32[]{:S(2)}) collective-permute-start(bf16[64,640]{1,0:T(8,128)(2,1)} %bitcast.7), channel_id=1, source_target_pairs={{0,4},{4,0},{8,12},{12,8},{1,5},{5,1},{9,13},{13,9},{2,6},{6,2},{1... | collective-permute-start | bytes 245768 | tf_op jit(solution)/shard_map/ppermute | solution.py:214
  3.8 0.0 copy-done
  3.8 2.6 %collective-permute-start.2 = (bf16[64,640]{1,0:T(8,128)(2,1)S(1)}, bf16[64,640]{1,0:T(8,128)(2,1)S(1)}, u32[]{:S(2)}, u32[]{:S(2)}) collective-permute-start(bf16[64,640]{1,0:T(8,128)(2,1)S(1)} %bitcast.3), channel_id=1, source_target_pairs={{0,2},{1,3},{2,0},{3,1},{4,6},{5,7},{6,4},{7,5},{8,10},{9,11},{10,... | collective-permute-start | bytes 245768 | tf_op jit(solution)/shard_map/ppermute | solution.py:220
  6.4 0.0 collective-permute-done.1.odd_ref.near_ref.co_ref
  6.4 0.0 collective-permute-done.even_ref.ce_ref
  6.4 0.0 copy-done.1
  6.4 0.0 copy-done.2
  6.4 1.3 %input_grad.1 = (f32[64,640]{1,0:T(8,128)S(1)}, f32[64,640]{1,0:T(8,128)S(1)}, f32[64,640]{1,0:T(8,128)S(1)}, f32[64,640]{1,0:T(8,128)S(1)}, f32[8,128]{1,0:T(8,128)S(1)}) custom-call(f32[8,128]{1,0:T(8,128)S(1)} %begin.1.begin_ref, bf16[64,640]{1,0:T(8,128)(2,1)S(1)} %bitcast.8, bf16[64,640]{1,0:T(8,128)(2,1)S(1)} %collective-permute-done.even_ref.ce_ref, ...), custom_call_target="tpu_custom_call" | custom-call | flops 566231040 | tf_op jit(solution)/shard_map/input_grad/pallas_call | solution.py:180
  7.7 2.3 %collective-permute-start.8 = (f32[64,640]{1,0:T(8,128)S(1)}, f32[64,640]{1,0:T(8,128)S(1)}, u32[]{:S(2)}, u32[]{:S(2)}) collective-permute-start(f32[64,640]{1,0:T(8,128)S(1)} %get-tuple-element.33), channel_id=1, source_target_pairs={{0,1},{1,0},{2,3},{3,2},{4,5},{5,4},{6,7},{7,6},{8,9},{9,8},{10,11... | collective-permute-start | bytes 491528 | tf_op jit(solution)/shard_map/ppermute | solution.py:234
  10.0 0.1 collective-permute-start.3
  10.1 0.8 %collective-permute-done.2.refs_1_ = bf16[64,640]{1,0:T(8,128)(2,1)S(1)} collective-permute-done((bf16[64,640]{1,0:T(8,128)(2,1)S(1)}, bf16[64,640]{1,0:T(8,128)(2,1)S(1)}, u32[]{:S(2)}, u32[]{:S(2)}) %collective-permute-start.2) | collective-permute-done | bytes 81952 | tf_op jit(solution)/shard_map/ppermute | solution.py:220
  10.9 1.2 %collective-permute-start.4 = (bf16[64,640]{1,0:T(8,128)(2,1)S(1)}, bf16[64,640]{1,0:T(8,128)(2,1)S(1)}, u32[]{:S(2)}, u32[]{:S(2)}) collective-permute-start(bf16[64,640]{1,0:T(8,128)(2,1)S(1)} %collective-permute-done.2.refs_1_), channel_id=1, source_target_pairs={{0,1},{1,0},{2,3},{3,2},{4,5},{5,4},{6,7},{7,6},{8,9},{9,8},{10,11... | collective-permute-start | bytes 245768 | tf_op jit(solution)/shard_map/ppermute | solution.py:222
  12.1 0.8 %collective-permute-start.10 = (f32[64,640]{1,0:T(8,128)S(1)}, f32[64,640]{1,0:T(8,128)S(1)}, u32[]{:S(2)}, u32[]{:S(2)}) collective-permute-start(f32[64,640]{1,0:T(8,128)S(1)} %get-tuple-element.34), channel_id=1, source_target_pairs={{0,1},{1,0},{2,3},{3,2},{4,5},{5,4},{6,7},{7,6},{8,9},{9,8},{10,11... | collective-permute-start | bytes 491528 | tf_op jit(solution)/shard_map/ppermute | solution.py:237
  12.9 3.9 %collective-permute-done.3.refs_2_ = bf16[64,640]{1,0:T(8,128)(2,1)S(1)} collective-permute-done((bf16[64,640]{1,0:T(8,128)(2,1)S(1)}, bf16[64,640]{1,0:T(8,128)(2,1)S(1)}, u32[]{:S(2)}, u32[]{:S(2)}) %collective-permute-start.3) | collective-permute-done | bytes 81952 | tf_op jit(solution)/shard_map/ppermute | solution.py:222
  16.8 1.8 %collective-permute-done.4.refs_3_ = bf16[64,640]{1,0:T(8,128)(2,1)S(1)} collective-permute-done((bf16[64,640]{1,0:T(8,128)(2,1)S(1)}, bf16[64,640]{1,0:T(8,128)(2,1)S(1)}, u32[]{:S(2)}, u32[]{:S(2)}) %collective-permute-start.4) | collective-permute-done | bytes 81952 | tf_op jit(solution)/shard_map/ppermute | solution.py:222
  18.5 0.1 gather.1
  18.6 0.1 collective-permute-start.6
  18.7 2.0 %collective-permute-start.7 = (bf16[64,640]{1,0:T(8,128)(2,1)S(1)}, bf16[64,640]{1,0:T(8,128)(2,1)S(1)}, u32[]{:S(2)}, u32[]{:S(2)}) collective-permute-start(bf16[64,640]{1,0:T(8,128)(2,1)S(1)} %get-tuple-element.29), channel_id=1, source_target_pairs={{0,8},{4,12},{8,0},{12,4},{1,9},{5,13},{9,1},{13,5},{2,10},{6,14},... | collective-permute-start | bytes 245768 | tf_op jit(solution)/shard_map/ppermute | solution.py:250
  20.8 0.0 collective-permute-start.5
  20.8 0.0 collective-permute-done.8.got_ref
  20.8 2.9 %collective-permute-start.9 = (f32[64,640]{1,0:T(8,128)S(1)}, f32[64,640]{1,0:T(8,128)S(1)}, u32[]{:S(2)}, u32[]{:S(2)}) collective-permute-start(f32[64,640]{1,0:T(8,128)S(1)} %fold.1), channel_id=1, source_target_pairs={{0,2},{1,3},{2,0},{3,1},{4,6},{5,7},{6,4},{7,5},{8,10},{9,11},{10,... | collective-permute-start | bytes 491528 | tf_op jit(solution)/shard_map/ppermute | solution.py:236
  23.7 1.4 %early.1 = (f32[64,640]{1,0:T(8,128)S(1)}, f32[64,640]{1,0:T(8,128)S(1)}, f32[64,640]{1,0:T(8,128)S(1)}, bf16[3,192,640]{2,1,0:T(8,128)(2,1)S(1)}) custom-call(bf16[1728,256]{1,0:T(8,128)(2,1)S(1)} %bitcast.12, bf16[256,640]{1,0:T(8,128)(2,1)S(1)} %get-tuple-element.25.f_ref, bf16[64,640]{1,0:T(8,128)(2,1)S(1)} %bitcast.10, ...), custom_call_target="tpu_custom_call" | custom-call | flops 1132462080 | tf_op jit(solution)/shard_map/early/pallas_call | solution.py:180
  25.1 0.0 collective-permute-done.6.go_ref
  25.1 0.9 %collective-permute-start.11 = (f32[64,640]{1,0:T(8,128)S(1)}, f32[64,640]{1,0:T(8,128)S(1)}, u32[]{:S(2)}, u32[]{:S(2)}) collective-permute-start(f32[64,640]{1,0:T(8,128)S(1)} %get-tuple-element.36), channel_id=1, source_target_pairs={{0,12},{4,8},{8,4},{12,0},{1,13},{5,9},{9,5},{13,1},{2,14},{6,10},... | collective-permute-start | bytes 491528 | tf_op jit(solution)/shard_map/ppermute | solution.py:261
  26.1 0.0 collective-permute-done.7.refs_0_
  26.1 0.8 %collective-permute-start.12 = (f32[64,640]{1,0:T(8,128)S(1)}, f32[64,640]{1,0:T(8,128)S(1)}, u32[]{:S(2)}, u32[]{:S(2)}) collective-permute-start(f32[64,640]{1,0:T(8,128)S(1)} %get-tuple-element.37), channel_id=1, source_target_pairs={{0,4},{4,0},{8,12},{12,8},{1,5},{5,1},{9,13},{13,9},{2,6},{6,2},{1... | collective-permute-start | bytes 491528 | tf_op jit(solution)/shard_map/ppermute | solution.py:262
  26.9 0.0 collective-permute-done.5.ge_ref
  26.9 2.3 %weight_grad.1 = (f32[27,64,64]{2,1,0:T(8,128)}, f32[8,128]{1,0:T(8,128)S(1)}) custom-call(bf16[3,192,640]{2,1,0:T(8,128)(2,1)S(1)} %get-tuple-element.26.moved_ref, bf16[256,640]{1,0:T(8,128)(2,1)S(1)} %get-tuple-element.25.f_ref, bf16[128,640]{1,0:T(8,128)(2,1)S(1)} %collective-permute-done.5.ge_ref, bf16[64,640]{1,0:T(8,128)(2,1)S(1)} %collective-permute-done.6.go_ref, ...), custom_call_target="tpu_custom_call" | custom-call | tf_op jit(solution)/shard_map/weight_grad/pallas_call | solution.py:180
  29.1 0.0 collective-permute-done.10.refs_3_.refs_2_
  29.1 2.7 %collective-permute-done.9.refs_2_.refs_1_ = f32[64,640]{1,0:T(8,128)S(1)} collective-permute-done((f32[64,640]{1,0:T(8,128)S(1)}, f32[64,640]{1,0:T(8,128)S(1)}, u32[]{:S(2)}, u32[]{:S(2)}) %collective-permute-start.9) | collective-permute-done | bytes 163872 | tf_op jit(solution)/shard_map/ppermute | solution.py:236
  31.9 0.0 collective-permute-done.11.odd_ref
  31.9 0.0 collective-permute-done.12.even_ref
  31.9 0.8 %total.1 = (f32[64,1,640]{2,1,0:T(1,128)}, f32[64,1,640]{2,1,0:T(1,128)}) custom-call(f32[8,128]{1,0:T(8,128)S(1)} %hold.1.token_ref, f32[64,640]{1,0:T(8,128)S(1)} %get-tuple-element.35.own_ref, f32[64,640]{1,0:T(8,128)S(1)} %collective-permute-done.11.odd_ref, f32[64,640]{1,0:T(8,128)S(1)} %collective-permute-done.12.even_ref, ...), custom_call_target="tpu_custom_call" | custom-call | tf_op jit(solution)/shard_map/total/pallas_call | solution.py:180
  (3 shorter events, 0.0 us)
Async XLA Ops:
  0.6 3.2 %copy-start = (bf16[64,1,640]{2,0,1:T(8,128)(2,1)S(1)}, bf16[64,1,640]{2,0,1:T(8,128)(2,1)}, u32[]{:S(2)}) copy-start(bf16[64,1,640]{2,0,1:T(8,128)(2,1)} %param.3) | copy-start | bytes 245764
  0.6 5.7 %copy-start.1 = (bf16[64,1,640]{2,0,1:T(8,128)(2,1)S(1)}, bf16[64,1,640]{2,0,1:T(8,128)(2,1)}, u32[]{:S(2)}) copy-start(bf16[64,1,640]{2,0,1:T(8,128)(2,1)} %param.5) | copy-start | bytes 245764
  0.7 5.7 %copy-start.2 = (bf16[27,64,256]{2,1,0:T(8,128)(2,1)S(1)}, bf16[27,64,256]{2,1,0:T(8,128)(2,1)}, u32[]{:S(2)}) copy-start(bf16[27,64,256]{2,1,0:T(8,128)(2,1)} %param.4) | copy-start | bytes 2654212
  0.7 5.7 %collective-permute-start.1 = (bf16[64,640]{1,0:T(8,128)(2,1)}, bf16[64,640]{1,0:T(8,128)(2,1)S(1)}, u32[]{:S(2)}, u32[]{:S(2)}) collective-permute-start(bf16[64,640]{1,0:T(8,128)(2,1)} %bitcast.6), channel_id=1, source_target_pairs={{0,12},{4,8},{8,4},{12,0},{1,13},{5,9},{9,5},{13,1},{2,14},{6,10},... | collective-permute-start | bytes 245768 | tf_op jit(solution)/shard_map/ppermute | solution.py:215
  3.1 3.3 %collective-permute-start = (bf16[64,640]{1,0:T(8,128)(2,1)}, bf16[64,640]{1,0:T(8,128)(2,1)S(1)}, u32[]{:S(2)}, u32[]{:S(2)}) collective-permute-start(bf16[64,640]{1,0:T(8,128)(2,1)} %bitcast.7), channel_id=1, source_target_pairs={{0,4},{4,0},{8,12},{12,8},{1,5},{5,1},{9,13},{13,9},{2,6},{6,2},{1... | collective-permute-start | bytes 245768 | tf_op jit(solution)/shard_map/ppermute | solution.py:214
  3.8 7.1 %collective-permute-start.2 = (bf16[64,640]{1,0:T(8,128)(2,1)S(1)}, bf16[64,640]{1,0:T(8,128)(2,1)S(1)}, u32[]{:S(2)}, u32[]{:S(2)}) collective-permute-start(bf16[64,640]{1,0:T(8,128)(2,1)S(1)} %bitcast.3), channel_id=1, source_target_pairs={{0,2},{1,3},{2,0},{3,1},{4,6},{5,7},{6,4},{7,5},{8,10},{9,11},{10,... | collective-permute-start | bytes 245768 | tf_op jit(solution)/shard_map/ppermute | solution.py:220
  7.7 13.1 %collective-permute-start.8 = (f32[64,640]{1,0:T(8,128)S(1)}, f32[64,640]{1,0:T(8,128)S(1)}, u32[]{:S(2)}, u32[]{:S(2)}) collective-permute-start(f32[64,640]{1,0:T(8,128)S(1)} %get-tuple-element.33), channel_id=1, source_target_pairs={{0,1},{1,0},{2,3},{3,2},{4,5},{5,4},{6,7},{7,6},{8,9},{9,8},{10,11... | collective-permute-start | bytes 491528 | tf_op jit(solution)/shard_map/ppermute | solution.py:234
  10.0 6.7 %collective-permute-start.3 = (bf16[64,640]{1,0:T(8,128)(2,1)S(1)}, bf16[64,640]{1,0:T(8,128)(2,1)S(1)}, u32[]{:S(2)}, u32[]{:S(2)}) collective-permute-start(bf16[64,640]{1,0:T(8,128)(2,1)S(1)} %bitcast.4), channel_id=1, source_target_pairs={{0,1},{1,0},{2,3},{3,2},{4,5},{5,4},{6,7},{7,6},{8,9},{9,8},{10,11... | collective-permute-start | bytes 245768 | tf_op jit(solution)/shard_map/ppermute | solution.py:222
  10.9 7.7 %collective-permute-start.4 = (bf16[64,640]{1,0:T(8,128)(2,1)S(1)}, bf16[64,640]{1,0:T(8,128)(2,1)S(1)}, u32[]{:S(2)}, u32[]{:S(2)}) collective-permute-start(bf16[64,640]{1,0:T(8,128)(2,1)S(1)} %collective-permute-done.2.refs_1_), channel_id=1, source_target_pairs={{0,1},{1,0},{2,3},{3,2},{4,5},{5,4},{6,7},{7,6},{8,9},{9,8},{10,11... | collective-permute-start | bytes 245768 | tf_op jit(solution)/shard_map/ppermute | solution.py:222
  12.1 17.1 %collective-permute-start.10 = (f32[64,640]{1,0:T(8,128)S(1)}, f32[64,640]{1,0:T(8,128)S(1)}, u32[]{:S(2)}, u32[]{:S(2)}) collective-permute-start(f32[64,640]{1,0:T(8,128)S(1)} %get-tuple-element.34), channel_id=1, source_target_pairs={{0,1},{1,0},{2,3},{3,2},{4,5},{5,4},{6,7},{7,6},{8,9},{9,8},{10,11... | collective-permute-start | bytes 491528 | tf_op jit(solution)/shard_map/ppermute | solution.py:237
  18.6 6.5 %collective-permute-start.6 = (bf16[64,640]{1,0:T(8,128)(2,1)S(1)}, bf16[64,640]{1,0:T(8,128)(2,1)S(1)}, u32[]{:S(2)}, u32[]{:S(2)}) collective-permute-start(bf16[64,640]{1,0:T(8,128)(2,1)S(1)} %get-tuple-element.28), channel_id=1, source_target_pairs={{0,12},{4,8},{8,4},{12,0},{1,13},{5,9},{9,5},{13,1},{2,14},{6,10},... | collective-permute-start | bytes 245768 | tf_op jit(solution)/shard_map/ppermute | solution.py:248
  18.7 7.3 %collective-permute-start.7 = (bf16[64,640]{1,0:T(8,128)(2,1)S(1)}, bf16[64,640]{1,0:T(8,128)(2,1)S(1)}, u32[]{:S(2)}, u32[]{:S(2)}) collective-permute-start(bf16[64,640]{1,0:T(8,128)(2,1)S(1)} %get-tuple-element.29), channel_id=1, source_target_pairs={{0,8},{4,12},{8,0},{12,4},{1,9},{5,13},{9,1},{13,5},{2,10},{6,14},... | collective-permute-start | bytes 245768 | tf_op jit(solution)/shard_map/ppermute | solution.py:250
  20.8 6.1 %collective-permute-start.5 = (bf16[128,640]{1,0:T(8,128)(2,1)S(1)}, bf16[128,640]{1,0:T(8,128)(2,1)S(1)}, u32[]{:S(2)}, u32[]{:S(2)}) collective-permute-start(bf16[128,640]{1,0:T(8,128)(2,1)S(1)} %get-tuple-element.27), channel_id=1, source_target_pairs={{0,4},{4,0},{8,12},{12,8},{1,5},{5,1},{9,13},{13,9},{2,6},{6,2},{1... | collective-permute-start | bytes 491528 | tf_op jit(solution)/shard_map/ppermute | solution.py:253
  20.8 11.1 %collective-permute-start.9 = (f32[64,640]{1,0:T(8,128)S(1)}, f32[64,640]{1,0:T(8,128)S(1)}, u32[]{:S(2)}, u32[]{:S(2)}) collective-permute-start(f32[64,640]{1,0:T(8,128)S(1)} %fold.1), channel_id=1, source_target_pairs={{0,2},{1,3},{2,0},{3,1},{4,6},{5,7},{6,4},{7,5},{8,10},{9,11},{10,... | collective-permute-start | bytes 491528 | tf_op jit(solution)/shard_map/ppermute | solution.py:236
  25.1 6.7 %collective-permute-start.11 = (f32[64,640]{1,0:T(8,128)S(1)}, f32[64,640]{1,0:T(8,128)S(1)}, u32[]{:S(2)}, u32[]{:S(2)}) collective-permute-start(f32[64,640]{1,0:T(8,128)S(1)} %get-tuple-element.36), channel_id=1, source_target_pairs={{0,12},{4,8},{8,4},{12,0},{1,13},{5,9},{9,5},{13,1},{2,14},{6,10},... | collective-permute-start | bytes 491528 | tf_op jit(solution)/shard_map/ppermute | solution.py:261
  26.1 5.8 %collective-permute-start.12 = (f32[64,640]{1,0:T(8,128)S(1)}, f32[64,640]{1,0:T(8,128)S(1)}, u32[]{:S(2)}, u32[]{:S(2)}) collective-permute-start(f32[64,640]{1,0:T(8,128)S(1)} %get-tuple-element.37), channel_id=1, source_target_pairs={{0,4},{4,0},{8,12},{12,8},{1,5},{5,1},{9,13},{13,9},{2,6},{6,2},{1... | collective-permute-start | bytes 491528 | tf_op jit(solution)/shard_map/ppermute | solution.py:262

commit v21 on v19

--- a/solution.py
+++ b/solution.py
@@ -214,7 +214,7 @@
     cot_even = lax.ppermute(cot, "sp", even_pairs)
     cot_odd = lax.ppermute(cot, "sp", odd_pairs)
     (begin,) = kernel_call(token_kernel, "begin", [small], [], weight=W_BEGIN * work)
-    feat, begin = lax.optimization_barrier((feat, begin))
+    feat, cot_even = lax.optimization_barrier((feat, cot_even))
     pieces = {0: feat}
     for k in range(2, nc, 2):
         pieces[k] = lax.ppermute(feat, "ch", mixed(k))
@@ -234,7 +234,8 @@
         got = lax.ppermute(parts[k + 1], "ch", mixed(1))
         (both,) = kernel_call(fold_kernel, "fold", [of(blocks, F32)], [parts[k], got], weight=W_FOLD * work)
         terms.append(lax.ppermute(both, "ch", mixed(k)))
-    terms.append(lax.ppermute(parts[1], "ch", mixed(1)))
+    near, both = lax.optimization_barrier((parts[1], both))
+    terms.append(lax.ppermute(near, "ch", mixed(1)))
 
     far_rows = cols if nz == 4 else cols + blocks
     f_all, to_even, to_odd, *packs = kernel_call(

time: 31.5 us -> 35.2 us (1.12)
  waiting for transfers between devices: 6.67 us -> 12.4 us
  starting transfers between devices: 17.2 us -> 16.1 us
  local copies, waits for them, and re-layouts: 0.86 us -> 0.01 us
    ppermute x1, starting transfers between devices: 3.55 us -> 0.07 us  [per_device(): terms.append(lax.ppermute(both, 'ch', mixed(k)))]
    ppermute x1, waiting for transfers between devices: 2.81 us -> 0.01 us  [per_device(): got = lax.ppermute(parts[k + 1], 'ch', mixed(1))]
    ppermute x1, waiting for transfers between devices: 1.01 us -> 3.28 us  [per_device(): pieces[k] = lax.ppermute(feat, 'ch', mixed(k))]
    ppermute x1, waiting for transfers between devices: 0.01 us -> 1.83 us  [per_device(): lax.ppermute(packs[k - 2], 'sp', [(i, (i + k) % nz) for i in range(nz)])]
    ppermute x1, starting transfers between devices: 0.65 us -> 2.44 us  [per_device(): cot_odd = lax.ppermute(cot, 'sp', odd_pairs)]
    ppermute x2, starting transfers between devices: 2.35 us -> 3.93 us  [per_device(): pieces[k + 1] = lax.ppermute(pieces[k], 'ch', mixed(1))]
    ppermute x1, starting transfers between devices: 1.59 us -> 0.03 us  [per_device(): out_even = lax.ppermute(out_even, 'sp', even_pairs)]
    ppermute x1, starting transfers between devices: 4.04 us -> 2.59 us  [per_device(): pieces[k] = lax.ppermute(feat, 'ch', mixed(k))]
  transfers between devices with their start and end apart: 13 -> 13, of which waited for: 5 -> 7; matrix products, arithmetic and copies ran while one was open for 0% -> 0% of each run, Pallas kernels for 16% -> 11%
where the time goes in v21:
time: 35.2 us; the launch traced here: 35.1 us
  starting transfers between devices  16.1 us (46%)
  waiting for transfers between devices  12.4 us (35%)
  Pallas kernels  5.88 us (17%)
  between operations  0.7 us (2%)
    pallas_call x8, Pallas kernels, kernel_call(): pl.pallas_call(body, out_shape=outs, in_specs=[SMEM if a.dtype == jnp.int...  5.88 us
    ppermute x2, starting transfers between devices, per_device(): pieces[k + 1] = lax.ppermute(pieces[k], 'ch', mixed(1))  3.93 us
    ppermute x1, waiting for transfers between devices, per_device(): pieces[k] = lax.ppermute(feat, 'ch', mixed(k))  3.28 us
    ppermute x1, starting transfers between devices, per_device(): pieces[k] = lax.ppermute(feat, 'ch', mixed(k))  2.59 us
    ppermute x1, starting transfers between devices, per_device(): got = lax.ppermute(parts[k + 1], 'ch', mixed(1))  2.48 us
    ppermute x1, starting transfers between devices, per_device(): cot_odd = lax.ppermute(cot, 'sp', odd_pairs)  2.44 us
    ppermute x1, waiting for transfers between devices, per_device(): out_odd = lax.ppermute(out_odd, 'sp', odd_pairs)  1.98 us
    ppermute x1, starting transfers between devices, per_device(): terms.append(lax.ppermute(near, 'ch', mixed(1)))  1.9 us
  transfers between devices with their start and end apart: 13, of which 7 were waited for; matrix products, arithmetic and copies ran while one was open for 0% of the time, Pallas kernels for 11%

profile of v21, /device:TPU:0, one launch (start us, length us, event | category | flops | bytes accessed | tf_op | source)
XLA Modules:
  0.0 35.1 jit_solution(18381782062031239086)
XLA Ops:
  0.6 0.0 copy-start
  0.6 0.0 copy-start.2
  0.7 2.4 %collective-permute-start.1 = (bf16[64,640]{1,0:T(8,128)(2,1)}, bf16[64,640]{1,0:T(8,128)(2,1)S(1)}, u32[]{:S(2)}, u32[]{:S(2)}) collective-permute-start(bf16[64,640]{1,0:T(8,128)(2,1)} %bitcast.8), channel_id=1, source_target_pairs={{0,12},{4,8},{8,4},{12,0},{1,13},{5,9},{9,5},{13,1},{2,14},{6,10},... | collective-permute-start | bytes 245768 | tf_op jit(solution)/shard_map/ppermute | solution.py:215
  3.1 0.7 %collective-permute-start = (bf16[64,640]{1,0:T(8,128)(2,1)}, bf16[64,640]{1,0:T(8,128)(2,1)S(1)}, u32[]{:S(2)}, u32[]{:S(2)}) collective-permute-start(bf16[64,640]{1,0:T(8,128)(2,1)} %bitcast.9), channel_id=1, source_target_pairs={{0,4},{4,0},{8,12},{12,8},{1,5},{5,1},{9,13},{13,9},{2,6},{6,2},{1... | collective-permute-start | bytes 245768 | tf_op jit(solution)/shard_map/ppermute | solution.py:214
  3.8 1.1 %collective-permute-done.even_ref.ce_ref = bf16[64,640]{1,0:T(8,128)(2,1)S(1)} collective-permute-done((bf16[64,640]{1,0:T(8,128)(2,1)}, bf16[64,640]{1,0:T(8,128)(2,1)S(1)}, u32[]{:S(2)}, u32[]{:S(2)}) %collective-permute-start) | collective-permute-done | bytes 81952 | tf_op jit(solution)/shard_map/ppermute | solution.py:214
  4.9 1.3 %collective-permute-done.1.odd_ref.near_ref.co_ref = bf16[64,640]{1,0:T(8,128)(2,1)S(1)} collective-permute-done((bf16[64,640]{1,0:T(8,128)(2,1)}, bf16[64,640]{1,0:T(8,128)(2,1)S(1)}, u32[]{:S(2)}, u32[]{:S(2)}) %collective-permute-start.1) | collective-permute-done | bytes 81952 | tf_op jit(solution)/shard_map/ppermute | solution.py:215
  6.2 0.0 copy-done
  6.2 0.0 copy-done.2
  6.2 0.0 copy-start.1
  6.2 1.3 %input_grad.1 = (f32[64,640]{1,0:T(8,128)S(1)}, f32[64,640]{1,0:T(8,128)S(1)}, f32[64,640]{1,0:T(8,128)S(1)}, f32[64,640]{1,0:T(8,128)S(1)}, f32[8,128]{1,0:T(8,128)S(1)}) custom-call(f32[8,128]{1,0:T(8,128)S(1)} %begin.1.begin_ref, bf16[64,640]{1,0:T(8,128)(2,1)S(1)} %bitcast.10, bf16[64,640]{1,0:T(8,128)(2,1)S(1)} %collective-permute-done.even_ref.ce_ref, ...), custom_call_target="tpu_custom_call" | custom-call | flops 566231040 | tf_op jit(solution)/shard_map/input_grad/pallas_call | solution.py:180
  7.6 2.5 %collective-permute-start.8 = (f32[64,640]{1,0:T(8,128)S(1)}, f32[64,640]{1,0:T(8,128)S(1)}, u32[]{:S(2)}, u32[]{:S(2)}) collective-permute-start(f32[64,640]{1,0:T(8,128)S(1)} %get-tuple-element.34), channel_id=1, source_target_pairs={{0,1},{1,0},{2,3},{3,2},{4,5},{5,4},{6,7},{7,6},{8,9},{9,8},{10,11... | collective-permute-start | bytes 491528 | tf_op jit(solution)/shard_map/ppermute | solution.py:234
  10.0 0.0 copy-done.1
  10.0 2.6 %collective-permute-start.2 = (bf16[64,640]{1,0:T(8,128)(2,1)S(1)}, bf16[64,640]{1,0:T(8,128)(2,1)S(1)}, u32[]{:S(2)}, u32[]{:S(2)}) collective-permute-start(bf16[64,640]{1,0:T(8,128)(2,1)S(1)} %bitcast.5), channel_id=1, source_target_pairs={{0,2},{1,3},{2,0},{3,1},{4,6},{5,7},{6,4},{7,5},{8,10},{9,11},{10,... | collective-permute-start | bytes 245768 | tf_op jit(solution)/shard_map/ppermute | solution.py:220
  12.6 0.4 %collective-permute-start.3 = (bf16[64,640]{1,0:T(8,128)(2,1)S(1)}, bf16[64,640]{1,0:T(8,128)(2,1)S(1)}, u32[]{:S(2)}, u32[]{:S(2)}) collective-permute-start(bf16[64,640]{1,0:T(8,128)(2,1)S(1)} %bitcast.6), channel_id=1, source_target_pairs={{0,1},{1,0},{2,3},{3,2},{4,5},{5,4},{6,7},{7,6},{8,9},{9,8},{10,11... | collective-permute-start | bytes 245768 | tf_op jit(solution)/shard_map/ppermute | solution.py:222
  13.1 3.3 %collective-permute-done.2.refs_1_ = bf16[64,640]{1,0:T(8,128)(2,1)S(1)} collective-permute-done((bf16[64,640]{1,0:T(8,128)(2,1)S(1)}, bf16[64,640]{1,0:T(8,128)(2,1)S(1)}, u32[]{:S(2)}, u32[]{:S(2)}) %collective-permute-start.2) | collective-permute-done | bytes 81952 | tf_op jit(solution)/shard_map/ppermute | solution.py:220
  16.4 3.5 %collective-permute-start.4 = (bf16[64,640]{1,0:T(8,128)(2,1)S(1)}, bf16[64,640]{1,0:T(8,128)(2,1)S(1)}, u32[]{:S(2)}, u32[]{:S(2)}) collective-permute-start(bf16[64,640]{1,0:T(8,128)(2,1)S(1)} %collective-permute-done.2.refs_1_), channel_id=1, source_target_pairs={{0,1},{1,0},{2,3},{3,2},{4,5},{5,4},{6,7},{7,6},{8,9},{9,8},{10,11... | collective-permute-start | bytes 245768 | tf_op jit(solution)/shard_map/ppermute | solution.py:222
  19.9 0.0 collective-permute-done.8.got_ref
  19.9 0.1 collective-permute-start.9
  20.0 1.9 %collective-permute-start.10 = (f32[64,640]{1,0:T(8,128)S(1)}, f32[64,640]{1,0:T(8,128)S(1)}, u32[]{:S(2)}, u32[]{:S(2)}) collective-permute-start(f32[64,640]{1,0:T(8,128)S(1)} %get-tuple-element.36), channel_id=1, source_target_pairs={{0,1},{1,0},{2,3},{3,2},{4,5},{5,4},{6,7},{7,6},{8,9},{9,8},{10,11... | collective-permute-start | bytes 491528 | tf_op jit(solution)/shard_map/ppermute | solution.py:238
  21.9 0.0 collective-permute-done.3.refs_2_
  21.9 1.5 %collective-permute-done.4.refs_3_ = bf16[64,640]{1,0:T(8,128)(2,1)S(1)} collective-permute-done((bf16[64,640]{1,0:T(8,128)(2,1)S(1)}, bf16[64,640]{1,0:T(8,128)(2,1)S(1)}, u32[]{:S(2)}, u32[]{:S(2)}) %collective-permute-start.4) | collective-permute-done | bytes 81952 | tf_op jit(solution)/shard_map/ppermute | solution.py:222
  23.4 0.1 gather.1
  23.4 0.1 collective-permute-start.6
  23.5 1.6 %collective-permute-start.7 = (bf16[64,640]{1,0:T(8,128)(2,1)S(1)}, bf16[64,640]{1,0:T(8,128)(2,1)S(1)}, u32[]{:S(2)}, u32[]{:S(2)}) collective-permute-start(bf16[64,640]{1,0:T(8,128)(2,1)S(1)} %get-tuple-element.30), channel_id=1, source_target_pairs={{0,8},{4,12},{8,0},{12,4},{1,9},{5,13},{9,1},{13,5},{2,10},{6,14},... | collective-permute-start | bytes 245768 | tf_op jit(solution)/shard_map/ppermute | solution.py:251
  25.1 0.3 collective-permute-start.5
  25.4 1.4 %early.1 = (f32[64,640]{1,0:T(8,128)S(1)}, f32[64,640]{1,0:T(8,128)S(1)}, f32[64,640]{1,0:T(8,128)S(1)}, bf16[3,192,640]{2,1,0:T(8,128)(2,1)S(1)}) custom-call(bf16[1728,256]{1,0:T(8,128)(2,1)S(1)} %bitcast.4, bf16[256,640]{1,0:T(8,128)(2,1)S(1)} %get-tuple-element.26.f_ref, bf16[64,640]{1,0:T(8,128)(2,1)S(1)} %bitcast.12, ...), custom_call_target="tpu_custom_call" | custom-call | flops 1132462080 | tf_op jit(solution)/shard_map/early/pallas_call | solution.py:180
  26.8 1.4 %collective-permute-done.6.go_ref = bf16[64,640]{1,0:T(8,128)(2,1)S(1)} collective-permute-done((bf16[64,640]{1,0:T(8,128)(2,1)S(1)}, bf16[64,640]{1,0:T(8,128)(2,1)S(1)}, u32[]{:S(2)}, u32[]{:S(2)}) %collective-permute-start.6) | collective-permute-done | bytes 81952 | tf_op jit(solution)/shard_map/ppermute | solution.py:249
  28.2 0.0 collective-permute-start.11
  28.2 1.8 %collective-permute-done.7.refs_0_ = bf16[64,640]{1,0:T(8,128)(2,1)S(1)} collective-permute-done((bf16[64,640]{1,0:T(8,128)(2,1)S(1)}, bf16[64,640]{1,0:T(8,128)(2,1)S(1)}, u32[]{:S(2)}, u32[]{:S(2)}) %collective-permute-start.7) | collective-permute-done | bytes 81952 | tf_op jit(solution)/shard_map/ppermute | solution.py:251
  30.0 0.0 collective-permute-start.12
  30.0 0.0 collective-permute-done.5.ge_ref
  30.0 2.3 %weight_grad.1 = (f32[27,64,64]{2,1,0:T(8,128)}, f32[8,128]{1,0:T(8,128)S(1)}) custom-call(bf16[3,192,640]{2,1,0:T(8,128)(2,1)S(1)} %get-tuple-element.27.moved_ref, bf16[256,640]{1,0:T(8,128)(2,1)S(1)} %get-tuple-element.26.f_ref, bf16[128,640]{1,0:T(8,128)(2,1)S(1)} %collective-permute-done.5.ge_ref, bf16[64,640]{1,0:T(8,128)(2,1)S(1)} %collective-permute-done.6.go_ref, ...), custom_call_target="tpu_custom_call" | custom-call | tf_op jit(solution)/shard_map/weight_grad/pallas_call | solution.py:180
  32.3 0.0 collective-permute-done.10.refs_3_.refs_2_
  32.3 0.0 collective-permute-done.9.refs_2_.refs_1_
  32.3 2.0 %collective-permute-done.11.odd_ref = f32[64,640]{1,0:T(8,128)S(1)} collective-permute-done((f32[64,640]{1,0:T(8,128)S(1)}, f32[64,640]{1,0:T(8,128)S(1)}, u32[]{:S(2)}, u32[]{:S(2)}) %collective-permute-start.11) | collective-permute-done | bytes 163872 | tf_op jit(solution)/shard_map/ppermute | solution.py:262
  34.3 0.0 collective-permute-done.12.even_ref
  34.3 0.8 %total.1 = (f32[64,1,640]{2,1,0:T(1,128)}, f32[64,1,640]{2,1,0:T(1,128)}) custom-call(f32[8,128]{1,0:T(8,128)S(1)} %hold.1.token_ref, f32[64,640]{1,0:T(8,128)S(1)} %get-tuple-element.37.own_ref, f32[64,640]{1,0:T(8,128)S(1)} %collective-permute-done.11.odd_ref, f32[64,640]{1,0:T(8,128)S(1)} %collective-permute-done.12.even_ref, ...), custom_call_target="tpu_custom_call" | custom-call | tf_op jit(solution)/shard_map/total/pallas_call | solution.py:180
  (3 shorter events, 0.0 us)
Async XLA Ops:
  0.6 5.6 %copy-start = (bf16[27,64,256]{2,1,0:T(8,128)(2,1)S(1)}, bf16[27,64,256]{2,1,0:T(8,128)(2,1)}, u32[]{:S(2)}) copy-start(bf16[27,64,256]{2,1,0:T(8,128)(2,1)} %param.4) | copy-start | bytes 2654212
  0.6 5.6 %copy-start.2 = (bf16[64,1,640]{2,0,1:T(8,128)(2,1)S(1)}, bf16[64,1,640]{2,0,1:T(8,128)(2,1)}, u32[]{:S(2)}) copy-start(bf16[64,1,640]{2,0,1:T(8,128)(2,1)} %param.5) | copy-start | bytes 245764
  0.7 5.6 %collective-permute-start.1 = (bf16[64,640]{1,0:T(8,128)(2,1)}, bf16[64,640]{1,0:T(8,128)(2,1)S(1)}, u32[]{:S(2)}, u32[]{:S(2)}) collective-permute-start(bf16[64,640]{1,0:T(8,128)(2,1)} %bitcast.8), channel_id=1, source_target_pairs={{0,12},{4,8},{8,4},{12,0},{1,13},{5,9},{9,5},{13,1},{2,14},{6,10},... | collective-permute-start | bytes 245768 | tf_op jit(solution)/shard_map/ppermute | solution.py:215
  3.1 1.8 %collective-permute-start = (bf16[64,640]{1,0:T(8,128)(2,1)}, bf16[64,640]{1,0:T(8,128)(2,1)S(1)}, u32[]{:S(2)}, u32[]{:S(2)}) collective-permute-start(bf16[64,640]{1,0:T(8,128)(2,1)} %bitcast.9), channel_id=1, source_target_pairs={{0,4},{4,0},{8,12},{12,8},{1,5},{5,1},{9,13},{13,9},{2,6},{6,2},{1... | collective-permute-start | bytes 245768 | tf_op jit(solution)/shard_map/ppermute | solution.py:214
  6.2 3.8 %copy-start.1 = (bf16[64,1,640]{2,0,1:T(8,128)(2,1)S(1)}, bf16[64,1,640]{2,0,1:T(8,128)(2,1)}, u32[]{:S(2)}) copy-start(bf16[64,1,640]{2,0,1:T(8,128)(2,1)} %param.3) | copy-start | bytes 245764
  7.6 12.3 %collective-permute-start.8 = (f32[64,640]{1,0:T(8,128)S(1)}, f32[64,640]{1,0:T(8,128)S(1)}, u32[]{:S(2)}, u32[]{:S(2)}) collective-permute-start(f32[64,640]{1,0:T(8,128)S(1)} %get-tuple-element.34), channel_id=1, source_target_pairs={{0,1},{1,0},{2,3},{3,2},{4,5},{5,4},{6,7},{7,6},{8,9},{9,8},{10,11... | collective-permute-start | bytes 491528 | tf_op jit(solution)/shard_map/ppermute | solution.py:234
  10.0 6.3 %collective-permute-start.2 = (bf16[64,640]{1,0:T(8,128)(2,1)S(1)}, bf16[64,640]{1,0:T(8,128)(2,1)S(1)}, u32[]{:S(2)}, u32[]{:S(2)}) collective-permute-start(bf16[64,640]{1,0:T(8,128)(2,1)S(1)} %bitcast.5), channel_id=1, source_target_pairs={{0,2},{1,3},{2,0},{3,1},{4,6},{5,7},{6,4},{7,5},{8,10},{9,11},{10,... | collective-permute-start | bytes 245768 | tf_op jit(solution)/shard_map/ppermute | solution.py:220
  12.6 9.2 %collective-permute-start.3 = (bf16[64,640]{1,0:T(8,128)(2,1)S(1)}, bf16[64,640]{1,0:T(8,128)(2,1)S(1)}, u32[]{:S(2)}, u32[]{:S(2)}) collective-permute-start(bf16[64,640]{1,0:T(8,128)(2,1)S(1)} %bitcast.6), channel_id=1, source_target_pairs={{0,1},{1,0},{2,3},{3,2},{4,5},{5,4},{6,7},{7,6},{8,9},{9,8},{10,11... | collective-permute-start | bytes 245768 | tf_op jit(solution)/shard_map/ppermute | solution.py:222
  16.4 7.0 %collective-permute-start.4 = (bf16[64,640]{1,0:T(8,128)(2,1)S(1)}, bf16[64,640]{1,0:T(8,128)(2,1)S(1)}, u32[]{:S(2)}, u32[]{:S(2)}) collective-permute-start(bf16[64,640]{1,0:T(8,128)(2,1)S(1)} %collective-permute-done.2.refs_1_), channel_id=1, source_target_pairs={{0,1},{1,0},{2,3},{3,2},{4,5},{5,4},{6,7},{7,6},{8,9},{9,8},{10,11... | collective-permute-start | bytes 245768 | tf_op jit(solution)/shard_map/ppermute | solution.py:222
  19.9 12.4 %collective-permute-start.9 = (f32[64,640]{1,0:T(8,128)S(1)}, f32[64,640]{1,0:T(8,128)S(1)}, u32[]{:S(2)}, u32[]{:S(2)}) collective-permute-start(f32[64,640]{1,0:T(8,128)S(1)} %fold.1), channel_id=1, source_target_pairs={{0,2},{1,3},{2,0},{3,1},{4,6},{5,7},{6,4},{7,5},{8,10},{9,11},{10,... | collective-permute-start | bytes 491528 | tf_op jit(solution)/shard_map/ppermute | solution.py:236
  20.0 12.3 %collective-permute-start.10 = (f32[64,640]{1,0:T(8,128)S(1)}, f32[64,640]{1,0:T(8,128)S(1)}, u32[]{:S(2)}, u32[]{:S(2)}) collective-permute-start(f32[64,640]{1,0:T(8,128)S(1)} %get-tuple-element.36), channel_id=1, source_target_pairs={{0,1},{1,0},{2,3},{3,2},{4,5},{5,4},{6,7},{7,6},{8,9},{9,8},{10,11... | collective-permute-start | bytes 491528 | tf_op jit(solution)/shard_map/ppermute | solution.py:238
  23.4 4.7 %collective-permute-start.6 = (bf16[64,640]{1,0:T(8,128)(2,1)S(1)}, bf16[64,640]{1,0:T(8,128)(2,1)S(1)}, u32[]{:S(2)}, u32[]{:S(2)}) collective-permute-start(bf16[64,640]{1,0:T(8,128)(2,1)S(1)} %get-tuple-element.29), channel_id=1, source_target_pairs={{0,12},{4,8},{8,4},{12,0},{1,13},{5,9},{9,5},{13,1},{2,14},{6,10},... | collective-permute-start | bytes 245768 | tf_op jit(solution)/shard_map/ppermute | solution.py:249
  23.5 6.5 %collective-permute-start.7 = (bf16[64,640]{1,0:T(8,128)(2,1)S(1)}, bf16[64,640]{1,0:T(8,128)(2,1)S(1)}, u32[]{:S(2)}, u32[]{:S(2)}) collective-permute-start(bf16[64,640]{1,0:T(8,128)(2,1)S(1)} %get-tuple-element.30), channel_id=1, source_target_pairs={{0,8},{4,12},{8,0},{12,4},{1,9},{5,13},{9,1},{13,5},{2,10},{6,14},... | collective-permute-start | bytes 245768 | tf_op jit(solution)/shard_map/ppermute | solution.py:251
  25.1 4.9 %collective-permute-start.5 = (bf16[128,640]{1,0:T(8,128)(2,1)S(1)}, bf16[128,640]{1,0:T(8,128)(2,1)S(1)}, u32[]{:S(2)}, u32[]{:S(2)}) collective-permute-start(bf16[128,640]{1,0:T(8,128)(2,1)S(1)} %get-tuple-element.28), channel_id=1, source_target_pairs={{0,4},{4,0},{8,12},{12,8},{1,5},{5,1},{9,13},{13,9},{2,6},{6,2},{1... | collective-permute-start | bytes 491528 | tf_op jit(solution)/shard_map/ppermute | solution.py:254
  28.2 6.1 %collective-permute-start.11 = (f32[64,640]{1,0:T(8,128)S(1)}, f32[64,640]{1,0:T(8,128)S(1)}, u32[]{:S(2)}, u32[]{:S(2)}) collective-permute-start(f32[64,640]{1,0:T(8,128)S(1)} %get-tuple-element.38), channel_id=1, source_target_pairs={{0,12},{4,8},{8,4},{12,0},{1,13},{5,9},{9,5},{13,1},{2,14},{6,10},... | collective-permute-start | bytes 491528 | tf_op jit(solution)/shard_map/ppermute | solution.py:262
  30.0 4.3 %collective-permute-start.12 = (f32[64,640]{1,0:T(8,128)S(1)}, f32[64,640]{1,0:T(8,128)S(1)}, u32[]{:S(2)}, u32[]{:S(2)}) collective-permute-start(f32[64,640]{1,0:T(8,128)S(1)} %get-tuple-element.39), channel_id=1, source_target_pairs={{0,4},{4,0},{8,12},{12,8},{1,5},{5,1},{9,13},{13,9},{2,6},{6,2},{1... | collective-permute-start | bytes 491528 | tf_op jit(solution)/shard_map/ppermute | solution.py:263

commit v22 on v18

--- a/solution.py
+++ b/solution.py
@@ -230,7 +230,8 @@
         got = lax.ppermute(parts[k + 1], "ch", mixed(1))
         (both,) = kernel_call(fold_kernel, "fold", [of(blocks, F32)], [parts[k], got], weight=W_FOLD * work)
         terms.append(lax.ppermute(both, "ch", mixed(k)))
-    terms.append(lax.ppermute(parts[1], "ch", mixed(1)))
+    near, both = lax.optimization_barrier((parts[1], both))
+    terms.append(lax.ppermute(near, "ch", mixed(1)))
 
     far_rows = cols if nz == 4 else cols + blocks
     f_all, to_even, to_odd, *packs = kernel_call(

time: 28.3 us -> 29.3 us (1.035)
  starting transfers between devices: 13.5 us -> 15.1 us
  waiting for transfers between devices: 7.98 us -> 7.39 us
    ppermute x1, waiting for transfers between devices: 3.7 us -> 0.84 us  [per_device(): terms.append(lax.ppermute(both, 'ch', mixed(k)))]
    ppermute x1, starting transfers between devices: 0.78 us -> 2.48 us  [per_device(): terms.append(lax.ppermute(near, 'ch', mixed(1)))]
    ppermute x1, waiting for transfers between devices: 0.01 us -> 1.08 us  [per_device(): terms.append(lax.ppermute(near, 'ch', mixed(1)))]
    ppermute x1, waiting for transfers between devices: 0.01 us -> 1.06 us  [per_device(): out_odd = lax.ppermute(out_odd, 'sp', odd_pairs)]
    ppermute x3, waiting for transfers between devices: 2.99 us -> 3.77 us  [per_device(): pieces = [feat] + [lax.ppermute(feat, 'ch', mixed(k)) for k in range(1, nc)]]
    ppermute x1, waiting for transfers between devices: 1.27 us -> 0.63 us  [per_device(): got = lax.ppermute(parts[k + 1], 'ch', mixed(1))]
  transfers between devices with their start and end apart: 13 -> 13, of which waited for: 3 -> 5; matrix products, arithmetic and copies ran while one was open for 0% -> 0% of each run, Pallas kernels for 18% -> 17%
where the time goes in v22:
time: 29.3 us; the launch traced here: 29.1 us
  starting transfers between devices  15.1 us (52%)
  waiting for transfers between devices  7.39 us (25%)
  Pallas kernels  5.87 us (20%)
  between operations  0.73 us (2%)
    pallas_call x8, Pallas kernels, kernel_call(): pl.pallas_call(body, out_shape=outs, in_specs=[SMEM if a.dtype == jnp.int...  5.87 us
    ppermute x3, starting transfers between devices, per_device(): pieces = [feat] + [lax.ppermute(feat, 'ch', mixed(k)) for k in range(1, nc)]  4.39 us
    ppermute x3, waiting for transfers between devices, per_device(): pieces = [feat] + [lax.ppermute(feat, 'ch', mixed(k)) for k in range(1, nc)]  3.77 us
    ppermute x1, starting transfers between devices, per_device(): terms.append(lax.ppermute(near, 'ch', mixed(1)))  2.48 us
    ppermute x1, starting transfers between devices, per_device(): cot_odd = lax.ppermute(cot, 'sp', odd_pairs)  2.44 us
    ppermute x1, starting transfers between devices, per_device(): got = lax.ppermute(parts[k + 1], 'ch', mixed(1))  1.31 us
    ppermute x1, starting transfers between devices, per_device(): terms.append(lax.ppermute(both, 'ch', mixed(k)))  1.2 us
    ppermute x1, waiting for transfers between devices, per_device(): terms.append(lax.ppermute(near, 'ch', mixed(1)))  1.08 us
  transfers between devices with their start and end apart: 13, of which 5 were waited for; matrix products, arithmetic and copies ran while one was open for 0% of the time, Pallas kernels for 17%

profile of v22, /device:TPU:0, one launch (start us, length us, event | category | flops | bytes accessed | tf_op | source)
XLA Modules:
  0.0 29.1 jit_solution(4184907239656956480)
XLA Ops:
  0.6 0.0 copy-start.1
  0.6 0.0 copy-start
  0.7 0.0 copy-start.2
  0.7 2.4 %collective-permute-start.1 = (bf16[64,640]{1,0:T(8,128)(2,1)}, bf16[64,640]{1,0:T(8,128)(2,1)S(1)}, u32[]{:S(2)}, u32[]{:S(2)}) collective-permute-start(bf16[64,640]{1,0:T(8,128)(2,1)} %bitcast.9), channel_id=1, source_target_pairs={{0,12},{4,8},{8,4},{12,0},{1,13},{5,9},{9,5},{13,1},{2,14},{6,10},... | collective-permute-start | bytes 245768 | tf_op jit(solution)/shard_map/ppermute | solution.py:215
  3.1 0.7 %collective-permute-start = (bf16[64,640]{1,0:T(8,128)(2,1)}, bf16[64,640]{1,0:T(8,128)(2,1)S(1)}, u32[]{:S(2)}, u32[]{:S(2)}) collective-permute-start(bf16[64,640]{1,0:T(8,128)(2,1)} %bitcast.10), channel_id=1, source_target_pairs={{0,4},{4,0},{8,12},{12,8},{1,5},{5,1},{9,13},{13,9},{2,6},{6,2},{1... | collective-permute-start | bytes 245768 | tf_op jit(solution)/shard_map/ppermute | solution.py:214
  3.8 0.0 copy-done.1
  3.8 3.6 %collective-permute-start.4 = (bf16[64,640]{1,0:T(8,128)(2,1)S(1)}, bf16[64,640]{1,0:T(8,128)(2,1)S(1)}, u32[]{:S(2)}, u32[]{:S(2)}) collective-permute-start(bf16[64,640]{1,0:T(8,128)(2,1)S(1)} %bitcast.5), channel_id=1, source_target_pairs={{0,3},{1,2},{2,1},{3,0},{4,7},{5,6},{6,5},{7,4},{8,11},{9,10},{10,... | collective-permute-start | bytes 245768 | tf_op jit(solution)/shard_map/ppermute | solution.py:218
  7.4 0.0 collective-permute-start.3
  7.4 0.8 %collective-permute-start.2 = (bf16[64,640]{1,0:T(8,128)(2,1)S(1)}, bf16[64,640]{1,0:T(8,128)(2,1)S(1)}, u32[]{:S(2)}, u32[]{:S(2)}) collective-permute-start(bf16[64,640]{1,0:T(8,128)(2,1)S(1)} %bitcast.7), channel_id=1, source_target_pairs={{0,1},{1,0},{2,3},{3,2},{4,5},{5,4},{6,7},{7,6},{8,9},{9,8},{10,11... | collective-permute-start | bytes 245768 | tf_op jit(solution)/shard_map/ppermute | solution.py:218
  8.2 0.0 collective-permute-done.1.odd_ref.near_ref.co_ref
  8.2 0.0 collective-permute-done.even_ref.ce_ref
  8.2 0.0 copy-done
  8.2 0.0 copy-done.2
  8.2 1.3 %input_grad.1 = (f32[64,640]{1,0:T(8,128)S(1)}, f32[64,640]{1,0:T(8,128)S(1)}, f32[64,640]{1,0:T(8,128)S(1)}, f32[64,640]{1,0:T(8,128)S(1)}, f32[8,128]{1,0:T(8,128)S(1)}) custom-call(f32[8,128]{1,0:T(8,128)S(1)} %begin.1.begin_ref, bf16[64,640]{1,0:T(8,128)(2,1)S(1)} %bitcast.11, bf16[64,640]{1,0:T(8,128)(2,1)S(1)} %collective-permute-done.even_ref.ce_ref, ...), custom_call_target="tpu_custom_call" | custom-call | flops 566231040 | tf_op jit(solution)/shard_map/input_grad/pallas_call | solution.py:180
  9.5 1.3 %collective-permute-start.8 = (f32[64,640]{1,0:T(8,128)S(1)}, f32[64,640]{1,0:T(8,128)S(1)}, u32[]{:S(2)}, u32[]{:S(2)}) collective-permute-start(f32[64,640]{1,0:T(8,128)S(1)} %get-tuple-element.34), channel_id=1, source_target_pairs={{0,1},{1,0},{2,3},{3,2},{4,5},{5,4},{6,7},{7,6},{8,9},{9,8},{10,11... | collective-permute-start | bytes 491528 | tf_op jit(solution)/shard_map/ppermute | solution.py:230
  10.8 0.0 collective-permute-done.4.refs_3_
  10.8 3.8 %collective-permute-done.3.refs_2_ = bf16[64,640]{1,0:T(8,128)(2,1)S(1)} collective-permute-done((bf16[64,640]{1,0:T(8,128)(2,1)S(1)}, bf16[64,640]{1,0:T(8,128)(2,1)S(1)}, u32[]{:S(2)}, u32[]{:S(2)}) %collective-permute-start.3) | collective-permute-done | bytes 81952 | tf_op jit(solution)/shard_map/ppermute | solution.py:218
  14.6 0.0 collective-permute-done.2.refs_1_
  14.6 0.1 gather.1
  14.7 0.1 collective-permute-start.6
  14.7 0.8 %collective-permute-start.7 = (bf16[64,640]{1,0:T(8,128)(2,1)S(1)}, bf16[64,640]{1,0:T(8,128)(2,1)S(1)}, u32[]{:S(2)}, u32[]{:S(2)}) collective-permute-start(bf16[64,640]{1,0:T(8,128)(2,1)S(1)} %get-tuple-element.30), channel_id=1, source_target_pairs={{0,8},{4,12},{8,0},{12,4},{1,9},{5,13},{9,1},{13,5},{2,10},{6,14},... | collective-permute-start | bytes 245768 | tf_op jit(solution)/shard_map/ppermute | solution.py:247
  15.5 1.0 %collective-permute-start.5 = (bf16[128,640]{1,0:T(8,128)(2,1)S(1)}, bf16[128,640]{1,0:T(8,128)(2,1)S(1)}, u32[]{:S(2)}, u32[]{:S(2)}) collective-permute-start(bf16[128,640]{1,0:T(8,128)(2,1)S(1)} %get-tuple-element.28), channel_id=1, source_target_pairs={{0,4},{4,0},{8,12},{12,8},{1,5},{5,1},{9,13},{13,9},{2,6},{6,2},{1... | collective-permute-start | bytes 491528 | tf_op jit(solution)/shard_map/ppermute | solution.py:250
  16.6 0.6 %collective-permute-done.8.got_ref = f32[64,640]{1,0:T(8,128)S(1)} collective-permute-done((f32[64,640]{1,0:T(8,128)S(1)}, f32[64,640]{1,0:T(8,128)S(1)}, u32[]{:S(2)}, u32[]{:S(2)}) %collective-permute-start.8) | collective-permute-done | bytes 163872 | tf_op jit(solution)/shard_map/ppermute | solution.py:230
  17.2 1.2 %collective-permute-start.9 = (f32[64,640]{1,0:T(8,128)S(1)}, f32[64,640]{1,0:T(8,128)S(1)}, u32[]{:S(2)}, u32[]{:S(2)}) collective-permute-start(f32[64,640]{1,0:T(8,128)S(1)} %fold.1), channel_id=1, source_target_pairs={{0,2},{1,3},{2,0},{3,1},{4,6},{5,7},{6,4},{7,5},{8,10},{9,11},{10,... | collective-permute-start | bytes 491528 | tf_op jit(solution)/shard_map/ppermute | solution.py:232
  18.4 2.5 %collective-permute-start.10 = (f32[64,640]{1,0:T(8,128)S(1)}, f32[64,640]{1,0:T(8,128)S(1)}, u32[]{:S(2)}, u32[]{:S(2)}) collective-permute-start(f32[64,640]{1,0:T(8,128)S(1)} %get-tuple-element.36), channel_id=1, source_target_pairs={{0,1},{1,0},{2,3},{3,2},{4,5},{5,4},{6,7},{7,6},{8,9},{9,8},{10,11... | collective-permute-start | bytes 491528 | tf_op jit(solution)/shard_map/ppermute | solution.py:234
  20.9 1.4 %early.1 = (f32[64,640]{1,0:T(8,128)S(1)}, f32[64,640]{1,0:T(8,128)S(1)}, f32[64,640]{1,0:T(8,128)S(1)}, bf16[3,192,640]{2,1,0:T(8,128)(2,1)S(1)}) custom-call(bf16[1728,256]{1,0:T(8,128)(2,1)S(1)} %bitcast.4, bf16[256,640]{1,0:T(8,128)(2,1)S(1)} %get-tuple-element.26.f_ref, bf16[64,640]{1,0:T(8,128)(2,1)S(1)} %bitcast.13, ...), custom_call_target="tpu_custom_call" | custom-call | flops 1132462080 | tf_op jit(solution)/shard_map/early/pallas_call | solution.py:180
  22.4 0.0 collective-permute-done.6.go_ref
  22.4 0.1 collective-permute-start.11
  22.4 0.0 collective-permute-done.7.refs_0_
  22.5 0.6 %collective-permute-start.12 = (f32[64,640]{1,0:T(8,128)S(1)}, f32[64,640]{1,0:T(8,128)S(1)}, u32[]{:S(2)}, u32[]{:S(2)}) collective-permute-start(f32[64,640]{1,0:T(8,128)S(1)} %get-tuple-element.39), channel_id=1, source_target_pairs={{0,4},{4,0},{8,12},{12,8},{1,5},{5,1},{9,13},{13,9},{2,6},{6,2},{1... | collective-permute-start | bytes 491528 | tf_op jit(solution)/shard_map/ppermute | solution.py:259
  23.1 0.0 collective-permute-done.5.ge_ref
  23.1 2.3 %weight_grad.1 = (f32[27,64,64]{2,1,0:T(8,128)}, f32[8,128]{1,0:T(8,128)S(1)}) custom-call(bf16[3,192,640]{2,1,0:T(8,128)(2,1)S(1)} %get-tuple-element.27.moved_ref, bf16[256,640]{1,0:T(8,128)(2,1)S(1)} %get-tuple-element.26.f_ref, bf16[128,640]{1,0:T(8,128)(2,1)S(1)} %collective-permute-done.5.ge_ref, bf16[64,640]{1,0:T(8,128)(2,1)S(1)} %collective-permute-done.6.go_ref, ...), custom_call_target="tpu_custom_call" | custom-call | tf_op jit(solution)/shard_map/weight_grad/pallas_call | solution.py:180
  25.4 1.1 %collective-permute-done.10.refs_3_.refs_2_ = f32[64,640]{1,0:T(8,128)S(1)} collective-permute-done((f32[64,640]{1,0:T(8,128)S(1)}, f32[64,640]{1,0:T(8,128)S(1)}, u32[]{:S(2)}, u32[]{:S(2)}) %collective-permute-start.10) | collective-permute-done | bytes 163872 | tf_op jit(solution)/shard_map/ppermute | solution.py:234
  26.4 0.8 %collective-permute-done.9.refs_2_.refs_1_ = f32[64,640]{1,0:T(8,128)S(1)} collective-permute-done((f32[64,640]{1,0:T(8,128)S(1)}, f32[64,640]{1,0:T(8,128)S(1)}, u32[]{:S(2)}, u32[]{:S(2)}) %collective-permute-start.9) | collective-permute-done | bytes 163872 | tf_op jit(solution)/shard_map/ppermute | solution.py:232
  27.3 1.1 %collective-permute-done.11.odd_ref = f32[64,640]{1,0:T(8,128)S(1)} collective-permute-done((f32[64,640]{1,0:T(8,128)S(1)}, f32[64,640]{1,0:T(8,128)S(1)}, u32[]{:S(2)}, u32[]{:S(2)}) %collective-permute-start.11) | collective-permute-done | bytes 163872 | tf_op jit(solution)/shard_map/ppermute | solution.py:258
  28.3 0.0 collective-permute-done.12.even_ref
  28.3 0.8 %total.1 = (f32[64,1,640]{2,1,0:T(1,128)}, f32[64,1,640]{2,1,0:T(1,128)}) custom-call(f32[8,128]{1,0:T(8,128)S(1)} %hold.1.token_ref, f32[64,640]{1,0:T(8,128)S(1)} %get-tuple-element.37.own_ref, f32[64,640]{1,0:T(8,128)S(1)} %collective-permute-done.11.odd_ref, f32[64,640]{1,0:T(8,128)S(1)} %collective-permute-done.12.even_ref, ...), custom_call_target="tpu_custom_call" | custom-call | tf_op jit(solution)/shard_map/total/pallas_call | solution.py:180
  (3 shorter events, 0.0 us)
Async XLA Ops:
  0.6 3.2 %copy-start.1 = (bf16[64,1,640]{2,0,1:T(8,128)(2,1)S(1)}, bf16[64,1,640]{2,0,1:T(8,128)(2,1)}, u32[]{:S(2)}) copy-start(bf16[64,1,640]{2,0,1:T(8,128)(2,1)} %param.3) | copy-start | bytes 245764
  0.6 7.5 %copy-start = (bf16[27,64,256]{2,1,0:T(8,128)(2,1)S(1)}, bf16[27,64,256]{2,1,0:T(8,128)(2,1)}, u32[]{:S(2)}) copy-start(bf16[27,64,256]{2,1,0:T(8,128)(2,1)} %param.4) | copy-start | bytes 2654212
  0.7 7.5 %copy-start.2 = (bf16[64,1,640]{2,0,1:T(8,128)(2,1)S(1)}, bf16[64,1,640]{2,0,1:T(8,128)(2,1)}, u32[]{:S(2)}) copy-start(bf16[64,1,640]{2,0,1:T(8,128)(2,1)} %param.5) | copy-start | bytes 245764
  0.7 7.5 %collective-permute-start.1 = (bf16[64,640]{1,0:T(8,128)(2,1)}, bf16[64,640]{1,0:T(8,128)(2,1)S(1)}, u32[]{:S(2)}, u32[]{:S(2)}) collective-permute-start(bf16[64,640]{1,0:T(8,128)(2,1)} %bitcast.9), channel_id=1, source_target_pairs={{0,12},{4,8},{8,4},{12,0},{1,13},{5,9},{9,5},{13,1},{2,14},{6,10},... | collective-permute-start | bytes 245768 | tf_op jit(solution)/shard_map/ppermute | solution.py:215
  3.1 5.1 %collective-permute-start = (bf16[64,640]{1,0:T(8,128)(2,1)}, bf16[64,640]{1,0:T(8,128)(2,1)S(1)}, u32[]{:S(2)}, u32[]{:S(2)}) collective-permute-start(bf16[64,640]{1,0:T(8,128)(2,1)} %bitcast.10), channel_id=1, source_target_pairs={{0,4},{4,0},{8,12},{12,8},{1,5},{5,1},{9,13},{13,9},{2,6},{6,2},{1... | collective-permute-start | bytes 245768 | tf_op jit(solution)/shard_map/ppermute | solution.py:214
  3.8 7.0 %collective-permute-start.4 = (bf16[64,640]{1,0:T(8,128)(2,1)S(1)}, bf16[64,640]{1,0:T(8,128)(2,1)S(1)}, u32[]{:S(2)}, u32[]{:S(2)}) collective-permute-start(bf16[64,640]{1,0:T(8,128)(2,1)S(1)} %bitcast.5), channel_id=1, source_target_pairs={{0,3},{1,2},{2,1},{3,0},{4,7},{5,6},{6,5},{7,4},{8,11},{9,10},{10,... | collective-permute-start | bytes 245768 | tf_op jit(solution)/shard_map/ppermute | solution.py:218
  7.4 7.2 %collective-permute-start.3 = (bf16[64,640]{1,0:T(8,128)(2,1)S(1)}, bf16[64,640]{1,0:T(8,128)(2,1)S(1)}, u32[]{:S(2)}, u32[]{:S(2)}) collective-permute-start(bf16[64,640]{1,0:T(8,128)(2,1)S(1)} %bitcast.6), channel_id=1, source_target_pairs={{0,2},{1,3},{2,0},{3,1},{4,6},{5,7},{6,4},{7,5},{8,10},{9,11},{10,... | collective-permute-start | bytes 245768 | tf_op jit(solution)/shard_map/ppermute | solution.py:218
  7.4 7.2 %collective-permute-start.2 = (bf16[64,640]{1,0:T(8,128)(2,1)S(1)}, bf16[64,640]{1,0:T(8,128)(2,1)S(1)}, u32[]{:S(2)}, u32[]{:S(2)}) collective-permute-start(bf16[64,640]{1,0:T(8,128)(2,1)S(1)} %bitcast.7), channel_id=1, source_target_pairs={{0,1},{1,0},{2,3},{3,2},{4,5},{5,4},{6,7},{7,6},{8,9},{9,8},{10,11... | collective-permute-start | bytes 245768 | tf_op jit(solution)/shard_map/ppermute | solution.py:218
  9.5 7.7 %collective-permute-start.8 = (f32[64,640]{1,0:T(8,128)S(1)}, f32[64,640]{1,0:T(8,128)S(1)}, u32[]{:S(2)}, u32[]{:S(2)}) collective-permute-start(f32[64,640]{1,0:T(8,128)S(1)} %get-tuple-element.34), channel_id=1, source_target_pairs={{0,1},{1,0},{2,3},{3,2},{4,5},{5,4},{6,7},{7,6},{8,9},{9,8},{10,11... | collective-permute-start | bytes 491528 | tf_op jit(solution)/shard_map/ppermute | solution.py:230
  14.7 7.7 %collective-permute-start.6 = (bf16[64,640]{1,0:T(8,128)(2,1)S(1)}, bf16[64,640]{1,0:T(8,128)(2,1)S(1)}, u32[]{:S(2)}, u32[]{:S(2)}) collective-permute-start(bf16[64,640]{1,0:T(8,128)(2,1)S(1)} %get-tuple-element.29), channel_id=1, source_target_pairs={{0,12},{4,8},{8,4},{12,0},{1,13},{5,9},{9,5},{13,1},{2,14},{6,10},... | collective-permute-start | bytes 245768 | tf_op jit(solution)/shard_map/ppermute | solution.py:245
  14.7 7.7 %collective-permute-start.7 = (bf16[64,640]{1,0:T(8,128)(2,1)S(1)}, bf16[64,640]{1,0:T(8,128)(2,1)S(1)}, u32[]{:S(2)}, u32[]{:S(2)}) collective-permute-start(bf16[64,640]{1,0:T(8,128)(2,1)S(1)} %get-tuple-element.30), channel_id=1, source_target_pairs={{0,8},{4,12},{8,0},{12,4},{1,9},{5,13},{9,1},{13,5},{2,10},{6,14},... | collective-permute-start | bytes 245768 | tf_op jit(solution)/shard_map/ppermute | solution.py:247
  15.5 7.5 %collective-permute-start.5 = (bf16[128,640]{1,0:T(8,128)(2,1)S(1)}, bf16[128,640]{1,0:T(8,128)(2,1)S(1)}, u32[]{:S(2)}, u32[]{:S(2)}) collective-permute-start(bf16[128,640]{1,0:T(8,128)(2,1)S(1)} %get-tuple-element.28), channel_id=1, source_target_pairs={{0,4},{4,0},{8,12},{12,8},{1,5},{5,1},{9,13},{13,9},{2,6},{6,2},{1... | collective-permute-start | bytes 491528 | tf_op jit(solution)/shard_map/ppermute | solution.py:250
  17.2 10.0 %collective-permute-start.9 = (f32[64,640]{1,0:T(8,128)S(1)}, f32[64,640]{1,0:T(8,128)S(1)}, u32[]{:S(2)}, u32[]{:S(2)}) collective-permute-start(f32[64,640]{1,0:T(8,128)S(1)} %fold.1), channel_id=1, source_target_pairs={{0,2},{1,3},{2,0},{3,1},{4,6},{5,7},{6,4},{7,5},{8,10},{9,11},{10,... | collective-permute-start | bytes 491528 | tf_op jit(solution)/shard_map/ppermute | solution.py:232
  18.4 8.0 %collective-permute-start.10 = (f32[64,640]{1,0:T(8,128)S(1)}, f32[64,640]{1,0:T(8,128)S(1)}, u32[]{:S(2)}, u32[]{:S(2)}) collective-permute-start(f32[64,640]{1,0:T(8,128)S(1)} %get-tuple-element.36), channel_id=1, source_target_pairs={{0,1},{1,0},{2,3},{3,2},{4,5},{5,4},{6,7},{7,6},{8,9},{9,8},{10,11... | collective-permute-start | bytes 491528 | tf_op jit(solution)/shard_map/ppermute | solution.py:234
  22.4 6.0 %collective-permute-start.11 = (f32[64,640]{1,0:T(8,128)S(1)}, f32[64,640]{1,0:T(8,128)S(1)}, u32[]{:S(2)}, u32[]{:S(2)}) collective-permute-start(f32[64,640]{1,0:T(8,128)S(1)} %get-tuple-element.38), channel_id=1, source_target_pairs={{0,12},{4,8},{8,4},{12,0},{1,13},{5,9},{9,5},{13,1},{2,14},{6,10},... | collective-permute-start | bytes 491528 | tf_op jit(solution)/shard_map/ppermute | solution.py:258
  22.5 5.9 %collective-permute-start.12 = (f32[64,640]{1,0:T(8,128)S(1)}, f32[64,640]{1,0:T(8,128)S(1)}, u32[]{:S(2)}, u32[]{:S(2)}) collective-permute-start(f32[64,640]{1,0:T(8,128)S(1)} %get-tuple-element.39), channel_id=1, source_target_pairs={{0,4},{4,0},{8,12},{12,8},{1,5},{5,1},{9,13},{13,9},{2,6},{6,2},{1... | collective-permute-start | bytes 491528 | tf_op jit(solution)/shard_map/ppermute | solution.py:259

commit v23 on v19

--- a/solution.py
+++ b/solution.py
@@ -215,11 +215,8 @@
     cot_odd = lax.ppermute(cot, "sp", odd_pairs)
     (begin,) = kernel_call(token_kernel, "begin", [small], [], weight=W_BEGIN * work)
     feat, begin = lax.optimization_barrier((feat, begin))
-    pieces = {0: feat}
-    for k in range(2, nc, 2):
-        pieces[k] = lax.ppermute(feat, "ch", mixed(k))
-    for k in range(0, nc, 2):
-        pieces[k + 1] = lax.ppermute(pieces[k], "ch", mixed(1))
+    steps = (0, 1, *range(nc - 1, 1, -1))
+    pieces = [feat] + [lax.ppermute(feat, "ch", mixed(k)) for k in steps[1:]]
 
     *parts, token = kernel_call(
         functools.partial(input_grad_kernel, nz, nc),
@@ -238,11 +235,11 @@
 
     far_rows = cols if nz == 4 else cols + blocks
     f_all, to_even, to_odd, *packs = kernel_call(
-        functools.partial(gather_kernel, nz, nc, tuple(pieces)),
+        functools.partial(gather_kernel, nz, nc, steps),
         "gather",
         [of(channels, BF16), of(cols + blocks, BF16), of(cols, BF16)]
         + [of(far_rows, BF16)] * (nz - 3),
-        [token, cot, cot_odd, *pieces.values()],
+        [token, cot, cot_odd] + pieces,
         weight=W_GATHER * work,
     )
     g_odd = lax.ppermute(to_odd, "sp", odd_pairs)

time: 31.5 us -> 28.5 us (0.905)
  starting transfers between devices: 17.2 us -> 13.4 us
  waiting for transfers between devices: 6.67 us -> 8.3 us
  local copies, waits for them, and re-layouts: 0.86 us -> 0.01 us
    ppermute x1, waiting for transfers between devices: 0.56 us -> 3.42 us  [per_device(): terms.append(lax.ppermute(both, 'ch', mixed(k)))]
    ppermute x3, starting transfers between devices: 6.38 us -> 4.17 us  [per_device(): pieces = [feat] + [lax.ppermute(feat, 'ch', mixed(k)) for k in steps[1:]]]
    ppermute x1, starting transfers between devices: 3.55 us -> 1.44 us  [per_device(): terms.append(lax.ppermute(both, 'ch', mixed(k)))]
    ppermute x3, waiting for transfers between devices: 1.27 us -> 3.34 us  [per_device(): pieces = [feat] + [lax.ppermute(feat, 'ch', mixed(k)) for k in steps[1:]]]
    ppermute x1, waiting for transfers between devices: 2.01 us -> 0.01 us  [per_device(): out_odd = lax.ppermute(out_odd, 'sp', odd_pairs)]
    ppermute x1, starting transfers between devices: 0.65 us -> 2.44 us  [per_device(): cot_odd = lax.ppermute(cot, 'sp', odd_pairs)]
    ppermute x1, waiting for transfers between devices: 2.81 us -> 1.52 us  [per_device(): got = lax.ppermute(parts[k + 1], 'ch', mixed(1))]
    ppermute x1, starting transfers between devices: 1.59 us -> 0.63 us  [per_device(): out_even = lax.ppermute(out_even, 'sp', even_pairs)]
  transfers between devices with their start and end apart: 13 -> 13, of which waited for: 5 -> 4; matrix products, arithmetic and copies ran while one was open for 0% -> 0% of each run, Pallas kernels for 16% -> 18%
where the time goes in v23:
time: 28.5 us; the launch traced here: 28.4 us
  starting transfers between devices  13.4 us (47%)
  waiting for transfers between devices  8.3 us (29%)
  Pallas kernels  5.87 us (21%)
  between operations  0.74 us (3%)
    pallas_call x8, Pallas kernels, kernel_call(): pl.pallas_call(body, out_shape=outs, in_specs=[SMEM if a.dtype == jnp.int...  5.87 us
    ppermute x3, starting transfers between devices, per_device(): pieces = [feat] + [lax.ppermute(feat, 'ch', mixed(k)) for k in steps[1:]]  4.17 us
    ppermute x1, waiting for transfers between devices, per_device(): terms.append(lax.ppermute(both, 'ch', mixed(k)))  3.42 us
    ppermute x3, waiting for transfers between devices, per_device(): pieces = [feat] + [lax.ppermute(feat, 'ch', mixed(k)) for k in steps[1:]]  3.34 us
    ppermute x1, starting transfers between devices, per_device(): cot_odd = lax.ppermute(cot, 'sp', odd_pairs)  2.44 us
    ppermute x1, starting transfers between devices, per_device(): got = lax.ppermute(parts[k + 1], 'ch', mixed(1))  1.87 us
    ppermute x1, waiting for transfers between devices, per_device(): got = lax.ppermute(parts[k + 1], 'ch', mixed(1))  1.52 us
    ppermute x1, starting transfers between devices, per_device(): terms.append(lax.ppermute(both, 'ch', mixed(k)))  1.44 us
  transfers between devices with their start and end apart: 13, of which 4 were waited for; matrix products, arithmetic and copies ran while one was open for 0% of the time, Pallas kernels for 18%

profile of v23, /device:TPU:0, one launch (start us, length us, event | category | flops | bytes accessed | tf_op | source)
XLA Modules:
  0.0 28.4 jit_solution(17764354767050999842)
XLA Ops:
  0.6 0.0 copy-start.1
  0.6 0.0 copy-start
  0.7 0.0 copy-start.2
  0.7 2.4 %collective-permute-start.1 = (bf16[64,640]{1,0:T(8,128)(2,1)}, bf16[64,640]{1,0:T(8,128)(2,1)S(1)}, u32[]{:S(2)}, u32[]{:S(2)}) collective-permute-start(bf16[64,640]{1,0:T(8,128)(2,1)} %bitcast.9), channel_id=1, source_target_pairs={{0,12},{4,8},{8,4},{12,0},{1,13},{5,9},{9,5},{13,1},{2,14},{6,10},... | collective-permute-start | bytes 245768 | tf_op jit(solution)/shard_map/ppermute | solution.py:215
  3.1 0.7 %collective-permute-start = (bf16[64,640]{1,0:T(8,128)(2,1)}, bf16[64,640]{1,0:T(8,128)(2,1)S(1)}, u32[]{:S(2)}, u32[]{:S(2)}) collective-permute-start(bf16[64,640]{1,0:T(8,128)(2,1)} %bitcast.10), channel_id=1, source_target_pairs={{0,4},{4,0},{8,12},{12,8},{1,5},{5,1},{9,13},{13,9},{2,6},{6,2},{1... | collective-permute-start | bytes 245768 | tf_op jit(solution)/shard_map/ppermute | solution.py:214
  3.8 0.0 copy-done.1
  3.8 2.6 %collective-permute-start.4 = (bf16[64,640]{1,0:T(8,128)(2,1)S(1)}, bf16[64,640]{1,0:T(8,128)(2,1)S(1)}, u32[]{:S(2)}, u32[]{:S(2)}) collective-permute-start(bf16[64,640]{1,0:T(8,128)(2,1)S(1)} %bitcast.5), channel_id=1, source_target_pairs={{0,2},{1,3},{2,0},{3,1},{4,6},{5,7},{6,4},{7,5},{8,10},{9,11},{10,... | collective-permute-start | bytes 245768 | tf_op jit(solution)/shard_map/ppermute | solution.py:219
  6.4 1.3 %collective-permute-start.3 = (bf16[64,640]{1,0:T(8,128)(2,1)S(1)}, bf16[64,640]{1,0:T(8,128)(2,1)S(1)}, u32[]{:S(2)}, u32[]{:S(2)}) collective-permute-start(bf16[64,640]{1,0:T(8,128)(2,1)S(1)} %bitcast.6), channel_id=1, source_target_pairs={{0,3},{1,2},{2,1},{3,0},{4,7},{5,6},{6,5},{7,4},{8,11},{9,10},{10,... | collective-permute-start | bytes 245768 | tf_op jit(solution)/shard_map/ppermute | solution.py:219
  7.7 0.2 collective-permute-start.2
  8.0 0.0 collective-permute-done.1.odd_ref.near_ref.co_ref
  8.0 0.0 collective-permute-done.even_ref.ce_ref
  8.0 0.0 copy-done
  8.0 0.0 copy-done.2
  8.0 1.3 %input_grad.1 = (f32[64,640]{1,0:T(8,128)S(1)}, f32[64,640]{1,0:T(8,128)S(1)}, f32[64,640]{1,0:T(8,128)S(1)}, f32[64,640]{1,0:T(8,128)S(1)}, f32[8,128]{1,0:T(8,128)S(1)}) custom-call(f32[8,128]{1,0:T(8,128)S(1)} %begin.1.begin_ref, bf16[64,640]{1,0:T(8,128)(2,1)S(1)} %bitcast.11, bf16[64,640]{1,0:T(8,128)(2,1)S(1)} %collective-permute-done.even_ref.ce_ref, ...), custom_call_target="tpu_custom_call" | custom-call | flops 566231040 | tf_op jit(solution)/shard_map/input_grad/pallas_call | solution.py:180
  9.3 1.9 %collective-permute-start.8 = (f32[64,640]{1,0:T(8,128)S(1)}, f32[64,640]{1,0:T(8,128)S(1)}, u32[]{:S(2)}, u32[]{:S(2)}) collective-permute-start(f32[64,640]{1,0:T(8,128)S(1)} %get-tuple-element.33), channel_id=1, source_target_pairs={{0,1},{1,0},{2,3},{3,2},{4,5},{5,4},{6,7},{7,6},{8,9},{9,8},{10,11... | collective-permute-start | bytes 491528 | tf_op jit(solution)/shard_map/ppermute | solution.py:231
  11.2 0.2 collective-permute-start.10
  11.4 1.9 %collective-permute-done.4.refs_3_ = bf16[64,640]{1,0:T(8,128)(2,1)S(1)} collective-permute-done((bf16[64,640]{1,0:T(8,128)(2,1)S(1)}, bf16[64,640]{1,0:T(8,128)(2,1)S(1)}, u32[]{:S(2)}, u32[]{:S(2)}) %collective-permute-start.4) | collective-permute-done | bytes 81952 | tf_op jit(solution)/shard_map/ppermute | solution.py:219
  13.3 0.0 collective-permute-done.3.refs_2_
  13.3 1.4 %collective-permute-done.2.refs_1_ = bf16[64,640]{1,0:T(8,128)(2,1)S(1)} collective-permute-done((bf16[64,640]{1,0:T(8,128)(2,1)S(1)}, bf16[64,640]{1,0:T(8,128)(2,1)S(1)}, u32[]{:S(2)}, u32[]{:S(2)}) %collective-permute-start.2) | collective-permute-done | bytes 81952 | tf_op jit(solution)/shard_map/ppermute | solution.py:219
  14.7 0.1 gather.1
  14.8 0.1 collective-permute-start.6
  14.9 0.7 %collective-permute-start.7 = (bf16[64,640]{1,0:T(8,128)(2,1)S(1)}, bf16[64,640]{1,0:T(8,128)(2,1)S(1)}, u32[]{:S(2)}, u32[]{:S(2)}) collective-permute-start(bf16[64,640]{1,0:T(8,128)(2,1)S(1)} %get-tuple-element.29), channel_id=1, source_target_pairs={{0,8},{4,12},{8,0},{12,4},{1,9},{5,13},{9,1},{13,5},{2,10},{6,14},... | collective-permute-start | bytes 245768 | tf_op jit(solution)/shard_map/ppermute | solution.py:247
  15.5 1.2 %collective-permute-start.5 = (bf16[128,640]{1,0:T(8,128)(2,1)S(1)}, bf16[128,640]{1,0:T(8,128)(2,1)S(1)}, u32[]{:S(2)}, u32[]{:S(2)}) collective-permute-start(bf16[128,640]{1,0:T(8,128)(2,1)S(1)} %get-tuple-element.27), channel_id=1, source_target_pairs={{0,4},{4,0},{8,12},{12,8},{1,5},{5,1},{9,13},{13,9},{2,6},{6,2},{1... | collective-permute-start | bytes 491528 | tf_op jit(solution)/shard_map/ppermute | solution.py:250
  16.7 1.5 %collective-permute-done.8.got_ref = f32[64,640]{1,0:T(8,128)S(1)} collective-permute-done((f32[64,640]{1,0:T(8,128)S(1)}, f32[64,640]{1,0:T(8,128)S(1)}, u32[]{:S(2)}, u32[]{:S(2)}) %collective-permute-start.8) | collective-permute-done | bytes 163872 | tf_op jit(solution)/shard_map/ppermute | solution.py:231
  18.3 1.4 %collective-permute-start.9 = (f32[64,640]{1,0:T(8,128)S(1)}, f32[64,640]{1,0:T(8,128)S(1)}, u32[]{:S(2)}, u32[]{:S(2)}) collective-permute-start(f32[64,640]{1,0:T(8,128)S(1)} %fold.1), channel_id=1, source_target_pairs={{0,2},{1,3},{2,0},{3,1},{4,6},{5,7},{6,4},{7,5},{8,10},{9,11},{10,... | collective-permute-start | bytes 491528 | tf_op jit(solution)/shard_map/ppermute | solution.py:233
  19.7 1.4 %early.1 = (f32[64,640]{1,0:T(8,128)S(1)}, f32[64,640]{1,0:T(8,128)S(1)}, f32[64,640]{1,0:T(8,128)S(1)}, bf16[3,192,640]{2,1,0:T(8,128)(2,1)S(1)}) custom-call(bf16[1728,256]{1,0:T(8,128)(2,1)S(1)} %bitcast.4, bf16[256,640]{1,0:T(8,128)(2,1)S(1)} %get-tuple-element.25.f_ref, bf16[64,640]{1,0:T(8,128)(2,1)S(1)} %bitcast.13, ...), custom_call_target="tpu_custom_call" | custom-call | flops 1132462080 | tf_op jit(solution)/shard_map/early/pallas_call | solution.py:180
  21.1 0.0 collective-permute-done.6.go_ref
  21.2 0.1 collective-permute-start.11
  21.2 0.0 collective-permute-done.7.refs_0_
  21.2 0.6 %collective-permute-start.12 = (f32[64,640]{1,0:T(8,128)S(1)}, f32[64,640]{1,0:T(8,128)S(1)}, u32[]{:S(2)}, u32[]{:S(2)}) collective-permute-start(f32[64,640]{1,0:T(8,128)S(1)} %get-tuple-element.37), channel_id=1, source_target_pairs={{0,4},{4,0},{8,12},{12,8},{1,5},{5,1},{9,13},{13,9},{2,6},{6,2},{1... | collective-permute-start | bytes 491528 | tf_op jit(solution)/shard_map/ppermute | solution.py:259
  21.9 0.0 collective-permute-done.5.ge_ref
  21.9 2.3 %weight_grad.1 = (f32[27,64,64]{2,1,0:T(8,128)}, f32[8,128]{1,0:T(8,128)S(1)}) custom-call(bf16[3,192,640]{2,1,0:T(8,128)(2,1)S(1)} %get-tuple-element.26.moved_ref, bf16[256,640]{1,0:T(8,128)(2,1)S(1)} %get-tuple-element.25.f_ref, bf16[128,640]{1,0:T(8,128)(2,1)S(1)} %collective-permute-done.5.ge_ref, bf16[64,640]{1,0:T(8,128)(2,1)S(1)} %collective-permute-done.6.go_ref, ...), custom_call_target="tpu_custom_call" | custom-call | tf_op jit(solution)/shard_map/weight_grad/pallas_call | solution.py:180
  24.1 0.0 collective-permute-done.10.refs_3_.refs_2_
  24.1 3.4 %collective-permute-done.9.refs_2_.refs_1_ = f32[64,640]{1,0:T(8,128)S(1)} collective-permute-done((f32[64,640]{1,0:T(8,128)S(1)}, f32[64,640]{1,0:T(8,128)S(1)}, u32[]{:S(2)}, u32[]{:S(2)}) %collective-permute-start.9) | collective-permute-done | bytes 163872 | tf_op jit(solution)/shard_map/ppermute | solution.py:233
  27.6 0.0 collective-permute-done.11.odd_ref
  27.6 0.0 collective-permute-done.12.even_ref
  27.6 0.8 %total.1 = (f32[64,1,640]{2,1,0:T(1,128)}, f32[64,1,640]{2,1,0:T(1,128)}) custom-call(f32[8,128]{1,0:T(8,128)S(1)} %hold.1.token_ref, f32[64,640]{1,0:T(8,128)S(1)} %get-tuple-element.35.own_ref, f32[64,640]{1,0:T(8,128)S(1)} %collective-permute-done.11.odd_ref, f32[64,640]{1,0:T(8,128)S(1)} %collective-permute-done.12.even_ref, ...), custom_call_target="tpu_custom_call" | custom-call | tf_op jit(solution)/shard_map/total/pallas_call | solution.py:180
  (3 shorter events, 0.0 us)
Async XLA Ops:
  0.6 3.2 %copy-start.1 = (bf16[64,1,640]{2,0,1:T(8,128)(2,1)S(1)}, bf16[64,1,640]{2,0,1:T(8,128)(2,1)}, u32[]{:S(2)}) copy-start(bf16[64,1,640]{2,0,1:T(8,128)(2,1)} %param.3) | copy-start | bytes 245764
  0.6 7.3 %copy-start = (bf16[27,64,256]{2,1,0:T(8,128)(2,1)S(1)}, bf16[27,64,256]{2,1,0:T(8,128)(2,1)}, u32[]{:S(2)}) copy-start(bf16[27,64,256]{2,1,0:T(8,128)(2,1)} %param.4) | copy-start | bytes 2654212
  0.7 7.3 %copy-start.2 = (bf16[64,1,640]{2,0,1:T(8,128)(2,1)S(1)}, bf16[64,1,640]{2,0,1:T(8,128)(2,1)}, u32[]{:S(2)}) copy-start(bf16[64,1,640]{2,0,1:T(8,128)(2,1)} %param.5) | copy-start | bytes 245764
  0.7 7.3 %collective-permute-start.1 = (bf16[64,640]{1,0:T(8,128)(2,1)}, bf16[64,640]{1,0:T(8,128)(2,1)S(1)}, u32[]{:S(2)}, u32[]{:S(2)}) collective-permute-start(bf16[64,640]{1,0:T(8,128)(2,1)} %bitcast.9), channel_id=1, source_target_pairs={{0,12},{4,8},{8,4},{12,0},{1,13},{5,9},{9,5},{13,1},{2,14},{6,10},... | collective-permute-start | bytes 245768 | tf_op jit(solution)/shard_map/ppermute | solution.py:215
  3.1 4.9 %collective-permute-start = (bf16[64,640]{1,0:T(8,128)(2,1)}, bf16[64,640]{1,0:T(8,128)(2,1)S(1)}, u32[]{:S(2)}, u32[]{:S(2)}) collective-permute-start(bf16[64,640]{1,0:T(8,128)(2,1)} %bitcast.10), channel_id=1, source_target_pairs={{0,4},{4,0},{8,12},{12,8},{1,5},{5,1},{9,13},{13,9},{2,6},{6,2},{1... | collective-permute-start | bytes 245768 | tf_op jit(solution)/shard_map/ppermute | solution.py:214
  3.8 9.5 %collective-permute-start.4 = (bf16[64,640]{1,0:T(8,128)(2,1)S(1)}, bf16[64,640]{1,0:T(8,128)(2,1)S(1)}, u32[]{:S(2)}, u32[]{:S(2)}) collective-permute-start(bf16[64,640]{1,0:T(8,128)(2,1)S(1)} %bitcast.5), channel_id=1, source_target_pairs={{0,2},{1,3},{2,0},{3,1},{4,6},{5,7},{6,4},{7,5},{8,10},{9,11},{10,... | collective-permute-start | bytes 245768 | tf_op jit(solution)/shard_map/ppermute | solution.py:219
  6.4 6.9 %collective-permute-start.3 = (bf16[64,640]{1,0:T(8,128)(2,1)S(1)}, bf16[64,640]{1,0:T(8,128)(2,1)S(1)}, u32[]{:S(2)}, u32[]{:S(2)}) collective-permute-start(bf16[64,640]{1,0:T(8,128)(2,1)S(1)} %bitcast.6), channel_id=1, source_target_pairs={{0,3},{1,2},{2,1},{3,0},{4,7},{5,6},{6,5},{7,4},{8,11},{9,10},{10,... | collective-permute-start | bytes 245768 | tf_op jit(solution)/shard_map/ppermute | solution.py:219
  7.7 7.0 %collective-permute-start.2 = (bf16[64,640]{1,0:T(8,128)(2,1)S(1)}, bf16[64,640]{1,0:T(8,128)(2,1)S(1)}, u32[]{:S(2)}, u32[]{:S(2)}) collective-permute-start(bf16[64,640]{1,0:T(8,128)(2,1)S(1)} %bitcast.7), channel_id=1, source_target_pairs={{0,1},{1,0},{2,3},{3,2},{4,5},{5,4},{6,7},{7,6},{8,9},{9,8},{10,11... | collective-permute-start | bytes 245768 | tf_op jit(solution)/shard_map/ppermute | solution.py:219
  9.3 8.9 %collective-permute-start.8 = (f32[64,640]{1,0:T(8,128)S(1)}, f32[64,640]{1,0:T(8,128)S(1)}, u32[]{:S(2)}, u32[]{:S(2)}) collective-permute-start(f32[64,640]{1,0:T(8,128)S(1)} %get-tuple-element.33), channel_id=1, source_target_pairs={{0,1},{1,0},{2,3},{3,2},{4,5},{5,4},{6,7},{7,6},{8,9},{9,8},{10,11... | collective-permute-start | bytes 491528 | tf_op jit(solution)/shard_map/ppermute | solution.py:231
  11.2 13.0 %collective-permute-start.10 = (f32[64,640]{1,0:T(8,128)S(1)}, f32[64,640]{1,0:T(8,128)S(1)}, u32[]{:S(2)}, u32[]{:S(2)}) collective-permute-start(f32[64,640]{1,0:T(8,128)S(1)} %get-tuple-element.34), channel_id=1, source_target_pairs={{0,1},{1,0},{2,3},{3,2},{4,5},{5,4},{6,7},{7,6},{8,9},{9,8},{10,11... | collective-permute-start | bytes 491528 | tf_op jit(solution)/shard_map/ppermute | solution.py:234
  14.8 6.4 %collective-permute-start.6 = (bf16[64,640]{1,0:T(8,128)(2,1)S(1)}, bf16[64,640]{1,0:T(8,128)(2,1)S(1)}, u32[]{:S(2)}, u32[]{:S(2)}) collective-permute-start(bf16[64,640]{1,0:T(8,128)(2,1)S(1)} %get-tuple-element.28), channel_id=1, source_target_pairs={{0,12},{4,8},{8,4},{12,0},{1,13},{5,9},{9,5},{13,1},{2,14},{6,10},... | collective-permute-start | bytes 245768 | tf_op jit(solution)/shard_map/ppermute | solution.py:245
  14.9 6.4 %collective-permute-start.7 = (bf16[64,640]{1,0:T(8,128)(2,1)S(1)}, bf16[64,640]{1,0:T(8,128)(2,1)S(1)}, u32[]{:S(2)}, u32[]{:S(2)}) collective-permute-start(bf16[64,640]{1,0:T(8,128)(2,1)S(1)} %get-tuple-element.29), channel_id=1, source_target_pairs={{0,8},{4,12},{8,0},{12,4},{1,9},{5,13},{9,1},{13,5},{2,10},{6,14},... | collective-permute-start | bytes 245768 | tf_op jit(solution)/shard_map/ppermute | solution.py:247
  15.5 6.3 %collective-permute-start.5 = (bf16[128,640]{1,0:T(8,128)(2,1)S(1)}, bf16[128,640]{1,0:T(8,128)(2,1)S(1)}, u32[]{:S(2)}, u32[]{:S(2)}) collective-permute-start(bf16[128,640]{1,0:T(8,128)(2,1)S(1)} %get-tuple-element.27), channel_id=1, source_target_pairs={{0,4},{4,0},{8,12},{12,8},{1,5},{5,1},{9,13},{13,9},{2,6},{6,2},{1... | collective-permute-start | bytes 491528 | tf_op jit(solution)/shard_map/ppermute | solution.py:250
  18.3 9.3 %collective-permute-start.9 = (f32[64,640]{1,0:T(8,128)S(1)}, f32[64,640]{1,0:T(8,128)S(1)}, u32[]{:S(2)}, u32[]{:S(2)}) collective-permute-start(f32[64,640]{1,0:T(8,128)S(1)} %fold.1), channel_id=1, source_target_pairs={{0,2},{1,3},{2,0},{3,1},{4,6},{5,7},{6,4},{7,5},{8,10},{9,11},{10,... | collective-permute-start | bytes 491528 | tf_op jit(solution)/shard_map/ppermute | solution.py:233
  21.2 6.4 %collective-permute-start.11 = (f32[64,640]{1,0:T(8,128)S(1)}, f32[64,640]{1,0:T(8,128)S(1)}, u32[]{:S(2)}, u32[]{:S(2)}) collective-permute-start(f32[64,640]{1,0:T(8,128)S(1)} %get-tuple-element.36), channel_id=1, source_target_pairs={{0,12},{4,8},{8,4},{12,0},{1,13},{5,9},{9,5},{13,1},{2,14},{6,10},... | collective-permute-start | bytes 491528 | tf_op jit(solution)/shard_map/ppermute | solution.py:258
  21.2 6.3 %collective-permute-start.12 = (f32[64,640]{1,0:T(8,128)S(1)}, f32[64,640]{1,0:T(8,128)S(1)}, u32[]{:S(2)}, u32[]{:S(2)}) collective-permute-start(f32[64,640]{1,0:T(8,128)S(1)} %get-tuple-element.37), channel_id=1, source_target_pairs={{0,4},{4,0},{8,12},{12,8},{1,5},{5,1},{9,13},{13,9},{2,6},{6,2},{1... | collective-permute-start | bytes 491528 | tf_op jit(solution)/shard_map/ppermute | solution.py:259

commit v24 on v22

--- a/solution.py
+++ b/solution.py
@@ -106,9 +106,14 @@
     return jnp.concatenate([shifted(plane, -dy, 0).astype(BF16) for dy in (-1, 0, 1)], 0)
 
 
-def early_kernel(w_ref, f_ref, cot_ref, ce_ref, co_ref, own_ref, even_ref, odd_ref, moved_ref):
+def odd_kernel(w_ref, f_ref, odd_ref):
     side = 1 - 2 * lax.rem(lax.axis_index("sp"), 2)
-    for ref, dz in ((odd_ref, side), (even_ref, -side), (own_ref, 0)):
+    odd_ref[...] = moved_sum(conv_part(w_ref, f_ref[...], side))
+
+
+def early_kernel(after_ref, w_ref, f_ref, cot_ref, ce_ref, co_ref, own_ref, even_ref, moved_ref):
+    side = 1 - 2 * lax.rem(lax.axis_index("sp"), 2)
+    for ref, dz in ((even_ref, -side), (own_ref, 0)):
         ref[...] = moved_sum(conv_part(w_ref, f_ref[...], dz))
     for i, ref in enumerate((cot_ref, ce_ref, co_ref)):
         moved_ref[i] = moved_rows(ref[...])
@@ -248,11 +253,12 @@
         for k in range(2, nz - 1)
     ]
     g_even = lax.ppermute(to_even, "sp", even_pairs)
-    out_own, out_even, out_odd, moved = kernel_call(
+    (out_odd,) = kernel_call(odd_kernel, "odd", [of(blocks, F32)], [w2, f_all], weight=W_EARLY * work)
+    out_own, out_even, moved = kernel_call(
         early_kernel,
         "early",
-        [of(blocks, F32)] * 3 + [jax.ShapeDtypeStruct((3, 3 * blocks, plane), BF16)],
-        [w2, f_all, cot, cot_even, cot_odd],
+        [of(blocks, F32)] * 2 + [jax.ShapeDtypeStruct((3, 3 * blocks, plane), BF16)],
+        [g_odd, w2, f_all, cot, cot_even, cot_odd],
         weight=W_EARLY * work,
     )
     out_odd = lax.ppermute(out_odd, "sp", odd_pairs)

time: 29.3 us -> 29.4 us (level)
  starting transfers between devices: 15.1 us -> 13.9 us
  waiting for transfers between devices: 7.39 us -> 8.57 us
    ppermute x1, waiting for transfers between devices: 1.08 us -> 2.4 us  [per_device(): terms.append(lax.ppermute(near, 'ch', mixed(1)))]
    ppermute x1, starting transfers between devices: 0.07 us -> 1.24 us  [per_device(): out_odd = lax.ppermute(out_odd, 'sp', odd_pairs)]
    ppermute x1, waiting for transfers between devices: 1.06 us -> 0.01 us  [per_device(): out_odd = lax.ppermute(out_odd, 'sp', odd_pairs)]
    ppermute x1, starting transfers between devices: 2.48 us -> 1.55 us  [per_device(): terms.append(lax.ppermute(near, 'ch', mixed(1)))]
    ppermute x1, waiting for transfers between devices: 0.84 us -> 1.76 us  [per_device(): terms.append(lax.ppermute(both, 'ch', mixed(k)))]
    ppermute x1, starting transfers between devices: 1.03 us -> 0.22 us  [per_device(): g_even = lax.ppermute(to_even, 'sp', even_pairs)]
    ppermute x1, waiting for transfers between devices: 0.01 us -> 0.63 us  [per_device(): g_odd = lax.ppermute(to_odd, 'sp', odd_pairs)]
    ppermute x1, waiting for transfers between devices: 0.63 us -> 0.01 us  [per_device(): got = lax.ppermute(parts[k + 1], 'ch', mixed(1))]
  transfers between devices with their start and end apart: 13 -> 13, of which waited for: 5 -> 4; matrix products, arithmetic and copies ran while one was open for 0% -> 0% of each run, Pallas kernels for 17% -> 18%
where the time goes in v24:
time: 29.4 us; the launch traced here: 29.3 us
  starting transfers between devices  13.9 us (47%)
  waiting for transfers between devices  8.57 us (29%)
  Pallas kernels  6.07 us (21%)
  between operations  0.74 us (3%)
    pallas_call x9, Pallas kernels, kernel_call(): pl.pallas_call(body, out_shape=outs, in_specs=[SMEM if a.dtype == jnp.int...  6.07 us
    ppermute x3, starting transfers between devices, per_device(): pieces = [feat] + [lax.ppermute(feat, 'ch', mixed(k)) for k in range(1, nc)]  4.39 us
    ppermute x3, waiting for transfers between devices, per_device(): pieces = [feat] + [lax.ppermute(feat, 'ch', mixed(k)) for k in range(1, nc)]  3.77 us
    ppermute x1, starting transfers between devices, per_device(): cot_odd = lax.ppermute(cot, 'sp', odd_pairs)  2.44 us
    ppermute x1, waiting for transfers between devices, per_device(): terms.append(lax.ppermute(near, 'ch', mixed(1)))  2.4 us
    ppermute x1, waiting for transfers between devices, per_device(): terms.append(lax.ppermute(both, 'ch', mixed(k)))  1.76 us
    ppermute x1, starting transfers between devices, per_device(): terms.append(lax.ppermute(near, 'ch', mixed(1)))  1.55 us
    ppermute x1, starting transfers between devices, per_device(): got = lax.ppermute(parts[k + 1], 'ch', mixed(1))  1.31 us
  transfers between devices with their start and end apart: 13, of which 4 were waited for; matrix products, arithmetic and copies ran while one was open for 0% of the time, Pallas kernels for 18%

profile of v24, /device:TPU:0, one launch (start us, length us, event | category | flops | bytes accessed | tf_op | source)
XLA Modules:
  0.0 29.3 jit_solution(1303012159077587147)
XLA Ops:
  0.6 0.0 copy-start.1
  0.6 0.0 copy-start
  0.7 0.0 copy-start.2
  0.7 2.4 %collective-permute-start.1 = (bf16[64,640]{1,0:T(8,128)(2,1)}, bf16[64,640]{1,0:T(8,128)(2,1)S(1)}, u32[]{:S(2)}, u32[]{:S(2)}) collective-permute-start(bf16[64,640]{1,0:T(8,128)(2,1)} %bitcast.10), channel_id=1, source_target_pairs={{0,12},{4,8},{8,4},{12,0},{1,13},{5,9},{9,5},{13,1},{2,14},{6,10},... | collective-permute-start | bytes 245768 | tf_op jit(solution)/shard_map/ppermute | solution.py:220
  3.1 0.7 %collective-permute-start = (bf16[64,640]{1,0:T(8,128)(2,1)}, bf16[64,640]{1,0:T(8,128)(2,1)S(1)}, u32[]{:S(2)}, u32[]{:S(2)}) collective-permute-start(bf16[64,640]{1,0:T(8,128)(2,1)} %bitcast.11), channel_id=1, source_target_pairs={{0,4},{4,0},{8,12},{12,8},{1,5},{5,1},{9,13},{13,9},{2,6},{6,2},{1... | collective-permute-start | bytes 245768 | tf_op jit(solution)/shard_map/ppermute | solution.py:219
  3.8 0.0 copy-done.1
  3.8 3.6 %collective-permute-start.4 = (bf16[64,640]{1,0:T(8,128)(2,1)S(1)}, bf16[64,640]{1,0:T(8,128)(2,1)S(1)}, u32[]{:S(2)}, u32[]{:S(2)}) collective-permute-start(bf16[64,640]{1,0:T(8,128)(2,1)S(1)} %bitcast.6), channel_id=1, source_target_pairs={{0,3},{1,2},{2,1},{3,0},{4,7},{5,6},{6,5},{7,4},{8,11},{9,10},{10,... | collective-permute-start | bytes 245768 | tf_op jit(solution)/shard_map/ppermute | solution.py:223
  7.4 0.0 collective-permute-start.3
  7.4 0.8 %collective-permute-start.2 = (bf16[64,640]{1,0:T(8,128)(2,1)S(1)}, bf16[64,640]{1,0:T(8,128)(2,1)S(1)}, u32[]{:S(2)}, u32[]{:S(2)}) collective-permute-start(bf16[64,640]{1,0:T(8,128)(2,1)S(1)} %bitcast.8), channel_id=1, source_target_pairs={{0,1},{1,0},{2,3},{3,2},{4,5},{5,4},{6,7},{7,6},{8,9},{9,8},{10,11... | collective-permute-start | bytes 245768 | tf_op jit(solution)/shard_map/ppermute | solution.py:223
  8.2 0.0 collective-permute-done.1.odd_ref.near_ref.co_ref
  8.2 0.0 collective-permute-done.even_ref.ce_ref
  8.2 0.0 copy-done
  8.2 0.0 copy-done.2
  8.2 1.3 %input_grad.1 = (f32[64,640]{1,0:T(8,128)S(1)}, f32[64,640]{1,0:T(8,128)S(1)}, f32[64,640]{1,0:T(8,128)S(1)}, f32[64,640]{1,0:T(8,128)S(1)}, f32[8,128]{1,0:T(8,128)S(1)}) custom-call(f32[8,128]{1,0:T(8,128)S(1)} %begin.1.begin_ref, bf16[64,640]{1,0:T(8,128)(2,1)S(1)} %bitcast.12, bf16[64,640]{1,0:T(8,128)(2,1)S(1)} %collective-permute-done.even_ref.ce_ref, ...), custom_call_target="tpu_custom_call" | custom-call | flops 566231040 | tf_op jit(solution)/shard_map/input_grad/pallas_call | solution.py:185
  9.5 1.3 %collective-permute-start.8 = (f32[64,640]{1,0:T(8,128)S(1)}, f32[64,640]{1,0:T(8,128)S(1)}, u32[]{:S(2)}, u32[]{:S(2)}) collective-permute-start(f32[64,640]{1,0:T(8,128)S(1)} %get-tuple-element.33), channel_id=1, source_target_pairs={{0,1},{1,0},{2,3},{3,2},{4,5},{5,4},{6,7},{7,6},{8,9},{9,8},{10,11... | collective-permute-start | bytes 491528 | tf_op jit(solution)/shard_map/ppermute | solution.py:235
  10.8 0.0 collective-permute-done.4.refs_3_
  10.8 3.8 %collective-permute-done.3.refs_2_ = bf16[64,640]{1,0:T(8,128)(2,1)S(1)} collective-permute-done((bf16[64,640]{1,0:T(8,128)(2,1)S(1)}, bf16[64,640]{1,0:T(8,128)(2,1)S(1)}, u32[]{:S(2)}, u32[]{:S(2)}) %collective-permute-start.3) | collective-permute-done | bytes 81952 | tf_op jit(solution)/shard_map/ppermute | solution.py:223
  14.6 0.0 collective-permute-done.2.refs_1_
  14.6 0.1 gather.1
  14.7 0.1 collective-permute-start.5
  14.7 0.8 %collective-permute-start.7 = (bf16[64,640]{1,0:T(8,128)(2,1)S(1)}, bf16[64,640]{1,0:T(8,128)(2,1)S(1)}, u32[]{:S(2)}, u32[]{:S(2)}) collective-permute-start(bf16[64,640]{1,0:T(8,128)(2,1)S(1)} %get-tuple-element.29), channel_id=1, source_target_pairs={{0,8},{4,12},{8,0},{12,4},{1,9},{5,13},{9,1},{13,5},{2,10},{6,14},... | collective-permute-start | bytes 245768 | tf_op jit(solution)/shard_map/ppermute | solution.py:252
  15.5 0.6 %odd.1 = f32[64,640]{1,0:T(8,128)S(1)} custom-call(bf16[1728,256]{1,0:T(8,128)(2,1)S(1)} %bitcast.4, bf16[256,640]{1,0:T(8,128)(2,1)S(1)} %get-tuple-element.26.f_ref), custom_call_target="tpu_custom_call" | custom-call | flops 1132462080 | tf_op jit(solution)/shard_map/odd/pallas_call | solution.py:185
  16.1 1.2 %collective-permute-start.11 = (f32[64,640]{1,0:T(8,128)S(1)}, f32[64,640]{1,0:T(8,128)S(1)}, u32[]{:S(2)}, u32[]{:S(2)}) collective-permute-start(f32[64,640]{1,0:T(8,128)S(1)} %odd.1), channel_id=1, source_target_pairs={{0,12},{4,8},{8,4},{12,0},{1,13},{5,9},{9,5},{13,1},{2,14},{6,10},... | collective-permute-start | bytes 491528 | tf_op jit(solution)/shard_map/ppermute | solution.py:264
  17.4 0.2 collective-permute-start.6
  17.6 0.0 collective-permute-done.8.got_ref
  17.6 1.1 %collective-permute-start.9 = (f32[64,640]{1,0:T(8,128)S(1)}, f32[64,640]{1,0:T(8,128)S(1)}, u32[]{:S(2)}, u32[]{:S(2)}) collective-permute-start(f32[64,640]{1,0:T(8,128)S(1)} %fold.1), channel_id=1, source_target_pairs={{0,2},{1,3},{2,0},{3,1},{4,6},{5,7},{6,4},{7,5},{8,10},{9,11},{10,... | collective-permute-start | bytes 491528 | tf_op jit(solution)/shard_map/ppermute | solution.py:237
  18.7 0.6 %collective-permute-done.5.after_ref.go_ref = bf16[64,640]{1,0:T(8,128)(2,1)S(1)} collective-permute-done((bf16[64,640]{1,0:T(8,128)(2,1)S(1)}, bf16[64,640]{1,0:T(8,128)(2,1)S(1)}, u32[]{:S(2)}, u32[]{:S(2)}) %collective-permute-start.5) | collective-permute-done | bytes 81952 | tf_op jit(solution)/shard_map/ppermute | solution.py:250
  19.4 1.6 %collective-permute-start.10 = (f32[64,640]{1,0:T(8,128)S(1)}, f32[64,640]{1,0:T(8,128)S(1)}, u32[]{:S(2)}, u32[]{:S(2)}) collective-permute-start(f32[64,640]{1,0:T(8,128)S(1)} %get-tuple-element.35), channel_id=1, source_target_pairs={{0,1},{1,0},{2,3},{3,2},{4,5},{5,4},{6,7},{7,6},{8,9},{9,8},{10,11... | collective-permute-start | bytes 491528 | tf_op jit(solution)/shard_map/ppermute | solution.py:239
  20.9 1.0 %early.1 = (f32[64,640]{1,0:T(8,128)S(1)}, f32[64,640]{1,0:T(8,128)S(1)}, bf16[3,192,640]{2,1,0:T(8,128)(2,1)S(1)}) custom-call(bf16[64,640]{1,0:T(8,128)(2,1)S(1)} %collective-permute-done.5.after_ref.go_ref, bf16[1728,256]{1,0:T(8,128)(2,1)S(1)} %bitcast.5, bf16[256,640]{1,0:T(8,128)(2,1)S(1)} %get-tuple-element.26.f_ref, bf16[64,640]{1,0:T(8,128)(2,1)S(1)} %bitcast.14, ...), custom_call_target="tpu_custom_call" | custom-call | flops 1132462080 | tf_op jit(solution)/shard_map/early/pallas_call | solution.py:185
  22.0 0.0 collective-permute-done.7.refs_0_
  22.0 0.1 collective-permute-start.12
  22.1 0.0 collective-permute-done.6.ge_ref
  22.1 2.3 %weight_grad.1 = (f32[27,64,64]{2,1,0:T(8,128)}, f32[8,128]{1,0:T(8,128)S(1)}) custom-call(bf16[3,192,640]{2,1,0:T(8,128)(2,1)S(1)} %get-tuple-element.27.moved_ref, bf16[256,640]{1,0:T(8,128)(2,1)S(1)} %get-tuple-element.26.f_ref, bf16[128,640]{1,0:T(8,128)(2,1)S(1)} %collective-permute-done.6.ge_ref, ...), custom_call_target="tpu_custom_call" | custom-call | tf_op jit(solution)/shard_map/weight_grad/pallas_call | solution.py:185
  24.3 2.4 %collective-permute-done.10.refs_3_.refs_2_ = f32[64,640]{1,0:T(8,128)S(1)} collective-permute-done((f32[64,640]{1,0:T(8,128)S(1)}, f32[64,640]{1,0:T(8,128)S(1)}, u32[]{:S(2)}, u32[]{:S(2)}) %collective-permute-start.10) | collective-permute-done | bytes 163872 | tf_op jit(solution)/shard_map/ppermute | solution.py:239
  26.7 1.8 %collective-permute-done.9.refs_2_.refs_1_ = f32[64,640]{1,0:T(8,128)S(1)} collective-permute-done((f32[64,640]{1,0:T(8,128)S(1)}, f32[64,640]{1,0:T(8,128)S(1)}, u32[]{:S(2)}, u32[]{:S(2)}) %collective-permute-start.9) | collective-permute-done | bytes 163872 | tf_op jit(solution)/shard_map/ppermute | solution.py:237
  28.5 0.0 collective-permute-done.11.odd_ref
  28.5 0.0 collective-permute-done.12.even_ref
  28.5 0.8 %total.1 = (f32[64,1,640]{2,1,0:T(1,128)}, f32[64,1,640]{2,1,0:T(1,128)}) custom-call(f32[8,128]{1,0:T(8,128)S(1)} %hold.1.token_ref, f32[64,640]{1,0:T(8,128)S(1)} %get-tuple-element.36.own_ref, f32[64,640]{1,0:T(8,128)S(1)} %collective-permute-done.11.odd_ref, f32[64,640]{1,0:T(8,128)S(1)} %collective-permute-done.12.even_ref, ...), custom_call_target="tpu_custom_call" | custom-call | tf_op jit(solution)/shard_map/total/pallas_call | solution.py:185
  (3 shorter events, 0.0 us)
Async XLA Ops:
  0.6 3.2 %copy-start.1 = (bf16[64,1,640]{2,0,1:T(8,128)(2,1)S(1)}, bf16[64,1,640]{2,0,1:T(8,128)(2,1)}, u32[]{:S(2)}) copy-start(bf16[64,1,640]{2,0,1:T(8,128)(2,1)} %param.3) | copy-start | bytes 245764
  0.6 7.5 %copy-start = (bf16[27,64,256]{2,1,0:T(8,128)(2,1)S(1)}, bf16[27,64,256]{2,1,0:T(8,128)(2,1)}, u32[]{:S(2)}) copy-start(bf16[27,64,256]{2,1,0:T(8,128)(2,1)} %param.4) | copy-start | bytes 2654212
  0.7 7.5 %copy-start.2 = (bf16[64,1,640]{2,0,1:T(8,128)(2,1)S(1)}, bf16[64,1,640]{2,0,1:T(8,128)(2,1)}, u32[]{:S(2)}) copy-start(bf16[64,1,640]{2,0,1:T(8,128)(2,1)} %param.5) | copy-start | bytes 245764
  0.7 7.5 %collective-permute-start.1 = (bf16[64,640]{1,0:T(8,128)(2,1)}, bf16[64,640]{1,0:T(8,128)(2,1)S(1)}, u32[]{:S(2)}, u32[]{:S(2)}) collective-permute-start(bf16[64,640]{1,0:T(8,128)(2,1)} %bitcast.10), channel_id=1, source_target_pairs={{0,12},{4,8},{8,4},{12,0},{1,13},{5,9},{9,5},{13,1},{2,14},{6,10},... | collective-permute-start | bytes 245768 | tf_op jit(solution)/shard_map/ppermute | solution.py:220
  3.1 5.1 %collective-permute-start = (bf16[64,640]{1,0:T(8,128)(2,1)}, bf16[64,640]{1,0:T(8,128)(2,1)S(1)}, u32[]{:S(2)}, u32[]{:S(2)}) collective-permute-start(bf16[64,640]{1,0:T(8,128)(2,1)} %bitcast.11), channel_id=1, source_target_pairs={{0,4},{4,0},{8,12},{12,8},{1,5},{5,1},{9,13},{13,9},{2,6},{6,2},{1... | collective-permute-start | bytes 245768 | tf_op jit(solution)/shard_map/ppermute | solution.py:219
  3.8 7.0 %collective-permute-start.4 = (bf16[64,640]{1,0:T(8,128)(2,1)S(1)}, bf16[64,640]{1,0:T(8,128)(2,1)S(1)}, u32[]{:S(2)}, u32[]{:S(2)}) collective-permute-start(bf16[64,640]{1,0:T(8,128)(2,1)S(1)} %bitcast.6), channel_id=1, source_target_pairs={{0,3},{1,2},{2,1},{3,0},{4,7},{5,6},{6,5},{7,4},{8,11},{9,10},{10,... | collective-permute-start | bytes 245768 | tf_op jit(solution)/shard_map/ppermute | solution.py:223
  7.4 7.2 %collective-permute-start.3 = (bf16[64,640]{1,0:T(8,128)(2,1)S(1)}, bf16[64,640]{1,0:T(8,128)(2,1)S(1)}, u32[]{:S(2)}, u32[]{:S(2)}) collective-permute-start(bf16[64,640]{1,0:T(8,128)(2,1)S(1)} %bitcast.7), channel_id=1, source_target_pairs={{0,2},{1,3},{2,0},{3,1},{4,6},{5,7},{6,4},{7,5},{8,10},{9,11},{10,... | collective-permute-start | bytes 245768 | tf_op jit(solution)/shard_map/ppermute | solution.py:223
  7.4 7.2 %collective-permute-start.2 = (bf16[64,640]{1,0:T(8,128)(2,1)S(1)}, bf16[64,640]{1,0:T(8,128)(2,1)S(1)}, u32[]{:S(2)}, u32[]{:S(2)}) collective-permute-start(bf16[64,640]{1,0:T(8,128)(2,1)S(1)} %bitcast.8), channel_id=1, source_target_pairs={{0,1},{1,0},{2,3},{3,2},{4,5},{5,4},{6,7},{7,6},{8,9},{9,8},{10,11... | collective-permute-start | bytes 245768 | tf_op jit(solution)/shard_map/ppermute | solution.py:223
  9.5 8.1 %collective-permute-start.8 = (f32[64,640]{1,0:T(8,128)S(1)}, f32[64,640]{1,0:T(8,128)S(1)}, u32[]{:S(2)}, u32[]{:S(2)}) collective-permute-start(f32[64,640]{1,0:T(8,128)S(1)} %get-tuple-element.33), channel_id=1, source_target_pairs={{0,1},{1,0},{2,3},{3,2},{4,5},{5,4},{6,7},{7,6},{8,9},{9,8},{10,11... | collective-permute-start | bytes 491528 | tf_op jit(solution)/shard_map/ppermute | solution.py:235
  14.7 4.7 %collective-permute-start.5 = (bf16[64,640]{1,0:T(8,128)(2,1)S(1)}, bf16[64,640]{1,0:T(8,128)(2,1)S(1)}, u32[]{:S(2)}, u32[]{:S(2)}) collective-permute-start(bf16[64,640]{1,0:T(8,128)(2,1)S(1)} %get-tuple-element.25), channel_id=1, source_target_pairs={{0,12},{4,8},{8,4},{12,0},{1,13},{5,9},{9,5},{13,1},{2,14},{6,10},... | collective-permute-start | bytes 245768 | tf_op jit(solution)/shard_map/ppermute | solution.py:250
  14.7 7.2 %collective-permute-start.7 = (bf16[64,640]{1,0:T(8,128)(2,1)S(1)}, bf16[64,640]{1,0:T(8,128)(2,1)S(1)}, u32[]{:S(2)}, u32[]{:S(2)}) collective-permute-start(bf16[64,640]{1,0:T(8,128)(2,1)S(1)} %get-tuple-element.29), channel_id=1, source_target_pairs={{0,8},{4,12},{8,0},{12,4},{1,9},{5,13},{9,1},{13,5},{2,10},{6,14},... | collective-permute-start | bytes 245768 | tf_op jit(solution)/shard_map/ppermute | solution.py:252
  16.1 12.4 %collective-permute-start.11 = (f32[64,640]{1,0:T(8,128)S(1)}, f32[64,640]{1,0:T(8,128)S(1)}, u32[]{:S(2)}, u32[]{:S(2)}) collective-permute-start(f32[64,640]{1,0:T(8,128)S(1)} %odd.1), channel_id=1, source_target_pairs={{0,12},{4,8},{8,4},{12,0},{1,13},{5,9},{9,5},{13,1},{2,14},{6,10},... | collective-permute-start | bytes 491528 | tf_op jit(solution)/shard_map/ppermute | solution.py:264
  17.4 4.7 %collective-permute-start.6 = (bf16[128,640]{1,0:T(8,128)(2,1)S(1)}, bf16[128,640]{1,0:T(8,128)(2,1)S(1)}, u32[]{:S(2)}, u32[]{:S(2)}) collective-permute-start(bf16[128,640]{1,0:T(8,128)(2,1)S(1)} %get-tuple-element.28), channel_id=1, source_target_pairs={{0,4},{4,0},{8,12},{12,8},{1,5},{5,1},{9,13},{13,9},{2,6},{6,2},{1... | collective-permute-start | bytes 491528 | tf_op jit(solution)/shard_map/ppermute | solution.py:255
  17.6 10.9 %collective-permute-start.9 = (f32[64,640]{1,0:T(8,128)S(1)}, f32[64,640]{1,0:T(8,128)S(1)}, u32[]{:S(2)}, u32[]{:S(2)}) collective-permute-start(f32[64,640]{1,0:T(8,128)S(1)} %fold.1), channel_id=1, source_target_pairs={{0,2},{1,3},{2,0},{3,1},{4,6},{5,7},{6,4},{7,5},{8,10},{9,11},{10,... | collective-permute-start | bytes 491528 | tf_op jit(solution)/shard_map/ppermute | solution.py:237
  19.4 7.4 %collective-permute-start.10 = (f32[64,640]{1,0:T(8,128)S(1)}, f32[64,640]{1,0:T(8,128)S(1)}, u32[]{:S(2)}, u32[]{:S(2)}) collective-permute-start(f32[64,640]{1,0:T(8,128)S(1)} %get-tuple-element.35), channel_id=1, source_target_pairs={{0,1},{1,0},{2,3},{3,2},{4,5},{5,4},{6,7},{7,6},{8,9},{9,8},{10,11... | collective-permute-start | bytes 491528 | tf_op jit(solution)/shard_map/ppermute | solution.py:239
  22.0 6.5 %collective-permute-start.12 = (f32[64,640]{1,0:T(8,128)S(1)}, f32[64,640]{1,0:T(8,128)S(1)}, u32[]{:S(2)}, u32[]{:S(2)}) collective-permute-start(f32[64,640]{1,0:T(8,128)S(1)} %get-tuple-element.37), channel_id=1, source_target_pairs={{0,4},{4,0},{8,12},{12,8},{1,5},{5,1},{9,13},{13,9},{2,6},{6,2},{1... | collective-permute-start | bytes 491528 | tf_op jit(solution)/shard_map/ppermute | solution.py:265

commit v25 on v24

--- a/solution.py
+++ b/solution.py
@@ -235,8 +235,7 @@
         got = lax.ppermute(parts[k + 1], "ch", mixed(1))
         (both,) = kernel_call(fold_kernel, "fold", [of(blocks, F32)], [parts[k], got], weight=W_FOLD * work)
         terms.append(lax.ppermute(both, "ch", mixed(k)))
-    near, both = lax.optimization_barrier((parts[1], both))
-    terms.append(lax.ppermute(near, "ch", mixed(1)))
+    terms.append(lax.ppermute(parts[1], "ch", mixed(1)))
 
     far_rows = cols if nz == 4 else cols + blocks
     f_all, to_even, to_odd, *packs = kernel_call(

time: 29.4 us -> 29.9 us (1.017)
  waiting for transfers between devices: 8.57 us -> 10.6 us
  starting transfers between devices: 13.9 us -> 12.3 us
    ppermute x1, waiting for transfers between devices: 1.76 us -> 5.66 us  [per_device(): terms.append(lax.ppermute(both, 'ch', mixed(k)))]
    ppermute x1, waiting for transfers between devices: 2.4 us -> 0.01 us  [per_device(): terms.append(lax.ppermute(parts[1], 'ch', mixed(1)))]
    ppermute x1, waiting for transfers between devices: 0.63 us -> 1.48 us  [per_device(): g_odd = lax.ppermute(to_odd, 'sp', odd_pairs)]
    ppermute x3, waiting for transfers between devices: 3.77 us -> 2.99 us  [per_device(): pieces = [feat] + [lax.ppermute(feat, 'ch', mixed(k)) for k in range(1, nc)]]
    ppermute x1, starting transfers between devices: 1.55 us -> 0.78 us  [per_device(): terms.append(lax.ppermute(parts[1], 'ch', mixed(1)))]
    ppermute x1, starting transfers between devices: 1.11 us -> 0.53 us  [per_device(): terms.append(lax.ppermute(both, 'ch', mixed(k)))]
    ppermute x1, waiting for transfers between devices: 0.01 us -> 0.48 us  [per_device(): got = lax.ppermute(parts[k + 1], 'ch', mixed(1))]
where the time goes in v25:
time: 29.9 us; the launch traced here: 29.8 us
  starting transfers between devices  12.3 us (41%)
  waiting for transfers between devices  10.6 us (35%)
  Pallas kernels  6.07 us (20%)
  between operations  0.74 us (2%)
    pallas_call x9, Pallas kernels, kernel_call(): pl.pallas_call(body, out_shape=outs, in_specs=[SMEM if a.dtype == jnp.int...  6.07 us
    ppermute x1, waiting for transfers between devices, per_device(): terms.append(lax.ppermute(both, 'ch', mixed(k)))  5.66 us
    ppermute x3, starting transfers between devices, per_device(): pieces = [feat] + [lax.ppermute(feat, 'ch', mixed(k)) for k in range(1, nc)]  4.39 us
    ppermute x3, waiting for transfers between devices, per_device(): pieces = [feat] + [lax.ppermute(feat, 'ch', mixed(k)) for k in range(1, nc)]  2.99 us
    ppermute x1, starting transfers between devices, per_device(): cot_odd = lax.ppermute(cot, 'sp', odd_pairs)  2.44 us
    ppermute x1, waiting for transfers between devices, per_device(): g_odd = lax.ppermute(to_odd, 'sp', odd_pairs)  1.48 us
    ppermute x1, starting transfers between devices, per_device(): got = lax.ppermute(parts[k + 1], 'ch', mixed(1))  1.31 us
    ppermute x1, starting transfers between devices, per_device(): out_odd = lax.ppermute(out_odd, 'sp', odd_pairs)  1.24 us
  transfers between devices with their start and end apart: 13, of which 4 were waited for; matrix products, arithmetic and copies ran while one was open for 0% of the time, Pallas kernels for 18%

profile of v25, /device:TPU:0, one launch (start us, length us, event | category | flops | bytes accessed | tf_op | source)
XLA Modules:
  0.0 29.8 jit_solution(17543385748943817233)
XLA Ops:
  0.6 0.0 copy-start.1
  0.6 0.0 copy-start
  0.7 0.0 copy-start.2
  0.7 2.4 %collective-permute-start.1 = (bf16[64,640]{1,0:T(8,128)(2,1)}, bf16[64,640]{1,0:T(8,128)(2,1)S(1)}, u32[]{:S(2)}, u32[]{:S(2)}) collective-permute-start(bf16[64,640]{1,0:T(8,128)(2,1)} %bitcast.10), channel_id=1, source_target_pairs={{0,12},{4,8},{8,4},{12,0},{1,13},{5,9},{9,5},{13,1},{2,14},{6,10},... | collective-permute-start | bytes 245768 | tf_op jit(solution)/shard_map/ppermute | solution.py:220
  3.1 0.7 %collective-permute-start = (bf16[64,640]{1,0:T(8,128)(2,1)}, bf16[64,640]{1,0:T(8,128)(2,1)S(1)}, u32[]{:S(2)}, u32[]{:S(2)}) collective-permute-start(bf16[64,640]{1,0:T(8,128)(2,1)} %bitcast.11), channel_id=1, source_target_pairs={{0,4},{4,0},{8,12},{12,8},{1,5},{5,1},{9,13},{13,9},{2,6},{6,2},{1... | collective-permute-start | bytes 245768 | tf_op jit(solution)/shard_map/ppermute | solution.py:219
  3.8 0.0 copy-done.1
  3.8 3.6 %collective-permute-start.4 = (bf16[64,640]{1,0:T(8,128)(2,1)S(1)}, bf16[64,640]{1,0:T(8,128)(2,1)S(1)}, u32[]{:S(2)}, u32[]{:S(2)}) collective-permute-start(bf16[64,640]{1,0:T(8,128)(2,1)S(1)} %bitcast.6), channel_id=1, source_target_pairs={{0,3},{1,2},{2,1},{3,0},{4,7},{5,6},{6,5},{7,4},{8,11},{9,10},{10,... | collective-permute-start | bytes 245768 | tf_op jit(solution)/shard_map/ppermute | solution.py:223
  7.4 0.0 collective-permute-start.3
  7.4 0.8 %collective-permute-start.2 = (bf16[64,640]{1,0:T(8,128)(2,1)S(1)}, bf16[64,640]{1,0:T(8,128)(2,1)S(1)}, u32[]{:S(2)}, u32[]{:S(2)}) collective-permute-start(bf16[64,640]{1,0:T(8,128)(2,1)S(1)} %bitcast.8), channel_id=1, source_target_pairs={{0,1},{1,0},{2,3},{3,2},{4,5},{5,4},{6,7},{7,6},{8,9},{9,8},{10,11... | collective-permute-start | bytes 245768 | tf_op jit(solution)/shard_map/ppermute | solution.py:223
  8.2 0.0 collective-permute-done.1.odd_ref.near_ref.co_ref
  8.2 0.0 collective-permute-done.even_ref.ce_ref
  8.2 0.0 copy-done
  8.2 0.0 copy-done.2
  8.2 1.3 %input_grad.1 = (f32[64,640]{1,0:T(8,128)S(1)}, f32[64,640]{1,0:T(8,128)S(1)}, f32[64,640]{1,0:T(8,128)S(1)}, f32[64,640]{1,0:T(8,128)S(1)}, f32[8,128]{1,0:T(8,128)S(1)}) custom-call(f32[8,128]{1,0:T(8,128)S(1)} %begin.1.begin_ref, bf16[64,640]{1,0:T(8,128)(2,1)S(1)} %bitcast.12, bf16[64,640]{1,0:T(8,128)(2,1)S(1)} %collective-permute-done.even_ref.ce_ref, ...), custom_call_target="tpu_custom_call" | custom-call | flops 566231040 | tf_op jit(solution)/shard_map/input_grad/pallas_call | solution.py:185
  9.5 1.3 %collective-permute-start.8 = (f32[64,640]{1,0:T(8,128)S(1)}, f32[64,640]{1,0:T(8,128)S(1)}, u32[]{:S(2)}, u32[]{:S(2)}) collective-permute-start(f32[64,640]{1,0:T(8,128)S(1)} %get-tuple-element.32), channel_id=1, source_target_pairs={{0,1},{1,0},{2,3},{3,2},{4,5},{5,4},{6,7},{7,6},{8,9},{9,8},{10,11... | collective-permute-start | bytes 491528 | tf_op jit(solution)/shard_map/ppermute | solution.py:235
  10.8 0.8 %collective-permute-start.10 = (f32[64,640]{1,0:T(8,128)S(1)}, f32[64,640]{1,0:T(8,128)S(1)}, u32[]{:S(2)}, u32[]{:S(2)}) collective-permute-start(f32[64,640]{1,0:T(8,128)S(1)} %get-tuple-element.33), channel_id=1, source_target_pairs={{0,1},{1,0},{2,3},{3,2},{4,5},{5,4},{6,7},{7,6},{8,9},{9,8},{10,11... | collective-permute-start | bytes 491528 | tf_op jit(solution)/shard_map/ppermute | solution.py:238
  11.6 0.0 collective-permute-done.4.refs_3_
  11.6 3.0 %collective-permute-done.3.refs_2_ = bf16[64,640]{1,0:T(8,128)(2,1)S(1)} collective-permute-done((bf16[64,640]{1,0:T(8,128)(2,1)S(1)}, bf16[64,640]{1,0:T(8,128)(2,1)S(1)}, u32[]{:S(2)}, u32[]{:S(2)}) %collective-permute-start.3) | collective-permute-done | bytes 81952 | tf_op jit(solution)/shard_map/ppermute | solution.py:223
  14.6 0.0 collective-permute-done.2.refs_1_
  14.6 0.1 gather.1
  14.7 0.1 collective-permute-start.5
  14.7 0.8 %collective-permute-start.7 = (bf16[64,640]{1,0:T(8,128)(2,1)S(1)}, bf16[64,640]{1,0:T(8,128)(2,1)S(1)}, u32[]{:S(2)}, u32[]{:S(2)}) collective-permute-start(bf16[64,640]{1,0:T(8,128)(2,1)S(1)} %get-tuple-element.28), channel_id=1, source_target_pairs={{0,8},{4,12},{8,0},{12,4},{1,9},{5,13},{9,1},{13,5},{2,10},{6,14},... | collective-permute-start | bytes 245768 | tf_op jit(solution)/shard_map/ppermute | solution.py:251
  15.5 0.6 %odd.1 = f32[64,640]{1,0:T(8,128)S(1)} custom-call(bf16[1728,256]{1,0:T(8,128)(2,1)S(1)} %bitcast.4, bf16[256,640]{1,0:T(8,128)(2,1)S(1)} %get-tuple-element.25.f_ref), custom_call_target="tpu_custom_call" | custom-call | flops 1132462080 | tf_op jit(solution)/shard_map/odd/pallas_call | solution.py:185
  16.1 1.2 %collective-permute-start.11 = (f32[64,640]{1,0:T(8,128)S(1)}, f32[64,640]{1,0:T(8,128)S(1)}, u32[]{:S(2)}, u32[]{:S(2)}) collective-permute-start(f32[64,640]{1,0:T(8,128)S(1)} %odd.1), channel_id=1, source_target_pairs={{0,12},{4,8},{8,4},{12,0},{1,13},{5,9},{9,5},{13,1},{2,14},{6,10},... | collective-permute-start | bytes 491528 | tf_op jit(solution)/shard_map/ppermute | solution.py:263
  17.4 0.5 %collective-permute-done.8.got_ref = f32[64,640]{1,0:T(8,128)S(1)} collective-permute-done((f32[64,640]{1,0:T(8,128)S(1)}, f32[64,640]{1,0:T(8,128)S(1)}, u32[]{:S(2)}, u32[]{:S(2)}) %collective-permute-start.8) | collective-permute-done | bytes 163872 | tf_op jit(solution)/shard_map/ppermute | solution.py:235
  17.9 0.0 collective-permute-start.6
  17.9 1.5 %collective-permute-done.5.after_ref.go_ref = bf16[64,640]{1,0:T(8,128)(2,1)S(1)} collective-permute-done((bf16[64,640]{1,0:T(8,128)(2,1)S(1)}, bf16[64,640]{1,0:T(8,128)(2,1)S(1)}, u32[]{:S(2)}, u32[]{:S(2)}) %collective-permute-start.5) | collective-permute-done | bytes 81952 | tf_op jit(solution)/shard_map/ppermute | solution.py:249
  19.4 0.5 %collective-permute-start.9 = (f32[64,640]{1,0:T(8,128)S(1)}, f32[64,640]{1,0:T(8,128)S(1)}, u32[]{:S(2)}, u32[]{:S(2)}) collective-permute-start(f32[64,640]{1,0:T(8,128)S(1)} %fold.1), channel_id=1, source_target_pairs={{0,2},{1,3},{2,0},{3,1},{4,6},{5,7},{6,4},{7,5},{8,10},{9,11},{10,... | collective-permute-start | bytes 491528 | tf_op jit(solution)/shard_map/ppermute | solution.py:237
  19.9 1.0 %early.1 = (f32[64,640]{1,0:T(8,128)S(1)}, f32[64,640]{1,0:T(8,128)S(1)}, bf16[3,192,640]{2,1,0:T(8,128)(2,1)S(1)}) custom-call(bf16[64,640]{1,0:T(8,128)(2,1)S(1)} %collective-permute-done.5.after_ref.go_ref, bf16[1728,256]{1,0:T(8,128)(2,1)S(1)} %bitcast.5, bf16[256,640]{1,0:T(8,128)(2,1)S(1)} %get-tuple-element.25.f_ref, bf16[64,640]{1,0:T(8,128)(2,1)S(1)} %bitcast.14, ...), custom_call_target="tpu_custom_call" | custom-call | flops 1132462080 | tf_op jit(solution)/shard_map/early/pallas_call | solution.py:185
  20.9 0.0 collective-permute-done.7.refs_0_
  21.0 0.1 collective-permute-start.12
  21.0 0.0 collective-permute-done.6.ge_ref
  21.0 2.3 %weight_grad.1 = (f32[27,64,64]{2,1,0:T(8,128)}, f32[8,128]{1,0:T(8,128)S(1)}) custom-call(bf16[3,192,640]{2,1,0:T(8,128)(2,1)S(1)} %get-tuple-element.26.moved_ref, bf16[256,640]{1,0:T(8,128)(2,1)S(1)} %get-tuple-element.25.f_ref, bf16[128,640]{1,0:T(8,128)(2,1)S(1)} %collective-permute-done.6.ge_ref, ...), custom_call_target="tpu_custom_call" | custom-call | tf_op jit(solution)/shard_map/weight_grad/pallas_call | solution.py:185
  23.3 0.0 collective-permute-done.10.refs_3_.refs_2_
  23.3 5.7 %collective-permute-done.9.refs_2_.refs_1_ = f32[64,640]{1,0:T(8,128)S(1)} collective-permute-done((f32[64,640]{1,0:T(8,128)S(1)}, f32[64,640]{1,0:T(8,128)S(1)}, u32[]{:S(2)}, u32[]{:S(2)}) %collective-permute-start.9) | collective-permute-done | bytes 163872 | tf_op jit(solution)/shard_map/ppermute | solution.py:237
  29.0 0.0 collective-permute-done.11.odd_ref
  29.0 0.0 collective-permute-done.12.even_ref
  29.0 0.8 %total.1 = (f32[64,1,640]{2,1,0:T(1,128)}, f32[64,1,640]{2,1,0:T(1,128)}) custom-call(f32[8,128]{1,0:T(8,128)S(1)} %hold.1.token_ref, f32[64,640]{1,0:T(8,128)S(1)} %get-tuple-element.34.own_ref, f32[64,640]{1,0:T(8,128)S(1)} %collective-permute-done.11.odd_ref, f32[64,640]{1,0:T(8,128)S(1)} %collective-permute-done.12.even_ref, ...), custom_call_target="tpu_custom_call" | custom-call | tf_op jit(solution)/shard_map/total/pallas_call | solution.py:185
  (3 shorter events, 0.0 us)
Async XLA Ops:
  0.6 3.2 %copy-start.1 = (bf16[64,1,640]{2,0,1:T(8,128)(2,1)S(1)}, bf16[64,1,640]{2,0,1:T(8,128)(2,1)}, u32[]{:S(2)}) copy-start(bf16[64,1,640]{2,0,1:T(8,128)(2,1)} %param.3) | copy-start | bytes 245764
  0.6 7.5 %copy-start = (bf16[27,64,256]{2,1,0:T(8,128)(2,1)S(1)}, bf16[27,64,256]{2,1,0:T(8,128)(2,1)}, u32[]{:S(2)}) copy-start(bf16[27,64,256]{2,1,0:T(8,128)(2,1)} %param.4) | copy-start | bytes 2654212
  0.7 7.5 %copy-start.2 = (bf16[64,1,640]{2,0,1:T(8,128)(2,1)S(1)}, bf16[64,1,640]{2,0,1:T(8,128)(2,1)}, u32[]{:S(2)}) copy-start(bf16[64,1,640]{2,0,1:T(8,128)(2,1)} %param.5) | copy-start | bytes 245764
  0.7 7.5 %collective-permute-start.1 = (bf16[64,640]{1,0:T(8,128)(2,1)}, bf16[64,640]{1,0:T(8,128)(2,1)S(1)}, u32[]{:S(2)}, u32[]{:S(2)}) collective-permute-start(bf16[64,640]{1,0:T(8,128)(2,1)} %bitcast.10), channel_id=1, source_target_pairs={{0,12},{4,8},{8,4},{12,0},{1,13},{5,9},{9,5},{13,1},{2,14},{6,10},... | collective-permute-start | bytes 245768 | tf_op jit(solution)/shard_map/ppermute | solution.py:220
  3.1 5.1 %collective-permute-start = (bf16[64,640]{1,0:T(8,128)(2,1)}, bf16[64,640]{1,0:T(8,128)(2,1)S(1)}, u32[]{:S(2)}, u32[]{:S(2)}) collective-permute-start(bf16[64,640]{1,0:T(8,128)(2,1)} %bitcast.11), channel_id=1, source_target_pairs={{0,4},{4,0},{8,12},{12,8},{1,5},{5,1},{9,13},{13,9},{2,6},{6,2},{1... | collective-permute-start | bytes 245768 | tf_op jit(solution)/shard_map/ppermute | solution.py:219
  3.8 7.8 %collective-permute-start.4 = (bf16[64,640]{1,0:T(8,128)(2,1)S(1)}, bf16[64,640]{1,0:T(8,128)(2,1)S(1)}, u32[]{:S(2)}, u32[]{:S(2)}) collective-permute-start(bf16[64,640]{1,0:T(8,128)(2,1)S(1)} %bitcast.6), channel_id=1, source_target_pairs={{0,3},{1,2},{2,1},{3,0},{4,7},{5,6},{6,5},{7,4},{8,11},{9,10},{10,... | collective-permute-start | bytes 245768 | tf_op jit(solution)/shard_map/ppermute | solution.py:223
  7.4 7.2 %collective-permute-start.3 = (bf16[64,640]{1,0:T(8,128)(2,1)S(1)}, bf16[64,640]{1,0:T(8,128)(2,1)S(1)}, u32[]{:S(2)}, u32[]{:S(2)}) collective-permute-start(bf16[64,640]{1,0:T(8,128)(2,1)S(1)} %bitcast.7), channel_id=1, source_target_pairs={{0,2},{1,3},{2,0},{3,1},{4,6},{5,7},{6,4},{7,5},{8,10},{9,11},{10,... | collective-permute-start | bytes 245768 | tf_op jit(solution)/shard_map/ppermute | solution.py:223
  7.4 7.2 %collective-permute-start.2 = (bf16[64,640]{1,0:T(8,128)(2,1)S(1)}, bf16[64,640]{1,0:T(8,128)(2,1)S(1)}, u32[]{:S(2)}, u32[]{:S(2)}) collective-permute-start(bf16[64,640]{1,0:T(8,128)(2,1)S(1)} %bitcast.8), channel_id=1, source_target_pairs={{0,1},{1,0},{2,3},{3,2},{4,5},{5,4},{6,7},{7,6},{8,9},{9,8},{10,11... | collective-permute-start | bytes 245768 | tf_op jit(solution)/shard_map/ppermute | solution.py:223
  9.5 8.4 %collective-permute-start.8 = (f32[64,640]{1,0:T(8,128)S(1)}, f32[64,640]{1,0:T(8,128)S(1)}, u32[]{:S(2)}, u32[]{:S(2)}) collective-permute-start(f32[64,640]{1,0:T(8,128)S(1)} %get-tuple-element.32), channel_id=1, source_target_pairs={{0,1},{1,0},{2,3},{3,2},{4,5},{5,4},{6,7},{7,6},{8,9},{9,8},{10,11... | collective-permute-start | bytes 491528 | tf_op jit(solution)/shard_map/ppermute | solution.py:235
  10.8 12.5 %collective-permute-start.10 = (f32[64,640]{1,0:T(8,128)S(1)}, f32[64,640]{1,0:T(8,128)S(1)}, u32[]{:S(2)}, u32[]{:S(2)}) collective-permute-start(f32[64,640]{1,0:T(8,128)S(1)} %get-tuple-element.33), channel_id=1, source_target_pairs={{0,1},{1,0},{2,3},{3,2},{4,5},{5,4},{6,7},{7,6},{8,9},{9,8},{10,11... | collective-permute-start | bytes 491528 | tf_op jit(solution)/shard_map/ppermute | solution.py:238
  14.7 4.7 %collective-permute-start.5 = (bf16[64,640]{1,0:T(8,128)(2,1)S(1)}, bf16[64,640]{1,0:T(8,128)(2,1)S(1)}, u32[]{:S(2)}, u32[]{:S(2)}) collective-permute-start(bf16[64,640]{1,0:T(8,128)(2,1)S(1)} %get-tuple-element.24), channel_id=1, source_target_pairs={{0,12},{4,8},{8,4},{12,0},{1,13},{5,9},{9,5},{13,1},{2,14},{6,10},... | collective-permute-start | bytes 245768 | tf_op jit(solution)/shard_map/ppermute | solution.py:249
  14.7 6.2 %collective-permute-start.7 = (bf16[64,640]{1,0:T(8,128)(2,1)S(1)}, bf16[64,640]{1,0:T(8,128)(2,1)S(1)}, u32[]{:S(2)}, u32[]{:S(2)}) collective-permute-start(bf16[64,640]{1,0:T(8,128)(2,1)S(1)} %get-tuple-element.28), channel_id=1, source_target_pairs={{0,8},{4,12},{8,0},{12,4},{1,9},{5,13},{9,1},{13,5},{2,10},{6,14},... | collective-permute-start | bytes 245768 | tf_op jit(solution)/shard_map/ppermute | solution.py:251
  16.1 12.8 %collective-permute-start.11 = (f32[64,640]{1,0:T(8,128)S(1)}, f32[64,640]{1,0:T(8,128)S(1)}, u32[]{:S(2)}, u32[]{:S(2)}) collective-permute-start(f32[64,640]{1,0:T(8,128)S(1)} %odd.1), channel_id=1, source_target_pairs={{0,12},{4,8},{8,4},{12,0},{1,13},{5,9},{9,5},{13,1},{2,14},{6,10},... | collective-permute-start | bytes 491528 | tf_op jit(solution)/shard_map/ppermute | solution.py:263
  17.9 3.2 %collective-permute-start.6 = (bf16[128,640]{1,0:T(8,128)(2,1)S(1)}, bf16[128,640]{1,0:T(8,128)(2,1)S(1)}, u32[]{:S(2)}, u32[]{:S(2)}) collective-permute-start(bf16[128,640]{1,0:T(8,128)(2,1)S(1)} %get-tuple-element.27), channel_id=1, source_target_pairs={{0,4},{4,0},{8,12},{12,8},{1,5},{5,1},{9,13},{13,9},{2,6},{6,2},{1... | collective-permute-start | bytes 491528 | tf_op jit(solution)/shard_map/ppermute | solution.py:254
  19.4 9.6 %collective-permute-start.9 = (f32[64,640]{1,0:T(8,128)S(1)}, f32[64,640]{1,0:T(8,128)S(1)}, u32[]{:S(2)}, u32[]{:S(2)}) collective-permute-start(f32[64,640]{1,0:T(8,128)S(1)} %fold.1), channel_id=1, source_target_pairs={{0,2},{1,3},{2,0},{3,1},{4,6},{5,7},{6,4},{7,5},{8,10},{9,11},{10,... | collective-permute-start | bytes 491528 | tf_op jit(solution)/shard_map/ppermute | solution.py:237
  21.0 8.0 %collective-permute-start.12 = (f32[64,640]{1,0:T(8,128)S(1)}, f32[64,640]{1,0:T(8,128)S(1)}, u32[]{:S(2)}, u32[]{:S(2)}) collective-permute-start(f32[64,640]{1,0:T(8,128)S(1)} %get-tuple-element.35), channel_id=1, source_target_pairs={{0,4},{4,0},{8,12},{12,8},{1,5},{5,1},{9,13},{13,9},{2,6},{6,2},{1... | collective-permute-start | bytes 491528 | tf_op jit(solution)/shard_map/ppermute | solution.py:264
